TPU v7x, 32 devices: a whole 2x2x4 slice. The times are simulated.
32 devices in a mesh: rows: 8 (over z, y), tok: 4 (over x, core).
Axes of the slice: x: 2, y: 2, z: 4, core: 2. Of those that a mesh axis runs over, the one named last changes fastest.
Arguments:
- tokens: bfloat16 [2, 8, 512, 512], P(None, 'rows', 'tok'), may hold values from -6 to 6
- segments: int32 [2, 8, 512], P(None, 'rows', 'tok'), may hold values from 0 to 7, never falling along the last dimension, each value on 1 to 385 neighbouring positions
- cotangent: bfloat16 [2, 8, 512, 512], P(None, 'rows', 'tok'), may hold values from -6 to 6
- query_weight: bfloat16 [512, 512], replicated, may hold values from -0.25 to 0.25
- key_weight: bfloat16 [512, 512], replicated, may hold values from -0.25 to 0.25
- value_weight: bfloat16 [512, 512], replicated, may hold values from -0.25 to 0.25
- out_weight: bfloat16 [512, 512], replicated, may hold values from -2 to 2
- attend_gain: float32 [512], replicated, may hold values from 0.1 to 1.9
- attend_bias: float32 [512], replicated, may hold values from -4 to 4
- inner_weight: bfloat16 [512, 2048], replicated, may hold values from -0.25 to 0.25
- inner_bias: float32 [2048], replicated, may hold values from -6 to 6
- outer_weight: bfloat16 [2048, 512], replicated, may hold values from -0.125 to 0.125
- middle_gain: float32 [512], replicated, may hold values from 0.1 to 1.9
- middle_bias: float32 [512], replicated, may hold values from -4 to 4
- adapter_down: bfloat16 [512, 512], replicated, may hold values from -0.25 to 0.25
- adapter_up: bfloat16 [16, 32, 512], replicated, may hold values from -2 to 2
- joining_query: bfloat16 [512, 512], P('rows'), may hold values from -0.25 to 0.25
- joining_key: bfloat16 [512, 512], P('rows'), may hold values from -0.25 to 0.25
- joining_value: bfloat16 [512, 512], P('rows'), may hold values from -0.25 to 0.25
- final_gain: float32 [512], replicated, may hold values from 0.1 to 1.9
- final_bias: float32 [512], replicated, may hold values from -4 to 4
Outputs:
- output: bfloat16 [2, 8, 512, 512], P(None, 'rows', 'tok')
- input_grad: bfloat16 [2, 8, 512, 512], P(None, 'rows', 'tok')
- query_grad: float32 [512, 512], replicated
- key_grad: float32 [512, 512], replicated
- value_grad: float32 [512, 512], replicated
- out_grad: float32 [512, 512], replicated
- attend_gain_grad: float32 [512], replicated
- attend_bias_grad: float32 [512], replicated
- inner_grad: float32 [512, 2048], replicated
- inner_bias_grad: float32 [2048], replicated
- outer_grad: float32 [2048, 512], replicated
- middle_gain_grad: float32 [512], replicated
- middle_bias_grad: float32 [512], replicated
- joining_query_grad: float32 [512, 512], replicated
- joining_key_grad: float32 [512, 512], replicated
- joining_value_grad: float32 [512, 512], replicated
- final_gain_grad: float32 [512], replicated
- final_bias_grad: float32 [512], replicated
Inputs may be any that keep to these rules, and one draw needn't show every extreme that they name: `segments`: in every row the segment ids never fall and each document is a run of consecutive tokens; one document of every row has exactly 385 tokens.
All inputs are finite; a program needn't handle non-finite values.
Results may differ from a plain program's by a relative error of at most 0.03.
Values may be sent and summed in bfloat16 or wider, within the bound.
No kernel may reach another device: no remote copies, remote signals or barrier semaphores. Data moves between devices by JAX's collectives and lax.ppermute only.
A program may use at most 128 MiB of HBM per device.

v0:
```python
import jax
import jax.numpy as jnp
from jax import lax
from jax.sharding import PartitionSpec as P

HEAD = 64


norm_eps = 1e-06


def matmul(left_side, right_side):
    return jnp.dot(left_side, right_side, preferred_element_type=jnp.float32)


def matmul_tn(left_side, right_side):
    return lax.dot_general(
        left_side, right_side, (((0,), (0,)), ((), ())), preferred_element_type=jnp.float32
    )


def matmul_nt(left_side, right_side):
    return lax.dot_general(
        left_side, right_side, (((1,), (1,)), ((), ())), preferred_element_type=jnp.float32
    )


def rounded(values):
    return values.astype(jnp.bfloat16)


def normalize(values, norm_gain, norm_shift):
    row_mean = jnp.mean(values, -1, keepdims=True)
    centered = values - row_mean
    inv_std = lax.rsqrt(jnp.mean(centered * centered, -1, keepdims=True) + norm_eps)
    unit_value = centered * inv_std
    return (unit_value * norm_gain + norm_shift, unit_value, inv_std)


def normalize_back(upstream, unit_value, inv_std, norm_gain):
    grad_unit = upstream * norm_gain
    projected = grad_unit - jnp.mean(grad_unit, -1, keepdims=True)
    projected = projected - unit_value * jnp.mean(grad_unit * unit_value, -1, keepdims=True)
    return (projected * inv_std, jnp.sum(upstream * unit_value, 0), jnp.sum(upstream, 0))


def gelu_slope(values):
    normal_cdf = 0.5 * (1.0 + lax.erf(values * 0.7071067811865476))
    return normal_cdf + values * jnp.exp(-0.5 * values * values) * 0.3989422804014327


def attend_scores(queries, key_whole, seg_query, seg_key):
    scores = jnp.einsum(
        "bqhe,bkhe->bhqk", queries, key_whole, preferred_element_type=jnp.float32
    ) * HEAD ** (-0.5)
    same_doc = (seg_query[:, :, None] == seg_key[:, None, :])[:, None]
    return jnp.where(same_doc, scores, -1e30)


def per_device(
    tokens,
    segments,
    cotangent,
    query_weight,
    key_weight,
    value_weight,
    out_weight,
    attend_gain,
    attend_bias,
    inner_weight,
    inner_bias,
    outer_weight,
    middle_gain,
    middle_bias,
    adapter_down,
    adapter_up,
    joining_query,
    joining_key,
    joining_value,
    final_gain,
    final_bias,
):
    batches, row_count, local_len, model_width = tokens.shape
    head_count = model_width // HEAD
    adapters = adapter_up.shape[0]
    bottleneck = adapter_up.shape[1]
    join_scale = model_width ** (-0.5)
    row_segs = lax.all_gather(segments, "tok", axis=2, tiled=True)
    totals = None
    outputs = []
    input_grads = []
    for batch_index in range(batches):
        joining_whole = (
            lax.all_gather(joining_query, "rows", axis=0, tiled=True),
            lax.all_gather(joining_key, "rows", axis=0, tiled=True),
            lax.all_gather(joining_value, "rows", axis=0, tiled=True),
        )
        join_qw, join_kw, join_vw = joining_whole
        local_rows = tokens[batch_index]
        tok_flat = local_rows.reshape(-1, model_width)
        seg_query = segments[batch_index]
        seg_key = row_segs[batch_index]
        query_rows = rounded(matmul(tok_flat, query_weight))
        key_rows = rounded(matmul(tok_flat, key_weight)).reshape(row_count, local_len, model_width)
        value_rows = rounded(matmul(tok_flat, value_weight)).reshape(
            row_count, local_len, model_width
        )
        key_whole, value_whole = (
            lax.all_gather(key_rows, "tok", axis=1, tiled=True),
            lax.all_gather(value_rows, "tok", axis=1, tiled=True),
        )
        query_heads = query_rows.reshape(row_count, local_len, head_count, HEAD)
        key_heads = key_whole.reshape(row_count, -1, head_count, HEAD)
        value_heads = value_whole.reshape(row_count, -1, head_count, HEAD)
        scores = attend_scores(query_heads, key_heads, seg_query, seg_key)
        row_max = jnp.max(scores, -1, keepdims=True)
        exp_scores = jnp.exp(scores - row_max)
        row_total = jnp.sum(exp_scores, -1, keepdims=True)
        logsum = row_max + jnp.log(row_total)
        attn_probs = rounded(exp_scores / row_total)
        attended = rounded(
            jnp.einsum(
                "bhqk,bkhe->bqhe", attn_probs, value_heads, preferred_element_type=jnp.float32
            )
        ).reshape(-1, model_width)
        attn_out = matmul(attended, out_weight)
        first_norm, first_unit, first_scale = normalize(
            tok_flat.astype(jnp.float32) + attn_out, attend_gain, attend_bias
        )
        first_low = rounded(first_norm)
        inner_pre = matmul(first_low, inner_weight) + inner_bias
        active = rounded(jax.nn.gelu(inner_pre, approximate=False))
        outer_out = matmul(active, outer_weight)
        hidden, middle_unit, middle_scale = normalize(
            first_norm + outer_out, middle_gain, middle_bias
        )
        hidden_low = rounded(hidden)
        down_pre = matmul(hidden_low, adapter_down)
        bottle_act = rounded(jax.nn.gelu(down_pre, approximate=False)).reshape(
            -1, adapters, bottleneck
        )
        branch = jnp.einsum(
            "tnr,nrd->tnd", bottle_act, adapter_up, preferred_element_type=jnp.float32
        )
        adapted = rounded(hidden[:, None, :] + branch)
        join_query = rounded(matmul(hidden_low, join_qw))
        join_probe = rounded(matmul_nt(join_query, join_kw))
        join_scores = (
            jnp.einsum("tnd,td->tn", adapted, join_probe, preferred_element_type=jnp.float32)
            * join_scale
        )
        join_weights = jax.nn.softmax(join_scores, axis=-1)
        mix_low = rounded(join_weights)
        join_mixed = rounded(
            jnp.einsum("tn,tnd->td", mix_low, adapted, preferred_element_type=jnp.float32)
        )
        join_out = matmul(join_mixed, join_vw)
        final_norm, final_unit, final_scale = normalize(hidden + join_out, final_gain, final_bias)
        outputs.append(rounded(final_norm).reshape(local_rows.shape))
        grad_final = cotangent[batch_index].reshape(-1, model_width).astype(jnp.float32)
        grad_top, final_gain_term, final_bias_term = normalize_back(
            grad_final, final_unit, final_scale, final_gain
        )
        grad_joined = rounded(grad_top)
        joining_value_term = matmul_tn(join_mixed, grad_joined)
        grad_mixed = rounded(matmul_nt(grad_joined, join_vw))
        grad_mix = jnp.einsum("tnd,td->tn", adapted, grad_mixed, preferred_element_type=jnp.float32)
        grad_fscores = rounded(
            join_weights * (grad_mix - jnp.sum(join_weights * grad_mix, -1, keepdims=True))
        )
        grad_probe = rounded(
            jnp.einsum("tn,tnd->td", grad_fscores, adapted, preferred_element_type=jnp.float32)
            * join_scale
        )
        joining_key_term = matmul_tn(grad_probe, join_query)
        grad_fquery = rounded(matmul(grad_probe, join_kw))
        joining_query_term = matmul_tn(hidden_low, grad_fquery)
        grad_adapted = (
            mix_low.astype(jnp.float32)[:, :, None] * grad_mixed.astype(jnp.float32)[:, None, :]
            + (grad_fscores.astype(jnp.float32) * join_scale)[:, :, None]
            * join_probe.astype(jnp.float32)[:, None, :]
        )
        grad_branch = rounded(grad_adapted)
        grad_bottle = jnp.einsum(
            "tnd,nrd->tnr", grad_branch, adapter_up, preferred_element_type=jnp.float32
        ).reshape(-1, adapters * bottleneck)
        grad_down = rounded(grad_bottle * gelu_slope(down_pre))
        grad_hidden = (
            grad_top
            + jnp.sum(grad_adapted, 1)
            + matmul_nt(grad_fquery, join_qw)
            + matmul_nt(grad_down, adapter_down)
        )
        grad_middle, middle_gain_term, middle_bias_term = normalize_back(
            grad_hidden, middle_unit, middle_scale, middle_gain
        )
        grad_outer = rounded(grad_middle)
        outer_term = matmul_tn(active, grad_outer)
        grad_inner = rounded(matmul_nt(grad_outer, outer_weight) * gelu_slope(inner_pre))
        inner_term = matmul_tn(first_low, grad_inner)
        inner_bias_term = jnp.sum(grad_inner.astype(jnp.float32), 0)
        grad_first = grad_middle + matmul_nt(grad_inner, inner_weight)
        grad_start, attend_gain_term, attend_bias_term = normalize_back(
            grad_first, first_unit, first_scale, attend_gain
        )
        grad_attn = rounded(grad_start)
        out_term = matmul_tn(attended, grad_attn)
        grad_attended = rounded(matmul_nt(grad_attn, out_weight)).reshape(
            row_count, local_len, head_count, HEAD
        )
        scores_again = attend_scores(query_heads, key_heads, seg_query, seg_key)
        probs_again = jnp.exp(scores_again - logsum)
        value_term = jnp.einsum(
            "bhqk,bqhe->bkhe",
            rounded(probs_again),
            grad_attended,
            preferred_element_type=jnp.float32,
        )
        grad_probs = jnp.einsum(
            "bqhe,bkhe->bhqk", grad_attended, value_heads, preferred_element_type=jnp.float32
        )
        grad_scores = rounded(
            probs_again * (grad_probs - jnp.sum(probs_again * grad_probs, -1, keepdims=True))
        )
        grad_query = rounded(
            jnp.einsum(
                "bhqk,bkhe->bqhe", grad_scores, key_heads, preferred_element_type=jnp.float32
            )
            * HEAD ** (-0.5)
        ).reshape(-1, model_width)
        key_term = jnp.einsum(
            "bhqk,bqhe->bkhe", grad_scores, query_heads, preferred_element_type=jnp.float32
        ) * HEAD ** (-0.5)
        key_share, value_share = (
            lax.psum_scatter(
                key_term.reshape(row_count, -1, model_width).astype(jnp.bfloat16),
                "tok",
                scatter_dimension=1,
                tiled=True,
            ).astype(jnp.float32),
            lax.psum_scatter(
                value_term.reshape(row_count, -1, model_width).astype(jnp.bfloat16),
                "tok",
                scatter_dimension=1,
                tiled=True,
            ).astype(jnp.float32),
        )
        grad_key = rounded(key_share).reshape(-1, model_width)
        grad_value = rounded(value_share).reshape(-1, model_width)
        query_term = matmul_tn(tok_flat, grad_query)
        key_weight_term = matmul_tn(tok_flat, grad_key)
        value_weight_term = matmul_tn(tok_flat, grad_value)
        grad_input = (
            grad_start
            + matmul_nt(grad_query, query_weight)
            + matmul_nt(grad_key, key_weight)
            + matmul_nt(grad_value, value_weight)
        )
        input_grads.append(rounded(grad_input).reshape(local_rows.shape))
        batch_grads = (
            query_term,
            key_weight_term,
            value_weight_term,
            out_term,
            attend_gain_term,
            attend_bias_term,
            inner_term,
            inner_bias_term,
            outer_term,
            middle_gain_term,
            middle_bias_term,
            joining_query_term,
            joining_key_term,
            joining_value_term,
            final_gain_term,
            final_bias_term,
        )
        if totals is None:
            totals = batch_grads
        else:
            totals = jax.tree.map(jnp.add, totals, batch_grads)
    summed = lax.psum(
        (
            totals[0],
            totals[1],
            totals[2],
            totals[3],
            totals[4],
            totals[5],
            totals[6],
            totals[7],
            totals[8],
            totals[9],
            totals[10],
            totals[11],
            totals[12],
            totals[13],
            totals[14],
            totals[15],
        ),
        ("rows", "tok"),
    )
    return (jnp.stack(outputs), jnp.stack(input_grads)) + tuple(summed)


def solution(mesh):
    return jax.shard_map(
        per_device,
        mesh=mesh,
        in_specs=(
            P(None, "rows", "tok", None),
            P(None, "rows", "tok"),
            P(None, "rows", "tok", None),
            P(),
            P(),
            P(),
            P(),
            P(),
            P(),
            P(),
            P(),
            P(),
            P(),
            P(),
            P(),
            P(),
            P("rows", None),
            P("rows", None),
            P("rows", None),
            P(),
            P(),
        ),
        out_specs=(
            P(None, "rows", "tok", None),
            P(None, "rows", "tok", None),
            P(),
            P(),
            P(),
            P(),
            P(),
            P(),
            P(),
            P(),
            P(),
            P(),
            P(),
            P(),
            P(),
            P(),
            P(),
            P(),
        ),
        check_vma=False,
    )
```

profile of v0, /device:TPU:0, one launch (start us, length us, event | category | flops | bytes accessed | tf_op | source)
XLA Modules:
  0.0 662.7 jit_solution(11530024533407122883)
XLA Ops:
  7.3 1.3 slice_bitcast_fusion.1
  8.6 6.2 all_gather.28
  14.9 1.3 convolution_convert_fusion.11
  16.2 2.0 convolution_convert_fusion.16
  18.2 2.0 convolution_convert_fusion.10
  25.3 7.9 %all-gather = bf16[512,512]{1,0:T(8,128)(2,1)S(1)} all-gather(bf16[128,512]{1,0:T(8,128)(2,1)} %convolution_convert_fusion.17), channel_id=2, replica_groups=mesh['rows'=8,'tok'=4] {'tok'}, dimensions={0}, use_global_device_ids=true | all-gather | bytes 655360 | tf_op jit(solution)/shard_map/all_gather | solution.py:110
  34.1 7.3 %all-gather.2 = bf16[512,512]{1,0:T(8,128)(2,1)S(1)} all-gather(bf16[128,512]{1,0:T(8,128)(2,1)S(1)} %copy-done.113), channel_id=4, replica_groups=mesh['rows'=8,'tok'=4] {'tok'}, dimensions={0}, use_global_device_ids=true | all-gather | bytes 655360 | tf_op jit(solution)/shard_map/all_gather | solution.py:110
  42.4 7.3 %all-gather.1 = bf16[512,512]{1,0:T(8,128)(2,1)S(1)} all-gather(bf16[128,512]{1,0:T(8,128)(2,1)S(1)} %copy-done.112), channel_id=3, replica_groups=mesh['rows'=8,'tok'=4] {'tok'}, dimensions={0}, use_global_device_ids=true | all-gather | bytes 655360 | tf_op jit(solution)/shard_map/all_gather | solution.py:109
  50.7 7.3 %all-gather.3 = bf16[512,512]{1,0:T(8,128)(2,1)S(1)} all-gather(bf16[128,512]{1,0:T(8,128)(2,1)S(1)} %copy-done.111), channel_id=5, replica_groups=mesh['rows'=8,'tok'=4] {'tok'}, dimensions={0}, use_global_device_ids=true | all-gather | bytes 655360 | tf_op jit(solution)/shard_map/all_gather | solution.py:109
  58.2 32.7 %all_gather.30 = bf16[512,512]{1,0:T(8,128)(2,1)S(1)} all-gather(bf16[64,512]{1,0:T(8,128)(2,1)} %param.37), channel_id=1, replica_groups=mesh['rows'=8,'tok'=4] {'rows'}, dimensions={0}, use_global_device_ids=true | all-gather | bytes 589824 | tf_op jit(solution)/shard_map/all_gather | solution.py:94
  91.0 1.6 fusion.260
  95.0 3.8 fusion.56
  103.3 3.8 fusion.53
  108.8 1.4 fusion.103
  110.3 1.4 fusion.106
  111.7 31.6 %all_gather.31 = bf16[512,512]{1,0:T(8,128)(2,1)S(1)} all-gather(bf16[64,512]{1,0:T(8,128)(2,1)S(1)} %copy-done.129), channel_id=1, replica_groups=mesh['rows'=8,'tok'=4] {'rows'}, dimensions={0}, use_global_device_ids=true | all-gather | bytes 589824 | tf_op jit(solution)/shard_map/all_gather | solution.py:95
  143.3 33.4 %all_gather.32 = bf16[512,512]{1,0:T(8,128)(2,1)} all-gather(bf16[64,512]{1,0:T(8,128)(2,1)S(1)} %copy-done.130), channel_id=1, replica_groups=mesh['rows'=8,'tok'=4] {'rows'}, dimensions={0}, use_global_device_ids=true | all-gather | bytes 589824 | tf_op jit(solution)/shard_map/all_gather | solution.py:96
  179.9 1.7 copy.84
  181.5 3.3 fusion.21
  184.8 3.5 fusion.33
  191.0 3.1 fusion.31
  196.0 2.1 fusion.20
  198.1 2.9 fusion.41
  201.3 3.0 fusion.39
  205.0 1.5 fusion.96
  207.5 2.9 fusion.29
  210.6 2.9 fusion.8
  213.5 1.9 fusion.1
  216.5 2.9 fusion.37
  219.5 2.9 fusion.6
  222.4 1.4 fusion.3
  224.0 3.6 fusion.27
  227.7 3.0 fusion.35
  231.8 1.8 copy.87
  233.6 1.8 copy.85
  235.5 1.5 convolution_add_fusion.22
  237.1 2.4 multiply_reduce_fusion.3
  241.8 1.5 convert_reduce_fusion.1
  243.3 1.5 multiply_reduce_fusion.5
  245.0 1.5 convert_reduce_fusion
  246.5 2.2 multiply_reduce_fusion.4
  249.8 2.2 convolution_convert_fusion.1
  252.1 2.0 copy.112
  254.1 2.3 copy.168
  258.9 1.4 convolution_convert_fusion
  260.3 3.7 copy.116
  264.0 2.2 copy.166
  269.0 3.7 copy.114
  272.7 2.2 copy.167
  275.0 1.8 multiply_reduce_fusion.1
  280.6 1.4 fusion.190
  282.4 1.3 fusion.205
  287.4 1.4 convolution_add_fusion.4
  293.0 2.8 convolution_add_fusion.1
  297.1 2.8 convolution_add_fusion
  301.1 2.5 reduce-scatter.19.cloned.1.call-done
  304.8 23.5 %reduce-scatter.17.cloned.1.call-done = bf16[128,512]{1,0:T(8,128)(2,1)} async-done(((bf16[512,512]{1,0:T(8,128)(2,1)}), bf16[128,512]{1,0:T(8,128)(2,1)}) %reduce-scatter.17.cloned.1.call-update) | async-done | bytes 131088
  329.9 23.3 %reduce-scatter.13.cloned.1.call-done = bf16[128,512]{1,0:T(8,128)(2,1)} async-done(((bf16[512,512]{1,0:T(8,128)(2,1)}), bf16[128,512]{1,0:T(8,128)(2,1)}) %reduce-scatter.13.cloned.1.call-update) | async-done | bytes 131088
  358.1 41.6 %all-reduce = (f32[512]{0:T(512)}, f32[512]{0:T(512)}, f32[2048]{0:T(1024)}, f32[512]{0:T(512)}, f32[512]{0:T(512)}, /*index=5*/f32[512]{0:T(512)}, f32[512]{0:T(512)}) all-reduce(f32[512]{0:T(512)S(1)} %add.386, f32[512]{0:T(512)S(1)} %add.387, f32[2048]{0:T(1024)S(1)} %add.389, ...), channel_id=1, replica_groups=mesh['rows'=8,'tok'=4] {'rows','tok'}, use_global_device_ids=true, to_apply=%region_48.49 | all-reduce | flops 5120 | bytes 40960 | tf_op jit(solution)/shard_map/psum | solution.py:282
  403.1 236.2 %all-reduce.4.cloned.1.call-done = (f32[512,512]{0,1:T(8,128)}, f32[512,512]{0,1:T(8,128)}, f32[512,512]{0,1:T(8,128)}, f32[512,512]{1,0:T(8,128)}, f32[512,2048...) async-done(((f32[512,512]{0,1:T(8,128)}, f32[512,512]{0,1:T(8,128)}, f32[512,512]{0,1:T(8,128)}, ...) | async-done | bytes 15728656 | tf_op jit(solution)/shard_map/psum | solution.py:282
  639.3 2.7 copy.89
  642.0 1.3 copy.90
  645.6 4.8 copy.180
  650.4 2.0 copy.181
  (547 shorter events, 68.1 us)
Async XLA Ops:
  7.2 87.7 %copy-start = (bf16[512,2048]{1,0:T(8,128)(2,1)S(1)}, bf16[512,2048]{1,0:T(8,128)(2,1)}, u32[]{:S(2)}) copy-start(bf16[512,2048]{1,0:T(8,128)(2,1)} %param.30) | copy-start | bytes 6291460
  7.2 13.0 %copy-start.9 = (bf16[2,1,128,512]{3,2,1,0:T(8,128)(2,1)S(1)}, bf16[2,1,128,512]{3,2,1,0:T(8,128)(2,1)}, u32[]{:S(2)}) copy-start(bf16[2,1,128,512]{3,2,1,0:T(8,128)(2,1)} %param.21) | copy-start | bytes 786436
  7.2 13.0 %copy-start.30 = (bf16[512,512]{1,0:T(8,128)(2,1)S(1)}, bf16[512,512]{1,0:T(8,128)(2,1)}, u32[]{:S(2)}) copy-start(bf16[512,512]{1,0:T(8,128)(2,1)} %param.25) | copy-start | bytes 1572868
  7.2 13.9 %copy-start.32 = (bf16[512,512]{1,0:T(8,128)(2,1)S(1)}, bf16[512,512]{1,0:T(8,128)(2,1)}, u32[]{:S(2)}) copy-start(bf16[512,512]{1,0:T(8,128)(2,1)} %param.26) | copy-start | bytes 1572868
  7.2 292.6 %reduce-scatter.15.cloned.1.call-start = ((), (), s32[]{:S(2)}) async-start(), calls=%async_computation.5 | async-start | bytes 655360
  22.9 11.2 %copy-start.113 = (bf16[128,512]{1,0:T(8,128)(2,1)S(1)}, bf16[128,512]{1,0:T(8,128)(2,1)}, u32[]{:S(2)}) copy-start(bf16[128,512]{1,0:T(8,128)(2,1)} %convolution_convert_fusion.12) | copy-start | bytes 393220
  22.9 19.5 %copy-start.112 = (bf16[128,512]{1,0:T(8,128)(2,1)S(1)}, bf16[128,512]{1,0:T(8,128)(2,1)}, u32[]{:S(2)}) copy-start(bf16[128,512]{1,0:T(8,128)(2,1)} %convolution_convert_fusion.15) | copy-start | bytes 393220
  25.3 74.5 %copy-start.94 = (bf16[128,512]{0,1:T(8,128)(2,1)}, bf16[128,512]{0,1:T(8,128)(2,1)S(1)}, u32[]{:S(2)}) copy-start(bf16[128,512]{0,1:T(8,128)(2,1)S(1)} %copy.78) | copy-start | bytes 393220
  33.1 17.6 %copy-start.111 = (bf16[128,512]{1,0:T(8,128)(2,1)S(1)}, bf16[128,512]{1,0:T(8,128)(2,1)}, u32[]{:S(2)}) copy-start(bf16[128,512]{1,0:T(8,128)(2,1)} %convolution_convert_fusion.10) | copy-start | bytes 393220
  58.2 35.1 %copy-start.51 = (bf16[512,512]{0,1:T(8,128)(2,1)}, bf16[512,512]{0,1:T(8,128)(2,1)S(1)}, u32[]{:S(2)}) copy-start(bf16[512,512]{0,1:T(8,128)(2,1)S(1)} %copy.83) | copy-start | bytes 1572868
  94.1 4.6 copy-start.114
  94.7 4.1 copy-start.19
  94.7 4.1 copy-start.145
  99.4 8.6 %copy-start.41 = (f32[128,512]{1,0:T(8,128)}, f32[128,512]{1,0:T(8,128)S(1)}, u32[]{:S(2)}) copy-start(f32[128,512]{1,0:T(8,128)S(1)} %get-tuple-element.147) | copy-start | bytes 786436
  99.4 8.5 %copy-start.161 = (f32[128]{0:T(128)}, f32[128]{0:T(128)S(1)}, u32[]{:S(2)}) copy-start(f32[128]{0:T(128)S(1)} %broadcast_multiply_fusion.13) | copy-start | bytes 1540
  99.6 8.3 %copy-start.186 = (f32[128]{0:T(128)}, f32[128]{0:T(128)S(1)}, u32[]{:S(2)}) copy-start(f32[128]{0:T(128)S(1)} %add_rsqrt_fusion.1) | copy-start | bytes 1540
  102.7 4.4 copy-start.118
  103.1 4.0 copy-start.22
  103.1 4.0 copy-start.148
  108.4 69.4 %copy-start.97 = (bf16[128,512]{1,0:T(8,128)(2,1)}, bf16[128,512]{1,0:T(8,128)(2,1)S(1)}, u32[]{:S(2)}) copy-start(bf16[128,512]{1,0:T(8,128)(2,1)S(1)} %convolution_convert_fusion.14) | copy-start | bytes 393220
  108.8 67.9 %copy-start.83 = (bf16[128,512]{1,0:T(8,128)(2,1)}, bf16[128,512]{1,0:T(8,128)(2,1)S(1)}, u32[]{:S(2)}) copy-start(bf16[128,512]{1,0:T(8,128)(2,1)S(1)} %convolution_convert_fusion.9) | copy-start | bytes 393220
  110.3 33.0 %copy-start.130 = (bf16[64,512]{1,0:T(8,128)(2,1)S(1)}, bf16[64,512]{1,0:T(8,128)(2,1)}, u32[]{:S(2)}) copy-start(bf16[64,512]{1,0:T(8,128)(2,1)} %param.39) | copy-start | bytes 196612
  191.0 4.9 copy-start.46
  191.0 4.9 copy-start.78
  201.0 3.9 copy-start.191
  204.7 10.7 %copy-start.141 = (f32[128]{0:T(128)}, f32[128]{0:T(128)S(1)}, u32[]{:S(2)}) copy-start(f32[128]{0:T(128)S(1)} %broadcast_multiply_fusion.15) | copy-start | bytes 1540
  204.9 10.5 %copy-start.153 = (f32[128]{0:T(128)}, f32[128]{0:T(128)S(1)}, u32[]{:S(2)}) copy-start(f32[128]{0:T(128)S(1)} %add_rsqrt_fusion.3) | copy-start | bytes 1540
  206.5 4.0 copy-start.157
  210.6 4.8 copy-start.8
  210.6 4.8 copy-start.17
  210.6 4.8 copy-start.35
  215.4 4.0 copy-start.159
  215.4 4.0 copy-start.160
  230.7 6.4 copy-start.135
  233.6 5.9 copy-start.14
  233.6 5.9 copy-start.36
  233.6 5.9 copy-start.139
  235.5 4.0 copy-start.110
  249.8 4.3 copy-start.98
  252.0 4.6 copy-start.194
  252.0 4.6 copy-start.193
  254.1 4.8 copy-start.3
  256.4 47.2 %reduce-scatter.19.cloned.1.call-start = ((), (), s32[]{:S(2)}) async-start(), calls=%async_computation.7 | async-start | bytes 655360
  257.8 6.2 copy-start.53
  260.3 6.0 copy-start.73
  266.2 62.2 %reduce-scatter.17.cloned.1.call-start = ((), (), s32[]{:S(2)}) async-start(), calls=%async_computation.6 | async-start | bytes 655360
  269.0 6.0 copy-start.5
  274.9 78.3 %reduce-scatter.13.cloned.1.call-start = ((), (), s32[]{:S(2)}) async-start(), calls=%async_computation.4 | async-start | bytes 655360
  280.5 358.8 %all-reduce.4.cloned.1.call-start = ((), (), s32[]{:S(2)}) async-start(), calls=%async_computation.8 | async-start | bytes 31457280 | tf_op jit(solution)/shard_map/psum | solution.py:282
  284.6 11.2 %copy-start.86 = (bf16[8,64,128]{2,1,0:T(8,128)(2,1)}, bf16[8,64,128]{2,1,0:T(8,128)(2,1)S(1)}, u32[]{:S(2)}) copy-start(bf16[8,64,128]{2,1,0:T(8,128)(2,1)S(1)} %fusion.48) | copy-start | bytes 393220
  285.1 7.5 %copy-start.88 = (bf16[8,64,128]{2,1,0:T(8,128)(2,1)}, bf16[8,64,128]{2,1,0:T(8,128)(2,1)S(1)}, u32[]{:S(2)}) copy-start(bf16[8,64,128]{2,1,0:T(8,128)(2,1)S(1)} %fusion.47) | copy-start | bytes 393220
  301.1 53.6 %copy-start.90 = (bf16[1,128,512]{1,2,0:T(8,128)(2,1)}, bf16[1,128,512]{1,2,0:T(8,128)(2,1)S(1)}, u32[]{:S(2)}) copy-start(bf16[1,128,512]{1,2,0:T(8,128)(2,1)S(1)} %copy.113) | copy-start | bytes 393220
  304.8 49.9 %copy-start.92 = (bf16[1,128,512]{1,2,0:T(8,128)(2,1)}, bf16[1,128,512]{1,2,0:T(8,128)(2,1)S(1)}, u32[]{:S(2)}) copy-start(bf16[1,128,512]{1,2,0:T(8,128)(2,1)S(1)} %copy.117) | copy-start | bytes 393220
  357.3 42.3 %copy-start.116 = (bf16[1,1,128,512]{3,2,1,0:T(8,128)(2,1)S(1)}, bf16[1,1,128,512]{3,2,1,0:T(8,128)(2,1)}, u32[]{:S(2)}) copy-start(bf16[1,1,128,512]{3,2,1,0:T(8,128)(2,1)} %get-tuple-element.118) | copy-start | bytes 393220
  357.3 42.3 %copy-start.117 = (bf16[1,1,128,512]{3,2,1,0:T(8,128)(2,1)S(1)}, bf16[1,1,128,512]{3,2,1,0:T(8,128)(2,1)}, u32[]{:S(2)}) copy-start(bf16[1,1,128,512]{3,2,1,0:T(8,128)(2,1)} %get-tuple-element.119) | copy-start | bytes 393220
  357.4 43.0 %copy-start.29 = (bf16[512,512]{1,0:T(8,128)(2,1)S(1)}, bf16[512,512]{1,0:T(8,128)(2,1)}, u32[]{:S(2)}) copy-start(bf16[512,512]{1,0:T(8,128)(2,1)} %param.24) | copy-start | bytes 1572868
  357.4 43.0 %copy-start.87 = (bf16[8,64,128]{2,1,0:T(8,128)(2,1)S(1)}, bf16[8,64,128]{2,1,0:T(8,128)(2,1)}, u32[]{:S(2)}) copy-start(bf16[8,64,128]{2,1,0:T(8,128)(2,1)} %copy-done.86) | copy-start | bytes 393220
  357.4 43.3 %copy-start.58 = (f32[128,512]{1,0:T(8,128)S(1)}, f32[128,512]{1,0:T(8,128)}, u32[]{:S(2)}) copy-start(f32[128,512]{1,0:T(8,128)} %copy-done.56) | copy-start | bytes 786436
  357.4 43.3 %copy-start.89 = (bf16[8,64,128]{2,1,0:T(8,128)(2,1)S(1)}, bf16[8,64,128]{2,1,0:T(8,128)(2,1)}, u32[]{:S(2)}) copy-start(bf16[8,64,128]{2,1,0:T(8,128)(2,1)} %copy-done.88) | copy-start | bytes 393220
  357.4 43.6 %copy-start.31 = (bf16[512,512]{1,0:T(8,128)(2,1)S(1)}, bf16[512,512]{1,0:T(8,128)(2,1)}, u32[]{:S(2)}) copy-start(bf16[512,512]{1,0:T(8,128)(2,1)} %param.25) | copy-start | bytes 1572868
  357.5 43.9 %copy-start.33 = (bf16[512,512]{1,0:T(8,128)(2,1)S(1)}, bf16[512,512]{1,0:T(8,128)(2,1)}, u32[]{:S(2)}) copy-start(bf16[512,512]{1,0:T(8,128)(2,1)} %param.26) | copy-start | bytes 1572868
  357.5 43.9 %copy-start.93 = (bf16[1,128,512]{1,2,0:T(8,128)(2,1)S(1)}, bf16[1,128,512]{1,2,0:T(8,128)(2,1)}, u32[]{:S(2)}) copy-start(bf16[1,128,512]{1,2,0:T(8,128)(2,1)} %copy-done.92) | copy-start | bytes 393220
  639.3 4.0 copy-start.106
  645.6 4.9 copy-start.55
  (139 other events, 279.4 us)
Sparse Core Ops, SparseCore 0:
  256.5 22.6 reduce-scatter.14
  281.9 21.6 reduce-scatter.18
  306.7 21.6 reduce-scatter.16
  331.4 21.6 reduce-scatter.12
  360.6 278.6 all-reduce.3
where the time goes:
time: 667 us; the launch traced here: 663 us
  waiting for transfers between devices  286 us (43%)
  blocking collectives  175 us (26%)
  matrix products  110 us (16%)
  local copies, waits for them, and re-layouts  61.4 us (9%)
  between operations  16.5 us (2%)
  other arithmetic  13.6 us (2%)
    psum x1, waiting for transfers between devices, per_device(): lax.psum((totals[0], totals[1], totals[2], totals[3], totals[4], totals[5...  236 us
    unnamed x9, waiting for transfers between devices  49.5 us
    unnamed x421, local copies, waits for them, and re-layouts  45.8 us
    psum x1, blocking collectives, per_device(): lax.psum((totals[0], totals[1], totals[2], totals[3], totals[4], totals[5...  41.6 us
    all_gather x1, blocking collectives, per_device(): lax.all_gather(joining_value, 'rows', axis=0, tiled=True)  33.4 us
    all_gather x1, blocking collectives, per_device(): lax.all_gather(joining_query, 'rows', axis=0, tiled=True)  32.7 us
    all_gather x1, blocking collectives, per_device(): lax.all_gather(joining_key, 'rows', axis=0, tiled=True)  31.6 us
    dot_general x20, matrix products, matmul(): return jnp.dot(left_side, right_side, preferred_element_type=jnp.float32)  22.4 us
  transfers between devices with their start and end apart: 5, of which 4 were waited for; matrix products, arithmetic and copies ran while one was open for 7% of the time, Pallas kernels for 0%

commit v1 on v0

v1 whole, which is shorter than its diff:
```python
import functools

import jax
import jax.numpy as jnp
from jax import lax
from jax.experimental import pallas as pl
from jax.experimental.pallas import tpu as pltpu
from jax.sharding import PartitionSpec as P

HEAD = 64
AXES = ("rows", "tok")
BF = jnp.bfloat16
F32 = jnp.float32
norm_eps = 1e-06

ORDER_XY = ((1, 2, 3, 4), (2, 1, 4, 3))
ORDER_Z = ((3, 4, 1, 2), (4, 3, 2, 1))
ORDER_JOIN = ((2, 3, 4), (2, 4, 3))
GROUP = 32
HALF = GROUP // 2

VM = pl.BlockSpec(memory_space=pltpu.VMEM)
ANY = pl.BlockSpec(memory_space=pl.ANY)


def dot(left, right):
    return jnp.dot(left, right, preferred_element_type=F32)


def dot_tn(left, right):
    return lax.dot_general(left, right, (((0,), (0,)), ((), ())), preferred_element_type=F32)


def dot_nt(left, right):
    return lax.dot_general(left, right, (((1,), (1,)), ((), ())), preferred_element_type=F32)


def low(values):
    return values.astype(BF)


def normalize(values, gain, shift):
    centered = values - jnp.mean(values, -1, keepdims=True)
    inv_std = lax.rsqrt(jnp.mean(centered * centered, -1, keepdims=True) + norm_eps)
    unit = centered * inv_std
    return unit * gain + shift, unit, inv_std


def normalize_back(upstream, unit, inv_std, gain):
    grad_unit = upstream * gain
    projected = grad_unit - jnp.mean(grad_unit, -1, keepdims=True)
    projected = projected - unit * jnp.mean(grad_unit * unit, -1, keepdims=True)
    gain_term = jnp.sum(upstream * unit, 0, keepdims=True)
    return projected * inv_std, gain_term, jnp.sum(upstream, 0, keepdims=True)


def gelu_both(values):
    normal_cdf = 0.5 * (1.0 + lax.erf(values * 0.7071067811865476))
    slope = normal_cdf + values * jnp.exp(-0.5 * values * values) * 0.3989422804014327
    return values * normal_cdf, slope


def device_number():
    return lax.axis_index("rows") * 4 + lax.axis_index("tok")


def bit_of(number, bit):
    return lax.rem(lax.div(number, 1 << bit), 2)


def own_place(number, orders, core):
    def along(order):
        total = 0
        for bit in order:
            total = total * 2 + bit_of(number, bit)
        return total

    return jnp.where(core == 0, along(orders[0]), along(orders[1]))


def block_copies(full, keep, send, sems, orders, rows_each):
    me = device_number()
    core = bit_of(me, 0)
    copies = []
    for which, target in ((0, keep), (1, send)):
        half = core if which == 0 else 1 - core
        place = own_place(me, orders, half)
        for spot in range(HALF):
            block = half * HALF + jnp.bitwise_xor(place, spot)
            source = full.at[pl.ds(pl.multiple_of(block * rows_each, rows_each), rows_each), :]
            copies.append(
                pltpu.make_async_copy(
                    source, target.at[pl.ds(spot * rows_each, rows_each), :], sems.at[which, spot]
                )
            )
    return copies


def forward_kernel(
    x0, x1, x2, x3, seg_own, seg_sib, wq, wk, wv, wo, wi, wu, wd, ag, ab, bi, mg, mb,
    qs_ref, k_ref, v_ref, p_ref, o_ref, n1_ref, rs1_ref, al_ref, u_ref, sz_ref,
    n2_ref, rs2_ref, h_ref, c_ref, st_ref, bias,
):
    pieces = (x0, x1, x2, x3)
    tokens_here, width = x0.shape
    batches = seg_own.shape[0] // 2
    length = tokens_here // batches
    qs_ref[...] = low(low(dot(x0[...], wq[...])) * HEAD ** (-0.5))
    for index, piece in enumerate(pieces):
        k_ref[pl.ds(index * tokens_here, tokens_here), :] = low(dot(piece[...], wk[...]))
        v_ref[pl.ds(index * tokens_here, tokens_here), :] = low(dot(piece[...], wv[...]))
    own = seg_own[...].astype(F32)
    sib = seg_sib[...].astype(F32)
    lane = lax.broadcasted_iota(jnp.int32, (1, 2 * HEAD), 1)
    first = (lane < HEAD).astype(BF)
    second = (lane >= HEAD).astype(BF)
    for batch in range(batches):
        query_seg = own[batch : batch + 1, :]
        rows = (
            own[batch : batch + 1, :],
            sib[batch : batch + 1, :],
            own[batches + batch : batches + batch + 1, :],
            sib[batches + batch : batches + batch + 1, :],
        )
        for index, row in enumerate(rows):
            key_seg = jnp.transpose(jnp.broadcast_to(row, (length, length)))
            bias[pl.ds(index * length, length), :] = jnp.where(key_seg == query_seg, 0.0, -1e30)
        both = jnp.concatenate([bias[...], bias[...]], 1)
        for pair in range(width // (2 * HEAD)):
            lanes = slice(pair * 2 * HEAD, (pair + 1) * 2 * HEAD)
            spans = [
                slice(index * tokens_here + batch * length, index * tokens_here + (batch + 1) * length)
                for index in range(4)
            ]
            kp = jnp.concatenate([k_ref[span, lanes] for span in spans], 0)
            vp = jnp.concatenate([v_ref[span, lanes] for span in spans], 0)
            qp = qs_ref[batch * length : (batch + 1) * length, lanes]
            stacked = jnp.concatenate([qp * first, qp * second], 0)
            scores = dot_nt(kp, stacked) + both
            exps = jnp.exp(scores - jnp.max(scores, 0, keepdims=True))
            probs = low(exps * (1.0 / jnp.sum(exps, 0, keepdims=True)))
            p_ref[batch * (width // (2 * HEAD)) + pair] = probs
            mixed = dot_tn(vp, probs)
            joined = jnp.concatenate([mixed[:HEAD, :length], mixed[HEAD:, length:]], 0)
            o_ref[batch * length : (batch + 1) * length, lanes] = low(jnp.transpose(joined))
    residual = x0[...].astype(F32) + dot(o_ref[...], wo[...])
    first_norm, unit, inv_std = normalize(residual, ag[...], ab[...])
    n1_ref[...] = unit
    rs1_ref[...] = jnp.broadcast_to(inv_std, rs1_ref.shape)
    al = low(first_norm)
    al_ref[...] = al
    outer = first_norm
    for part in range(wi.shape[1] // width):
        span = slice(part * width, (part + 1) * width)
        inner = dot(al, wi[:, span]) + bi[:, span]
        active, slope = gelu_both(inner)
        u_ref[:, span] = low(active)
        sz_ref[:, span] = low(slope)
        outer = outer + dot(low(active), wu[span, :])
    hidden, unit, inv_std = normalize(outer, mg[...], mb[...])
    n2_ref[...] = unit
    rs2_ref[...] = jnp.broadcast_to(inv_std, rs2_ref.shape)
    h_ref[...] = hidden
    active, slope = gelu_both(dot(low(hidden), wd[...]))
    c_ref[...] = low(active)
    st_ref[...] = low(slope)


def joining_kernel(
    gathered, bottleneck, adapters, h_ref, c_ref, st_ref, up, cot, fg, fb, *rest
):
    if gathered:
        jw_in, rest = rest[:4], rest[4:]
    else:
        jw_in, rest = rest[:1], rest[1:]
    out_ref, keep, send, dhp_ref, dt_ref, vec_ref, wj, full, sems, jsems = rest
    width = h_ref.shape[1]
    scale = width ** (-0.5)
    me = device_number()
    core = bit_of(me, 0)
    loads = []
    if gathered:
        shard = jw_in[0].shape[2]
        column = jw_in[0].shape[3]
        for which in range(2):
            half = core if which == 0 else 1 - core
            place = own_place(me, tuple(order[::-1] for order in ORDER_JOIN), half)
            for spot in range(8):
                mixed = jnp.bitwise_xor(place, spot)
                swapped = (
                    lax.rem(mixed, 2)
                    + lax.rem(lax.div(mixed, 2), 2) * 4
                    + lax.rem(lax.div(mixed, 4), 2) * 2
                )
                owner = jnp.where(half == 0, mixed, swapped)
                target = wj.at[
                    :,
                    pl.ds(pl.multiple_of(owner * shard, shard), shard),
                    pl.ds(pl.multiple_of(half * column, column), column),
                ]
                source = jw_in[which * 2 + spot // 4].at[spot % 4]
                loads.append(pltpu.make_async_copy(source, target, jsems.at[which, spot]))
    else:
        loads.append(pltpu.make_async_copy(jw_in[0], wj, jsems.at[0, 0]))
    for load in loads:
        load.start()
    hidden = h_ref[...]
    hidden_low = low(hidden)
    cf = c_ref[...].astype(F32)
    row_group = lax.broadcasted_iota(jnp.int32, (width, 128), 0) // bottleneck
    column_of = lax.broadcasted_iota(jnp.int32, (width, 128), 1)
    member = (row_group == column_of).astype(BF)
    valid = lax.broadcasted_iota(jnp.int32, (1, 128), 1) < adapters

    def per_adapter(values):
        high = low(values)
        rest_of = low(values - high.astype(F32))
        return dot(high, member) + dot(rest_of, member)

    for load in loads:
        load.wait()
    fq = low(dot(hidden_low, wj[0]))
    probe = low(dot_nt(fq, wj[1]))
    probe_f = probe.astype(F32)
    up_probe = dot_nt(probe, up[...])
    scores = (
        per_adapter(cf * up_probe) + jnp.sum(hidden * probe_f, -1, keepdims=True)
    ) * scale
    scores = jnp.where(valid, scores, -1e30)
    exps = jnp.exp(scores - jnp.max(scores, -1, keepdims=True))
    weights = exps * (1.0 / jnp.sum(exps, -1, keepdims=True))
    weights_low = low(weights)
    weights_wide = dot_nt(weights_low, member)
    weights_sum = jnp.sum(weights_low.astype(F32), -1, keepdims=True)
    mixed = low(weights_sum * hidden + dot(low(weights_wide * cf), up[...]))
    final, unit, inv_std = normalize(hidden + dot(mixed, wj[2]), fg[...], fb[...])
    out_ref[...] = low(final)
    d3, gain_term, shift_term = normalize_back(cot[...].astype(F32), unit, inv_std, fg[...])
    vec_ref[...] = jnp.concatenate(
        [gain_term, shift_term, jnp.zeros((vec_ref.shape[0] - 2, width), F32)], 0
    )
    dfo = low(d3)
    full[2 * width : 3 * width, :] = low(dot_tn(mixed, dfo))
    dm = low(dot_nt(dfo, wj[2]))
    dm_f = dm.astype(F32)
    up_dm = dot_nt(dm, up[...])
    dw = per_adapter(cf * up_dm) + jnp.sum(hidden * dm_f, -1, keepdims=True)
    df = low(weights * (dw - jnp.sum(weights * dw, -1, keepdims=True)))
    df_wide = dot_nt(df, member)
    df_sum = jnp.sum(df.astype(F32), -1, keepdims=True)
    dr = low((df_sum * hidden + dot(low(df_wide * cf), up[...])) * scale)
    full[width : 2 * width, :] = low(dot_tn(dr, fq))
    dfq = low(dot(dr, wj[1]))
    full[:width, :] = low(dot_tn(hidden_low, dfq))
    copies = block_copies(full, keep, send, sems, ORDER_XY, 3 * width // GROUP)
    for copy in copies:
        copy.start()
    dc = weights_wide * up_dm + (df_wide * scale) * up_probe
    dt_ref[...] = low(dc * st_ref[...].astype(F32))
    dhp_ref[...] = (
        d3 + weights_sum * dm_f + (df_sum * scale) * probe_f + dot_nt(dfq, wj[0])
    )
    for copy in copies:
        copy.wait()


def feed_back_kernel(
    dhp_ref, dt_ref, wd, n2_ref, rs2_ref, mg, u_ref, sz_ref, wi, wu, al_ref, n1_ref, rs1_ref, ag, vec_in,
    d1_ref, vec_ref, keep_u, send_u, keep_i, send_i, full_u, full_i, sems_u, sems_i,
):
    width = dhp_ref.shape[1]
    hidden_grad = dhp_ref[...] + dot_nt(dt_ref[...], wd[...])
    d2, mg_term, mb_term = normalize_back(hidden_grad, n2_ref[...], rs2_ref[:, :1], mg[...])
    dfw = low(d2)
    al = al_ref[...]
    total = d2
    bias_terms = []
    parts = wi.shape[1] // width
    for part in range(parts):
        span = slice(part * width, (part + 1) * width)
        full_u[span, :] = low(dot_tn(u_ref[:, span], dfw))
        dz_wide = dot_nt(dfw, wu[span, :]) * sz_ref[:, span].astype(F32)
        dz = low(dz_wide)
        bias_terms.append(jnp.sum(dz.astype(F32), 0, keepdims=True))
        full_i[span, :] = low(dot_tn(al, dz))
        total = total + dot_nt(dz, wi[:, span])
    copies = block_copies(full_u, keep_u, send_u, sems_u, ORDER_XY, parts * width // GROUP)
    copies += block_copies(full_i, keep_i, send_i, sems_i, ORDER_Z, parts * width // GROUP)
    for copy in copies:
        copy.start()
    d1, ag_term, ab_term = normalize_back(total, n1_ref[...], rs1_ref[:, :1], ag[...])
    d1_ref[...] = d1
    rows = [ag_term, ab_term, mg_term, mb_term, vec_in[0:1, :], vec_in[1:2, :]] + bias_terms
    rows.append(jnp.zeros((vec_ref.shape[0] - len(rows), width), F32))
    vec_ref[...] = jnp.concatenate(rows, 0)
    for copy in copies:
        copy.wait()


def attend_back_kernel(
    d1_ref, wo, o_ref, qs_ref, k_ref, v_ref, p_ref, x0, x1, x2, x3, wq, wk, wv, vec_ref,
    keep, send, gi_own, gi_keep, gi_send, full, dq_scr, dk_scr, dv_scr, do_scr, vec_scr, sems, vsems,
):
    tokens_here, width = x0.shape
    length = p_ref.shape[2] // 2
    batches = tokens_here // length
    pairs = width // (2 * HEAD)
    d1 = d1_ref[...]
    dao = low(d1)
    full[3 * width : 4 * width, :] = low(dot_tn(o_ref[...], dao))
    do_scr[...] = low(dot_nt(dao, wo[...]))
    vec_scr[...] = low(vec_ref[...])
    lane = lax.broadcasted_iota(jnp.int32, (1, 2 * HEAD), 1)
    first = (lane < HEAD).astype(BF)
    second = (lane >= HEAD).astype(BF)
    for batch in range(batches):
        here = slice(batch * length, (batch + 1) * length)
        spans = [
            slice(index * tokens_here + batch * length, index * tokens_here + (batch + 1) * length)
            for index in range(4)
        ]
        for pair in range(pairs):
            lanes = slice(pair * 2 * HEAD, (pair + 1) * 2 * HEAD)
            kp = jnp.concatenate([k_ref[span, lanes] for span in spans], 0)
            vp = jnp.concatenate([v_ref[span, lanes] for span in spans], 0)
            qp = qs_ref[here, lanes]
            dop = do_scr[here, lanes]
            q_stacked = jnp.concatenate([qp * first, qp * second], 0)
            do_stacked = jnp.concatenate([dop * first, dop * second], 0)
            probs = p_ref[batch * pairs + pair]
            weighted = probs.astype(F32) * dot_nt(vp, do_stacked)
            ds = low(weighted - probs.astype(F32) * jnp.sum(weighted, 0, keepdims=True))
            dv = low(dot(probs, do_stacked))
            dk = low(dot(ds, q_stacked))
            for index, span in enumerate(spans):
                rows = slice(index * length, (index + 1) * length)
                dk_scr[span, lanes] = dk[rows, :]
                dv_scr[span, lanes] = dv[rows, :]
            mixed = dot_tn(kp, ds)
            joined = jnp.concatenate([mixed[:HEAD, :length], mixed[HEAD:, length:]], 0)
            dq_scr[here, lanes] = low(jnp.transpose(joined) * HEAD ** (-0.5))
    row_x = jnp.concatenate([x0[...], x1[...], x2[...], x3[...]], 0)
    full[:width, :] = low(dot_tn(x0[...], dq_scr[...]))
    full[width : 2 * width, :] = low(dot_tn(row_x, dk_scr[...]))
    full[2 * width : 3 * width, :] = low(dot_tn(row_x, dv_scr[...]))
    rows_each = 4 * width // GROUP
    copies = block_copies(full, keep, send, sems, ORDER_XY, rows_each)
    for index, target in enumerate((keep, send)):
        spot = target.at[pl.ds(HALF * rows_each, vec_scr.shape[0]), :]
        copies.append(pltpu.make_async_copy(vec_scr, spot, vsems.at[index]))
    for copy in copies:
        copy.start()
    parts = []
    for index in range(4):
        span = slice(index * tokens_here, (index + 1) * tokens_here)
        parts.append(dot_nt(dk_scr[span, :], wk[...]) + dot_nt(dv_scr[span, :], wv[...]))
    gi_own[...] = parts[0] + d1 + dot_nt(dq_scr[...], wq[...])
    gi_keep[...] = low(parts[2])
    gi_send[:tokens_here, :] = low(parts[1])
    gi_send[tokens_here:, :] = low(parts[3])
    for copy in copies:
        copy.wait()


def finish_kernel(orders, columns, with_vec, a8, r1, s8, sr1, *rest):
    if with_vec:
        vec, rest = rest[0], rest[1:]
    full, sems = rest[-2:]
    outs = rest[:-2]
    me = device_number()
    core = bit_of(me, 0)
    each = a8.shape[0] // (HALF // 2)
    for which, (lower, upper) in enumerate(((a8, r1), (s8, sr1))):
        half = core if which == 0 else 1 - core
        place = own_place(me, orders, half)
        for spot in range(HALF):
            source = lower if spot < HALF // 2 else upper
            begin = (spot % (HALF // 2)) * each
            block = half * HALF + jnp.bitwise_xor(place, spot)
            full[pl.ds(pl.multiple_of(block * each, each), each), :] = source[
                begin : begin + each, :
            ].astype(F32)
    width = full.shape[1]
    copies = []
    if columns:
        out = outs[0]
        for part in range(full.shape[0] // width):
            copies.append(
                pltpu.make_async_copy(
                    full.at[pl.ds(part * width, width), :],
                    out.at[:, pl.ds(part * width, width)],
                    sems.at[part],
                )
            )
    else:
        begin = 0
        count = 0
        for out in outs:
            if len(out.shape) == 2 and out.shape[0] >= width:
                copies.append(
                    pltpu.make_async_copy(full.at[pl.ds(begin, out.shape[0]), :], out, sems.at[count])
                )
                begin += out.shape[0]
                count += 1
    for copy in copies:
        copy.start()
    if with_vec:
        values = vec[...].astype(F32)
        small = [out for out in outs if out.shape[0] == 1]
        for index in range(6):
            small[index][...] = values[index : index + 1, :]
        for part in range(small[6].shape[1] // width):
            small[6][:, part * width : (part + 1) * width] = values[6 + part : 7 + part, :]
    for copy in copies:
        copy.wait()


def call(kernel, name, out_shapes, out_specs, in_specs, scratch, *operands):
    return pl.pallas_call(
        kernel,
        out_shape=out_shapes,
        in_specs=in_specs,
        out_specs=out_specs,
        scratch_shapes=scratch,
        compiler_params=pltpu.CompilerParams(vmem_limit_bytes=50 * 1024 * 1024),
        name=name,
    )(*operands)


def shape(dims, kind=BF):
    return jax.ShapeDtypeStruct(dims, kind)


def per_device(
    row_total,
    tokens, segments, cotangent, query_weight, key_weight, value_weight, out_weight,
    attend_gain, attend_bias, inner_weight, inner_bias, outer_weight, middle_gain, middle_bias,
    adapter_down, adapter_up, joining_query, joining_key, joining_value, final_gain, final_bias,
):
    batches, row_count, length, width = tokens.shape
    here = batches * row_count * length
    hidden_units = inner_weight.shape[1]
    adapters, bottleneck = adapter_up.shape[0], adapter_up.shape[1]
    devices = row_total * 4
    pairs = width // (2 * HEAD)

    def swap(values, partner):
        return lax.ppermute(values, AXES, [(d, partner(d)) for d in range(devices)])

    def over_bit(values, bit):
        return swap(values, lambda d: d ^ (1 << bit))

    def over_stage(values, orders, stage):
        return swap(values, lambda d: d ^ (1 << orders[d & 1][stage]))

    x0 = tokens.reshape(here, width)
    x2 = over_bit(x0, 1)
    x1 = over_bit(x0, 0)
    seg = segments.reshape(batches, length)
    seg_own = jnp.concatenate([seg, over_bit(seg, 1)], 0)
    seg_sib = over_bit(seg_own, 0)
    x3 = over_bit(x2, 0)

    gathered = row_total == 8 and joining_query.shape[0] % 16 == 0
    stacked = jnp.stack([joining_query, joining_key, joining_value], 0)
    if gathered:
        core = lax.rem(lax.axis_index("tok"), 2)
        column = width // 2
        piece = lax.dynamic_slice_in_dim(stacked, core * column, column, 2)[None]
        for stage in range(2):
            piece = jnp.concatenate([piece, over_stage(piece, ORDER_JOIN, stage)], 0)
        upper = over_stage(piece, ORDER_JOIN, 2)
        jw = (piece, upper, over_bit(piece, 0), over_bit(upper, 0))
    else:
        jw = (lax.all_gather(stacked, "rows", axis=1, tiled=True),)

    row = lambda vector: vector.reshape(1, -1)
    (qs, keys, values, probs, attended, n1, rs1, al, active, slope_z, n2, rs2, hidden, bottle, slope_t) = call(
        forward_kernel,
        "forward",
        (
            shape((here, width)), shape((4 * here, width)), shape((4 * here, width)),
            shape((batches * pairs, 4 * length, 2 * length)), shape((here, width)),
            shape((here, width), F32), shape((here, 128), F32), shape((here, width)),
            shape((here, hidden_units)), shape((here, hidden_units)),
            shape((here, width), F32), shape((here, 128), F32), shape((here, width), F32),
            shape((here, width)), shape((here, width)),
        ),
        (VM,) * 15,
        (VM,) * 18,
        [pltpu.VMEM((4 * length, length), F32)],
        x0, x1, x2, x3, seg_own, seg_sib, query_weight, key_weight, value_weight, out_weight,
        inner_weight, outer_weight, adapter_down, row(attend_gain), row(attend_bias), row(inner_bias),
        row(middle_gain), row(middle_bias),
    )

    half_rows = lambda blocks: blocks * width // 2
    up = adapter_up.reshape(adapters * bottleneck, width)
    output, keep_j, send_j, dhp, dt, vec_final = call(
        functools.partial(joining_kernel, gathered, bottleneck, adapters),
        "joining",
        (
            shape((here, width)), shape((half_rows(3), width)), shape((half_rows(3), width)),
            shape((here, width), F32), shape((here, width)), shape((8, width), F32),
        ),
        (VM, ANY, ANY, VM, VM, VM),
        (VM,) * 7 + (ANY,) * len(jw),
        [
            pltpu.VMEM((3, width, width), BF), pltpu.VMEM((3 * width, width), BF),
            pltpu.SemaphoreType.DMA((2, HALF)), pltpu.SemaphoreType.DMA((2, 8)),
        ],
        hidden, bottle, slope_t, up, cotangent.reshape(here, width), row(final_gain), row(final_bias), *jw,
    )

    blocks = hidden_units // width
    d1, vec, keep_u, send_u, keep_i, send_i = call(
        feed_back_kernel,
        "feed_back",
        (
            shape((here, width), F32), shape((16, width), F32),
            shape((half_rows(blocks), width)), shape((half_rows(blocks), width)),
            shape((half_rows(blocks), width)), shape((half_rows(blocks), width)),
        ),
        (VM, VM, ANY, ANY, ANY, ANY),
        (VM,) * 15,
        [
            pltpu.VMEM((blocks * width, width), BF), pltpu.VMEM((blocks * width, width), BF),
            pltpu.SemaphoreType.DMA((2, HALF)), pltpu.SemaphoreType.DMA((2, HALF)),
        ],
        dhp, dt, adapter_down, n2, rs2, row(middle_gain), active, slope_z, inner_weight, outer_weight,
        al, n1, rs1, row(attend_gain), vec_final,
    )

    keep_t, send_t, gi_own, gi_keep, gi_send = call(
        attend_back_kernel,
        "attend_back",
        (
            shape((half_rows(4) + 16, width)), shape((half_rows(4) + 16, width)),
            shape((here, width), F32), shape((here, width)), shape((2 * here, width)),
        ),
        (ANY, ANY, VM, VM, VM),
        (VM,) * 15,
        [
            pltpu.VMEM((4 * width, width), BF), pltpu.VMEM((here, width), BF),
            pltpu.VMEM((4 * here, width), BF), pltpu.VMEM((4 * here, width), BF),
            pltpu.VMEM((here, width), BF), pltpu.VMEM((16, width), BF),
            pltpu.SemaphoreType.DMA((2, HALF)), pltpu.SemaphoreType.DMA((2,)),
        ],
        d1, out_weight, attended, qs, keys, values, probs, x0, x1, x2, x3,
        query_weight, key_weight, value_weight, vec,
    )

    def reduce_scatter(keep, send, orders, rows_each):
        got = over_bit(send, 0)
        rows = HALF * rows_each
        for stage in range(4):
            middle = rows // 2
            send = keep[middle:] + got[middle:]
            keep = jnp.concatenate([keep[:middle] + got[:middle], keep[rows:] + got[rows:]], 0)
            got = over_stage(send, orders, stage)
            rows = middle
        keep = keep + got
        for bit in range(5, devices.bit_length() - 1):
            keep = keep + over_bit(keep, bit)
        return keep

    def all_gather(block, orders):
        for stage in (3, 2, 1):
            block = jnp.concatenate([block, over_stage(block, orders, stage)], 0)
        upper = over_stage(block, orders, 0)
        return block, upper, over_bit(block, 0), over_bit(upper, 0)

    def finish(parts, orders, outs, columns, name, vector=None):
        rows = parts[0].shape[0] * 4
        small = [] if vector is None else [shape((1, width), F32)] * 6 + [shape((1, hidden_units), F32)]
        return call(
            functools.partial(finish_kernel, orders, columns, vector is not None),
            name,
            tuple(outs) + tuple(small),
            (ANY,) * len(outs) + (VM,) * len(small),
            (VM,) * (4 if vector is None else 5),
            [pltpu.VMEM((rows, width), F32), pltpu.SemaphoreType.DMA((4,))],
            *parts, *(() if vector is None else (vector,)),
        )

    square = shape((width, width), F32)
    sum_j = reduce_scatter(keep_j, send_j, ORDER_XY, 3 * width // GROUP)
    sum_u = reduce_scatter(keep_u, send_u, ORDER_XY, blocks * width // GROUP)
    sum_i = reduce_scatter(keep_i, send_i, ORDER_Z, blocks * width // GROUP)
    sum_t = reduce_scatter(keep_t, send_t, ORDER_XY, 4 * width // GROUP)
    each_t = 4 * width // GROUP
    joining = finish(all_gather(sum_j, ORDER_XY), ORDER_XY, [square] * 3, False, "finish_joining")
    outer = finish(
        all_gather(sum_u, ORDER_XY), ORDER_XY, [shape((hidden_units, width), F32)], False, "finish_outer"
    )
    inner = finish(
        all_gather(sum_i, ORDER_Z), ORDER_Z, [shape((width, hidden_units), F32)], True, "finish_inner"
    )
    last = finish(
        all_gather(sum_t[:each_t], ORDER_XY), ORDER_XY, [square] * 4, False, "finish_attend", sum_t[each_t:]
    )

    gi_got = over_bit(gi_send, 0)
    gi_far = over_bit(gi_keep + gi_got[here:], 1)
    input_grad = low(gi_own + gi_got[:here].astype(F32) + gi_far.astype(F32))

    flat = lambda values: values.reshape(-1)
    return (
        output.reshape(tokens.shape), input_grad.reshape(tokens.shape),
        last[0], last[1], last[2], last[3], flat(last[4]), flat(last[5]),
        inner[0], flat(last[10]), outer[0], flat(last[6]), flat(last[7]),
        joining[0], joining[1], joining[2], flat(last[8]), flat(last[9]),
    )


def solution(mesh):
    return jax.shard_map(
        functools.partial(per_device, mesh.shape["rows"]),
        mesh=mesh,
        in_specs=(
            P(None, "rows", "tok", None), P(None, "rows", "tok"), P(None, "rows", "tok", None),
        ) + (P(),) * 13 + (P("rows", None),) * 3 + (P(),) * 2,
        out_specs=(P(None, "rows", "tok", None),) * 2 + (P(),) * 16,
        check_vma=False,
    )
```

time: 667 us -> 184 us (0.28)
  waiting for transfers between devices: 286 us -> 64.8 us
  blocking collectives: 175 us -> 0 us
  matrix products: 110 us -> 0 us
  starting transfers between devices: 0.38 us -> 62 us
  local copies, waits for them, and re-layouts: 61.4 us -> 1.12 us
  Pallas kernels: 0 us -> 51 us
  between operations: 16.5 us -> 1.43 us
  other arithmetic: 13.6 us -> 3.01 us
    psum x1 -> x0, waiting for transfers between devices: 236 us -> none  [per_device(): lax.psum((totals[0], totals[1], totals[2], totals[3], totals[4], totals[5...]
    all_gather x8 -> x0, blocking collectives: 134 us -> none  [the longest x1 33.4 us: per_device(): lax.all_gather(joining_value, 'rows', axis=0, tiled=True)]
    dot_general x82 -> x0, matrix products: 110 us -> none  [the longest x20 22.4 us: matmul(): return jnp.dot(left_side, right_side, preferred_element_type=jnp.float32)]
    ppermute x0 -> x56, waiting for transfers between devices: none -> 64.8 us  [swap(): return lax.ppermute(values, AXES, [(d, partner(d)) for d in range(devices)])]
    ppermute x0 -> x56, starting transfers between devices: none -> 62 us  [swap(): return lax.ppermute(values, AXES, [(d, partner(d)) for d in range(devices)])]
    pallas_call x0 -> x8, Pallas kernels: none -> 51 us  [call(): pl.pallas_call(kernel, out_shape=out_shapes, in_specs=in_specs, out_specs...]
    unnamed x9 -> x0, waiting for transfers between devices: 49.5 us -> none
    unnamed x421 -> x34, local copies, waits for them, and re-layouts: 45.8 us -> 1.11 us
  transfers between devices with their start and end apart: 5 -> 56, of which waited for: 4 -> 22; matrix products, arithmetic and copies ran while one was open for 7% -> 1% of each run, Pallas kernels for 0% -> 22%
where the time goes in v1:
time: 184 us; the launch traced here: 183 us
  waiting for transfers between devices  64.8 us (35%)
  starting transfers between devices  62 us (34%)
  Pallas kernels  51 us (28%)
  other arithmetic  3.01 us (2%)
    ppermute x56, waiting for transfers between devices, swap(): return lax.ppermute(values, AXES, [(d, partner(d)) for d in range(devices)])  64.8 us
    ppermute x56, starting transfers between devices, swap(): return lax.ppermute(values, AXES, [(d, partner(d)) for d in range(devices)])  62 us
    pallas_call x8, Pallas kernels, call(): pl.pallas_call(kernel, out_shape=out_shapes, in_specs=in_specs, out_specs...  51 us
  transfers between devices with their start and end apart: 56, of which 22 were waited for; matrix products, arithmetic and copies ran while one was open for 1% of the time, Pallas kernels for 22%

profile of v1, /device:TPU:0, one launch (start us, length us, event | category | flops | bytes accessed | tf_op | source)
XLA Modules:
  0.0 183.5 jit_solution(10687808510787436661)
XLA Ops:
  0.7 0.9 fusion.2
  1.6 3.0 %collective-permute-start.5 = (bf16[1,3,64,256]{3,2,1,0:T(8,128)(2,1)S(1)}, bf16[1,3,64,256]{3,2,1,0:T(8,128)(2,1)S(1)}, u32[]{:S(2)}, u32[]{:S(2)}) collective-permute-start(bf16[1,3,64,256]{3,2,1,0:T(8,128)(2,1)S(1)} %fusion.2), channel_id=1, source_target_pairs={{0,4},{1,5},{2,6},{3,7},{4,0},{5,1},{6,2},{7,3},{8,12},{9,13},{10,... | collective-permute-start | bytes 294920 | tf_op jit(solution)/shard_map/ppermute | solution.py:448
  4.6 2.8 %collective-permute-done.5 = bf16[1,3,64,256]{3,2,1,0:T(8,128)(2,1)S(1)} collective-permute-done((bf16[1,3,64,256]{3,2,1,0:T(8,128)(2,1)S(1)}, bf16[1,3,64,256]{3,2,1,0:T(8,128)(2,1)S(1)}, u32[]{:S(2)}, u32[]{:S(2)}) %collective-permute-start.5) | collective-permute-done | bytes 98336 | tf_op jit(solution)/shard_map/ppermute | solution.py:448
  7.5 1.9 %collective-permute-start.6 = (bf16[2,3,64,256]{3,2,1,0:T(8,128)(2,1)S(1)}, bf16[2,3,64,256]{3,2,1,0:T(8,128)(2,1)S(1)}, u32[]{:S(2)}, u32[]{:S(2)}) collective-permute-start(bf16[2,3,64,256]{3,2,1,0:T(8,128)(2,1)S(1)} %pad_maximum_fusion.9), channel_id=1, source_target_pairs={{0,8},{1,17},{2,10},{3,19},{4,12},{5,21},{6,14},{7,23},{8,0},{9,25... | collective-permute-start | bytes 589832 | tf_op jit(solution)/shard_map/ppermute | solution.py:448
  9.4 4.0 %collective-permute-done.6 = bf16[2,3,64,256]{3,2,1,0:T(8,128)(2,1)S(1)} collective-permute-done((bf16[2,3,64,256]{3,2,1,0:T(8,128)(2,1)S(1)}, bf16[2,3,64,256]{3,2,1,0:T(8,128)(2,1)S(1)}, u32[]{:S(2)}, u32[]{:S(2)}) %collective-permute-start.6) | collective-permute-done | bytes 196640 | tf_op jit(solution)/shard_map/ppermute | solution.py:448
  13.5 3.8 %collective-permute-start.7 = (bf16[4,3,64,256]{3,2,1,0:T(8,128)(2,1)S(1)}, bf16[4,3,64,256]{3,2,1,0:T(8,128)(2,1)S(1)}, u32[]{:S(2)}, u32[]{:S(2)}) collective-permute-start(bf16[4,3,64,256]{3,2,1,0:T(8,128)(2,1)S(1)} %pad_maximum_fusion.3.rest_0_), channel_id=1, source_target_pairs={{0,16},{1,9},{2,18},{3,11},{4,20},{5,13},{6,22},{7,15},{8,24},{9,1... | collective-permute-start | bytes 1179656 | tf_op jit(solution)/shard_map/ppermute | solution.py:448
  17.3 1.5 collective-permute-start.1
  18.8 8.5 %collective-permute-done.7.rest_1_ = bf16[4,3,64,256]{3,2,1,0:T(8,128)(2,1)S(1)} collective-permute-done((bf16[4,3,64,256]{3,2,1,0:T(8,128)(2,1)S(1)}, bf16[4,3,64,256]{3,2,1,0:T(8,128)(2,1)S(1)}, u32[]{:S(2)}, u32[]{:S(2)}) %collective-permute-start.7) | collective-permute-done | bytes 393248 | tf_op jit(solution)/shard_map/ppermute | solution.py:448
  27.3 0.5 collective-permute-start
  27.8 1.8 collective-permute-start.3
  29.6 1.9 %collective-permute-done.3 = s32[2,128]{1,0:T(2,128)S(1)} collective-permute-done((s32[2,128]{1,0:T(2,128)S(1)}, s32[2,128]{1,0:T(2,128)S(1)}, u32[]{:S(2)}, u32[]{:S(2)}) %collective-permute-start.3) | collective-permute-done | bytes 1056 | tf_op jit(solution)/shard_map/ppermute | solution.py:448
  31.5 1.1 collective-permute-done.4.seg_sib
  32.7 13.2 %forward.1 = (bf16[256,512]{1,0:T(8,128)(2,1)S(1)}, bf16[1024,512]{1,0:T(8,128)(2,1)}, bf16[1024,512]{1,0:T(8,128)(2,1)}, bf16[8,512,256]{2,1,0:T(8,128)(2,1)}, ...) custom-call(bf16[256,512]{1,0:T(8,128)(2,1)S(1)} %bitcast.31, ...), custom_call_target="tpu_custom_call" | custom-call | tf_op jit(solution)/shard_map/forward/pallas_call | solution.py:419
  46.0 1.0 copy-done.3
  47.0 7.9 %joining.1 = (bf16[256,512]{1,0:T(8,128)(2,1)}, bf16[768,512]{1,0:T(8,128)(2,1)}, bf16[768,512]{1,0:T(8,128)(2,1)}, f32[256,512]{1,0:T(8,128)S(1)}, bf16[256,512]{1,0:T(8,128)(2,1)S(1)}, /*index=5*/f32[8,512]{1,0:T(8,128)S(1)}) custom-call(f32[256,512]{1,0:T(8,128)S(1)} %copy-done.3, bf16[256,512]{1,0:T(8,128)(2,1)S(1)} %get-tuple-element.65.c_ref, ...), custom_call_target="tpu_custom_call" | custom-call | tf_op jit(solution)/shard_map/joining/pallas_call | solution.py:419
  55.2 9.2 %feed_back.1 = (f32[256,512]{1,0:T(8,128)S(1)}, f32[16,512]{1,0:T(8,128)S(1)}, bf16[1024,512]{1,0:T(8,128)(2,1)}, bf16[1024,512]{1,0:T(8,128)(2,1)}, bf16[1024,5...) custom-call(f32[256,512]{1,0:T(8,128)S(1)} %get-tuple-element.68.dhp_ref, bf16[256,512]{1,0:T(8,128)(2,1)S(1)} %get-tuple-element.69.dt_ref, ...), custom_call_target="tpu_custom_call" | custom-call | tf_op jit(solution)/shard_map/feed_back/pallas_call | solution.py:419
  65.0 1.8 collective-permute-start.46
  66.8 11.0 %attend_back.1 = (bf16[1040,512]{1,0:T(8,128)(2,1)}, bf16[1040,512]{1,0:T(8,128)(2,1)}, f32[256,512]{1,0:T(8,128)S(1)}, bf16[256,512]{1,0:T(8,128)(2,1)S(1)}, bf16[512,512]{1,0:T(8,128)(2,1)S(1)}) custom-call(f32[256,512]{1,0:T(8,128)S(1)} %get-tuple-element.78.d1_ref, bf16[512,512]{1,0:T(8,128)(2,1)S(1)} %copy-done.1, ...), custom_call_target="tpu_custom_call" | custom-call | tf_op jit(solution)/shard_map/attend_back/pallas_call | solution.py:419
  78.5 1.3 collective-permute-start.24
  79.9 1.6 collective-permute-start.47
  81.6 0.9 collective-permute-start.35
  82.6 5.1 %collective-permute-done.47 = bf16[192,512]{1,0:T(8,128)(2,1)S(1)} collective-permute-done((bf16[192,512]{1,0:T(8,128)(2,1)S(1)}, bf16[192,512]{1,0:T(8,128)(2,1)S(1)}, u32[]{:S(2)}, u32[]{:S(2)}) %collective-permute-start.47) | collective-permute-done | bytes 196640 | tf_op jit(solution)/shard_map/ppermute | solution.py:448
  87.9 1.2 collective-permute-start.13
  89.1 6.4 %collective-permute-done.48 = bf16[96,512]{1,0:T(8,128)(2,1)S(1)} collective-permute-done((bf16[96,512]{1,0:T(8,128)(2,1)S(1)}, bf16[96,512]{1,0:T(8,128)(2,1)S(1)}, u32[]{:S(2)}, u32[]{:S(2)}) %collective-permute-start.48) | collective-permute-done | bytes 98336 | tf_op jit(solution)/shard_map/ppermute | solution.py:448
  95.5 2.2 %collective-permute-start.49 = (bf16[48,512]{1,0:T(8,128)(2,1)S(1)}, bf16[48,512]{1,0:T(8,128)(2,1)S(1)}, u32[]{:S(2)}, u32[]{:S(2)}) collective-permute-start(bf16[48,512]{1,0:T(8,128)(2,1)S(1)} %slice_add_fusion.31), channel_id=1, source_target_pairs={{0,16},{1,9},{2,18},{3,11},{4,20},{5,13},{6,22},{7,15},{8,24},{9,1... | collective-permute-start | bytes 147464 | tf_op jit(solution)/shard_map/ppermute | solution.py:448
  97.7 2.8 %collective-permute-done.49 = bf16[48,512]{1,0:T(8,128)(2,1)S(1)} collective-permute-done((bf16[48,512]{1,0:T(8,128)(2,1)S(1)}, bf16[48,512]{1,0:T(8,128)(2,1)S(1)}, u32[]{:S(2)}, u32[]{:S(2)}) %collective-permute-start.49) | collective-permute-done | bytes 49184 | tf_op jit(solution)/shard_map/ppermute | solution.py:448
  100.5 2.2 %collective-permute-start.50 = (bf16[48,512]{1,0:T(8,128)(2,1)S(1)}, bf16[48,512]{1,0:T(8,128)(2,1)S(1)}, u32[]{:S(2)}, u32[]{:S(2)}) collective-permute-start(bf16[48,512]{1,0:T(8,128)(2,1)S(1)} %fusion.5), channel_id=1, source_target_pairs={{0,16},{1,9},{2,18},{3,11},{4,20},{5,13},{6,22},{7,15},{8,24},{9,1... | collective-permute-start | bytes 147464 | tf_op jit(solution)/shard_map/ppermute | solution.py:448
  102.8 0.9 collective-permute-start.25
  103.7 1.6 collective-permute-start.36
  105.3 0.9 collective-permute-done.50
  106.2 4.1 %collective-permute-start.51 = (bf16[96,512]{1,0:T(8,128)(2,1)S(1)}, bf16[96,512]{1,0:T(8,128)(2,1)S(1)}, u32[]{:S(2)}, u32[]{:S(2)}) collective-permute-start(bf16[96,512]{1,0:T(8,128)(2,1)S(1)} %pad_maximum_fusion.15), channel_id=1, source_target_pairs={{0,8},{1,17},{2,10},{3,19},{4,12},{5,21},{6,14},{7,23},{8,0},{9,25... | collective-permute-start | bytes 294920 | tf_op jit(solution)/shard_map/ppermute | solution.py:448
  110.4 1.4 collective-permute-start.14
  111.8 3.9 %collective-permute-done.51 = bf16[96,512]{1,0:T(8,128)(2,1)S(1)} collective-permute-done((bf16[96,512]{1,0:T(8,128)(2,1)S(1)}, bf16[96,512]{1,0:T(8,128)(2,1)S(1)}, u32[]{:S(2)}, u32[]{:S(2)}) %collective-permute-start.51) | collective-permute-done | bytes 98336 | tf_op jit(solution)/shard_map/ppermute | solution.py:448
  115.8 1.1 collective-permute-start.52
  116.9 1.8 collective-permute-start.26
  118.8 4.6 %collective-permute-done.52 = bf16[192,512]{1,0:T(8,128)(2,1)S(1)} collective-permute-done((bf16[192,512]{1,0:T(8,128)(2,1)S(1)}, bf16[192,512]{1,0:T(8,128)(2,1)S(1)}, u32[]{:S(2)}, u32[]{:S(2)}) %collective-permute-start.52) | collective-permute-done | bytes 196640 | tf_op jit(solution)/shard_map/ppermute | solution.py:448
  123.4 1.8 %collective-permute-start.53 = (bf16[384,512]{1,0:T(8,128)(2,1)S(1)}, bf16[384,512]{1,0:T(8,128)(2,1)S(1)}, u32[]{:S(2)}, u32[]{:S(2)}) collective-permute-start(bf16[384,512]{1,0:T(8,128)(2,1)S(1)} %pad_maximum_fusion.4.a8), channel_id=1, source_target_pairs={{0,2},{1,5},{2,0},{3,7},{4,6},{5,1},{6,4},{7,3},{8,10},{9,13},{10,... | collective-permute-start | bytes 1179656 | tf_op jit(solution)/shard_map/ppermute | solution.py:448
  125.4 0.9 collective-permute-start.27
  126.3 4.2 %collective-permute-start.38 = (bf16[64,512]{1,0:T(8,128)(2,1)S(1)}, bf16[64,512]{1,0:T(8,128)(2,1)S(1)}, u32[]{:S(2)}, u32[]{:S(2)}) collective-permute-start(bf16[64,512]{1,0:T(8,128)(2,1)S(1)} %slice_add_fusion.26), channel_id=1, source_target_pairs={{0,16},{1,9},{2,18},{3,11},{4,20},{5,13},{6,22},{7,15},{8,24},{9,1... | collective-permute-start | bytes 196616 | tf_op jit(solution)/shard_map/ppermute | solution.py:448
  130.5 1.6 collective-permute-done.15
  132.1 2.3 %collective-permute-start.16 = (bf16[80,512]{1,0:T(8,128)(2,1)S(1)}, bf16[80,512]{1,0:T(8,128)(2,1)S(1)}, u32[]{:S(2)}, u32[]{:S(2)}) collective-permute-start(bf16[80,512]{1,0:T(8,128)(2,1)S(1)} %slice_add_fusion.25), channel_id=1, source_target_pairs={{0,16},{1,9},{2,18},{3,11},{4,20},{5,13},{6,22},{7,15},{8,24},{9,1... | collective-permute-start | bytes 245768 | tf_op jit(solution)/shard_map/ppermute | solution.py:448
  134.4 0.9 collective-permute-start.28
  135.9 2.9 %collective-permute-done.28 = bf16[64,512]{1,0:T(8,128)(2,1)S(1)} collective-permute-done((bf16[64,512]{1,0:T(8,128)(2,1)S(1)}, bf16[64,512]{1,0:T(8,128)(2,1)S(1)}, u32[]{:S(2)}, u32[]{:S(2)}) %collective-permute-start.28) | collective-permute-done | bytes 65568 | tf_op jit(solution)/shard_map/ppermute | solution.py:448
  139.2 1.6 collective-permute-start.17
  140.8 0.5 collective-permute-done.39
  141.3 1.1 collective-permute-start.40
  142.4 2.0 %collective-permute-done.17 = bf16[64,512]{1,0:T(8,128)(2,1)S(1)} collective-permute-done((bf16[64,512]{1,0:T(8,128)(2,1)S(1)}, bf16[64,512]{1,0:T(8,128)(2,1)S(1)}, u32[]{:S(2)}, u32[]{:S(2)}) %collective-permute-start.17) | collective-permute-done | bytes 65568 | tf_op jit(solution)/shard_map/ppermute | solution.py:448
  144.4 2.3 %collective-permute-start.18 = (bf16[128,512]{1,0:T(8,128)(2,1)S(1)}, bf16[128,512]{1,0:T(8,128)(2,1)S(1)}, u32[]{:S(2)}, u32[]{:S(2)}) collective-permute-start(bf16[128,512]{1,0:T(8,128)(2,1)S(1)} %pad_maximum_fusion.12), channel_id=1, source_target_pairs={{0,8},{1,17},{2,10},{3,19},{4,12},{5,21},{6,14},{7,23},{8,0},{9,25... | collective-permute-start | bytes 393224 | tf_op jit(solution)/shard_map/ppermute | solution.py:448
  146.8 1.5 collective-permute-start.30
  148.3 1.3 collective-permute-start.41
  149.8 2.8 %collective-permute-start.19 = (bf16[256,512]{1,0:T(8,128)(2,1)S(1)}, bf16[256,512]{1,0:T(8,128)(2,1)S(1)}, u32[]{:S(2)}, u32[]{:S(2)}) collective-permute-start(bf16[256,512]{1,0:T(8,128)(2,1)S(1)} %pad_maximum_fusion.6), channel_id=1, source_target_pairs={{0,4},{1,3},{2,6},{3,1},{4,0},{5,7},{6,2},{7,5},{8,12},{9,11},{10,... | collective-permute-start | bytes 786440 | tf_op jit(solution)/shard_map/ppermute | solution.py:448
  152.6 1.0 collective-permute-start.11
  153.6 2.8 %collective-permute-done.30 = bf16[256,512]{1,0:T(8,128)(2,1)S(1)} collective-permute-done((bf16[256,512]{1,0:T(8,128)(2,1)S(1)}, bf16[256,512]{1,0:T(8,128)(2,1)S(1)}, u32[]{:S(2)}, u32[]{:S(2)}) %collective-permute-start.30) | collective-permute-done | bytes 262176 | tf_op jit(solution)/shard_map/ppermute | solution.py:448
  156.6 1.0 collective-permute-done.19
  157.6 2.3 %collective-permute-start.42 = (bf16[512,512]{1,0:T(8,128)(2,1)S(1)}, bf16[512,512]{1,0:T(8,128)(2,1)S(1)}, u32[]{:S(2)}, u32[]{:S(2)}) collective-permute-start(bf16[512,512]{1,0:T(8,128)(2,1)S(1)} %pad_maximum_fusion.2.a8), channel_id=1, source_target_pairs={{0,2},{1,5},{2,0},{3,7},{4,6},{5,1},{6,4},{7,3},{8,10},{9,13},{10,... | collective-permute-start | bytes 1572872 | tf_op jit(solution)/shard_map/ppermute | solution.py:448
  160.5 1.9 %collective-permute-done.55.sr1 = bf16[384,512]{1,0:T(8,128)(2,1)S(1)} collective-permute-done((bf16[384,512]{1,0:T(8,128)(2,1)S(1)}, bf16[384,512]{1,0:T(8,128)(2,1)S(1)}, u32[]{:S(2)}, u32[]{:S(2)}) %collective-permute-start.55) | collective-permute-done | bytes 393248 | tf_op jit(solution)/shard_map/ppermute | solution.py:448
  162.6 8.8 %collective-permute-done.31.r1 = bf16[512,512]{1,0:T(8,128)(2,1)S(1)} collective-permute-done((bf16[512,512]{1,0:T(8,128)(2,1)S(1)}, bf16[512,512]{1,0:T(8,128)(2,1)S(1)}, u32[]{:S(2)}, u32[]{:S(2)}) %collective-permute-start.31) | collective-permute-done | bytes 524320 | tf_op jit(solution)/shard_map/ppermute | solution.py:448
  171.3 0.5 collective-permute-start.44
  171.9 0.7 collective-permute-done.20.r1
  172.6 0.8 add_convert_fusion
  173.4 2.0 %finish_joining.1 = (f32[512,512]{1,0:T(8,128)}, f32[512,512]{1,0:T(8,128)}, f32[512,512]{1,0:T(8,128)}) custom-call(bf16[384,512]{1,0:T(8,128)(2,1)S(1)} %pad_maximum_fusion.4.a8, bf16[384,512]{1,0:T(8,128)(2,1)S(1)} %collective-permute-done.53.r1, bf16[384,512]{1,0:T(8,128)(2,1)S(1)} %collective-permute-done.54.s8, ...), custom_call_target="tpu_custom_call" | custom-call | tf_op jit(solution)/shard_map/finish_joining/pallas_call | solution.py:419
  175.4 2.4 %finish_inner.1 = f32[512,2048]{1,0:T(8,128)} custom-call(bf16[512,512]{1,0:T(8,128)(2,1)S(1)} %pad_maximum_fusion.1.a8, bf16[512,512]{1,0:T(8,128)(2,1)S(1)} %collective-permute-done.31.r1, bf16[512,512]{1,0:T(8,128)(2,1)S(1)} %collective-permute-done.32.s8, bf16[512,512]{1,0:T(8,128)(2,1)S(1)} %collective-permute-done.33.sr1), custom_call_target="tpu_custom_call" | custom-call | tf_op jit(solution)/shard_map/finish_inner/pallas_call | solution.py:419
  177.8 2.4 %finish_outer.1 = f32[2048,512]{1,0:T(8,128)} custom-call(bf16[512,512]{1,0:T(8,128)(2,1)S(1)} %pad_maximum_fusion.2.a8, bf16[512,512]{1,0:T(8,128)(2,1)S(1)} %collective-permute-done.42.r1, bf16[512,512]{1,0:T(8,128)(2,1)S(1)} %collective-permute-done.43.s8, bf16[512,512]{1,0:T(8,128)(2,1)S(1)} %collective-permute-done.44.sr1), custom_call_target="tpu_custom_call" | custom-call | tf_op jit(solution)/shard_map/finish_outer/pallas_call | solution.py:419
  180.3 3.0 %finish_attend.1 = (f32[512,512]{1,0:T(8,128)}, f32[512,512]{1,0:T(8,128)}, f32[512,512]{1,0:T(8,128)}, f32[512,512]{1,0:T(8,128)}, f32[1,512]{1,0:T(1,128)}, /*...) custom-call(bf16[512,512]{1,0:T(8,128)(2,1)S(1)} %pad_maximum_fusion, ...), custom_call_target="tpu_custom_call" | custom-call | tf_op jit(solution)/shard_map/finish_attend/pallas_call | solution.py:419
  (136 shorter events, 5.0 us)
Async XLA Ops:
  0.7 16.7 %copy-start.2 = (bf16[2,1,128,512]{3,2,1,0:T(8,128)(2,1)S(1)}, bf16[2,1,128,512]{3,2,1,0:T(8,128)(2,1)}, u32[]{:S(2)}) copy-start(bf16[2,1,128,512]{3,2,1,0:T(8,128)(2,1)} %param.21) | copy-start | bytes 786436
  0.7 27.2 %copy-start.16 = (s32[2,1,128]{2,1,0:T(1,128)S(1)}, s32[2,1,128]{2,1,0:T(1,128)}, u32[]{:S(2)}) copy-start(s32[2,1,128]{2,1,0:T(1,128)} %param.22) | copy-start | bytes 3076
  0.7 32.0 %copy-start.6 = (f32[512]{0:T(512)S(1)}, f32[512]{0:T(512)}, u32[]{:S(2)}) copy-start(f32[512]{0:T(512)} %param.28) | copy-start | bytes 6148
  0.7 32.0 %copy-start.8 = (f32[512]{0:T(512)S(1)}, f32[512]{0:T(512)}, u32[]{:S(2)}) copy-start(f32[512]{0:T(512)} %param.29) | copy-start | bytes 6148
  0.7 32.0 %copy-start.5 = (f32[2048]{0:T(1024)S(1)}, f32[2048]{0:T(1024)}, u32[]{:S(2)}) copy-start(f32[2048]{0:T(1024)} %param.31) | copy-start | bytes 24580
  0.7 32.0 %copy-start.7 = (f32[512]{0:T(512)S(1)}, f32[512]{0:T(512)}, u32[]{:S(2)}) copy-start(f32[512]{0:T(512)} %param.33) | copy-start | bytes 6148
  0.7 32.0 %copy-start.9 = (f32[512]{0:T(512)S(1)}, f32[512]{0:T(512)}, u32[]{:S(2)}) copy-start(f32[512]{0:T(512)} %param.34) | copy-start | bytes 6148
  1.6 5.8 %collective-permute-start.5 = (bf16[1,3,64,256]{3,2,1,0:T(8,128)(2,1)S(1)}, bf16[1,3,64,256]{3,2,1,0:T(8,128)(2,1)S(1)}, u32[]{:S(2)}, u32[]{:S(2)}) collective-permute-start(bf16[1,3,64,256]{3,2,1,0:T(8,128)(2,1)S(1)} %fusion.2), channel_id=1, source_target_pairs={{0,4},{1,5},{2,6},{3,7},{4,0},{5,1},{6,2},{7,3},{8,12},{9,13},{10,... | collective-permute-start | bytes 294920 | tf_op jit(solution)/shard_map/ppermute | solution.py:448
  7.5 6.0 %collective-permute-start.6 = (bf16[2,3,64,256]{3,2,1,0:T(8,128)(2,1)S(1)}, bf16[2,3,64,256]{3,2,1,0:T(8,128)(2,1)S(1)}, u32[]{:S(2)}, u32[]{:S(2)}) collective-permute-start(bf16[2,3,64,256]{3,2,1,0:T(8,128)(2,1)S(1)} %pad_maximum_fusion.9), channel_id=1, source_target_pairs={{0,8},{1,17},{2,10},{3,19},{4,12},{5,21},{6,14},{7,23},{8,0},{9,25... | collective-permute-start | bytes 589832 | tf_op jit(solution)/shard_map/ppermute | solution.py:448
  13.5 13.8 %collective-permute-start.7 = (bf16[4,3,64,256]{3,2,1,0:T(8,128)(2,1)S(1)}, bf16[4,3,64,256]{3,2,1,0:T(8,128)(2,1)S(1)}, u32[]{:S(2)}, u32[]{:S(2)}) collective-permute-start(bf16[4,3,64,256]{3,2,1,0:T(8,128)(2,1)S(1)} %pad_maximum_fusion.3.rest_0_), channel_id=1, source_target_pairs={{0,16},{1,9},{2,18},{3,11},{4,20},{5,13},{6,22},{7,15},{8,24},{9,1... | collective-permute-start | bytes 1179656 | tf_op jit(solution)/shard_map/ppermute | solution.py:448
  17.3 10.5 %collective-permute-start.1 = (bf16[256,512]{1,0:T(8,128)(2,1)S(1)}, bf16[256,512]{1,0:T(8,128)(2,1)S(1)}, u32[]{:S(2)}, u32[]{:S(2)}) collective-permute-start(bf16[256,512]{1,0:T(8,128)(2,1)S(1)} %bitcast.29), channel_id=1, source_target_pairs={{0,2},{1,3},{2,0},{3,1},{4,6},{5,7},{6,4},{7,5},{8,10},{9,11},{10,... | collective-permute-start | bytes 786440 | tf_op jit(solution)/shard_map/ppermute | solution.py:448
  18.8 27.1 %collective-permute-start.8 = (bf16[4,3,64,256]{3,2,1,0:T(8,128)(2,1)S(1)}, bf16[4,3,64,256]{3,2,1,0:T(8,128)(2,1)S(1)}, u32[]{:S(2)}, u32[]{:S(2)}) collective-permute-start(bf16[4,3,64,256]{3,2,1,0:T(8,128)(2,1)S(1)} %pad_maximum_fusion.3.rest_0_), channel_id=1, source_target_pairs={{0,1},{1,0},{2,3},{3,2},{4,5},{5,4},{6,7},{7,6},{8,9},{9,8},{10,11... | collective-permute-start | bytes 1179656 | tf_op jit(solution)/shard_map/ppermute | solution.py:448
  27.3 18.6 %collective-permute-start.9 = (bf16[4,3,64,256]{3,2,1,0:T(8,128)(2,1)S(1)}, bf16[4,3,64,256]{3,2,1,0:T(8,128)(2,1)S(1)}, u32[]{:S(2)}, u32[]{:S(2)}) collective-permute-start(bf16[4,3,64,256]{3,2,1,0:T(8,128)(2,1)S(1)} %collective-permute-done.7.rest_1_), channel_id=1, source_target_pairs={{0,1},{1,0},{2,3},{3,2},{4,5},{5,4},{6,7},{7,6},{8,9},{9,8},{10,11... | collective-permute-start | bytes 1179656 | tf_op jit(solution)/shard_map/ppermute | solution.py:448
  27.3 5.3 %collective-permute-start = (bf16[256,512]{1,0:T(8,128)(2,1)S(1)}, bf16[256,512]{1,0:T(8,128)(2,1)S(1)}, u32[]{:S(2)}, u32[]{:S(2)}) collective-permute-start(bf16[256,512]{1,0:T(8,128)(2,1)S(1)} %bitcast.30), channel_id=1, source_target_pairs={{0,1},{1,0},{2,3},{3,2},{4,5},{5,4},{6,7},{7,6},{8,9},{9,8},{10,11... | collective-permute-start | bytes 786440 | tf_op jit(solution)/shard_map/ppermute | solution.py:448
  27.8 4.8 %collective-permute-start.2 = (bf16[256,512]{1,0:T(8,128)(2,1)S(1)}, bf16[256,512]{1,0:T(8,128)(2,1)S(1)}, u32[]{:S(2)}, u32[]{:S(2)}) collective-permute-start(bf16[256,512]{1,0:T(8,128)(2,1)S(1)} %collective-permute-done.1.x2), channel_id=1, source_target_pairs={{0,1},{1,0},{2,3},{3,2},{4,5},{5,4},{6,7},{7,6},{8,9},{9,8},{10,11... | collective-permute-start | bytes 786440 | tf_op jit(solution)/shard_map/ppermute | solution.py:448
  27.8 3.6 %collective-permute-start.3 = (s32[2,128]{1,0:T(2,128)S(1)}, s32[2,128]{1,0:T(2,128)S(1)}, u32[]{:S(2)}, u32[]{:S(2)}) collective-permute-start(s32[2,128]{1,0:T(2,128)S(1)} %bitcast.48), channel_id=1, source_target_pairs={{0,2},{1,3},{2,0},{3,1},{4,6},{5,7},{6,4},{7,5},{8,10},{9,11},{10,... | collective-permute-start | bytes 3080 | tf_op jit(solution)/shard_map/ppermute | solution.py:448
  31.5 1.2 collective-permute-start.4
  32.7 13.2 %copy-start.4 = (bf16[2,1,128,512]{3,2,1,0:T(8,128)(2,1)S(1)}, bf16[2,1,128,512]{3,2,1,0:T(8,128)(2,1)}, u32[]{:S(2)}) copy-start(bf16[2,1,128,512]{3,2,1,0:T(8,128)(2,1)} %param.23) | copy-start | bytes 786436
  54.9 10.0 %collective-permute-start.45 = (bf16[768,512]{1,0:T(8,128)(2,1)}, bf16[768,512]{1,0:T(8,128)(2,1)S(1)}, u32[]{:S(2)}, u32[]{:S(2)}) collective-permute-start(bf16[768,512]{1,0:T(8,128)(2,1)} %get-tuple-element.104), channel_id=1, source_target_pairs={{0,1},{1,0},{2,3},{3,2},{4,5},{5,4},{6,7},{7,6},{8,9},{9,8},{10,11... | collective-permute-start | bytes 2359304 | tf_op jit(solution)/shard_map/ppermute | solution.py:448
  64.4 14.0 %collective-permute-start.23 = (bf16[1024,512]{1,0:T(8,128)(2,1)}, bf16[1024,512]{1,0:T(8,128)(2,1)S(1)}, u32[]{:S(2)}, u32[]{:S(2)}) collective-permute-start(bf16[1024,512]{1,0:T(8,128)(2,1)} %get-tuple-element.97), channel_id=1, source_target_pairs={{0,1},{1,0},{2,3},{3,2},{4,5},{5,4},{6,7},{7,6},{8,9},{9,8},{10,11... | collective-permute-start | bytes 3145736 | tf_op jit(solution)/shard_map/ppermute | solution.py:448
  64.8 16.7 %collective-permute-start.34 = (bf16[1024,512]{1,0:T(8,128)(2,1)}, bf16[1024,512]{1,0:T(8,128)(2,1)S(1)}, u32[]{:S(2)}, u32[]{:S(2)}) collective-permute-start(bf16[1024,512]{1,0:T(8,128)(2,1)} %get-tuple-element.100), channel_id=1, source_target_pairs={{0,1},{1,0},{2,3},{3,2},{4,5},{5,4},{6,7},{7,6},{8,9},{9,8},{10,11... | collective-permute-start | bytes 3145736 | tf_op jit(solution)/shard_map/ppermute | solution.py:448
  65.0 14.8 %collective-permute-start.46 = (bf16[384,512]{1,0:T(8,128)(2,1)S(1)}, bf16[384,512]{1,0:T(8,128)(2,1)S(1)}, u32[]{:S(2)}, u32[]{:S(2)}) collective-permute-start(bf16[384,512]{1,0:T(8,128)(2,1)S(1)} %get-tuple-element.137), channel_id=1, source_target_pairs={{0,2},{1,5},{2,0},{3,7},{4,6},{5,1},{6,4},{7,3},{8,10},{9,13},{10,... | collective-permute-start | bytes 1179656 | tf_op jit(solution)/shard_map/ppermute | solution.py:448
  77.8 10.0 %collective-permute-start.12 = (bf16[1040,512]{1,0:T(8,128)(2,1)}, bf16[1040,512]{1,0:T(8,128)(2,1)S(1)}, u32[]{:S(2)}, u32[]{:S(2)}) collective-permute-start(bf16[1040,512]{1,0:T(8,128)(2,1)} %get-tuple-element.89), channel_id=1, source_target_pairs={{0,1},{1,0},{2,3},{3,2},{4,5},{5,4},{6,7},{7,6},{8,9},{9,8},{10,11... | collective-permute-start | bytes 3194888 | tf_op jit(solution)/shard_map/ppermute | solution.py:448
  77.9 74.6 %collective-permute-start.10 = (bf16[512,512]{1,0:T(8,128)(2,1)S(1)}, bf16[512,512]{1,0:T(8,128)(2,1)S(1)}, u32[]{:S(2)}, u32[]{:S(2)}) collective-permute-start(bf16[512,512]{1,0:T(8,128)(2,1)S(1)} %get-tuple-element.86), channel_id=1, source_target_pairs={{0,1},{1,0},{2,3},{3,2},{4,5},{5,4},{6,7},{7,6},{8,9},{9,8},{10,11... | collective-permute-start | bytes 1572872 | tf_op jit(solution)/shard_map/ppermute | solution.py:448
  78.5 24.2 %collective-permute-start.24 = (bf16[512,512]{1,0:T(8,128)(2,1)S(1)}, bf16[512,512]{1,0:T(8,128)(2,1)S(1)}, u32[]{:S(2)}, u32[]{:S(2)}) collective-permute-start(bf16[512,512]{1,0:T(8,128)(2,1)S(1)} %get-tuple-element.135), channel_id=1, source_target_pairs={{0,8},{1,17},{2,10},{3,19},{4,12},{5,21},{6,14},{7,23},{8,0},{9,25... | collective-permute-start | bytes 1572872 | tf_op jit(solution)/shard_map/ppermute | solution.py:448
  79.9 7.8 %collective-permute-start.47 = (bf16[192,512]{1,0:T(8,128)(2,1)S(1)}, bf16[192,512]{1,0:T(8,128)(2,1)S(1)}, u32[]{:S(2)}, u32[]{:S(2)}) collective-permute-start(bf16[192,512]{1,0:T(8,128)(2,1)S(1)} %get-tuple-element.143), channel_id=1, source_target_pairs={{0,4},{1,3},{2,6},{3,1},{4,0},{5,7},{6,2},{7,5},{8,12},{9,11},{10,... | collective-permute-start | bytes 589832 | tf_op jit(solution)/shard_map/ppermute | solution.py:448
  81.6 22.1 %collective-permute-start.35 = (bf16[512,512]{1,0:T(8,128)(2,1)S(1)}, bf16[512,512]{1,0:T(8,128)(2,1)S(1)}, u32[]{:S(2)}, u32[]{:S(2)}) collective-permute-start(bf16[512,512]{1,0:T(8,128)(2,1)S(1)} %get-tuple-element.133), channel_id=1, source_target_pairs={{0,2},{1,5},{2,0},{3,7},{4,6},{5,1},{6,4},{7,3},{8,10},{9,13},{10,... | collective-permute-start | bytes 1572872 | tf_op jit(solution)/shard_map/ppermute | solution.py:448
  87.7 7.7 %collective-permute-start.48 = (bf16[96,512]{1,0:T(8,128)(2,1)S(1)}, bf16[96,512]{1,0:T(8,128)(2,1)S(1)}, u32[]{:S(2)}, u32[]{:S(2)}) collective-permute-start(bf16[96,512]{1,0:T(8,128)(2,1)S(1)} %get-tuple-element.149), channel_id=1, source_target_pairs={{0,8},{1,17},{2,10},{3,19},{4,12},{5,21},{6,14},{7,23},{8,0},{9,25... | collective-permute-start | bytes 294920 | tf_op jit(solution)/shard_map/ppermute | solution.py:448
  87.9 22.4 %collective-permute-start.13 = (bf16[528,512]{1,0:T(8,128)(2,1)S(1)}, bf16[528,512]{1,0:T(8,128)(2,1)S(1)}, u32[]{:S(2)}, u32[]{:S(2)}) collective-permute-start(bf16[528,512]{1,0:T(8,128)(2,1)S(1)} %slice_add_fusion), channel_id=1, source_target_pairs={{0,2},{1,5},{2,0},{3,7},{4,6},{5,1},{6,4},{7,3},{8,10},{9,13},{10,... | collective-permute-start | bytes 1622024 | tf_op jit(solution)/shard_map/ppermute | solution.py:448
  95.5 5.0 %collective-permute-start.49 = (bf16[48,512]{1,0:T(8,128)(2,1)S(1)}, bf16[48,512]{1,0:T(8,128)(2,1)S(1)}, u32[]{:S(2)}, u32[]{:S(2)}) collective-permute-start(bf16[48,512]{1,0:T(8,128)(2,1)S(1)} %slice_add_fusion.31), channel_id=1, source_target_pairs={{0,16},{1,9},{2,18},{3,11},{4,20},{5,13},{6,22},{7,15},{8,24},{9,1... | collective-permute-start | bytes 147464 | tf_op jit(solution)/shard_map/ppermute | solution.py:448
  100.5 5.7 %collective-permute-start.50 = (bf16[48,512]{1,0:T(8,128)(2,1)S(1)}, bf16[48,512]{1,0:T(8,128)(2,1)S(1)}, u32[]{:S(2)}, u32[]{:S(2)}) collective-permute-start(bf16[48,512]{1,0:T(8,128)(2,1)S(1)} %fusion.5), channel_id=1, source_target_pairs={{0,16},{1,9},{2,18},{3,11},{4,20},{5,13},{6,22},{7,15},{8,24},{9,1... | collective-permute-start | bytes 147464 | tf_op jit(solution)/shard_map/ppermute | solution.py:448
  102.8 14.0 %collective-permute-start.25 = (bf16[256,512]{1,0:T(8,128)(2,1)S(1)}, bf16[256,512]{1,0:T(8,128)(2,1)S(1)}, u32[]{:S(2)}, u32[]{:S(2)}) collective-permute-start(bf16[256,512]{1,0:T(8,128)(2,1)S(1)} %get-tuple-element.141), channel_id=1, source_target_pairs={{0,16},{1,9},{2,18},{3,11},{4,20},{5,13},{6,22},{7,15},{8,24},{9,1... | collective-permute-start | bytes 786440 | tf_op jit(solution)/shard_map/ppermute | solution.py:448
  103.7 14.9 %collective-permute-start.36 = (bf16[256,512]{1,0:T(8,128)(2,1)S(1)}, bf16[256,512]{1,0:T(8,128)(2,1)S(1)}, u32[]{:S(2)}, u32[]{:S(2)}) collective-permute-start(bf16[256,512]{1,0:T(8,128)(2,1)S(1)} %get-tuple-element.139), channel_id=1, source_target_pairs={{0,4},{1,3},{2,6},{3,1},{4,0},{5,7},{6,2},{7,5},{8,12},{9,11},{10,... | collective-permute-start | bytes 786440 | tf_op jit(solution)/shard_map/ppermute | solution.py:448
  106.2 9.5 %collective-permute-start.51 = (bf16[96,512]{1,0:T(8,128)(2,1)S(1)}, bf16[96,512]{1,0:T(8,128)(2,1)S(1)}, u32[]{:S(2)}, u32[]{:S(2)}) collective-permute-start(bf16[96,512]{1,0:T(8,128)(2,1)S(1)} %pad_maximum_fusion.15), channel_id=1, source_target_pairs={{0,8},{1,17},{2,10},{3,19},{4,12},{5,21},{6,14},{7,23},{8,0},{9,25... | collective-permute-start | bytes 294920 | tf_op jit(solution)/shard_map/ppermute | solution.py:448
  110.4 14.8 %collective-permute-start.14 = (bf16[272,512]{1,0:T(8,128)(2,1)S(1)}, bf16[272,512]{1,0:T(8,128)(2,1)S(1)}, u32[]{:S(2)}, u32[]{:S(2)}) collective-permute-start(bf16[272,512]{1,0:T(8,128)(2,1)S(1)} %slice_add_fusion.8), channel_id=1, source_target_pairs={{0,4},{1,3},{2,6},{3,1},{4,0},{5,7},{6,2},{7,5},{8,12},{9,11},{10,... | collective-permute-start | bytes 835592 | tf_op jit(solution)/shard_map/ppermute | solution.py:448
  115.8 7.6 %collective-permute-start.52 = (bf16[192,512]{1,0:T(8,128)(2,1)S(1)}, bf16[192,512]{1,0:T(8,128)(2,1)S(1)}, u32[]{:S(2)}, u32[]{:S(2)}) collective-permute-start(bf16[192,512]{1,0:T(8,128)(2,1)S(1)} %pad_maximum_fusion.10), channel_id=1, source_target_pairs={{0,4},{1,3},{2,6},{3,1},{4,0},{5,7},{6,2},{7,5},{8,12},{9,11},{10,... | collective-permute-start | bytes 589832 | tf_op jit(solution)/shard_map/ppermute | solution.py:448
  116.9 8.5 %collective-permute-start.26 = (bf16[128,512]{1,0:T(8,128)(2,1)S(1)}, bf16[128,512]{1,0:T(8,128)(2,1)S(1)}, u32[]{:S(2)}, u32[]{:S(2)}) collective-permute-start(bf16[128,512]{1,0:T(8,128)(2,1)S(1)} %get-tuple-element.147), channel_id=1, source_target_pairs={{0,2},{1,5},{2,0},{3,7},{4,6},{5,1},{6,4},{7,3},{8,10},{9,13},{10,... | collective-permute-start | bytes 393224 | tf_op jit(solution)/shard_map/ppermute | solution.py:448
  118.7 7.6 %collective-permute-start.37 = (bf16[128,512]{1,0:T(8,128)(2,1)S(1)}, bf16[128,512]{1,0:T(8,128)(2,1)S(1)}, u32[]{:S(2)}, u32[]{:S(2)}) collective-permute-start(bf16[128,512]{1,0:T(8,128)(2,1)S(1)} %get-tuple-element.145), channel_id=1, source_target_pairs={{0,8},{1,17},{2,10},{3,19},{4,12},{5,21},{6,14},{7,23},{8,0},{9,25... | collective-permute-start | bytes 393224 | tf_op jit(solution)/shard_map/ppermute | solution.py:448
  123.4 36.6 %collective-permute-start.53 = (bf16[384,512]{1,0:T(8,128)(2,1)S(1)}, bf16[384,512]{1,0:T(8,128)(2,1)S(1)}, u32[]{:S(2)}, u32[]{:S(2)}) collective-permute-start(bf16[384,512]{1,0:T(8,128)(2,1)S(1)} %pad_maximum_fusion.4.a8), channel_id=1, source_target_pairs={{0,2},{1,5},{2,0},{3,7},{4,6},{5,1},{6,4},{7,3},{8,10},{9,13},{10,... | collective-permute-start | bytes 1179656 | tf_op jit(solution)/shard_map/ppermute | solution.py:448
  125.2 6.8 %collective-permute-start.15 = (bf16[144,512]{1,0:T(8,128)(2,1)S(1)}, bf16[144,512]{1,0:T(8,128)(2,1)S(1)}, u32[]{:S(2)}, u32[]{:S(2)}) collective-permute-start(bf16[144,512]{1,0:T(8,128)(2,1)S(1)} %slice_add_fusion.17), channel_id=1, source_target_pairs={{0,8},{1,17},{2,10},{3,19},{4,12},{5,21},{6,14},{7,23},{8,0},{9,25... | collective-permute-start | bytes 442376 | tf_op jit(solution)/shard_map/ppermute | solution.py:448
  125.4 9.0 %collective-permute-start.27 = (bf16[64,512]{1,0:T(8,128)(2,1)S(1)}, bf16[64,512]{1,0:T(8,128)(2,1)S(1)}, u32[]{:S(2)}, u32[]{:S(2)}) collective-permute-start(bf16[64,512]{1,0:T(8,128)(2,1)S(1)} %slice_add_fusion.28), channel_id=1, source_target_pairs={{0,4},{1,3},{2,6},{3,1},{4,0},{5,7},{6,2},{7,5},{8,12},{9,11},{10,... | collective-permute-start | bytes 196616 | tf_op jit(solution)/shard_map/ppermute | solution.py:448
  126.3 9.1 %collective-permute-start.38 = (bf16[64,512]{1,0:T(8,128)(2,1)S(1)}, bf16[64,512]{1,0:T(8,128)(2,1)S(1)}, u32[]{:S(2)}, u32[]{:S(2)}) collective-permute-start(bf16[64,512]{1,0:T(8,128)(2,1)S(1)} %slice_add_fusion.26), channel_id=1, source_target_pairs={{0,16},{1,9},{2,18},{3,11},{4,20},{5,13},{6,22},{7,15},{8,24},{9,1... | collective-permute-start | bytes 196616 | tf_op jit(solution)/shard_map/ppermute | solution.py:448
  132.1 7.0 %collective-permute-start.16 = (bf16[80,512]{1,0:T(8,128)(2,1)S(1)}, bf16[80,512]{1,0:T(8,128)(2,1)S(1)}, u32[]{:S(2)}, u32[]{:S(2)}) collective-permute-start(bf16[80,512]{1,0:T(8,128)(2,1)S(1)} %slice_add_fusion.25), channel_id=1, source_target_pairs={{0,16},{1,9},{2,18},{3,11},{4,20},{5,13},{6,22},{7,15},{8,24},{9,1... | collective-permute-start | bytes 245768 | tf_op jit(solution)/shard_map/ppermute | solution.py:448
  134.4 4.3 %collective-permute-start.28 = (bf16[64,512]{1,0:T(8,128)(2,1)S(1)}, bf16[64,512]{1,0:T(8,128)(2,1)S(1)}, u32[]{:S(2)}, u32[]{:S(2)}) collective-permute-start(bf16[64,512]{1,0:T(8,128)(2,1)S(1)} %fusion.4), channel_id=1, source_target_pairs={{0,4},{1,3},{2,6},{3,1},{4,0},{5,7},{6,2},{7,5},{8,12},{9,11},{10,... | collective-permute-start | bytes 196616 | tf_op jit(solution)/shard_map/ppermute | solution.py:448
  135.4 5.9 %collective-permute-start.39 = (bf16[64,512]{1,0:T(8,128)(2,1)S(1)}, bf16[64,512]{1,0:T(8,128)(2,1)S(1)}, u32[]{:S(2)}, u32[]{:S(2)}) collective-permute-start(bf16[64,512]{1,0:T(8,128)(2,1)S(1)} %fusion.3), channel_id=1, source_target_pairs={{0,16},{1,9},{2,18},{3,11},{4,20},{5,13},{6,22},{7,15},{8,24},{9,1... | collective-permute-start | bytes 196616 | tf_op jit(solution)/shard_map/ppermute | solution.py:448
  138.8 8.0 %collective-permute-start.29 = (bf16[128,512]{1,0:T(8,128)(2,1)S(1)}, bf16[128,512]{1,0:T(8,128)(2,1)S(1)}, u32[]{:S(2)}, u32[]{:S(2)}) collective-permute-start(bf16[128,512]{1,0:T(8,128)(2,1)S(1)} %pad_maximum_fusion.13), channel_id=1, source_target_pairs={{0,2},{1,5},{2,0},{3,7},{4,6},{5,1},{6,4},{7,3},{8,10},{9,13},{10,... | collective-permute-start | bytes 393224 | tf_op jit(solution)/shard_map/ppermute | solution.py:448
  139.2 5.2 %collective-permute-start.17 = (bf16[64,512]{1,0:T(8,128)(2,1)S(1)}, bf16[64,512]{1,0:T(8,128)(2,1)S(1)}, u32[]{:S(2)}, u32[]{:S(2)}) collective-permute-start(bf16[64,512]{1,0:T(8,128)(2,1)S(1)} %slice.309), channel_id=1, source_target_pairs={{0,16},{1,9},{2,18},{3,11},{4,20},{5,13},{6,22},{7,15},{8,24},{9,1... | collective-permute-start | bytes 196616 | tf_op jit(solution)/shard_map/ppermute | solution.py:448
  141.3 7.0 %collective-permute-start.40 = (bf16[128,512]{1,0:T(8,128)(2,1)S(1)}, bf16[128,512]{1,0:T(8,128)(2,1)S(1)}, u32[]{:S(2)}, u32[]{:S(2)}) collective-permute-start(bf16[128,512]{1,0:T(8,128)(2,1)S(1)} %pad_maximum_fusion.14), channel_id=1, source_target_pairs={{0,8},{1,17},{2,10},{3,19},{4,12},{5,21},{6,14},{7,23},{8,0},{9,25... | collective-permute-start | bytes 393224 | tf_op jit(solution)/shard_map/ppermute | solution.py:448
  144.4 5.3 %collective-permute-start.18 = (bf16[128,512]{1,0:T(8,128)(2,1)S(1)}, bf16[128,512]{1,0:T(8,128)(2,1)S(1)}, u32[]{:S(2)}, u32[]{:S(2)}) collective-permute-start(bf16[128,512]{1,0:T(8,128)(2,1)S(1)} %pad_maximum_fusion.12), channel_id=1, source_target_pairs={{0,8},{1,17},{2,10},{3,19},{4,12},{5,21},{6,14},{7,23},{8,0},{9,25... | collective-permute-start | bytes 393224 | tf_op jit(solution)/shard_map/ppermute | solution.py:448
  146.8 9.6 %collective-permute-start.30 = (bf16[256,512]{1,0:T(8,128)(2,1)S(1)}, bf16[256,512]{1,0:T(8,128)(2,1)S(1)}, u32[]{:S(2)}, u32[]{:S(2)}) collective-permute-start(bf16[256,512]{1,0:T(8,128)(2,1)S(1)} %pad_maximum_fusion.7), channel_id=1, source_target_pairs={{0,16},{1,9},{2,18},{3,11},{4,20},{5,13},{6,22},{7,15},{8,24},{9,1... | collective-permute-start | bytes 786440 | tf_op jit(solution)/shard_map/ppermute | solution.py:448
  148.3 8.2 %collective-permute-start.41 = (bf16[256,512]{1,0:T(8,128)(2,1)S(1)}, bf16[256,512]{1,0:T(8,128)(2,1)S(1)}, u32[]{:S(2)}, u32[]{:S(2)}) collective-permute-start(bf16[256,512]{1,0:T(8,128)(2,1)S(1)} %pad_maximum_fusion.8), channel_id=1, source_target_pairs={{0,4},{1,3},{2,6},{3,1},{4,0},{5,7},{6,2},{7,5},{8,12},{9,11},{10,... | collective-permute-start | bytes 786440 | tf_op jit(solution)/shard_map/ppermute | solution.py:448
  149.8 7.8 %collective-permute-start.19 = (bf16[256,512]{1,0:T(8,128)(2,1)S(1)}, bf16[256,512]{1,0:T(8,128)(2,1)S(1)}, u32[]{:S(2)}, u32[]{:S(2)}) collective-permute-start(bf16[256,512]{1,0:T(8,128)(2,1)S(1)} %pad_maximum_fusion.6), channel_id=1, source_target_pairs={{0,4},{1,3},{2,6},{3,1},{4,0},{5,7},{6,2},{7,5},{8,12},{9,11},{10,... | collective-permute-start | bytes 786440 | tf_op jit(solution)/shard_map/ppermute | solution.py:448
  152.6 7.3 %collective-permute-start.11 = (bf16[256,512]{1,0:T(8,128)(2,1)S(1)}, bf16[256,512]{1,0:T(8,128)(2,1)S(1)}, u32[]{:S(2)}, u32[]{:S(2)}) collective-permute-start(bf16[256,512]{1,0:T(8,128)(2,1)S(1)} %slice_add_fusion.14), channel_id=1, source_target_pairs={{0,2},{1,3},{2,0},{3,1},{4,6},{5,7},{6,4},{7,5},{8,10},{9,11},{10,... | collective-permute-start | bytes 786440 | tf_op jit(solution)/shard_map/ppermute | solution.py:448
  156.4 3.6 %collective-permute-start.54 = (bf16[384,512]{1,0:T(8,128)(2,1)S(1)}, bf16[384,512]{1,0:T(8,128)(2,1)S(1)}, u32[]{:S(2)}, u32[]{:S(2)}) collective-permute-start(bf16[384,512]{1,0:T(8,128)(2,1)S(1)} %pad_maximum_fusion.4.a8), channel_id=1, source_target_pairs={{0,1},{1,0},{2,3},{3,2},{4,5},{5,4},{6,7},{7,6},{8,9},{9,8},{10,11... | collective-permute-start | bytes 1179656 | tf_op jit(solution)/shard_map/ppermute | solution.py:448
  156.5 14.9 %collective-permute-start.31 = (bf16[512,512]{1,0:T(8,128)(2,1)S(1)}, bf16[512,512]{1,0:T(8,128)(2,1)S(1)}, u32[]{:S(2)}, u32[]{:S(2)}) collective-permute-start(bf16[512,512]{1,0:T(8,128)(2,1)S(1)} %pad_maximum_fusion.1.a8), channel_id=1, source_target_pairs={{0,8},{1,17},{2,10},{3,19},{4,12},{5,21},{6,14},{7,23},{8,0},{9,25... | collective-permute-start | bytes 1572872 | tf_op jit(solution)/shard_map/ppermute | solution.py:448
  157.6 13.8 %collective-permute-start.42 = (bf16[512,512]{1,0:T(8,128)(2,1)S(1)}, bf16[512,512]{1,0:T(8,128)(2,1)S(1)}, u32[]{:S(2)}, u32[]{:S(2)}) collective-permute-start(bf16[512,512]{1,0:T(8,128)(2,1)S(1)} %pad_maximum_fusion.2.a8), channel_id=1, source_target_pairs={{0,2},{1,5},{2,0},{3,7},{4,6},{5,1},{6,4},{7,3},{8,10},{9,13},{10,... | collective-permute-start | bytes 1572872 | tf_op jit(solution)/shard_map/ppermute | solution.py:448
  159.9 12.0 %collective-permute-start.32 = (bf16[512,512]{1,0:T(8,128)(2,1)S(1)}, bf16[512,512]{1,0:T(8,128)(2,1)S(1)}, u32[]{:S(2)}, u32[]{:S(2)}) collective-permute-start(bf16[512,512]{1,0:T(8,128)(2,1)S(1)} %pad_maximum_fusion.1.a8), channel_id=1, source_target_pairs={{0,1},{1,0},{2,3},{3,2},{4,5},{5,4},{6,7},{7,6},{8,9},{9,8},{10,11... | collective-permute-start | bytes 1572872 | tf_op jit(solution)/shard_map/ppermute | solution.py:448
  160.0 12.6 %collective-permute-start.20 = (bf16[512,512]{1,0:T(8,128)(2,1)S(1)}, bf16[512,512]{1,0:T(8,128)(2,1)S(1)}, u32[]{:S(2)}, u32[]{:S(2)}) collective-permute-start(bf16[512,512]{1,0:T(8,128)(2,1)S(1)} %pad_maximum_fusion.a8), channel_id=1, source_target_pairs={{0,2},{1,5},{2,0},{3,7},{4,6},{5,1},{6,4},{7,3},{8,10},{9,13},{10,... | collective-permute-start | bytes 1572872 | tf_op jit(solution)/shard_map/ppermute | solution.py:448
  160.1 2.4 %collective-permute-start.55 = (bf16[384,512]{1,0:T(8,128)(2,1)S(1)}, bf16[384,512]{1,0:T(8,128)(2,1)S(1)}, u32[]{:S(2)}, u32[]{:S(2)}) collective-permute-start(bf16[384,512]{1,0:T(8,128)(2,1)S(1)} %collective-permute-done.53.r1), channel_id=1, source_target_pairs={{0,1},{1,0},{2,3},{3,2},{4,5},{5,4},{6,7},{7,6},{8,9},{9,8},{10,11... | collective-permute-start | bytes 1179656 | tf_op jit(solution)/shard_map/ppermute | solution.py:448
  162.4 15.4 %collective-permute-start.43 = (bf16[512,512]{1,0:T(8,128)(2,1)S(1)}, bf16[512,512]{1,0:T(8,128)(2,1)S(1)}, u32[]{:S(2)}, u32[]{:S(2)}) collective-permute-start(bf16[512,512]{1,0:T(8,128)(2,1)S(1)} %pad_maximum_fusion.2.a8), channel_id=1, source_target_pairs={{0,1},{1,0},{2,3},{3,2},{4,5},{5,4},{6,7},{7,6},{8,9},{9,8},{10,11... | collective-permute-start | bytes 1572872 | tf_op jit(solution)/shard_map/ppermute | solution.py:448
  171.3 4.1 %collective-permute-start.33 = (bf16[512,512]{1,0:T(8,128)(2,1)S(1)}, bf16[512,512]{1,0:T(8,128)(2,1)S(1)}, u32[]{:S(2)}, u32[]{:S(2)}) collective-permute-start(bf16[512,512]{1,0:T(8,128)(2,1)S(1)} %collective-permute-done.31.r1), channel_id=1, source_target_pairs={{0,1},{1,0},{2,3},{3,2},{4,5},{5,4},{6,7},{7,6},{8,9},{9,8},{10,11... | collective-permute-start | bytes 1572872 | tf_op jit(solution)/shard_map/ppermute | solution.py:448
  171.3 6.5 %collective-permute-start.44 = (bf16[512,512]{1,0:T(8,128)(2,1)S(1)}, bf16[512,512]{1,0:T(8,128)(2,1)S(1)}, u32[]{:S(2)}, u32[]{:S(2)}) collective-permute-start(bf16[512,512]{1,0:T(8,128)(2,1)S(1)} %collective-permute-done.42.r1), channel_id=1, source_target_pairs={{0,1},{1,0},{2,3},{3,2},{4,5},{5,4},{6,7},{7,6},{8,9},{9,8},{10,11... | collective-permute-start | bytes 1572872 | tf_op jit(solution)/shard_map/ppermute | solution.py:448
  171.9 8.4 %collective-permute-start.21 = (bf16[512,512]{1,0:T(8,128)(2,1)S(1)}, bf16[512,512]{1,0:T(8,128)(2,1)S(1)}, u32[]{:S(2)}, u32[]{:S(2)}) collective-permute-start(bf16[512,512]{1,0:T(8,128)(2,1)S(1)} %pad_maximum_fusion.a8), channel_id=1, source_target_pairs={{0,1},{1,0},{2,3},{3,2},{4,5},{5,4},{6,7},{7,6},{8,9},{9,8},{10,11... | collective-permute-start | bytes 1572872 | tf_op jit(solution)/shard_map/ppermute | solution.py:448
  172.6 7.6 %collective-permute-start.22 = (bf16[512,512]{1,0:T(8,128)(2,1)S(1)}, bf16[512,512]{1,0:T(8,128)(2,1)S(1)}, u32[]{:S(2)}, u32[]{:S(2)}) collective-permute-start(bf16[512,512]{1,0:T(8,128)(2,1)S(1)} %collective-permute-done.20.r1), channel_id=1, source_target_pairs={{0,1},{1,0},{2,3},{3,2},{4,5},{5,4},{6,7},{7,6},{8,9},{9,8},{10,11... | collective-permute-start | bytes 1572872 | tf_op jit(solution)/shard_map/ppermute | solution.py:448
  (9 other events, 68.2 us)

commit v2 on v1

v2 whole, which is shorter than its diff:
```python
import functools

import jax
import jax.numpy as jnp
from jax import lax
from jax.experimental import pallas as pl
from jax.experimental.pallas import tpu as pltpu
from jax.sharding import PartitionSpec as P

HEAD = 64
AXES = ("rows", "tok")
BF = jnp.bfloat16
F32 = jnp.float32
norm_eps = 1e-06

ORDER_XY = ((1, 2, 3, 4), (2, 1, 4, 3))
ORDER_YX = ((2, 1, 3, 4), (1, 2, 4, 3))
ORDER_Z = ((3, 4, 1, 2), (4, 3, 2, 1))
ORDER_ZY = ((4, 3, 1, 2), (3, 4, 2, 1))
ORDERS = {"J": ORDER_XY, "U": ORDER_Z, "I": ORDER_XY, "T": ORDER_XY}
ORDER_JOIN = ((2, 4, 3), (4, 3, 2))
GROUP = 32
THREE = ((0, 1, False), (1, 1, False), (2, 1, False))
PLAN = (
    ("KJ",), ("KU",), ("KI",), ("J", "U",), ("I",), ("KT",), ("J", "U", "I", "T",), ("KG", "I", "U",),
    ("T",), ("I", "J", "g0", "U", "T",), ("I",), ("U", "J",), ("I",), ("U", "T", "J",), ("J",),
    ("I", "U", "T", "g1",), ("J",), ("T",), ("I", "J", "U",), ("T", "I",), ("J", "T",), ("U",),
    ("fI", "fU",), ("T",), ("fJ", "fT",),
)
HALF = GROUP // 2

VM = pl.BlockSpec(memory_space=pltpu.VMEM)
ANY = pl.BlockSpec(memory_space=pl.ANY)


def dot(left, right):
    return jnp.dot(left, right, preferred_element_type=F32)


def dot_tn(left, right):
    return lax.dot_general(left, right, (((0,), (0,)), ((), ())), preferred_element_type=F32)


def dot_nt(left, right):
    return lax.dot_general(left, right, (((1,), (1,)), ((), ())), preferred_element_type=F32)


def low(values):
    return values.astype(BF)


def normalize(values, gain, shift):
    centered = values - jnp.mean(values, -1, keepdims=True)
    inv_std = lax.rsqrt(jnp.mean(centered * centered, -1, keepdims=True) + norm_eps)
    unit = centered * inv_std
    return unit * gain + shift, unit, inv_std


def normalize_back(upstream, unit, inv_std, gain):
    grad_unit = upstream * gain
    projected = grad_unit - jnp.mean(grad_unit, -1, keepdims=True)
    projected = projected - unit * jnp.mean(grad_unit * unit, -1, keepdims=True)
    gain_term = jnp.sum(upstream * unit, 0, keepdims=True)
    return projected * inv_std, gain_term, jnp.sum(upstream, 0, keepdims=True)


def gelu_both(values):
    normal_cdf = 0.5 * (1.0 + lax.erf(values * 0.7071067811865476))
    slope = normal_cdf + values * jnp.exp(-0.5 * values * values) * 0.3989422804014327
    return values * normal_cdf, slope


def device_number():
    return lax.axis_index("rows") * 4 + lax.axis_index("tok")


def bit_of(number, bit):
    return lax.rem(lax.div(number, 1 << bit), 2)


def own_place(number, orders, core):
    def along(order):
        total = 0
        for bit in order:
            total = total * 2 + bit_of(number, bit)
        return total

    return jnp.where(core == 0, along(orders[0]), along(orders[1]))


def put_blocks(target, values, first_row, place, rows_each):
    row = first_row
    while row < first_row + values.shape[0]:
        block, within = divmod(row, rows_each)
        count = min(rows_each - within, first_row + values.shape[0] - row)
        spot = jnp.bitwise_xor(place, block) * rows_each + within
        target[pl.ds(pl.multiple_of(spot, 16), count), :] = values[row - first_row : row - first_row + count, :]
        row += count


def halves(keep, send, orders):
    me = device_number()
    core = bit_of(me, 0)
    return (
        (keep, core, own_place(me, orders, core)),
        (send, 1 - core, own_place(me, orders, 1 - core)),
    )


def half_columns(ref, half, begin=0, count=None):
    size = ref.shape[1] // 2
    count = size if count is None else count
    return ref[:, pl.ds(pl.multiple_of(half * size + begin, 128), count)]


def of_bank(bank, index):
    width = bank.shape[0]
    return bank[:, index * width : (index + 1) * width]


def row_slices(ref, batch, length, lanes):
    here = ref.shape[0] // 4
    begins = [place * here + batch * length for place in range(4)]
    return jnp.concatenate([ref[begin : begin + length, lanes] for begin in begins], 0)


def attend_kernel(
    x01, x2, x3, seg0, seg1, seg2, seg3, bank, ag, ab,
    qs_ref, k_ref, v_ref, p_ref, o_ref, n1_ref, rs1_ref, bias,
):
    tokens_here, width = x2.shape
    batches = seg0.shape[0]
    length = tokens_here // batches
    qs_ref[...] = low(low(dot(x01[:tokens_here, :], of_bank(bank, 0))) * HEAD ** (-0.5))
    row = 0
    for piece in (x01, x2, x3):
        span = slice(row, row + piece.shape[0])
        k_ref[span, :] = low(dot(piece[...], of_bank(bank, 1)))
        v_ref[span, :] = low(dot(piece[...], of_bank(bank, 2)))
        row += piece.shape[0]
    segments = [ref[...].astype(F32) for ref in (seg0, seg1, seg2, seg3)]
    lane = lax.broadcasted_iota(jnp.int32, (1, 2 * HEAD), 1)
    first = (lane < HEAD).astype(BF)
    second = (lane >= HEAD).astype(BF)
    for batch in range(batches):
        query_seg = segments[0][batch : batch + 1, :]
        for index, segment in enumerate(segments):
            row = segment[batch : batch + 1, :]
            key_seg = jnp.transpose(jnp.broadcast_to(row, (length, length)))
            bias[pl.ds(index * length, length), :] = jnp.where(key_seg == query_seg, 0.0, -1e30)
        both = jnp.concatenate([bias[...], bias[...]], 1)
        for pair in range(width // (2 * HEAD)):
            lanes = slice(pair * 2 * HEAD, (pair + 1) * 2 * HEAD)
            kp = row_slices(k_ref, batch, length, lanes)
            vp = row_slices(v_ref, batch, length, lanes)
            qp = qs_ref[batch * length : (batch + 1) * length, lanes]
            stacked = jnp.concatenate([qp * first, qp * second], 0)
            scores = dot_nt(kp, stacked) + both
            exps = jnp.exp(scores - jnp.max(scores, 0, keepdims=True))
            probs = low(exps * (1.0 / jnp.sum(exps, 0, keepdims=True)))
            p_ref[batch * (width // (2 * HEAD)) + pair] = probs
            mixed = dot_tn(vp, probs)
            joined = jnp.concatenate([mixed[:HEAD, :length], mixed[HEAD:, length:]], 0)
            o_ref[batch * length : (batch + 1) * length, lanes] = low(jnp.transpose(joined))
    residual = x01[:tokens_here, :].astype(F32) + dot(o_ref[...], of_bank(bank, 3))
    _, unit, inv_std = normalize(residual, ag[...], ab[...])
    n1_ref[...] = unit
    rs1_ref[...] = jnp.broadcast_to(inv_std, rs1_ref.shape)


def feed_kernel(
    n1_ref, ag, ab, wi, bi, wu, mg, mb, bank, u_ref, sz_ref, n2_ref, rs2_ref, c_ref, st_ref
):
    width = n1_ref.shape[1]
    outer = n1_ref[...] * ag[...] + ab[...]
    al = low(outer)
    for part in range(wi.shape[1] // width):
        span = slice(part * width, (part + 1) * width)
        inner = dot(al, wi[:, span]) + bi[:, span]
        active, slope = gelu_both(inner)
        u_ref[:, span] = low(active)
        sz_ref[:, span] = low(slope)
        outer = outer + dot(low(active), wu[span, :])
    hidden, unit, inv_std = normalize(outer, mg[...], mb[...])
    n2_ref[...] = unit
    rs2_ref[...] = jnp.broadcast_to(inv_std, rs2_ref.shape)
    active, slope = gelu_both(dot(low(hidden), of_bank(bank, 4)))
    c_ref[...] = low(active)
    st_ref[...] = low(slope)


def joining_kernel(
    gathered, bottleneck, adapters, n2_ref, mg, mb, c_ref, st_ref, up, cot, fg, fb, *rest
):
    if gathered:
        jw_in, rest = rest[:8], rest[8:]
    else:
        jw_in, rest = rest[:1], rest[1:]
    out_ref, keep, send, dhp_ref, dt_ref, vec_ref, wj, left, right = rest
    width = n2_ref.shape[1]
    scale = width ** (-0.5)
    me = device_number()
    core = bit_of(me, 0)
    if gathered:
        shard, column = jw_in[0].shape[2:]
        for which in range(2):
            half = core if which == 0 else 1 - core
            columns = pl.ds(pl.multiple_of(half * column, column), column)
            for spot in range(8):
                flips = [sum(((spot >> i) & 1) << (order[i] - 2) for i in range(3)) for order in ORDER_JOIN]
                owner = jnp.bitwise_xor(lax.div(me, 4), jnp.where(half == 0, flips[0], flips[1]))
                rows = pl.ds(pl.multiple_of(owner * shard, shard), shard)
                for matrix in range(3):
                    wj[matrix, rows, columns] = jw_in[which * 4 + spot // 2][spot % 2, matrix]
    else:
        wj[...] = jw_in[0][...]
    hidden = n2_ref[...] * mg[...] + mb[...]
    hidden_low = low(hidden)
    cf = c_ref[...].astype(F32)
    row_group = lax.broadcasted_iota(jnp.int32, (width, 128), 0) // bottleneck
    column_of = lax.broadcasted_iota(jnp.int32, (width, 128), 1)
    member = (row_group == column_of).astype(BF)
    valid = lax.broadcasted_iota(jnp.int32, (1, 128), 1) < adapters

    def per_adapter(values):
        high = low(values)
        rest_of = low(values - high.astype(F32))
        return dot(high, member) + dot(rest_of, member)

    fq = low(dot(hidden_low, wj[0]))
    probe = low(dot_nt(fq, wj[1]))
    probe_f = probe.astype(F32)
    up_probe = dot_nt(probe, up[...])
    scores = (
        per_adapter(cf * up_probe) + jnp.sum(hidden * probe_f, -1, keepdims=True)
    ) * scale
    scores = jnp.where(valid, scores, -1e30)
    exps = jnp.exp(scores - jnp.max(scores, -1, keepdims=True))
    weights = exps * (1.0 / jnp.sum(exps, -1, keepdims=True))
    weights_low = low(weights)
    weights_wide = dot_nt(weights_low, member)
    weights_sum = jnp.sum(weights_low.astype(F32), -1, keepdims=True)
    mixed = low(weights_sum * hidden + dot(low(weights_wide * cf), up[...]))
    final, unit, inv_std = normalize(hidden + dot(mixed, wj[2]), fg[...], fb[...])
    out_ref[...] = low(final)
    d3, gain_term, shift_term = normalize_back(cot[...].astype(F32), unit, inv_std, fg[...])
    vec_ref[...] = jnp.concatenate(
        [gain_term, shift_term, jnp.zeros((vec_ref.shape[0] - 2, width), F32)], 0
    )
    dfo = low(d3)
    left[2] = mixed
    right[2] = dfo
    dm = low(dot_nt(dfo, wj[2]))
    dm_f = dm.astype(F32)
    up_dm = dot_nt(dm, up[...])
    dw = per_adapter(cf * up_dm) + jnp.sum(hidden * dm_f, -1, keepdims=True)
    df = low(weights * (dw - jnp.sum(weights * dw, -1, keepdims=True)))
    df_wide = dot_nt(df, member)
    df_sum = jnp.sum(df.astype(F32), -1, keepdims=True)
    dr = low((df_sum * hidden + dot(low(df_wide * cf), up[...])) * scale)
    left[1] = dr
    right[1] = fq
    dfq = low(dot(dr, wj[1]))
    left[0] = hidden_low
    right[0] = dfq
    for target, half, place in halves(keep, send, ORDERS["J"]):
        for matrix in range(3):
            term = low(dot_tn(half_columns(left.at[matrix], half), right[matrix]))
            put_blocks(target, term, matrix * (width // 2), place, 3 * width // GROUP)
    dc = weights_wide * up_dm + (df_wide * scale) * up_probe
    dt_ref[...] = low(dc * st_ref[...].astype(F32))
    dhp_ref[...] = (
        d3 + weights_sum * dm_f + (df_sum * scale) * probe_f + dot_nt(dfq, wj[0])
    )


def outer_back_kernel(
    dhp_ref, dt_ref, bank, n2_ref, rs2_ref, mg, u_ref, d2_ref, vec_ref, keep, send
):
    width = dhp_ref.shape[1]
    hidden_grad = dhp_ref[...] + dot_nt(dt_ref[...], of_bank(bank, 4))
    d2, mg_term, mb_term = normalize_back(hidden_grad, n2_ref[...], rs2_ref[:, :1], mg[...])
    d2_ref[...] = d2
    dfw = low(d2)
    units = u_ref.shape[1]
    for target, half, place in halves(keep, send, ORDERS["U"]):
        for begin in range(0, units // 2, width):
            term = low(dot_tn(half_columns(u_ref, half, begin, width), dfw))
            put_blocks(target, term, begin, place, units // GROUP)
    vec_ref[...] = jnp.concatenate([mg_term, mb_term, jnp.zeros((vec_ref.shape[0] - 2, width), F32)], 0)


def inner_back_kernel(
    d2_ref, sz_ref, wi, wu, n1_ref, rs1_ref, ag, ab, o_ref, vec_final, vec_middle,
    d1_ref, vec_ref, keep, send, dz_scr, dao_scr,
):
    width = d2_ref.shape[1]
    total = d2_ref[...]
    dfw = low(total)
    al = low(n1_ref[...] * ag[...] + ab[...])
    bias_terms = []
    parts = wi.shape[1] // width
    for part in range(parts):
        span = slice(part * width, (part + 1) * width)
        dz = low(dot_nt(dfw, wu[span, :]) * sz_ref[:, span].astype(F32))
        bias_terms.append(jnp.sum(dz.astype(F32), 0, keepdims=True))
        dz_scr[:, span] = dz
        total = total + dot_nt(dz, wi[:, span])
    d1, ag_term, ab_term = normalize_back(total, n1_ref[...], rs1_ref[:, :1], ag[...])
    d1_ref[...] = d1
    dao_scr[...] = low(d1)
    units = wi.shape[1]
    rows_each = (units + width) // GROUP
    for target, half, place in halves(keep, send, ORDERS["I"]):
        for begin in range(0, units // 2, width):
            term = low(dot_tn(al, half_columns(dz_scr, half, begin, width)))
            put_blocks(target, term, begin, place, rows_each)
        term = low(dot_tn(half_columns(o_ref, half), dao_scr[...]))
        put_blocks(target, term, units // 2, place, rows_each)
    rows = [ag_term, ab_term, vec_middle[0:1, :], vec_middle[1:2, :], vec_final[0:1, :], vec_final[1:2, :]]
    rows += bias_terms
    rows.append(jnp.zeros((vec_ref.shape[0] - len(rows), width), F32))
    vec_ref[...] = low(jnp.concatenate(rows, 0))


def attend_back_kernel(
    d1_ref, bank, o_ref, qs_ref, k_ref, v_ref, p_ref, x01, x2, x3, vec_ref,
    keep, send, dq_ref, dk_ref, dv_ref, do_scr, row_x,
):
    tokens_here, width = x2.shape
    length = p_ref.shape[2] // 2
    batches = tokens_here // length
    pairs = width // (2 * HEAD)
    do_scr[...] = low(dot_nt(low(d1_ref[...]), of_bank(bank, 3)))
    lane = lax.broadcasted_iota(jnp.int32, (1, 2 * HEAD), 1)
    first = (lane < HEAD).astype(BF)
    second = (lane >= HEAD).astype(BF)
    for batch in range(batches):
        here = slice(batch * length, (batch + 1) * length)
        spans = [
            slice(index * tokens_here + batch * length, index * tokens_here + (batch + 1) * length)
            for index in range(4)
        ]
        for pair in range(pairs):
            lanes = slice(pair * 2 * HEAD, (pair + 1) * 2 * HEAD)
            kp = row_slices(k_ref, batch, length, lanes)
            vp = row_slices(v_ref, batch, length, lanes)
            qp = qs_ref[here, lanes]
            dop = do_scr[here, lanes]
            q_stacked = jnp.concatenate([qp * first, qp * second], 0)
            do_stacked = jnp.concatenate([dop * first, dop * second], 0)
            probs = p_ref[batch * pairs + pair]
            op = o_ref[here, lanes].astype(F32)
            product = dop.astype(F32) * op
            high = low(product)
            rest = low(product - high.astype(F32))
            spread = jnp.concatenate([high * first, high * second], 0)
            spread_rest = jnp.concatenate([rest * first, rest * second], 0)
            ones = jnp.ones((8, 2 * HEAD), BF)
            shift = (dot_nt(ones, spread) + dot_nt(ones, spread_rest))[:1, :]
            ds = low(probs.astype(F32) * (dot_nt(vp, do_stacked) - shift))
            dv = low(dot(probs, do_stacked))
            dk = low(dot(ds, q_stacked))
            for index, span in enumerate(spans):
                rows = slice(index * length, (index + 1) * length)
                dk_ref[span, lanes] = dk[rows, :]
                dv_ref[span, lanes] = dv[rows, :]
            mixed = dot_tn(kp, ds)
            joined = jnp.concatenate([mixed[:HEAD, :length], mixed[HEAD:, length:]], 0)
            dq_ref[here, lanes] = low(jnp.transpose(joined) * HEAD ** (-0.5))
    row_x[: 2 * tokens_here, :] = x01[...]
    row_x[2 * tokens_here : 3 * tokens_here, :] = x2[...]
    row_x[3 * tokens_here :, :] = x3[...]
    rows_each = 3 * width // GROUP
    for target, half, place in halves(keep, send, ORDERS["T"]):
        terms = (
            dot_tn(half_columns(x01.at[:tokens_here, :], half), dq_ref[...]),
            dot_tn(half_columns(row_x, half), dk_ref[...]),
            dot_tn(half_columns(row_x, half), dv_ref[...]),
        )
        for matrix, term in enumerate(terms):
            put_blocks(target, low(term), matrix * (width // 2), place, rows_each)
        target[HALF * rows_each :, :] = vec_ref[...]


def input_back_kernel(d1_ref, dq_ref, dk_ref, dv_ref, bank, gi_own, gi_keep, gi_send):
    tokens_here = d1_ref.shape[0]
    parts = []
    for index in range(4):
        span = slice(index * tokens_here, (index + 1) * tokens_here)
        parts.append(dot_nt(dk_ref[span, :], of_bank(bank, 1)) + dot_nt(dv_ref[span, :], of_bank(bank, 2)))
    gi_own[...] = parts[0] + d1_ref[...] + dot_nt(dq_ref[...], of_bank(bank, 0))
    gi_keep[...] = low(parts[2])
    gi_send[:tokens_here, :] = low(parts[1])
    gi_send[tokens_here:, :] = low(parts[3])


def finish_kernel(orders, layout, with_vec, a8, r1, s8, sr1, *rest):
    if with_vec:
        vec, rest = rest[0], rest[1:]
    full, sems = rest[-2:]
    outs = rest[:-2]
    me = device_number()
    core = bit_of(me, 0)
    each = a8.shape[0] // (HALF // 2)
    half_rows = HALF * each
    width = full.shape[1]
    copies = []
    for which, (lower, upper) in enumerate(((a8, r1), (s8, sr1))):
        half = core if which == 0 else 1 - core
        place = own_place(me, orders, half)
        base = pl.multiple_of(half * half_rows, half_rows)
        for spot in range(HALF):
            source = lower if spot < HALF // 2 else upper
            begin = (spot % (HALF // 2)) * each
            block = jnp.bitwise_xor(place, spot)
            full[pl.ds(pl.multiple_of(base + block * each, 8), each), :] = source[
                begin : begin + each, :
            ].astype(F32)
        row = 0
        for out, pieces, by_column in layout:
            for piece in range(pieces):
                target = outs[out]
                if by_column:
                    size = target.shape[0]
                    column = pl.multiple_of((half * pieces + piece) * width, width)
                    target = target.at[:, pl.ds(column, width)]
                else:
                    size = target.shape[0] // 2
                    target = target.at[pl.ds(pl.multiple_of(half * size, size), size), :]
                source = full.at[pl.ds(pl.multiple_of(base + row, 8), size), :]
                copies.append(pltpu.make_async_copy(source, target, sems.at[len(copies)]))
                copies[-1].start()
                row += size
    if with_vec:
        values = vec[...].astype(F32)
        small = [out for out in outs if out.shape[0] == 1]
        for index in range(6):
            small[index][...] = values[index : index + 1, :]
        for part in range(small[6].shape[1] // width):
            small[6][:, part * width : (part + 1) * width] = values[6 + part : 7 + part, :]
    for copy in copies:
        copy.wait()


def call(kernel, name, microseconds, out_shapes, out_specs, in_specs, scratch, *operands):
    return pl.pallas_call(
        kernel,
        out_shape=out_shapes,
        in_specs=in_specs,
        out_specs=out_specs,
        scratch_shapes=scratch,
        compiler_params=pltpu.CompilerParams(vmem_limit_bytes=32 * 1024 * 1024),
        cost_estimate=pl.CostEstimate(
            flops=int(microseconds * 1e4), bytes_accessed=int(microseconds * 1e2), transcendentals=0
        ),
        name=name,
    )(*operands)


def shape(dims, kind=BF):
    return jax.ShapeDtypeStruct(dims, kind)


def per_device(
    row_total,
    tokens, segments, cotangent, query_weight, key_weight, value_weight, out_weight,
    attend_gain, attend_bias, inner_weight, inner_bias, outer_weight, middle_gain, middle_bias,
    adapter_down, adapter_up, joining_query, joining_key, joining_value, final_gain, final_bias,
):
    batches, row_count, length, width = tokens.shape
    here = batches * row_count * length
    hidden_units = inner_weight.shape[1]
    adapters, bottleneck = adapter_up.shape[0], adapter_up.shape[1]
    devices = row_total * 4
    pairs = width // (2 * HEAD)

    def swap(values, partner):
        return lax.ppermute(values, AXES, [(d, partner(d)) for d in range(devices)])

    def over_bit(values, bit, label="over_bit"):
        with jax.named_scope(label):
            return swap(values, lambda d: d ^ (1 << bit))

    def over_stage(values, orders, stage, label="over_stage"):
        with jax.named_scope(label):
            return swap(values, lambda d: d ^ (1 << orders[d & 1][stage]))

    token = [lax.create_token()]

    def gate(values):
        return lax.optimization_barrier((token[0], values))[1]

    def mark(values):
        token[0], values = lax.optimization_barrier((token[0], values))
        return values

    row = lambda vector: vector.reshape(1, -1)

    gathered = row_total == 8 and joining_query.shape[0] % 16 == 0
    stacked = jnp.stack([joining_query, joining_key, joining_value], 0)
    if gathered:
        core = lax.rem(lax.axis_index("tok"), 2)
        column = width // 2
        piece = lax.dynamic_slice_in_dim(stacked, core * column, column, 2)[None]
        far = over_stage(piece, ORDER_JOIN, 0, "weights_first")

    x0 = tokens.reshape(here, width)
    x2 = over_bit(x0, 1, "row_far")
    x1 = over_bit(x0, 0, "row_near")
    seg = segments.reshape(batches, length)
    with jax.named_scope("segments"):
        segs = [seg] + [swap(seg, lambda d, flip=flip: d ^ flip) for flip in (1, 2, 3)]
    if gathered:
        far = mark(far)
    if gathered:
        near = mark(jnp.concatenate([piece, gate(far)], 0))
        far = over_stage(near, ORDER_JOIN, 1, "weights_second")
    bank = mark(
        jnp.concatenate([gate(query_weight), key_weight, value_weight, out_weight, adapter_down], 1)
    )
    x01 = mark(jnp.concatenate([x0, gate(x1)], 0))
    segs = mark(segs)
    x2 = mark(x2)
    x3 = over_bit(x2, 0, "row_cross")
    if gathered:
        far = mark(far)
        third = [over_stage(part, ORDER_JOIN, 2, "weights_third") for part in (near, far)]
    else:
        jw = (lax.all_gather(stacked, "rows", axis=1, tiled=True),)

    x3 = mark(x3)
    qs, keys, values, probs, attended, n1, rs1 = call(
        attend_kernel,
        "attend",
        6,
        (
            shape((here, width)), shape((4 * here, width)), shape((4 * here, width)),
            shape((batches * pairs, 4 * length, 2 * length)), shape((here, width)),
            shape((here, width), F32), shape((here, 128), F32),
        ),
        (VM,) * 7,
        (VM,) * 10,
        [pltpu.VMEM((4 * length, length), F32)],
        x01, x2, x3, *segs, bank,
        gate(row(attend_gain)), row(attend_bias),
    )
    if gathered:
        n1 = mark(n1)
        third = mark(third)
        jw = (near, far, *third)
        jw += tuple(over_bit(gate(part), 0, "weights_core") for part in jw)
    active, slope_z, n2, rs2, bottle, slope_t = call(
        feed_kernel,
        "feed",
        3,
        (
            shape((here, hidden_units)), shape((here, hidden_units)), shape((here, width), F32),
            shape((here, 128), F32), shape((here, width)), shape((here, width)),
        ),
        (VM,) * 6,
        (VM,) * 9,
        [],
        n1, row(attend_gain), row(attend_bias), inner_weight, row(inner_bias), outer_weight,
        gate(row(middle_gain)), row(middle_bias), bank,
    )
    n2 = mark(n2)

    waiting = []

    def later(values, travel, put):
        waiting.append((values, travel, put, len(waiting)))

    def start_waiting():
        for values, travel, put, place in waiting:
            put(travel(values if place == len(waiting) - 1 else gate(values)))
        waiting.clear()

    class Stream:
        def __init__(self, name, orders, rows_each):
            self.name, self.orders, self.rows_each, self.count = name, orders, rows_each, 0

        def send(self, values, stage, label, into="got"):
            def travel(operand):
                with jax.named_scope(f"{self.name}_{label}"):
                    if stage is None:
                        return over_bit(operand, 0)
                    return over_stage(operand, self.orders, stage)

            later(values, travel, lambda result: setattr(self, into, result))

        def begin(self, keep, send):
            self.keep, self.rows = keep, HALF * self.rows_each
            self.send(mark(send), None, "core")

        def step(self):
            stage, self.count = self.count, self.count + 1
            label = f"step_{stage}"
            keep, got = self.keep, gate(self.got)
            if stage < 4:
                middle = self.rows // 2
                send = mark(keep[middle:] + got[middle:])
                self.send(send, stage, label)
                self.keep = jnp.concatenate(
                    [keep[:middle] + got[:middle], keep[self.rows :] + got[self.rows :]], 0
                )
                self.rows = middle
            elif stage == 4:
                block = keep + got
                for bit in range(5, devices.bit_length() - 1):
                    block = block + over_bit(block, bit)
                self.extra = block[self.rows_each :]
                self.keep = mark(block[: self.rows_each])
                self.send(self.keep, 3, label)
            elif stage < 8:
                self.keep = mark(jnp.concatenate([keep, got], 0))
                self.send(self.keep, 7 - stage, label)
                if stage == 7:
                    self.send(self.keep, None, "sibling", "sibling")
            else:
                self.got, self.sibling = mark((got, self.sibling))
                self.send(self.got, None, "upper", "upper")

        def parts(self):
            return self.keep, self.got, self.sibling, self.upper

    def finish(stream, outs, layout, name, vector=None):
        parts = stream.parts()
        rows = parts[0].shape[0] * 4
        small = [] if vector is None else [shape((1, width), F32)] * 6 + [shape((1, hidden_units), F32)]
        out = call(
            functools.partial(finish_kernel, stream.orders, layout, vector is not None),
            name,
            2,
            tuple(outs) + tuple(small),
            (ANY,) * len(outs) + (VM,) * len(small),
            (VM,) * (4 if vector is None else 5),
            [pltpu.VMEM((rows, width), F32), pltpu.SemaphoreType.DMA((8,))],
            parts[0], parts[1], parts[2], gate(parts[3]), *(() if vector is None else (vector,)),
        )
        out = list(out)
        out[0] = mark(out[0])
        return out

    blocks = hidden_units // width
    square = shape((width, width), F32)
    each = lambda count: count * width // GROUP
    streams = {
        "J": Stream("joining_sum", ORDERS["J"], each(3)),
        "U": Stream("outer_sum", ORDERS["U"], each(blocks)),
        "I": Stream("inner_sum", ORDERS["I"], each(blocks + 1)),
        "T": Stream("attend_sum", ORDERS["T"], each(3)),
    }
    done = {}

    half_rows = lambda count: count * width // 2
    up = adapter_up.reshape(adapters * bottleneck, width)

    def joining_step():
        done["output"], keep, send, done["dhp"], done["dt"], done["vec_final"] = call(
            functools.partial(joining_kernel, gathered, bottleneck, adapters),
            "joining",
            8,
            (
                shape((here, width)), shape((half_rows(3), width)), shape((half_rows(3), width)),
                shape((here, width), F32), shape((here, width)), shape((8, width), F32),
            ),
            (VM,) * 6,
            (VM,) * (9 + len(jw)),
            [
                pltpu.VMEM((3, width, width), BF), pltpu.VMEM((3, here, width), BF),
                pltpu.VMEM((3, here, width), BF),
            ],
            n2, row(middle_gain), row(middle_bias), bottle, slope_t, up, cotangent.reshape(here, width),
            row(final_gain), row(final_bias), *jw,
        )
        streams["J"].begin(keep, send)

    def outer_step():
        done["d2"], done["vec_middle"], keep, send = call(
            outer_back_kernel,
            "outer_back",
            4,
            (
                shape((here, width), F32), shape((8, width), F32),
                shape((half_rows(blocks), width)), shape((half_rows(blocks), width)),
            ),
            (VM,) * 4,
            (VM,) * 7,
            [],
            done["dhp"], done["dt"], bank, n2, rs2, gate(row(middle_gain)), active,
        )
        streams["U"].begin(keep, send)

    def inner_step():
        done["d1"], done["vec"], keep, send = call(
            inner_back_kernel,
            "inner_back",
            6,
            (
                shape((here, width), F32), shape((16, width)),
                shape((half_rows(blocks + 1), width)), shape((half_rows(blocks + 1), width)),
            ),
            (VM,) * 4,
            (VM,) * 11,
            [pltpu.VMEM((here, hidden_units), BF), pltpu.VMEM((here, width), BF)],
            done["d2"], slope_z, inner_weight, outer_weight, n1, rs1, gate(row(attend_gain)),
            row(attend_bias), attended, done["vec_final"], done["vec_middle"],
        )
        streams["I"].begin(keep, send)

    def attend_step():
        keep, send, done["dq"], done["dk"], done["dv"] = call(
            attend_back_kernel,
            "attend_back",
            8,
            (
                shape((half_rows(3) + 16, width)), shape((half_rows(3) + 16, width)),
                shape((here, width)), shape((4 * here, width)), shape((4 * here, width)),
            ),
            (VM,) * 5,
            (VM,) * 11,
            [pltpu.VMEM((here, width), BF), pltpu.VMEM((4 * here, width), BF)],
            done["d1"], bank, attended, qs, keys, values, probs, x01, x2, x3, gate(done["vec"]),
        )
        streams["T"].begin(keep, send)

    def input_step():
        own, keep, send = call(
            input_back_kernel,
            "input_back",
            2,
            (shape((here, width), F32), shape((here, width)), shape((2 * here, width))),
            (VM,) * 3,
            (VM,) * 5,
            [],
            gate(done["d1"]), done["dq"], done["dk"], done["dv"], bank,
        )
        keep = mark(keep)
        done["gi"] = (own, keep)
        later(send, lambda values: over_bit(values, 0), lambda result: done.update(near=result))

    kernels = {"KJ": joining_step, "KU": outer_step, "KI": inner_step, "KT": attend_step, "KG": input_step}

    def run(plan):
        for step in [step for group in plan for step in group + (None,)]:
            if step is None:
                start_waiting()
            elif step in kernels:
                kernels[step]()
            elif step == "fJ":
                done["J"] = finish(streams["J"], [square] * 3, THREE, "finish_joining")
            elif step == "fU":
                done["U"] = finish(
                    streams["U"], [shape((hidden_units, width), F32)], ((0, 1, False),), "finish_outer"
                )
            elif step == "fI":
                done["I"] = finish(
                    streams["I"], [shape((width, hidden_units), F32), square],
                    ((0, blocks // 2, True), (1, 1, False)), "finish_inner",
                )
            elif step == "fT":
                done["T"] = finish(streams["T"], [square] * 3, THREE, "finish_attend", streams["T"].extra)
            elif step == "g0":
                got = gate(done["near"])
                send = mark(done["gi"][1] + got[here:])
                later(send, lambda values: over_bit(values, 1), lambda result: done.update(far=result))
                done["near"] = got[:here]
            elif step == "g1":
                far = gate(done["far"])
                done["input"] = mark(low(done["gi"][0] + done["near"].astype(F32) + far.astype(F32)))
            else:
                streams[step].step()

    run(PLAN)
    last, inner, out_grad = done["T"], done["I"][0], done["I"][1]
    outer, joining, output, input_grad = done["U"][0], done["J"], done["output"], done["input"]
    flat = lambda values: values.reshape(-1)
    return (
        output.reshape(tokens.shape), input_grad.reshape(tokens.shape),
        last[0], last[1], last[2], out_grad, flat(last[3]), flat(last[4]),
        inner, flat(last[9]), outer, flat(last[5]), flat(last[6]),
        joining[0], joining[1], joining[2], flat(last[7]), flat(last[8]),
    )


def solution(mesh):
    return jax.shard_map(
        functools.partial(per_device, mesh.shape["rows"]),
        mesh=mesh,
        in_specs=(
            P(None, "rows", "tok", None), P(None, "rows", "tok"), P(None, "rows", "tok", None),
        ) + (P(),) * 13 + (P("rows", None),) * 3 + (P(),) * 2,
        out_specs=(P(None, "rows", "tok", None),) * 2 + (P(),) * 16,
        check_vma=False,
    )
```

time: 184 us -> 148 us (0.80)
  Pallas kernels: 51 us -> 32.6 us
  waiting for transfers between devices: 64.8 us -> 52.2 us
  starting transfers between devices: 62 us -> 55.6 us
    pallas_call x8 -> x11, Pallas kernels: 51 us -> 32.6 us  [call(): pl.pallas_call(kernel, out_shape=out_shapes, in_specs=in_specs, out_specs...]
    ppermute x56 -> x60, waiting for transfers between devices: 64.8 us -> 52.2 us  [swap(): return lax.ppermute(values, AXES, [(d, partner(d)) for d in range(devices)])]
    ppermute x56 -> x60, starting transfers between devices: 62 us -> 55.6 us  [swap(): return lax.ppermute(values, AXES, [(d, partner(d)) for d in range(devices)])]
  transfers between devices with their start and end apart: 56 -> 60, of which waited for: 22 -> 24; matrix products, arithmetic and copies ran while one was open for 1% -> 3% of each run, Pallas kernels for 22% -> 17%
where the time goes in v2:
time: 148 us; the launch traced here: 147 us
  starting transfers between devices  55.6 us (38%)
  waiting for transfers between devices  52.2 us (35%)
  Pallas kernels  32.6 us (22%)
  other arithmetic  3.03 us (2%)
  local copies, waits for them, and re-layouts  2.37 us (2%)
  between operations  1.63 us (1%)
    ppermute x60, starting transfers between devices, swap(): return lax.ppermute(values, AXES, [(d, partner(d)) for d in range(devices)])  55.6 us
    ppermute x60, waiting for transfers between devices, swap(): return lax.ppermute(values, AXES, [(d, partner(d)) for d in range(devices)])  52.2 us
    pallas_call x11, Pallas kernels, call(): pl.pallas_call(kernel, out_shape=out_shapes, in_specs=in_specs, out_specs...  32.6 us
  transfers between devices with their start and end apart: 60, of which 24 were waited for; matrix products, arithmetic and copies ran while one was open for 3% of the time, Pallas kernels for 17%

profile of v2, /device:TPU:0, one launch (start us, length us, event | category | flops | bytes accessed | tf_op | source)
XLA Modules:
  0.0 147.5 jit_solution(12941709663906177572)
XLA Ops:
  0.7 0.9 fusion.4
  1.6 3.0 %collective-permute-start = (bf16[1,3,64,256]{3,2,1,0:T(8,128)(2,1)S(1)}, bf16[1,3,64,256]{3,2,1,0:T(8,128)(2,1)S(1)}, u32[]{:S(2)}, u32[]{:S(2)}) collective-permute-start(bf16[1,3,64,256]{3,2,1,0:T(8,128)(2,1)S(1)} %fusion.4), channel_id=1, source_target_pairs={{0,4},{1,17},{2,6},{3,19},{4,0},{5,21},{6,2},{7,23},{8,12},{9,25},... | collective-permute-start | bytes 294920 | tf_op jit(solution)/shard_map/weights_first/ppermute | solution.py:479
  4.6 1.7 %collective-permute-start.4 = (s32[2,128]{1,0:T(2,128)}, s32[2,128]{1,0:T(2,128)S(1)}, u32[]{:S(2)}, u32[]{:S(2)}) collective-permute-start(s32[2,128]{1,0:T(2,128)} %bitcast.45), channel_id=1, source_target_pairs={{0,3},{1,2},{2,1},{3,0},{4,7},{5,6},{6,5},{7,4},{8,11},{9,10},{10,... | collective-permute-start | bytes 3080 | tf_op jit(solution)/shard_map/segments/ppermute | solution.py:479
  6.9 1.5 %collective-permute-start.5 = (bf16[256,512]{1,0:T(8,128)(2,1)}, bf16[256,512]{1,0:T(8,128)(2,1)S(1)}, u32[]{:S(2)}, u32[]{:S(2)}) collective-permute-start(bf16[256,512]{1,0:T(8,128)(2,1)} %bitcast.50), channel_id=1, source_target_pairs={{0,2},{1,3},{2,0},{3,1},{4,6},{5,7},{6,4},{7,5},{8,10},{9,11},{10,... | collective-permute-start | bytes 786440 | tf_op jit(solution)/shard_map/row_far/ppermute | solution.py:479
  8.4 2.0 %collective-permute-start.6 = (bf16[2,3,64,256]{3,2,1,0:T(8,128)(2,1)S(1)}, bf16[2,3,64,256]{3,2,1,0:T(8,128)(2,1)S(1)}, u32[]{:S(2)}, u32[]{:S(2)}) collective-permute-start(bf16[2,3,64,256]{3,2,1,0:T(8,128)(2,1)S(1)} %pad_maximum_fusion.8.rest_0_), channel_id=1, source_target_pairs={{0,16},{1,9},{2,18},{3,11},{4,20},{5,13},{6,22},{7,15},{8,24},{9,1... | collective-permute-start | bytes 589832 | tf_op jit(solution)/shard_map/weights_second/ppermute | solution.py:479
  10.4 1.1 constant_dynamic-update-slice_fusion.4
  11.5 1.1 constant_dynamic-update-slice_fusion.3
  13.0 1.1 collective-permute-done.2.seg1
  14.1 0.9 collective-permute-done.5.x2
  14.9 1.6 %collective-permute-start.8 = (bf16[2,3,64,256]{3,2,1,0:T(8,128)(2,1)S(1)}, bf16[2,3,64,256]{3,2,1,0:T(8,128)(2,1)S(1)}, u32[]{:S(2)}, u32[]{:S(2)}) collective-permute-start(bf16[2,3,64,256]{3,2,1,0:T(8,128)(2,1)S(1)} %pad_maximum_fusion.8.rest_0_), channel_id=1, source_target_pairs={{0,8},{1,5},{2,10},{3,7},{4,12},{5,1},{6,14},{7,3},{8,0},{9,13},{1... | collective-permute-start | bytes 589832 | tf_op jit(solution)/shard_map/weights_third/ppermute | solution.py:479
  17.7 5.8 %attend.1 = (bf16[256,512]{1,0:T(8,128)(2,1)S(1)}, bf16[1024,512]{1,0:T(8,128)(2,1)S(1)}, bf16[1024,512]{1,0:T(8,128)(2,1)S(1)}, bf16[8,512,256]{2,1,0:T(8,128)(...) custom-call(bf16[512,512]{1,0:T(8,128)(2,1)S(1)} %pad_maximum_fusion.1.x01, ...), custom_call_target="tpu_custom_call" | custom-call | flops 60000 | bytes 600 | tf_op jit(solution)/shard_map/attend/pallas_call | solution.py:447
  24.7 2.7 %feed.1 = (bf16[256,2048]{1,0:T(8,128)(2,1)S(1)}, bf16[256,2048]{1,0:T(8,128)(2,1)S(1)}, f32[256,512]{1,0:T(8,128)S(1)}, f32[256,128]{1,0:T(8,128)S(1)}, bf16[25...) custom-call(f32[256,512]{1,0:T(8,128)S(1)} %get-tuple-element.291.n1_ref, f32[1,512]{1,0:T(1,128)S(1)} %bitcast.32, ...), custom_call_target="tpu_custom_call" | custom-call | flops 30000 | bytes 300 | tf_op jit(solution)/shard_map/feed/pallas_call | solution.py:447
  27.5 4.9 %joining.1 = (bf16[256,512]{1,0:T(8,128)(2,1)}, bf16[768,512]{1,0:T(8,128)(2,1)S(1)}, bf16[768,512]{1,0:T(8,128)(2,1)S(1)}, f32[256,512]{1,0:T(8,128)S(1)}, bf16...) custom-call(f32[256,512]{1,0:T(8,128)S(1)} %get-tuple-element.294.n2_ref, f32[1,512]{1,0:T(1,128)S(1)} %bitcast.38, ...), custom_call_target="tpu_custom_call" | custom-call | flops 80000 | bytes 800 | tf_op jit(solution)/shard_map/joining/pallas_call | solution.py:447
  32.5 1.5 outer_back.1
  34.4 2.5 %inner_back.1 = (f32[256,512]{1,0:T(8,128)S(1)}, bf16[16,512]{1,0:T(8,128)(2,1)S(1)}, bf16[1280,512]{1,0:T(8,128)(2,1)S(1)}, bf16[1280,512]{1,0:T(8,128)(2,1)S(1)}) custom-call(f32[256,512]{1,0:T(8,128)S(1)} %get-tuple-element.314.d2_ref, bf16[256,2048]{1,0:T(8,128)(2,1)S(1)} %get-tuple-element.315.sz_ref, bf16[512,2048]{1,0:T(8,128)(2,1)S(1)} %copy-done, ...), custom_call_target="tpu_custom_call" | custom-call | flops 60000 | bytes 600 | tf_op jit(solution)/shard_map/inner_back/pallas_call | solution.py:447
  37.3 1.5 collective-permute-start.17
  38.8 0.9 collective-permute-start.18
  40.2 1.5 collective-permute-start.19
  41.6 4.4 %attend_back.1 = (bf16[784,512]{1,0:T(8,128)(2,1)S(1)}, bf16[784,512]{1,0:T(8,128)(2,1)S(1)}, bf16[256,512]{1,0:T(8,128)(2,1)S(1)}, bf16[1024,512]{1,0:T(8,128)(2,1)S(1)}, bf16[1024,512]{1,0:T(8,128)(2,1)S(1)}) custom-call(f32[256,512]{1,0:T(8,128)S(1)} %get-tuple-element.358.d1_ref, bf16[512,2560]{1,0:T(8,128)(2,1)S(1)} %constant_dynamic-update-slice_fusion.bank, ...), custom_call_target="tpu_custom_call" | custom-call | flops 80000 | bytes 800 | tf_op jit(solution)/shard_map/attend_back/pallas_call | solution.py:447
  46.7 5.9 %collective-permute-done.18 = bf16[512,512]{1,0:T(8,128)(2,1)S(1)} collective-permute-done((bf16[512,512]{1,0:T(8,128)(2,1)S(1)}, bf16[512,512]{1,0:T(8,128)(2,1)S(1)}, u32[]{:S(2)}, u32[]{:S(2)}) %collective-permute-start.18) | collective-permute-done | bytes 524320 | tf_op jit(solution)/shard_map/outer_sum_step_0/over_stage/ppermute | solution.py:479
  52.8 1.1 collective-permute-start.21
  53.9 2.9 %collective-permute-start.22 = (bf16[256,512]{1,0:T(8,128)(2,1)S(1)}, bf16[256,512]{1,0:T(8,128)(2,1)S(1)}, u32[]{:S(2)}, u32[]{:S(2)}) collective-permute-start(bf16[256,512]{1,0:T(8,128)(2,1)S(1)} %get-tuple-element.369), channel_id=1, source_target_pairs={{0,16},{1,9},{2,18},{3,11},{4,20},{5,13},{6,22},{7,15},{8,24},{9,1... | collective-permute-start | bytes 786440 | tf_op jit(solution)/shard_map/outer_sum_step_1/over_stage/ppermute | solution.py:479
  56.9 1.4 input_back.1
  58.3 0.9 collective-permute-start.25
  59.2 1.2 collective-permute-start.23
  60.4 2.6 %collective-permute-done.22 = bf16[256,512]{1,0:T(8,128)(2,1)S(1)} collective-permute-done((bf16[256,512]{1,0:T(8,128)(2,1)S(1)}, bf16[256,512]{1,0:T(8,128)(2,1)S(1)}, u32[]{:S(2)}, u32[]{:S(2)}) %collective-permute-start.22) | collective-permute-done | bytes 262176 | tf_op jit(solution)/shard_map/outer_sum_step_1/over_stage/ppermute | solution.py:479
  63.1 2.5 %collective-permute-start.27 = (bf16[128,512]{1,0:T(8,128)(2,1)S(1)}, bf16[128,512]{1,0:T(8,128)(2,1)S(1)}, u32[]{:S(2)}, u32[]{:S(2)}) collective-permute-start(bf16[128,512]{1,0:T(8,128)(2,1)S(1)} %get-tuple-element.388), channel_id=1, source_target_pairs={{0,2},{1,5},{2,0},{3,7},{4,6},{5,1},{6,4},{7,3},{8,10},{9,13},{10,... | collective-permute-start | bytes 393224 | tf_op jit(solution)/shard_map/outer_sum_step_2/over_stage/ppermute | solution.py:479
  65.8 1.4 collective-permute-done.23
  67.3 1.2 collective-permute-start.28
  68.5 2.8 %collective-permute-done.24 = bf16[160,512]{1,0:T(8,128)(2,1)S(1)} collective-permute-done((bf16[160,512]{1,0:T(8,128)(2,1)S(1)}, bf16[160,512]{1,0:T(8,128)(2,1)S(1)}, u32[]{:S(2)}, u32[]{:S(2)}) %collective-permute-start.24) | collective-permute-done | bytes 163872 | tf_op jit(solution)/shard_map/inner_sum_step_2/over_stage/ppermute | solution.py:479
  71.4 1.7 %collective-permute-done.28 = bf16[208,512]{1,0:T(8,128)(2,1)S(1)} collective-permute-done((bf16[208,512]{1,0:T(8,128)(2,1)S(1)}, bf16[208,512]{1,0:T(8,128)(2,1)S(1)}, u32[]{:S(2)}, u32[]{:S(2)}) %collective-permute-start.28) | collective-permute-done | bytes 213024 | tf_op jit(solution)/shard_map/attend_sum_step_1/over_stage/ppermute | solution.py:479
  73.2 2.1 %collective-permute-start.29 = (bf16[80,512]{1,0:T(8,128)(2,1)S(1)}, bf16[80,512]{1,0:T(8,128)(2,1)S(1)}, u32[]{:S(2)}, u32[]{:S(2)}) collective-permute-start(bf16[80,512]{1,0:T(8,128)(2,1)S(1)} %slice_add_fusion.24), channel_id=1, source_target_pairs={{0,16},{1,9},{2,18},{3,11},{4,20},{5,13},{6,22},{7,15},{8,24},{9,1... | collective-permute-start | bytes 245768 | tf_op jit(solution)/shard_map/inner_sum_step_3/over_stage/ppermute | solution.py:479
  75.3 1.0 collective-permute-start.30
  76.6 1.7 %collective-permute-start.34 = (bf16[112,512]{1,0:T(8,128)(2,1)S(1)}, bf16[112,512]{1,0:T(8,128)(2,1)S(1)}, u32[]{:S(2)}, u32[]{:S(2)}) collective-permute-start(bf16[112,512]{1,0:T(8,128)(2,1)S(1)} %fusion.1), channel_id=1, source_target_pairs={{0,8},{1,17},{2,10},{3,19},{4,12},{5,21},{6,14},{7,23},{8,0},{9,25... | collective-permute-start | bytes 344072 | tf_op jit(solution)/shard_map/attend_sum_step_2/over_stage/ppermute | solution.py:479
  78.3 1.2 collective-permute-start.40
  79.4 3.2 %collective-permute-done.29 = bf16[80,512]{1,0:T(8,128)(2,1)S(1)} collective-permute-done((bf16[80,512]{1,0:T(8,128)(2,1)S(1)}, bf16[80,512]{1,0:T(8,128)(2,1)S(1)}, u32[]{:S(2)}, u32[]{:S(2)}) %collective-permute-start.29) | collective-permute-done | bytes 81952 | tf_op jit(solution)/shard_map/inner_sum_step_3/over_stage/ppermute | solution.py:479
  82.7 1.6 %collective-permute-done.31 = bf16[96,512]{1,0:T(8,128)(2,1)S(1)} collective-permute-done((bf16[96,512]{1,0:T(8,128)(2,1)S(1)}, bf16[96,512]{1,0:T(8,128)(2,1)S(1)}, u32[]{:S(2)}, u32[]{:S(2)}) %collective-permute-start.31) | collective-permute-done | bytes 98336 | tf_op jit(solution)/shard_map/joining_sum_step_2/over_stage/ppermute | solution.py:479
  84.3 1.4 collective-permute-start.35
  85.7 0.8 collective-permute-start.33
  86.5 4.1 %collective-permute-done.32 = bf16[80,512]{1,0:T(8,128)(2,1)S(1)} collective-permute-done((bf16[80,512]{1,0:T(8,128)(2,1)S(1)}, bf16[80,512]{1,0:T(8,128)(2,1)S(1)}, u32[]{:S(2)}, u32[]{:S(2)}) %collective-permute-start.32) | collective-permute-done | bytes 81952 | tf_op jit(solution)/shard_map/inner_sum_step_4/over_stage/ppermute | solution.py:479
  90.8 0.9 collective-permute-done.35
  91.9 2.9 %collective-permute-start.39 = (bf16[64,512]{1,0:T(8,128)(2,1)S(1)}, bf16[64,512]{1,0:T(8,128)(2,1)S(1)}, u32[]{:S(2)}, u32[]{:S(2)}) collective-permute-start(bf16[64,512]{1,0:T(8,128)(2,1)S(1)} %fusion.6), channel_id=1, source_target_pairs={{0,16},{1,9},{2,18},{3,11},{4,20},{5,13},{6,22},{7,15},{8,24},{9,1... | collective-permute-start | bytes 196616 | tf_op jit(solution)/shard_map/attend_sum_step_3/over_stage/ppermute | solution.py:479
  94.8 1.8 %collective-permute-start.38 = (bf16[128,512]{1,0:T(8,128)(2,1)S(1)}, bf16[128,512]{1,0:T(8,128)(2,1)S(1)}, u32[]{:S(2)}, u32[]{:S(2)}) collective-permute-start(bf16[128,512]{1,0:T(8,128)(2,1)S(1)} %pad_maximum_fusion.12), channel_id=1, source_target_pairs={{0,2},{1,5},{2,0},{3,7},{4,6},{5,1},{6,4},{7,3},{8,10},{9,13},{10,... | collective-permute-start | bytes 393224 | tf_op jit(solution)/shard_map/outer_sum_step_5/over_stage/ppermute | solution.py:479
  96.8 1.2 collective-permute-start.41
  98.1 2.9 %collective-permute-done.38 = bf16[128,512]{1,0:T(8,128)(2,1)S(1)} collective-permute-done((bf16[128,512]{1,0:T(8,128)(2,1)S(1)}, bf16[128,512]{1,0:T(8,128)(2,1)S(1)}, u32[]{:S(2)}, u32[]{:S(2)}) %collective-permute-start.38) | collective-permute-done | bytes 131104 | tf_op jit(solution)/shard_map/outer_sum_step_5/over_stage/ppermute | solution.py:479
  101.9 1.5 %collective-permute-start.43 = (bf16[320,512]{1,0:T(8,128)(2,1)S(1)}, bf16[320,512]{1,0:T(8,128)(2,1)S(1)}, u32[]{:S(2)}, u32[]{:S(2)}) collective-permute-start(bf16[320,512]{1,0:T(8,128)(2,1)S(1)} %pad_maximum_fusion.5), channel_id=1, source_target_pairs={{0,4},{1,3},{2,6},{3,1},{4,0},{5,7},{6,2},{7,5},{8,12},{9,11},{10,... | collective-permute-start | bytes 983048 | tf_op jit(solution)/shard_map/inner_sum_step_6/over_stage/ppermute | solution.py:479
  103.6 0.9 collective-permute-start.44
  104.5 2.5 %collective-permute-start.45 = (bf16[256,512]{1,0:T(8,128)(2,1)S(1)}, bf16[256,512]{1,0:T(8,128)(2,1)S(1)}, u32[]{:S(2)}, u32[]{:S(2)}) collective-permute-start(bf16[256,512]{1,0:T(8,128)(2,1)S(1)} %pad_maximum_fusion.6), channel_id=1, source_target_pairs={{0,16},{1,9},{2,18},{3,11},{4,20},{5,13},{6,22},{7,15},{8,24},{9,1... | collective-permute-start | bytes 786440 | tf_op jit(solution)/shard_map/outer_sum_step_6/over_stage/ppermute | solution.py:479
  107.0 1.5 collective-permute-done.42
  108.5 2.3 %collective-permute-done.43 = bf16[320,512]{1,0:T(8,128)(2,1)S(1)} collective-permute-done((bf16[320,512]{1,0:T(8,128)(2,1)S(1)}, bf16[320,512]{1,0:T(8,128)(2,1)S(1)}, u32[]{:S(2)}, u32[]{:S(2)}) %collective-permute-start.43) | collective-permute-done | bytes 327712 | tf_op jit(solution)/shard_map/inner_sum_step_6/over_stage/ppermute | solution.py:479
  110.8 4.2 %collective-permute-done.44 = bf16[192,512]{1,0:T(8,128)(2,1)S(1)} collective-permute-done((bf16[192,512]{1,0:T(8,128)(2,1)S(1)}, bf16[192,512]{1,0:T(8,128)(2,1)S(1)}, u32[]{:S(2)}, u32[]{:S(2)}) %collective-permute-start.44) | collective-permute-done | bytes 196640 | tf_op jit(solution)/shard_map/joining_sum_step_6/over_stage/ppermute | solution.py:479
  115.1 3.0 %collective-permute-start.47 = (bf16[640,512]{1,0:T(8,128)(2,1)S(1)}, bf16[640,512]{1,0:T(8,128)(2,1)S(1)}, u32[]{:S(2)}, u32[]{:S(2)}) collective-permute-start(bf16[640,512]{1,0:T(8,128)(2,1)S(1)} %pad_maximum_fusion.a8), channel_id=1, source_target_pairs={{0,2},{1,5},{2,0},{3,7},{4,6},{5,1},{6,4},{7,3},{8,10},{9,13},{10,... | collective-permute-start | bytes 1966088 | tf_op jit(solution)/shard_map/inner_sum_step_7/over_stage/ppermute | solution.py:479
  118.1 1.9 %collective-permute-start.46 = (bf16[96,512]{1,0:T(8,128)(2,1)S(1)}, bf16[96,512]{1,0:T(8,128)(2,1)S(1)}, u32[]{:S(2)}, u32[]{:S(2)}) collective-permute-start(bf16[96,512]{1,0:T(8,128)(2,1)S(1)} %pad_maximum_fusion.15), channel_id=1, source_target_pairs={{0,8},{1,17},{2,10},{3,19},{4,12},{5,21},{6,14},{7,23},{8,0},{9,25... | collective-permute-start | bytes 294920 | tf_op jit(solution)/shard_map/attend_sum_step_5/over_stage/ppermute | solution.py:479
  120.3 4.3 %collective-permute-done.46 = bf16[96,512]{1,0:T(8,128)(2,1)S(1)} collective-permute-done((bf16[96,512]{1,0:T(8,128)(2,1)S(1)}, bf16[96,512]{1,0:T(8,128)(2,1)S(1)}, u32[]{:S(2)}, u32[]{:S(2)}) %collective-permute-start.46) | collective-permute-done | bytes 98336 | tf_op jit(solution)/shard_map/attend_sum_step_5/over_stage/ppermute | solution.py:479
  124.6 2.1 %collective-permute-done.47.r1 = bf16[640,512]{1,0:T(8,128)(2,1)S(1)} collective-permute-done((bf16[640,512]{1,0:T(8,128)(2,1)S(1)}, bf16[640,512]{1,0:T(8,128)(2,1)S(1)}, u32[]{:S(2)}, u32[]{:S(2)}) %collective-permute-start.47) | collective-permute-done | bytes 655392 | tf_op jit(solution)/shard_map/inner_sum_step_7/over_stage/ppermute | solution.py:479
  126.7 1.6 %collective-permute-start.51 = (bf16[192,512]{1,0:T(8,128)(2,1)S(1)}, bf16[192,512]{1,0:T(8,128)(2,1)S(1)}, u32[]{:S(2)}, u32[]{:S(2)}) collective-permute-start(bf16[192,512]{1,0:T(8,128)(2,1)S(1)} %pad_maximum_fusion.10), channel_id=1, source_target_pairs={{0,4},{1,3},{2,6},{3,1},{4,0},{5,7},{6,2},{7,5},{8,12},{9,11},{10,... | collective-permute-start | bytes 589832 | tf_op jit(solution)/shard_map/attend_sum_step_6/over_stage/ppermute | solution.py:479
  128.3 3.2 %collective-permute-done.49.r1 = bf16[384,512]{1,0:T(8,128)(2,1)S(1)} collective-permute-done((bf16[384,512]{1,0:T(8,128)(2,1)S(1)}, bf16[384,512]{1,0:T(8,128)(2,1)S(1)}, u32[]{:S(2)}, u32[]{:S(2)}) %collective-permute-start.49) | collective-permute-done | bytes 393248 | tf_op jit(solution)/shard_map/joining_sum_step_7/over_stage/ppermute | solution.py:479
  131.6 0.9 collective-permute-done.51
  132.5 2.5 %collective-permute-done.52.r1 = bf16[512,512]{1,0:T(8,128)(2,1)S(1)} collective-permute-done((bf16[512,512]{1,0:T(8,128)(2,1)S(1)}, bf16[512,512]{1,0:T(8,128)(2,1)S(1)}, u32[]{:S(2)}, u32[]{:S(2)}) %collective-permute-start.52) | collective-permute-done | bytes 524320 | tf_op jit(solution)/shard_map/outer_sum_step_7/over_stage/ppermute | solution.py:479
  135.0 1.5 %collective-permute-start.56 = (bf16[384,512]{1,0:T(8,128)(2,1)S(1)}, bf16[384,512]{1,0:T(8,128)(2,1)S(1)}, u32[]{:S(2)}, u32[]{:S(2)}) collective-permute-start(bf16[384,512]{1,0:T(8,128)(2,1)S(1)} %pad_maximum_fusion.4.a8), channel_id=1, source_target_pairs={{0,2},{1,5},{2,0},{3,7},{4,6},{5,1},{6,4},{7,3},{8,10},{9,13},{10,... | collective-permute-start | bytes 1179656 | tf_op jit(solution)/shard_map/attend_sum_step_7/over_stage/ppermute | solution.py:479
  137.0 2.7 %finish_inner.1 = (f32[512,2048]{1,0:T(8,128)}, f32[512,512]{1,0:T(8,128)}) custom-call(bf16[640,512]{1,0:T(8,128)(2,1)S(1)} %pad_maximum_fusion.a8, bf16[640,512]{1,0:T(8,128)(2,1)S(1)} %collective-permute-done.47.r1, bf16[640,512]{1,0:T(8,128)(2,1)S(1)} %collective-permute-done.48.s8, bf16[640,512]{1,0:T(8,128)(2,1)S(1)} %collective-permute-done.54.sr1), custom_call_target="tpu_custom_call" | custom-call | flops 20000 | bytes 200 | tf_op jit(solution)/shard_map/finish_inner/pallas_call | solution.py:447
  139.7 2.3 %finish_outer.1 = f32[2048,512]{1,0:T(8,128)} custom-call(bf16[512,512]{1,0:T(8,128)(2,1)S(1)} %pad_maximum_fusion.2.a8, bf16[512,512]{1,0:T(8,128)(2,1)S(1)} %collective-permute-done.52.r1, bf16[512,512]{1,0:T(8,128)(2,1)S(1)} %collective-permute-done.53.s8, bf16[512,512]{1,0:T(8,128)(2,1)S(1)} %collective-permute-done.55.sr1), custom_call_target="tpu_custom_call" | custom-call | flops 20000 | bytes 200 | tf_op jit(solution)/shard_map/finish_outer/pallas_call | solution.py:447
  142.8 1.9 %finish_joining.1 = (f32[512,512]{1,0:T(8,128)}, f32[512,512]{1,0:T(8,128)}, f32[512,512]{1,0:T(8,128)}) custom-call(bf16[384,512]{1,0:T(8,128)(2,1)S(1)} %pad_maximum_fusion.3.a8, bf16[384,512]{1,0:T(8,128)(2,1)S(1)} %collective-permute-done.49.r1, bf16[384,512]{1,0:T(8,128)(2,1)S(1)} %collective-permute-done.50.s8, ...), custom_call_target="tpu_custom_call" | custom-call | flops 20000 | bytes 200 | tf_op jit(solution)/shard_map/finish_joining/pallas_call | solution.py:447
  144.8 2.5 %finish_attend.1 = (f32[512,512]{1,0:T(8,128)}, f32[512,512]{1,0:T(8,128)}, f32[512,512]{1,0:T(8,128)}, f32[1,512]{1,0:T(1,128)}, f32[1,512]{1,0:T(1,128)}, /*in...) custom-call(bf16[384,512]{1,0:T(8,128)(2,1)S(1)} %pad_maximum_fusion.4.a8, ...), custom_call_target="tpu_custom_call" | custom-call | flops 20000 | bytes 200 | tf_op jit(solution)/shard_map/finish_attend/pallas_call | solution.py:447
  (149 shorter events, 9.5 us)
Async XLA Ops:
  0.7 12.0 %copy-start.12 = (bf16[512,512]{1,0:T(8,128)(2,1)S(1)}, bf16[512,512]{1,0:T(8,128)(2,1)}, u32[]{:S(2)}) copy-start(bf16[512,512]{1,0:T(8,128)(2,1)} %param.26) | copy-start | bytes 1572868
  0.7 12.0 %copy-start.13 = (bf16[512,512]{1,0:T(8,128)(2,1)S(1)}, bf16[512,512]{1,0:T(8,128)(2,1)}, u32[]{:S(2)}) copy-start(bf16[512,512]{1,0:T(8,128)(2,1)} %param.27) | copy-start | bytes 1572868
  0.7 12.1 %copy-start.14 = (bf16[512,512]{1,0:T(8,128)(2,1)S(1)}, bf16[512,512]{1,0:T(8,128)(2,1)}, u32[]{:S(2)}) copy-start(bf16[512,512]{1,0:T(8,128)(2,1)} %param.35) | copy-start | bytes 1572868
  1.6 6.8 %collective-permute-start = (bf16[1,3,64,256]{3,2,1,0:T(8,128)(2,1)S(1)}, bf16[1,3,64,256]{3,2,1,0:T(8,128)(2,1)S(1)}, u32[]{:S(2)}, u32[]{:S(2)}) collective-permute-start(bf16[1,3,64,256]{3,2,1,0:T(8,128)(2,1)S(1)} %fusion.4), channel_id=1, source_target_pairs={{0,4},{1,17},{2,6},{3,19},{4,0},{5,21},{6,2},{7,23},{8,12},{9,25},... | collective-permute-start | bytes 294920 | tf_op jit(solution)/shard_map/weights_first/ppermute | solution.py:479
  4.6 8.4 %collective-permute-start.4 = (s32[2,128]{1,0:T(2,128)}, s32[2,128]{1,0:T(2,128)S(1)}, u32[]{:S(2)}, u32[]{:S(2)}) collective-permute-start(s32[2,128]{1,0:T(2,128)} %bitcast.45), channel_id=1, source_target_pairs={{0,3},{1,2},{2,1},{3,0},{4,7},{5,6},{6,5},{7,4},{8,11},{9,10},{10,... | collective-permute-start | bytes 3080 | tf_op jit(solution)/shard_map/segments/ppermute | solution.py:479
  6.4 6.7 %collective-permute-start.3 = (s32[2,128]{1,0:T(2,128)}, s32[2,128]{1,0:T(2,128)S(1)}, u32[]{:S(2)}, u32[]{:S(2)}) collective-permute-start(s32[2,128]{1,0:T(2,128)} %bitcast.46), channel_id=1, source_target_pairs={{0,2},{1,3},{2,0},{3,1},{4,6},{5,7},{6,4},{7,5},{8,10},{9,11},{10,... | collective-permute-start | bytes 3080 | tf_op jit(solution)/shard_map/segments/ppermute | solution.py:479
  6.9 8.1 %collective-permute-start.5 = (bf16[256,512]{1,0:T(8,128)(2,1)}, bf16[256,512]{1,0:T(8,128)(2,1)S(1)}, u32[]{:S(2)}, u32[]{:S(2)}) collective-permute-start(bf16[256,512]{1,0:T(8,128)(2,1)} %bitcast.50), channel_id=1, source_target_pairs={{0,2},{1,3},{2,0},{3,1},{4,6},{5,7},{6,4},{7,5},{8,10},{9,11},{10,... | collective-permute-start | bytes 786440 | tf_op jit(solution)/shard_map/row_far/ppermute | solution.py:479
  8.4 4.5 %collective-permute-start.1 = (bf16[256,512]{1,0:T(8,128)(2,1)}, bf16[256,512]{1,0:T(8,128)(2,1)S(1)}, u32[]{:S(2)}, u32[]{:S(2)}) collective-permute-start(bf16[256,512]{1,0:T(8,128)(2,1)} %bitcast.51), channel_id=1, source_target_pairs={{0,1},{1,0},{2,3},{3,2},{4,5},{5,4},{6,7},{7,6},{8,9},{9,8},{10,11... | collective-permute-start | bytes 786440 | tf_op jit(solution)/shard_map/row_near/ppermute | solution.py:479
  8.4 8.8 %collective-permute-start.6 = (bf16[2,3,64,256]{3,2,1,0:T(8,128)(2,1)S(1)}, bf16[2,3,64,256]{3,2,1,0:T(8,128)(2,1)S(1)}, u32[]{:S(2)}, u32[]{:S(2)}) collective-permute-start(bf16[2,3,64,256]{3,2,1,0:T(8,128)(2,1)S(1)} %pad_maximum_fusion.8.rest_0_), channel_id=1, source_target_pairs={{0,16},{1,9},{2,18},{3,11},{4,20},{5,13},{6,22},{7,15},{8,24},{9,1... | collective-permute-start | bytes 589832 | tf_op jit(solution)/shard_map/weights_second/ppermute | solution.py:479
  12.8 11.8 %copy-start = (bf16[512,2048]{1,0:T(8,128)(2,1)S(1)}, bf16[512,2048]{1,0:T(8,128)(2,1)}, u32[]{:S(2)}) copy-start(bf16[512,2048]{1,0:T(8,128)(2,1)} %wi.3) | copy-start | bytes 6291460
  12.9 1.2 collective-permute-start.2
  14.9 2.8 %collective-permute-start.7 = (bf16[256,512]{1,0:T(8,128)(2,1)S(1)}, bf16[256,512]{1,0:T(8,128)(2,1)S(1)}, u32[]{:S(2)}, u32[]{:S(2)}) collective-permute-start(bf16[256,512]{1,0:T(8,128)(2,1)S(1)} %collective-permute-done.5.x2), channel_id=1, source_target_pairs={{0,1},{1,0},{2,3},{3,2},{4,5},{5,4},{6,7},{7,6},{8,9},{9,8},{10,11... | collective-permute-start | bytes 786440 | tf_op jit(solution)/shard_map/row_cross/ppermute | solution.py:479
  14.9 8.6 %collective-permute-start.8 = (bf16[2,3,64,256]{3,2,1,0:T(8,128)(2,1)S(1)}, bf16[2,3,64,256]{3,2,1,0:T(8,128)(2,1)S(1)}, u32[]{:S(2)}, u32[]{:S(2)}) collective-permute-start(bf16[2,3,64,256]{3,2,1,0:T(8,128)(2,1)S(1)} %pad_maximum_fusion.8.rest_0_), channel_id=1, source_target_pairs={{0,8},{1,5},{2,10},{3,7},{4,12},{5,1},{6,14},{7,3},{8,0},{9,13},{1... | collective-permute-start | bytes 589832 | tf_op jit(solution)/shard_map/weights_third/ppermute | solution.py:479
  17.2 6.3 %collective-permute-start.9 = (bf16[2,3,64,256]{3,2,1,0:T(8,128)(2,1)S(1)}, bf16[2,3,64,256]{3,2,1,0:T(8,128)(2,1)S(1)}, u32[]{:S(2)}, u32[]{:S(2)}) collective-permute-start(bf16[2,3,64,256]{3,2,1,0:T(8,128)(2,1)S(1)} %collective-permute-done.6.rest_1_), channel_id=1, source_target_pairs={{0,8},{1,5},{2,10},{3,7},{4,12},{5,1},{6,14},{7,3},{8,0},{9,13},{1... | collective-permute-start | bytes 589832 | tf_op jit(solution)/shard_map/weights_third/ppermute | solution.py:479
  23.5 3.9 %collective-permute-start.10 = (bf16[2,3,64,256]{3,2,1,0:T(8,128)(2,1)S(1)}, bf16[2,3,64,256]{3,2,1,0:T(8,128)(2,1)S(1)}, u32[]{:S(2)}, u32[]{:S(2)}) collective-permute-start(bf16[2,3,64,256]{3,2,1,0:T(8,128)(2,1)S(1)} %pad_maximum_fusion.8.rest_0_), channel_id=1, source_target_pairs={{0,1},{1,0},{2,3},{3,2},{4,5},{5,4},{6,7},{7,6},{8,9},{9,8},{10,11... | collective-permute-start | bytes 589832 | tf_op jit(solution)/shard_map/weights_core/ppermute | solution.py:479
  23.6 3.8 %collective-permute-start.11 = (bf16[2,3,64,256]{3,2,1,0:T(8,128)(2,1)S(1)}, bf16[2,3,64,256]{3,2,1,0:T(8,128)(2,1)S(1)}, u32[]{:S(2)}, u32[]{:S(2)}) collective-permute-start(bf16[2,3,64,256]{3,2,1,0:T(8,128)(2,1)S(1)} %collective-permute-done.6.rest_1_), channel_id=1, source_target_pairs={{0,1},{1,0},{2,3},{3,2},{4,5},{5,4},{6,7},{7,6},{8,9},{9,8},{10,11... | collective-permute-start | bytes 589832 | tf_op jit(solution)/shard_map/weights_core/ppermute | solution.py:479
  24.1 3.3 %collective-permute-start.13 = (bf16[2,3,64,256]{3,2,1,0:T(8,128)(2,1)S(1)}, bf16[2,3,64,256]{3,2,1,0:T(8,128)(2,1)S(1)}, u32[]{:S(2)}, u32[]{:S(2)}) collective-permute-start(bf16[2,3,64,256]{3,2,1,0:T(8,128)(2,1)S(1)} %collective-permute-done.9.rest_3_), channel_id=1, source_target_pairs={{0,1},{1,0},{2,3},{3,2},{4,5},{5,4},{6,7},{7,6},{8,9},{9,8},{10,11... | collective-permute-start | bytes 589832 | tf_op jit(solution)/shard_map/weights_core/ppermute | solution.py:479
  24.2 3.3 %collective-permute-start.12 = (bf16[2,3,64,256]{3,2,1,0:T(8,128)(2,1)S(1)}, bf16[2,3,64,256]{3,2,1,0:T(8,128)(2,1)S(1)}, u32[]{:S(2)}, u32[]{:S(2)}) collective-permute-start(bf16[2,3,64,256]{3,2,1,0:T(8,128)(2,1)S(1)} %collective-permute-done.8.rest_2_), channel_id=1, source_target_pairs={{0,1},{1,0},{2,3},{3,2},{4,5},{5,4},{6,7},{7,6},{8,9},{9,8},{10,11... | collective-permute-start | bytes 589832 | tf_op jit(solution)/shard_map/weights_core/ppermute | solution.py:479
  32.4 4.7 %collective-permute-start.14 = (bf16[768,512]{1,0:T(8,128)(2,1)S(1)}, bf16[768,512]{1,0:T(8,128)(2,1)S(1)}, u32[]{:S(2)}, u32[]{:S(2)}) collective-permute-start(bf16[768,512]{1,0:T(8,128)(2,1)S(1)} %get-tuple-element.324), channel_id=1, source_target_pairs={{0,1},{1,0},{2,3},{3,2},{4,5},{5,4},{6,7},{7,6},{8,9},{9,8},{10,11... | collective-permute-start | bytes 2359304 | tf_op jit(solution)/shard_map/joining_sum_core/over_bit/ppermute | solution.py:479
  33.9 3.3 %collective-permute-start.15 = (bf16[1024,512]{1,0:T(8,128)(2,1)S(1)}, bf16[1024,512]{1,0:T(8,128)(2,1)S(1)}, u32[]{:S(2)}, u32[]{:S(2)}) collective-permute-start(bf16[1024,512]{1,0:T(8,128)(2,1)S(1)} %get-tuple-element.328), channel_id=1, source_target_pairs={{0,1},{1,0},{2,3},{3,2},{4,5},{5,4},{6,7},{7,6},{8,9},{9,8},{10,11... | collective-permute-start | bytes 3145736 | tf_op jit(solution)/shard_map/outer_sum_core/over_bit/ppermute | solution.py:479
  36.9 3.1 %collective-permute-start.16 = (bf16[1280,512]{1,0:T(8,128)(2,1)S(1)}, bf16[1280,512]{1,0:T(8,128)(2,1)S(1)}, u32[]{:S(2)}, u32[]{:S(2)}) collective-permute-start(bf16[1280,512]{1,0:T(8,128)(2,1)S(1)} %get-tuple-element.332), channel_id=1, source_target_pairs={{0,1},{1,0},{2,3},{3,2},{4,5},{5,4},{6,7},{7,6},{8,9},{9,8},{10,11... | collective-permute-start | bytes 3932168 | tf_op jit(solution)/shard_map/inner_sum_core/over_bit/ppermute | solution.py:479
  37.3 9.3 %collective-permute-start.17 = (bf16[384,512]{1,0:T(8,128)(2,1)S(1)}, bf16[384,512]{1,0:T(8,128)(2,1)S(1)}, u32[]{:S(2)}, u32[]{:S(2)}) collective-permute-start(bf16[384,512]{1,0:T(8,128)(2,1)S(1)} %get-tuple-element.345), channel_id=1, source_target_pairs={{0,2},{1,5},{2,0},{3,7},{4,6},{5,1},{6,4},{7,3},{8,10},{9,13},{10,... | collective-permute-start | bytes 1179656 | tf_op jit(solution)/shard_map/joining_sum_step_0/over_stage/ppermute | solution.py:479
  38.8 13.8 %collective-permute-start.18 = (bf16[512,512]{1,0:T(8,128)(2,1)S(1)}, bf16[512,512]{1,0:T(8,128)(2,1)S(1)}, u32[]{:S(2)}, u32[]{:S(2)}) collective-permute-start(bf16[512,512]{1,0:T(8,128)(2,1)S(1)} %get-tuple-element.348), channel_id=1, source_target_pairs={{0,8},{1,17},{2,10},{3,19},{4,12},{5,21},{6,14},{7,23},{8,0},{9,25... | collective-permute-start | bytes 1572872 | tf_op jit(solution)/shard_map/outer_sum_step_0/over_stage/ppermute | solution.py:479
  40.2 12.4 %collective-permute-start.19 = (bf16[640,512]{1,0:T(8,128)(2,1)S(1)}, bf16[640,512]{1,0:T(8,128)(2,1)S(1)}, u32[]{:S(2)}, u32[]{:S(2)}) collective-permute-start(bf16[640,512]{1,0:T(8,128)(2,1)S(1)} %get-tuple-element.351), channel_id=1, source_target_pairs={{0,2},{1,5},{2,0},{3,7},{4,6},{5,1},{6,4},{7,3},{8,10},{9,13},{10,... | collective-permute-start | bytes 1966088 | tf_op jit(solution)/shard_map/inner_sum_step_0/over_stage/ppermute | solution.py:479
  46.1 6.6 %collective-permute-start.20 = (bf16[784,512]{1,0:T(8,128)(2,1)S(1)}, bf16[784,512]{1,0:T(8,128)(2,1)S(1)}, u32[]{:S(2)}, u32[]{:S(2)}) collective-permute-start(bf16[784,512]{1,0:T(8,128)(2,1)S(1)} %get-tuple-element.355), channel_id=1, source_target_pairs={{0,1},{1,0},{2,3},{3,2},{4,5},{5,4},{6,7},{7,6},{8,9},{9,8},{10,11... | collective-permute-start | bytes 2408456 | tf_op jit(solution)/shard_map/attend_sum_core/over_bit/ppermute | solution.py:479
  52.8 7.6 %collective-permute-start.21 = (bf16[320,512]{1,0:T(8,128)(2,1)S(1)}, bf16[320,512]{1,0:T(8,128)(2,1)S(1)}, u32[]{:S(2)}, u32[]{:S(2)}) collective-permute-start(bf16[320,512]{1,0:T(8,128)(2,1)S(1)} %get-tuple-element.365), channel_id=1, source_target_pairs={{0,4},{1,3},{2,6},{3,1},{4,0},{5,7},{6,2},{7,5},{8,12},{9,11},{10,... | collective-permute-start | bytes 983048 | tf_op jit(solution)/shard_map/inner_sum_step_1/over_stage/ppermute | solution.py:479
  53.9 9.2 %collective-permute-start.22 = (bf16[256,512]{1,0:T(8,128)(2,1)S(1)}, bf16[256,512]{1,0:T(8,128)(2,1)S(1)}, u32[]{:S(2)}, u32[]{:S(2)}) collective-permute-start(bf16[256,512]{1,0:T(8,128)(2,1)S(1)} %get-tuple-element.369), channel_id=1, source_target_pairs={{0,16},{1,9},{2,18},{3,11},{4,20},{5,13},{6,22},{7,15},{8,24},{9,1... | collective-permute-start | bytes 786440 | tf_op jit(solution)/shard_map/outer_sum_step_1/over_stage/ppermute | solution.py:479
  58.3 13.0 %collective-permute-start.25 = (bf16[192,512]{1,0:T(8,128)(2,1)S(1)}, bf16[192,512]{1,0:T(8,128)(2,1)S(1)}, u32[]{:S(2)}, u32[]{:S(2)}) collective-permute-start(bf16[192,512]{1,0:T(8,128)(2,1)S(1)} %get-tuple-element.380), channel_id=1, source_target_pairs={{0,4},{1,3},{2,6},{3,1},{4,0},{5,7},{6,2},{7,5},{8,12},{9,11},{10,... | collective-permute-start | bytes 589832 | tf_op jit(solution)/shard_map/joining_sum_step_1/over_stage/ppermute | solution.py:479
  59.2 8.0 %collective-permute-start.23 = (bf16[400,512]{1,0:T(8,128)(2,1)S(1)}, bf16[400,512]{1,0:T(8,128)(2,1)S(1)}, u32[]{:S(2)}, u32[]{:S(2)}) collective-permute-start(bf16[400,512]{1,0:T(8,128)(2,1)S(1)} %slice_add_fusion.4), channel_id=1, source_target_pairs={{0,2},{1,5},{2,0},{3,7},{4,6},{5,1},{6,4},{7,3},{8,10},{9,13},{10,... | collective-permute-start | bytes 1228808 | tf_op jit(solution)/shard_map/attend_sum_step_0/over_stage/ppermute | solution.py:479
  63.1 8.3 %collective-permute-start.27 = (bf16[128,512]{1,0:T(8,128)(2,1)S(1)}, bf16[128,512]{1,0:T(8,128)(2,1)S(1)}, u32[]{:S(2)}, u32[]{:S(2)}) collective-permute-start(bf16[128,512]{1,0:T(8,128)(2,1)S(1)} %get-tuple-element.388), channel_id=1, source_target_pairs={{0,2},{1,5},{2,0},{3,7},{4,6},{5,1},{6,4},{7,3},{8,10},{9,13},{10,... | collective-permute-start | bytes 393224 | tf_op jit(solution)/shard_map/outer_sum_step_2/over_stage/ppermute | solution.py:479
  65.7 5.6 %collective-permute-start.24 = (bf16[160,512]{1,0:T(8,128)(2,1)S(1)}, bf16[160,512]{1,0:T(8,128)(2,1)S(1)}, u32[]{:S(2)}, u32[]{:S(2)}) collective-permute-start(bf16[160,512]{1,0:T(8,128)(2,1)S(1)} %get-tuple-element.376), channel_id=1, source_target_pairs={{0,8},{1,17},{2,10},{3,19},{4,12},{5,21},{6,14},{7,23},{8,0},{9,25... | collective-permute-start | bytes 491528 | tf_op jit(solution)/shard_map/inner_sum_step_2/over_stage/ppermute | solution.py:479
  65.7 5.6 %collective-permute-start.26 = (bf16[512,512]{1,0:T(8,128)(2,1)S(1)}, bf16[512,512]{1,0:T(8,128)(2,1)S(1)}, u32[]{:S(2)}, u32[]{:S(2)}) collective-permute-start(bf16[512,512]{1,0:T(8,128)(2,1)S(1)} %get-tuple-element.385), channel_id=1, source_target_pairs={{0,1},{1,0},{2,3},{3,2},{4,5},{5,4},{6,7},{7,6},{8,9},{9,8},{10,11... | collective-permute-start | bytes 1572872 | tf_op jit(solution)/shard_map/over_bit/ppermute | solution.py:479
  67.3 5.9 %collective-permute-start.28 = (bf16[208,512]{1,0:T(8,128)(2,1)S(1)}, bf16[208,512]{1,0:T(8,128)(2,1)S(1)}, u32[]{:S(2)}, u32[]{:S(2)}) collective-permute-start(bf16[208,512]{1,0:T(8,128)(2,1)S(1)} %fusion), channel_id=1, source_target_pairs={{0,4},{1,3},{2,6},{3,1},{4,0},{5,7},{6,2},{7,5},{8,12},{9,11},{10,... | collective-permute-start | bytes 638984 | tf_op jit(solution)/shard_map/attend_sum_step_1/over_stage/ppermute | solution.py:479
  73.2 9.4 %collective-permute-start.29 = (bf16[80,512]{1,0:T(8,128)(2,1)S(1)}, bf16[80,512]{1,0:T(8,128)(2,1)S(1)}, u32[]{:S(2)}, u32[]{:S(2)}) collective-permute-start(bf16[80,512]{1,0:T(8,128)(2,1)S(1)} %slice_add_fusion.24), channel_id=1, source_target_pairs={{0,16},{1,9},{2,18},{3,11},{4,20},{5,13},{6,22},{7,15},{8,24},{9,1... | collective-permute-start | bytes 245768 | tf_op jit(solution)/shard_map/inner_sum_step_3/over_stage/ppermute | solution.py:479
  75.3 7.3 %collective-permute-start.30 = (bf16[64,512]{1,0:T(8,128)(2,1)S(1)}, bf16[64,512]{1,0:T(8,128)(2,1)S(1)}, u32[]{:S(2)}, u32[]{:S(2)}) collective-permute-start(bf16[64,512]{1,0:T(8,128)(2,1)S(1)} %slice_add_fusion.26), channel_id=1, source_target_pairs={{0,4},{1,3},{2,6},{3,1},{4,0},{5,7},{6,2},{7,5},{8,12},{9,11},{10,... | collective-permute-start | bytes 196616 | tf_op jit(solution)/shard_map/outer_sum_step_3/over_stage/ppermute | solution.py:479
  76.2 8.1 %collective-permute-start.31 = (bf16[96,512]{1,0:T(8,128)(2,1)S(1)}, bf16[96,512]{1,0:T(8,128)(2,1)S(1)}, u32[]{:S(2)}, u32[]{:S(2)}) collective-permute-start(bf16[96,512]{1,0:T(8,128)(2,1)S(1)} %get-tuple-element.403), channel_id=1, source_target_pairs={{0,8},{1,17},{2,10},{3,19},{4,12},{5,21},{6,14},{7,23},{8,0},{9,25... | collective-permute-start | bytes 294920 | tf_op jit(solution)/shard_map/joining_sum_step_2/over_stage/ppermute | solution.py:479
  76.6 14.2 %collective-permute-start.34 = (bf16[112,512]{1,0:T(8,128)(2,1)S(1)}, bf16[112,512]{1,0:T(8,128)(2,1)S(1)}, u32[]{:S(2)}, u32[]{:S(2)}) collective-permute-start(bf16[112,512]{1,0:T(8,128)(2,1)S(1)} %fusion.1), channel_id=1, source_target_pairs={{0,8},{1,17},{2,10},{3,19},{4,12},{5,21},{6,14},{7,23},{8,0},{9,25... | collective-permute-start | bytes 344072 | tf_op jit(solution)/shard_map/attend_sum_step_2/over_stage/ppermute | solution.py:479
  78.3 22.9 %collective-permute-start.40 = (bf16[256,512]{1,0:T(8,128)(2,1)S(1)}, bf16[256,512]{1,0:T(8,128)(2,1)S(1)}, u32[]{:S(2)}, u32[]{:S(2)}) collective-permute-start(bf16[256,512]{1,0:T(8,128)(2,1)S(1)} %slice_add_fusion.12), channel_id=1, source_target_pairs={{0,2},{1,3},{2,0},{3,1},{4,6},{5,7},{6,4},{7,5},{8,10},{9,11},{10,... | collective-permute-start | bytes 786440 | tf_op jit(solution)/shard_map/over_bit/ppermute | solution.py:479
  82.6 8.0 %collective-permute-start.32 = (bf16[80,512]{1,0:T(8,128)(2,1)S(1)}, bf16[80,512]{1,0:T(8,128)(2,1)S(1)}, u32[]{:S(2)}, u32[]{:S(2)}) collective-permute-start(bf16[80,512]{1,0:T(8,128)(2,1)S(1)} %fusion.5), channel_id=1, source_target_pairs={{0,16},{1,9},{2,18},{3,11},{4,20},{5,13},{6,22},{7,15},{8,24},{9,1... | collective-permute-start | bytes 245768 | tf_op jit(solution)/shard_map/inner_sum_step_4/over_stage/ppermute | solution.py:479
  84.3 7.4 %collective-permute-start.35 = (bf16[48,512]{1,0:T(8,128)(2,1)S(1)}, bf16[48,512]{1,0:T(8,128)(2,1)S(1)}, u32[]{:S(2)}, u32[]{:S(2)}) collective-permute-start(bf16[48,512]{1,0:T(8,128)(2,1)S(1)} %slice_add_fusion.29), channel_id=1, source_target_pairs={{0,16},{1,9},{2,18},{3,11},{4,20},{5,13},{6,22},{7,15},{8,24},{9,1... | collective-permute-start | bytes 147464 | tf_op jit(solution)/shard_map/joining_sum_step_3/over_stage/ppermute | solution.py:479
  85.7 5.0 %collective-permute-start.33 = (bf16[64,512]{1,0:T(8,128)(2,1)S(1)}, bf16[64,512]{1,0:T(8,128)(2,1)S(1)}, u32[]{:S(2)}, u32[]{:S(2)}) collective-permute-start(bf16[64,512]{1,0:T(8,128)(2,1)S(1)} %fusion.7), channel_id=1, source_target_pairs={{0,4},{1,3},{2,6},{3,1},{4,0},{5,7},{6,2},{7,5},{8,12},{9,11},{10,... | collective-permute-start | bytes 196616 | tf_op jit(solution)/shard_map/outer_sum_step_4/over_stage/ppermute | solution.py:479
  90.6 7.4 %collective-permute-start.37 = (bf16[160,512]{1,0:T(8,128)(2,1)S(1)}, bf16[160,512]{1,0:T(8,128)(2,1)S(1)}, u32[]{:S(2)}, u32[]{:S(2)}) collective-permute-start(bf16[160,512]{1,0:T(8,128)(2,1)S(1)} %pad_maximum_fusion.11), channel_id=1, source_target_pairs={{0,8},{1,17},{2,10},{3,19},{4,12},{5,21},{6,14},{7,23},{8,0},{9,25... | collective-permute-start | bytes 491528 | tf_op jit(solution)/shard_map/inner_sum_step_5/over_stage/ppermute | solution.py:479
  91.8 5.1 %collective-permute-start.36 = (bf16[48,512]{1,0:T(8,128)(2,1)S(1)}, bf16[48,512]{1,0:T(8,128)(2,1)S(1)}, u32[]{:S(2)}, u32[]{:S(2)}) collective-permute-start(bf16[48,512]{1,0:T(8,128)(2,1)S(1)} %fusion.8), channel_id=1, source_target_pairs={{0,16},{1,9},{2,18},{3,11},{4,20},{5,13},{6,22},{7,15},{8,24},{9,1... | collective-permute-start | bytes 147464 | tf_op jit(solution)/shard_map/joining_sum_step_4/over_stage/ppermute | solution.py:479
  91.9 9.2 %collective-permute-start.39 = (bf16[64,512]{1,0:T(8,128)(2,1)S(1)}, bf16[64,512]{1,0:T(8,128)(2,1)S(1)}, u32[]{:S(2)}, u32[]{:S(2)}) collective-permute-start(bf16[64,512]{1,0:T(8,128)(2,1)S(1)} %fusion.6), channel_id=1, source_target_pairs={{0,16},{1,9},{2,18},{3,11},{4,20},{5,13},{6,22},{7,15},{8,24},{9,1... | collective-permute-start | bytes 196616 | tf_op jit(solution)/shard_map/attend_sum_step_3/over_stage/ppermute | solution.py:479
  94.8 6.3 %collective-permute-start.38 = (bf16[128,512]{1,0:T(8,128)(2,1)S(1)}, bf16[128,512]{1,0:T(8,128)(2,1)S(1)}, u32[]{:S(2)}, u32[]{:S(2)}) collective-permute-start(bf16[128,512]{1,0:T(8,128)(2,1)S(1)} %pad_maximum_fusion.12), channel_id=1, source_target_pairs={{0,2},{1,5},{2,0},{3,7},{4,6},{5,1},{6,4},{7,3},{8,10},{9,13},{10,... | collective-permute-start | bytes 393224 | tf_op jit(solution)/shard_map/outer_sum_step_5/over_stage/ppermute | solution.py:479
  96.8 6.7 %collective-permute-start.41 = (bf16[96,512]{1,0:T(8,128)(2,1)S(1)}, bf16[96,512]{1,0:T(8,128)(2,1)S(1)}, u32[]{:S(2)}, u32[]{:S(2)}) collective-permute-start(bf16[96,512]{1,0:T(8,128)(2,1)S(1)} %pad_maximum_fusion.14), channel_id=1, source_target_pairs={{0,8},{1,17},{2,10},{3,19},{4,12},{5,21},{6,14},{7,23},{8,0},{9,25... | collective-permute-start | bytes 294920 | tf_op jit(solution)/shard_map/joining_sum_step_5/over_stage/ppermute | solution.py:479
  101.9 8.8 %collective-permute-start.43 = (bf16[320,512]{1,0:T(8,128)(2,1)S(1)}, bf16[320,512]{1,0:T(8,128)(2,1)S(1)}, u32[]{:S(2)}, u32[]{:S(2)}) collective-permute-start(bf16[320,512]{1,0:T(8,128)(2,1)S(1)} %pad_maximum_fusion.5), channel_id=1, source_target_pairs={{0,4},{1,3},{2,6},{3,1},{4,0},{5,7},{6,2},{7,5},{8,12},{9,11},{10,... | collective-permute-start | bytes 983048 | tf_op jit(solution)/shard_map/inner_sum_step_6/over_stage/ppermute | solution.py:479
  103.5 5.0 %collective-permute-start.42 = (bf16[48,512]{1,0:T(8,128)(2,1)S(1)}, bf16[48,512]{1,0:T(8,128)(2,1)S(1)}, u32[]{:S(2)}, u32[]{:S(2)}) collective-permute-start(bf16[48,512]{1,0:T(8,128)(2,1)S(1)} %slice.313), channel_id=1, source_target_pairs={{0,16},{1,9},{2,18},{3,11},{4,20},{5,13},{6,22},{7,15},{8,24},{9,1... | collective-permute-start | bytes 147464 | tf_op jit(solution)/shard_map/attend_sum_step_4/over_stage/ppermute | solution.py:479
  103.6 11.4 %collective-permute-start.44 = (bf16[192,512]{1,0:T(8,128)(2,1)S(1)}, bf16[192,512]{1,0:T(8,128)(2,1)S(1)}, u32[]{:S(2)}, u32[]{:S(2)}) collective-permute-start(bf16[192,512]{1,0:T(8,128)(2,1)S(1)} %pad_maximum_fusion.9), channel_id=1, source_target_pairs={{0,4},{1,3},{2,6},{3,1},{4,0},{5,7},{6,2},{7,5},{8,12},{9,11},{10,... | collective-permute-start | bytes 589832 | tf_op jit(solution)/shard_map/joining_sum_step_6/over_stage/ppermute | solution.py:479
  104.5 10.5 %collective-permute-start.45 = (bf16[256,512]{1,0:T(8,128)(2,1)S(1)}, bf16[256,512]{1,0:T(8,128)(2,1)S(1)}, u32[]{:S(2)}, u32[]{:S(2)}) collective-permute-start(bf16[256,512]{1,0:T(8,128)(2,1)S(1)} %pad_maximum_fusion.6), channel_id=1, source_target_pairs={{0,16},{1,9},{2,18},{3,11},{4,20},{5,13},{6,22},{7,15},{8,24},{9,1... | collective-permute-start | bytes 786440 | tf_op jit(solution)/shard_map/outer_sum_step_6/over_stage/ppermute | solution.py:479
  115.1 11.6 %collective-permute-start.47 = (bf16[640,512]{1,0:T(8,128)(2,1)S(1)}, bf16[640,512]{1,0:T(8,128)(2,1)S(1)}, u32[]{:S(2)}, u32[]{:S(2)}) collective-permute-start(bf16[640,512]{1,0:T(8,128)(2,1)S(1)} %pad_maximum_fusion.a8), channel_id=1, source_target_pairs={{0,2},{1,5},{2,0},{3,7},{4,6},{5,1},{6,4},{7,3},{8,10},{9,13},{10,... | collective-permute-start | bytes 1966088 | tf_op jit(solution)/shard_map/inner_sum_step_7/over_stage/ppermute | solution.py:479
  118.1 8.6 %collective-permute-start.48 = (bf16[640,512]{1,0:T(8,128)(2,1)S(1)}, bf16[640,512]{1,0:T(8,128)(2,1)S(1)}, u32[]{:S(2)}, u32[]{:S(2)}) collective-permute-start(bf16[640,512]{1,0:T(8,128)(2,1)S(1)} %pad_maximum_fusion.a8), channel_id=1, source_target_pairs={{0,1},{1,0},{2,3},{3,2},{4,5},{5,4},{6,7},{7,6},{8,9},{9,8},{10,11... | collective-permute-start | bytes 1966088 | tf_op jit(solution)/shard_map/inner_sum_sibling/over_bit/ppermute | solution.py:479
  118.1 6.5 %collective-permute-start.46 = (bf16[96,512]{1,0:T(8,128)(2,1)S(1)}, bf16[96,512]{1,0:T(8,128)(2,1)S(1)}, u32[]{:S(2)}, u32[]{:S(2)}) collective-permute-start(bf16[96,512]{1,0:T(8,128)(2,1)S(1)} %pad_maximum_fusion.15), channel_id=1, source_target_pairs={{0,8},{1,17},{2,10},{3,19},{4,12},{5,21},{6,14},{7,23},{8,0},{9,25... | collective-permute-start | bytes 294920 | tf_op jit(solution)/shard_map/attend_sum_step_5/over_stage/ppermute | solution.py:479
  120.0 11.6 %collective-permute-start.49 = (bf16[384,512]{1,0:T(8,128)(2,1)S(1)}, bf16[384,512]{1,0:T(8,128)(2,1)S(1)}, u32[]{:S(2)}, u32[]{:S(2)}) collective-permute-start(bf16[384,512]{1,0:T(8,128)(2,1)S(1)} %pad_maximum_fusion.3.a8), channel_id=1, source_target_pairs={{0,2},{1,5},{2,0},{3,7},{4,6},{5,1},{6,4},{7,3},{8,10},{9,13},{10,... | collective-permute-start | bytes 1179656 | tf_op jit(solution)/shard_map/joining_sum_step_7/over_stage/ppermute | solution.py:479
  120.2 14.9 %collective-permute-start.52 = (bf16[512,512]{1,0:T(8,128)(2,1)S(1)}, bf16[512,512]{1,0:T(8,128)(2,1)S(1)}, u32[]{:S(2)}, u32[]{:S(2)}) collective-permute-start(bf16[512,512]{1,0:T(8,128)(2,1)S(1)} %pad_maximum_fusion.2.a8), channel_id=1, source_target_pairs={{0,8},{1,17},{2,10},{3,19},{4,12},{5,21},{6,14},{7,23},{8,0},{9,25... | collective-permute-start | bytes 1572872 | tf_op jit(solution)/shard_map/outer_sum_step_7/over_stage/ppermute | solution.py:479
  124.6 10.4 %collective-permute-start.53 = (bf16[512,512]{1,0:T(8,128)(2,1)S(1)}, bf16[512,512]{1,0:T(8,128)(2,1)S(1)}, u32[]{:S(2)}, u32[]{:S(2)}) collective-permute-start(bf16[512,512]{1,0:T(8,128)(2,1)S(1)} %pad_maximum_fusion.2.a8), channel_id=1, source_target_pairs={{0,1},{1,0},{2,3},{3,2},{4,5},{5,4},{6,7},{7,6},{8,9},{9,8},{10,11... | collective-permute-start | bytes 1572872 | tf_op jit(solution)/shard_map/outer_sum_sibling/over_bit/ppermute | solution.py:479
  126.7 4.9 %collective-permute-start.50 = (bf16[384,512]{1,0:T(8,128)(2,1)S(1)}, bf16[384,512]{1,0:T(8,128)(2,1)S(1)}, u32[]{:S(2)}, u32[]{:S(2)}) collective-permute-start(bf16[384,512]{1,0:T(8,128)(2,1)S(1)} %pad_maximum_fusion.3.a8), channel_id=1, source_target_pairs={{0,1},{1,0},{2,3},{3,2},{4,5},{5,4},{6,7},{7,6},{8,9},{9,8},{10,11... | collective-permute-start | bytes 1179656 | tf_op jit(solution)/shard_map/joining_sum_sibling/over_bit/ppermute | solution.py:479
  126.7 5.7 %collective-permute-start.51 = (bf16[192,512]{1,0:T(8,128)(2,1)S(1)}, bf16[192,512]{1,0:T(8,128)(2,1)S(1)}, u32[]{:S(2)}, u32[]{:S(2)}) collective-permute-start(bf16[192,512]{1,0:T(8,128)(2,1)S(1)} %pad_maximum_fusion.10), channel_id=1, source_target_pairs={{0,4},{1,3},{2,6},{3,1},{4,0},{5,7},{6,2},{7,5},{8,12},{9,11},{10,... | collective-permute-start | bytes 589832 | tf_op jit(solution)/shard_map/attend_sum_step_6/over_stage/ppermute | solution.py:479
  131.5 5.5 %collective-permute-start.54 = (bf16[640,512]{1,0:T(8,128)(2,1)S(1)}, bf16[640,512]{1,0:T(8,128)(2,1)S(1)}, u32[]{:S(2)}, u32[]{:S(2)}) collective-permute-start(bf16[640,512]{1,0:T(8,128)(2,1)S(1)} %collective-permute-done.47.r1), channel_id=1, source_target_pairs={{0,1},{1,0},{2,3},{3,2},{4,5},{5,4},{6,7},{7,6},{8,9},{9,8},{10,11... | collective-permute-start | bytes 1966088 | tf_op jit(solution)/shard_map/inner_sum_upper/over_bit/ppermute | solution.py:479
  135.0 4.7 %collective-permute-start.55 = (bf16[512,512]{1,0:T(8,128)(2,1)S(1)}, bf16[512,512]{1,0:T(8,128)(2,1)S(1)}, u32[]{:S(2)}, u32[]{:S(2)}) collective-permute-start(bf16[512,512]{1,0:T(8,128)(2,1)S(1)} %collective-permute-done.52.r1), channel_id=1, source_target_pairs={{0,1},{1,0},{2,3},{3,2},{4,5},{5,4},{6,7},{7,6},{8,9},{9,8},{10,11... | collective-permute-start | bytes 1572872 | tf_op jit(solution)/shard_map/outer_sum_upper/over_bit/ppermute | solution.py:479
  135.0 7.8 %collective-permute-start.56 = (bf16[384,512]{1,0:T(8,128)(2,1)S(1)}, bf16[384,512]{1,0:T(8,128)(2,1)S(1)}, u32[]{:S(2)}, u32[]{:S(2)}) collective-permute-start(bf16[384,512]{1,0:T(8,128)(2,1)S(1)} %pad_maximum_fusion.4.a8), channel_id=1, source_target_pairs={{0,2},{1,5},{2,0},{3,7},{4,6},{5,1},{6,4},{7,3},{8,10},{9,13},{10,... | collective-permute-start | bytes 1179656 | tf_op jit(solution)/shard_map/attend_sum_step_7/over_stage/ppermute | solution.py:479
  136.5 6.3 %collective-permute-start.57 = (bf16[384,512]{1,0:T(8,128)(2,1)S(1)}, bf16[384,512]{1,0:T(8,128)(2,1)S(1)}, u32[]{:S(2)}, u32[]{:S(2)}) collective-permute-start(bf16[384,512]{1,0:T(8,128)(2,1)S(1)} %pad_maximum_fusion.4.a8), channel_id=1, source_target_pairs={{0,1},{1,0},{2,3},{3,2},{4,5},{5,4},{6,7},{7,6},{8,9},{9,8},{10,11... | collective-permute-start | bytes 1179656 | tf_op jit(solution)/shard_map/attend_sum_sibling/over_bit/ppermute | solution.py:479
  136.5 6.3 %collective-permute-start.58 = (bf16[384,512]{1,0:T(8,128)(2,1)S(1)}, bf16[384,512]{1,0:T(8,128)(2,1)S(1)}, u32[]{:S(2)}, u32[]{:S(2)}) collective-permute-start(bf16[384,512]{1,0:T(8,128)(2,1)S(1)} %collective-permute-done.49.r1), channel_id=1, source_target_pairs={{0,1},{1,0},{2,3},{3,2},{4,5},{5,4},{6,7},{7,6},{8,9},{9,8},{10,11... | collective-permute-start | bytes 1179656 | tf_op jit(solution)/shard_map/joining_sum_upper/over_bit/ppermute | solution.py:479
  142.8 1.9 %collective-permute-start.59 = (bf16[384,512]{1,0:T(8,128)(2,1)S(1)}, bf16[384,512]{1,0:T(8,128)(2,1)S(1)}, u32[]{:S(2)}, u32[]{:S(2)}) collective-permute-start(bf16[384,512]{1,0:T(8,128)(2,1)S(1)} %collective-permute-done.56.r1), channel_id=1, source_target_pairs={{0,1},{1,0},{2,3},{3,2},{4,5},{5,4},{6,7},{7,6},{8,9},{9,8},{10,11... | collective-permute-start | bytes 1179656 | tf_op jit(solution)/shard_map/attend_sum_upper/over_bit/ppermute | solution.py:479
  (12 other events, 79.9 us)

commit v3 on v2

--- a/solution.py
+++ b/solution.py
@@ -13,8 +13,8 @@
 F32 = jnp.float32
 norm_eps = 1e-06
 
-ORDER_XY = ((1, 2, 3, 4), (2, 1, 4, 3))
-ORDER_YX = ((2, 1, 3, 4), (1, 2, 4, 3))
+ORDER_XY = ((1, 2, 3, 4), (2, 1, 3, 4))
+ORDER_YX = ((2, 1, 3, 4), (1, 2, 3, 4))
 ORDER_Z = ((3, 4, 1, 2), (4, 3, 2, 1))
 ORDER_ZY = ((4, 3, 1, 2), (3, 4, 2, 1))
 ORDERS = {"J": ORDER_XY, "U": ORDER_Z, "I": ORDER_XY, "T": ORDER_XY}
@@ -25,7 +25,7 @@
     ("KJ",), ("KU",), ("KI",), ("J", "U",), ("I",), ("KT",), ("J", "U", "I", "T",), ("KG", "I", "U",),
     ("T",), ("I", "J", "g0", "U", "T",), ("I",), ("U", "J",), ("I",), ("U", "T", "J",), ("J",),
     ("I", "U", "T", "g1",), ("J",), ("T",), ("I", "J", "U",), ("T", "I",), ("J", "T",), ("U",),
-    ("fI", "fU",), ("T",), ("fJ", "fT",),
+    ("fI", "fU", "fJ",), ("T",), ("hT",), ("fT",),
 )
 HALF = GROUP // 2
 
@@ -395,21 +395,24 @@
     gi_send[tokens_here:, :] = low(parts[3])
 
 
-def finish_kernel(orders, layout, with_vec, a8, r1, s8, sr1, *rest):
+def finish_kernel(orders, layout, whose, with_vec, parts, kept, *rest):
+    sources, rest = rest[:parts], rest[parts:]
     if with_vec:
         vec, rest = rest[0], rest[1:]
+    rest = rest[kept:]
     full, sems = rest[-2:]
     outs = rest[:-2]
     me = device_number()
     core = bit_of(me, 0)
-    each = a8.shape[0] // (HALF // 2)
+    each = sources[0].shape[0] // (HALF // 2)
     half_rows = HALF * each
     width = full.shape[1]
     copies = []
-    for which, (lower, upper) in enumerate(((a8, r1), (s8, sr1))):
+    for number, which in enumerate(whose):
+        lower, upper = sources[2 * number : 2 * number + 2]
         half = core if which == 0 else 1 - core
         place = own_place(me, orders, half)
-        base = pl.multiple_of(half * half_rows, half_rows)
+        base = number * half_rows
         for spot in range(HALF):
             source = lower if spot < HALF // 2 else upper
             begin = (spot % (HALF // 2)) * each
@@ -417,7 +420,7 @@
             full[pl.ds(pl.multiple_of(base + block * each, 8), each), :] = source[
                 begin : begin + each, :
             ].astype(F32)
-        row = 0
+        row = base
         for out, pieces, by_column in layout:
             for piece in range(pieces):
                 target = outs[out]
@@ -428,7 +431,7 @@
                 else:
                     size = target.shape[0] // 2
                     target = target.at[pl.ds(pl.multiple_of(half * size, size), size), :]
-                source = full.at[pl.ds(pl.multiple_of(base + row, 8), size), :]
+                source = full.at[pl.ds(row, size), :]
                 copies.append(pltpu.make_async_copy(source, target, sems.at[len(copies)]))
                 copies[-1].start()
                 row += size
@@ -443,13 +446,14 @@
         copy.wait()
 
 
-def call(kernel, name, microseconds, out_shapes, out_specs, in_specs, scratch, *operands):
+def call(kernel, name, microseconds, out_shapes, out_specs, in_specs, scratch, *operands, aliases=()):
     return pl.pallas_call(
         kernel,
         out_shape=out_shapes,
         in_specs=in_specs,
         out_specs=out_specs,
         scratch_shapes=scratch,
+        input_output_aliases=dict(aliases),
         compiler_params=pltpu.CompilerParams(vmem_limit_bytes=32 * 1024 * 1024),
         cost_estimate=pl.CostEstimate(
             flops=int(microseconds * 1e4), bytes_accessed=int(microseconds * 1e2), transcendentals=0
@@ -622,21 +626,27 @@
                 self.send(self.got, None, "upper", "upper")
 
         def parts(self):
-            return self.keep, self.got, self.sibling, self.upper
-
-    def finish(stream, outs, layout, name, vector=None):
-        parts = stream.parts()
-        rows = parts[0].shape[0] * 4
+            return self.keep, self.got, self.sibling, getattr(self, "upper", None)
+
+    def finish(stream, outs, layout, name, vector=None, whose=(0, 1), kept=()):
+        sources = stream.parts()[2 * whose[0] : 2 * whose[-1] + 2]
+        sources = list(sources[:-1]) + [gate(sources[-1])]
+        vectors = [] if vector is None else [vector]
         small = [] if vector is None else [shape((1, width), F32)] * 6 + [shape((1, hidden_units), F32)]
+        rows = sources[0].shape[0] * 2 * len(whose)
+        first = len(sources) + len(vectors)
         out = call(
-            functools.partial(finish_kernel, stream.orders, layout, vector is not None),
+            functools.partial(
+                finish_kernel, stream.orders, layout, whose, vector is not None, len(sources), len(kept)
+            ),
             name,
             2,
             tuple(outs) + tuple(small),
             (ANY,) * len(outs) + (VM,) * len(small),
-            (VM,) * (4 if vector is None else 5),
+            (VM,) * first + (ANY,) * len(kept),
             [pltpu.VMEM((rows, width), F32), pltpu.SemaphoreType.DMA((8,))],
-            parts[0], parts[1], parts[2], gate(parts[3]), *(() if vector is None else (vector,)),
+            *sources, *vectors, *kept,
+            aliases=[(first + index, index) for index in range(len(kept))],
         )
         out = list(out)
         out[0] = mark(out[0])
@@ -760,7 +770,11 @@
                     ((0, blocks // 2, True), (1, 1, False)), "finish_inner",
                 )
             elif step == "fT":
-                done["T"] = finish(streams["T"], [square] * 3, THREE, "finish_attend", streams["T"].extra)
+                done["T"] = finish(
+                    streams["T"], [square] * 3, THREE, "finish_attend", streams["T"].extra, (1,), done["hT"]
+                )
+            elif step == "hT":
+                done["hT"] = finish(streams["T"], [square] * 3, THREE, "finish_half", whose=(0,))
             elif step == "g0":
                 got = gate(done["near"])
                 send = mark(done["gi"][1] + got[here:])

time: 148 us -> 142 us (0.959)
  waiting for transfers between devices: 52.2 us -> 46.1 us
    ppermute x60, waiting for transfers between devices: 52.2 us -> 46.1 us  [swap(): return lax.ppermute(values, AXES, [(d, partner(d)) for d in range(devices)])]
    pallas_call x11 -> x12, Pallas kernels: 32.6 us -> 33.3 us  [call(): pl.pallas_call(kernel, out_shape=out_shapes, in_specs=in_specs, out_specs...]
  transfers between devices with their start and end apart: 60 -> 60, of which waited for: 24 -> 27; matrix products, arithmetic and copies ran while one was open for 3% -> 3% of each run, Pallas kernels for 17% -> 19%
where the time goes in v3:
time: 142 us
  starting transfers between devices  55.2 us (39%)
  waiting for transfers between devices  46.1 us (32%)
  Pallas kernels  33.3 us (23%)
  other arithmetic  3.02 us (2%)
  local copies, waits for them, and re-layouts  2.37 us (2%)
  between operations  1.58 us (1%)
    ppermute x60, starting transfers between devices, swap(): return lax.ppermute(values, AXES, [(d, partner(d)) for d in range(devices)])  55.2 us
    ppermute x60, waiting for transfers between devices, swap(): return lax.ppermute(values, AXES, [(d, partner(d)) for d in range(devices)])  46.1 us
    pallas_call x12, Pallas kernels, call(): pl.pallas_call(kernel, out_shape=out_shapes, in_specs=in_specs, out_specs...  33.3 us
  transfers between devices with their start and end apart: 60, of which 27 were waited for; matrix products, arithmetic and copies ran while one was open for 3% of the time, Pallas kernels for 19%

profile of v3, /device:TPU:0, one launch (start us, length us, event | category | flops | bytes accessed | tf_op | source)
XLA Modules:
  0.0 141.5 jit_solution(14169245501374800492)
XLA Ops:
  0.7 0.9 fusion.4
  1.6 3.0 %collective-permute-start = (bf16[1,3,64,256]{3,2,1,0:T(8,128)(2,1)S(1)}, bf16[1,3,64,256]{3,2,1,0:T(8,128)(2,1)S(1)}, u32[]{:S(2)}, u32[]{:S(2)}) collective-permute-start(bf16[1,3,64,256]{3,2,1,0:T(8,128)(2,1)S(1)} %fusion.4), channel_id=1, source_target_pairs={{0,4},{1,17},{2,6},{3,19},{4,0},{5,21},{6,2},{7,23},{8,12},{9,25},... | collective-permute-start | bytes 294920 | tf_op jit(solution)/shard_map/weights_first/ppermute | solution.py:483
  4.6 1.7 %collective-permute-start.4 = (s32[2,128]{1,0:T(2,128)}, s32[2,128]{1,0:T(2,128)S(1)}, u32[]{:S(2)}, u32[]{:S(2)}) collective-permute-start(s32[2,128]{1,0:T(2,128)} %bitcast.45), channel_id=1, source_target_pairs={{0,3},{1,2},{2,1},{3,0},{4,7},{5,6},{6,5},{7,4},{8,11},{9,10},{10,... | collective-permute-start | bytes 3080 | tf_op jit(solution)/shard_map/segments/ppermute | solution.py:483
  6.9 1.5 %collective-permute-start.5 = (bf16[256,512]{1,0:T(8,128)(2,1)}, bf16[256,512]{1,0:T(8,128)(2,1)S(1)}, u32[]{:S(2)}, u32[]{:S(2)}) collective-permute-start(bf16[256,512]{1,0:T(8,128)(2,1)} %bitcast.50), channel_id=1, source_target_pairs={{0,2},{1,3},{2,0},{3,1},{4,6},{5,7},{6,4},{7,5},{8,10},{9,11},{10,... | collective-permute-start | bytes 786440 | tf_op jit(solution)/shard_map/row_far/ppermute | solution.py:483
  8.4 2.0 %collective-permute-start.6 = (bf16[2,3,64,256]{3,2,1,0:T(8,128)(2,1)S(1)}, bf16[2,3,64,256]{3,2,1,0:T(8,128)(2,1)S(1)}, u32[]{:S(2)}, u32[]{:S(2)}) collective-permute-start(bf16[2,3,64,256]{3,2,1,0:T(8,128)(2,1)S(1)} %pad_maximum_fusion.8.rest_0_), channel_id=1, source_target_pairs={{0,16},{1,9},{2,18},{3,11},{4,20},{5,13},{6,22},{7,15},{8,24},{9,1... | collective-permute-start | bytes 589832 | tf_op jit(solution)/shard_map/weights_second/ppermute | solution.py:483
  10.4 1.1 constant_dynamic-update-slice_fusion.4
  11.5 1.1 constant_dynamic-update-slice_fusion.3
  13.0 1.1 collective-permute-done.2.seg1
  14.1 0.9 collective-permute-done.5.x2
  14.9 1.6 %collective-permute-start.8 = (bf16[2,3,64,256]{3,2,1,0:T(8,128)(2,1)S(1)}, bf16[2,3,64,256]{3,2,1,0:T(8,128)(2,1)S(1)}, u32[]{:S(2)}, u32[]{:S(2)}) collective-permute-start(bf16[2,3,64,256]{3,2,1,0:T(8,128)(2,1)S(1)} %pad_maximum_fusion.8.rest_0_), channel_id=1, source_target_pairs={{0,8},{1,5},{2,10},{3,7},{4,12},{5,1},{6,14},{7,3},{8,0},{9,13},{1... | collective-permute-start | bytes 589832 | tf_op jit(solution)/shard_map/weights_third/ppermute | solution.py:483
  17.7 5.8 %attend.1 = (bf16[256,512]{1,0:T(8,128)(2,1)S(1)}, bf16[1024,512]{1,0:T(8,128)(2,1)S(1)}, bf16[1024,512]{1,0:T(8,128)(2,1)S(1)}, bf16[8,512,256]{2,1,0:T(8,128)(...) custom-call(bf16[512,512]{1,0:T(8,128)(2,1)S(1)} %pad_maximum_fusion.1.x01, ...), custom_call_target="tpu_custom_call" | custom-call | flops 60000 | bytes 600 | tf_op jit(solution)/shard_map/attend/pallas_call | solution.py:450
  24.7 2.7 %feed.1 = (bf16[256,2048]{1,0:T(8,128)(2,1)S(1)}, bf16[256,2048]{1,0:T(8,128)(2,1)S(1)}, f32[256,512]{1,0:T(8,128)S(1)}, f32[256,128]{1,0:T(8,128)S(1)}, bf16[25...) custom-call(f32[256,512]{1,0:T(8,128)S(1)} %get-tuple-element.297.n1_ref, f32[1,512]{1,0:T(1,128)S(1)} %bitcast.32, ...), custom_call_target="tpu_custom_call" | custom-call | flops 30000 | bytes 300 | tf_op jit(solution)/shard_map/feed/pallas_call | solution.py:450
  27.5 4.9 %joining.1 = (bf16[256,512]{1,0:T(8,128)(2,1)}, bf16[768,512]{1,0:T(8,128)(2,1)S(1)}, bf16[768,512]{1,0:T(8,128)(2,1)S(1)}, f32[256,512]{1,0:T(8,128)S(1)}, bf16...) custom-call(f32[256,512]{1,0:T(8,128)S(1)} %get-tuple-element.300.n2_ref, f32[1,512]{1,0:T(1,128)S(1)} %bitcast.38, ...), custom_call_target="tpu_custom_call" | custom-call | flops 80000 | bytes 800 | tf_op jit(solution)/shard_map/joining/pallas_call | solution.py:450
  32.5 1.5 %outer_back.1 = (f32[256,512]{1,0:T(8,128)S(1)}, f32[8,512]{1,0:T(8,128)S(1)}, bf16[1024,512]{1,0:T(8,128)(2,1)S(1)}, bf16[1024,512]{1,0:T(8,128)(2,1)S(1)}) custom-call(f32[256,512]{1,0:T(8,128)S(1)} %get-tuple-element.313.dhp_ref, bf16[256,512]{1,0:T(8,128)(2,1)S(1)} %get-tuple-element.314.dt_ref, ...), custom_call_target="tpu_custom_call" | custom-call | flops 40000 | bytes 400 | tf_op jit(solution)/shard_map/outer_back/pallas_call | solution.py:450
  34.4 2.5 %inner_back.1 = (f32[256,512]{1,0:T(8,128)S(1)}, bf16[16,512]{1,0:T(8,128)(2,1)S(1)}, bf16[1280,512]{1,0:T(8,128)(2,1)S(1)}, bf16[1280,512]{1,0:T(8,128)(2,1)S(1)}) custom-call(f32[256,512]{1,0:T(8,128)S(1)} %get-tuple-element.320.d2_ref, bf16[256,2048]{1,0:T(8,128)(2,1)S(1)} %get-tuple-element.321.sz_ref, bf16[512,2048]{1,0:T(8,128)(2,1)S(1)} %copy-done, ...), custom_call_target="tpu_custom_call" | custom-call | flops 60000 | bytes 600 | tf_op jit(solution)/shard_map/inner_back/pallas_call | solution.py:450
  37.3 1.5 %collective-permute-start.17 = (bf16[384,512]{1,0:T(8,128)(2,1)S(1)}, bf16[384,512]{1,0:T(8,128)(2,1)S(1)}, u32[]{:S(2)}, u32[]{:S(2)}) collective-permute-start(bf16[384,512]{1,0:T(8,128)(2,1)S(1)} %get-tuple-element.351), channel_id=1, source_target_pairs={{0,2},{1,5},{2,0},{3,7},{4,6},{5,1},{6,4},{7,3},{8,10},{9,13},{10,... | collective-permute-start | bytes 1179656 | tf_op jit(solution)/shard_map/joining_sum_step_0/over_stage/ppermute | solution.py:483
  38.8 0.9 collective-permute-start.18
  40.2 1.5 %collective-permute-start.19 = (bf16[640,512]{1,0:T(8,128)(2,1)S(1)}, bf16[640,512]{1,0:T(8,128)(2,1)S(1)}, u32[]{:S(2)}, u32[]{:S(2)}) collective-permute-start(bf16[640,512]{1,0:T(8,128)(2,1)S(1)} %get-tuple-element.357), channel_id=1, source_target_pairs={{0,2},{1,5},{2,0},{3,7},{4,6},{5,1},{6,4},{7,3},{8,10},{9,13},{10,... | collective-permute-start | bytes 1966088 | tf_op jit(solution)/shard_map/inner_sum_step_0/over_stage/ppermute | solution.py:483
  41.6 4.4 %attend_back.1 = (bf16[784,512]{1,0:T(8,128)(2,1)S(1)}, bf16[784,512]{1,0:T(8,128)(2,1)S(1)}, bf16[256,512]{1,0:T(8,128)(2,1)S(1)}, bf16[1024,512]{1,0:T(8,128)(2,1)S(1)}, bf16[1024,512]{1,0:T(8,128)(2,1)S(1)}) custom-call(f32[256,512]{1,0:T(8,128)S(1)} %get-tuple-element.364.d1_ref, bf16[512,2560]{1,0:T(8,128)(2,1)S(1)} %constant_dynamic-update-slice_fusion.bank, ...), custom_call_target="tpu_custom_call" | custom-call | flops 80000 | bytes 800 | tf_op jit(solution)/shard_map/attend_back/pallas_call | solution.py:450
  46.7 5.9 %collective-permute-done.18 = bf16[512,512]{1,0:T(8,128)(2,1)S(1)} collective-permute-done((bf16[512,512]{1,0:T(8,128)(2,1)S(1)}, bf16[512,512]{1,0:T(8,128)(2,1)S(1)}, u32[]{:S(2)}, u32[]{:S(2)}) %collective-permute-start.18) | collective-permute-done | bytes 524320 | tf_op jit(solution)/shard_map/outer_sum_step_0/over_stage/ppermute | solution.py:483
  52.8 1.1 collective-permute-start.21
  53.9 2.9 %collective-permute-start.22 = (bf16[256,512]{1,0:T(8,128)(2,1)S(1)}, bf16[256,512]{1,0:T(8,128)(2,1)S(1)}, u32[]{:S(2)}, u32[]{:S(2)}) collective-permute-start(bf16[256,512]{1,0:T(8,128)(2,1)S(1)} %get-tuple-element.375), channel_id=1, source_target_pairs={{0,16},{1,9},{2,18},{3,11},{4,20},{5,13},{6,22},{7,15},{8,24},{9,1... | collective-permute-start | bytes 786440 | tf_op jit(solution)/shard_map/outer_sum_step_1/over_stage/ppermute | solution.py:483
  56.9 1.4 input_back.1
  58.3 0.9 collective-permute-start.25
  59.2 1.2 collective-permute-start.23
  60.4 2.6 %collective-permute-done.22 = bf16[256,512]{1,0:T(8,128)(2,1)S(1)} collective-permute-done((bf16[256,512]{1,0:T(8,128)(2,1)S(1)}, bf16[256,512]{1,0:T(8,128)(2,1)S(1)}, u32[]{:S(2)}, u32[]{:S(2)}) %collective-permute-start.22) | collective-permute-done | bytes 262176 | tf_op jit(solution)/shard_map/outer_sum_step_1/over_stage/ppermute | solution.py:483
  63.1 2.5 %collective-permute-start.27 = (bf16[128,512]{1,0:T(8,128)(2,1)S(1)}, bf16[128,512]{1,0:T(8,128)(2,1)S(1)}, u32[]{:S(2)}, u32[]{:S(2)}) collective-permute-start(bf16[128,512]{1,0:T(8,128)(2,1)S(1)} %get-tuple-element.394), channel_id=1, source_target_pairs={{0,2},{1,5},{2,0},{3,7},{4,6},{5,1},{6,4},{7,3},{8,10},{9,13},{10,... | collective-permute-start | bytes 393224 | tf_op jit(solution)/shard_map/outer_sum_step_2/over_stage/ppermute | solution.py:483
  65.7 1.4 collective-permute-done.23
  67.2 1.3 collective-permute-start.28
  68.5 2.5 %collective-permute-done.24 = bf16[160,512]{1,0:T(8,128)(2,1)S(1)} collective-permute-done((bf16[160,512]{1,0:T(8,128)(2,1)S(1)}, bf16[160,512]{1,0:T(8,128)(2,1)S(1)}, u32[]{:S(2)}, u32[]{:S(2)}) %collective-permute-start.24) | collective-permute-done | bytes 163872 | tf_op jit(solution)/shard_map/inner_sum_step_2/over_stage/ppermute | solution.py:483
  71.1 2.0 %collective-permute-done.28 = bf16[208,512]{1,0:T(8,128)(2,1)S(1)} collective-permute-done((bf16[208,512]{1,0:T(8,128)(2,1)S(1)}, bf16[208,512]{1,0:T(8,128)(2,1)S(1)}, u32[]{:S(2)}, u32[]{:S(2)}) %collective-permute-start.28) | collective-permute-done | bytes 213024 | tf_op jit(solution)/shard_map/attend_sum_step_1/over_stage/ppermute | solution.py:483
  73.2 2.1 %collective-permute-start.29 = (bf16[80,512]{1,0:T(8,128)(2,1)S(1)}, bf16[80,512]{1,0:T(8,128)(2,1)S(1)}, u32[]{:S(2)}, u32[]{:S(2)}) collective-permute-start(bf16[80,512]{1,0:T(8,128)(2,1)S(1)} %slice_add_fusion.24), channel_id=1, source_target_pairs={{0,16},{1,17},{2,18},{3,19},{4,20},{5,21},{6,22},{7,23},{8,24},{9,... | collective-permute-start | bytes 245768 | tf_op jit(solution)/shard_map/inner_sum_step_3/over_stage/ppermute | solution.py:483
  75.3 1.0 collective-permute-start.30
  76.6 1.8 %collective-permute-start.34 = (bf16[112,512]{1,0:T(8,128)(2,1)S(1)}, bf16[112,512]{1,0:T(8,128)(2,1)S(1)}, u32[]{:S(2)}, u32[]{:S(2)}) collective-permute-start(bf16[112,512]{1,0:T(8,128)(2,1)S(1)} %fusion.1), channel_id=1, source_target_pairs={{0,8},{1,9},{2,10},{3,11},{4,12},{5,13},{6,14},{7,15},{8,0},{9,1},... | collective-permute-start | bytes 344072 | tf_op jit(solution)/shard_map/attend_sum_step_2/over_stage/ppermute | solution.py:483
  78.4 1.1 collective-permute-start.40
  79.6 2.0 %collective-permute-start.32 = (bf16[80,512]{1,0:T(8,128)(2,1)S(1)}, bf16[80,512]{1,0:T(8,128)(2,1)S(1)}, u32[]{:S(2)}, u32[]{:S(2)}) collective-permute-start(bf16[80,512]{1,0:T(8,128)(2,1)S(1)} %fusion.5), channel_id=1, source_target_pairs={{0,16},{1,17},{2,18},{3,19},{4,20},{5,21},{6,22},{7,23},{8,24},{9,... | collective-permute-start | bytes 245768 | tf_op jit(solution)/shard_map/inner_sum_step_4/over_stage/ppermute | solution.py:483
  82.1 1.1 collective-permute-start.35
  83.2 0.9 collective-permute-start.33
  84.1 2.2 %collective-permute-done.32 = bf16[80,512]{1,0:T(8,128)(2,1)S(1)} collective-permute-done((bf16[80,512]{1,0:T(8,128)(2,1)S(1)}, bf16[80,512]{1,0:T(8,128)(2,1)S(1)}, u32[]{:S(2)}, u32[]{:S(2)}) %collective-permute-start.32) | collective-permute-done | bytes 81952 | tf_op jit(solution)/shard_map/inner_sum_step_4/over_stage/ppermute | solution.py:483
  86.5 1.1 collective-permute-done.33
  87.8 1.8 %collective-permute-start.36 = (bf16[48,512]{1,0:T(8,128)(2,1)S(1)}, bf16[48,512]{1,0:T(8,128)(2,1)S(1)}, u32[]{:S(2)}, u32[]{:S(2)}) collective-permute-start(bf16[48,512]{1,0:T(8,128)(2,1)S(1)} %fusion.8), channel_id=1, source_target_pairs={{0,16},{1,17},{2,18},{3,19},{4,20},{5,21},{6,22},{7,23},{8,24},{9,... | collective-permute-start | bytes 147464 | tf_op jit(solution)/shard_map/joining_sum_step_4/over_stage/ppermute | solution.py:483
  89.6 1.2 collective-permute-start.39
  90.8 1.1 collective-permute-start.38
  91.8 1.1 collective-permute-done.36
  92.9 2.0 %collective-permute-start.41 = (bf16[96,512]{1,0:T(8,128)(2,1)S(1)}, bf16[96,512]{1,0:T(8,128)(2,1)S(1)}, u32[]{:S(2)}, u32[]{:S(2)}) collective-permute-start(bf16[96,512]{1,0:T(8,128)(2,1)S(1)} %pad_maximum_fusion.14), channel_id=1, source_target_pairs={{0,8},{1,9},{2,10},{3,11},{4,12},{5,13},{6,14},{7,15},{8,0},{9,1},... | collective-permute-start | bytes 294920 | tf_op jit(solution)/shard_map/joining_sum_step_5/over_stage/ppermute | solution.py:483
  95.0 1.6 %collective-permute-done.38 = bf16[128,512]{1,0:T(8,128)(2,1)S(1)} collective-permute-done((bf16[128,512]{1,0:T(8,128)(2,1)S(1)}, bf16[128,512]{1,0:T(8,128)(2,1)S(1)}, u32[]{:S(2)}, u32[]{:S(2)}) %collective-permute-start.38) | collective-permute-done | bytes 131104 | tf_op jit(solution)/shard_map/outer_sum_step_5/over_stage/ppermute | solution.py:483
  97.5 1.6 %collective-permute-start.43 = (bf16[320,512]{1,0:T(8,128)(2,1)S(1)}, bf16[320,512]{1,0:T(8,128)(2,1)S(1)}, u32[]{:S(2)}, u32[]{:S(2)}) collective-permute-start(bf16[320,512]{1,0:T(8,128)(2,1)S(1)} %pad_maximum_fusion.5), channel_id=1, source_target_pairs={{0,4},{1,3},{2,6},{3,1},{4,0},{5,7},{6,2},{7,5},{8,12},{9,11},{10,... | collective-permute-start | bytes 983048 | tf_op jit(solution)/shard_map/inner_sum_step_6/over_stage/ppermute | solution.py:483
  99.1 2.5 %collective-permute-start.42 = (bf16[48,512]{1,0:T(8,128)(2,1)S(1)}, bf16[48,512]{1,0:T(8,128)(2,1)S(1)}, u32[]{:S(2)}, u32[]{:S(2)}) collective-permute-start(bf16[48,512]{1,0:T(8,128)(2,1)S(1)} %slice.313), channel_id=1, source_target_pairs={{0,16},{1,17},{2,18},{3,19},{4,20},{5,21},{6,22},{7,23},{8,24},{9,... | collective-permute-start | bytes 147464 | tf_op jit(solution)/shard_map/attend_sum_step_4/over_stage/ppermute | solution.py:483
  101.6 0.9 collective-permute-start.45
  102.5 2.0 %collective-permute-done.42 = bf16[48,512]{1,0:T(8,128)(2,1)S(1)} collective-permute-done((bf16[48,512]{1,0:T(8,128)(2,1)S(1)}, bf16[48,512]{1,0:T(8,128)(2,1)S(1)}, u32[]{:S(2)}, u32[]{:S(2)}) %collective-permute-start.42) | collective-permute-done | bytes 49184 | tf_op jit(solution)/shard_map/attend_sum_step_4/over_stage/ppermute | solution.py:483
  104.9 4.5 %collective-permute-done.44 = bf16[192,512]{1,0:T(8,128)(2,1)S(1)} collective-permute-done((bf16[192,512]{1,0:T(8,128)(2,1)S(1)}, bf16[192,512]{1,0:T(8,128)(2,1)S(1)}, u32[]{:S(2)}, u32[]{:S(2)}) %collective-permute-start.44) | collective-permute-done | bytes 196640 | tf_op jit(solution)/shard_map/joining_sum_step_6/over_stage/ppermute | solution.py:483
  109.4 1.9 %collective-permute-done.45 = bf16[256,512]{1,0:T(8,128)(2,1)S(1)} collective-permute-done((bf16[256,512]{1,0:T(8,128)(2,1)S(1)}, bf16[256,512]{1,0:T(8,128)(2,1)S(1)}, u32[]{:S(2)}, u32[]{:S(2)}) %collective-permute-start.45) | collective-permute-done | bytes 262176 | tf_op jit(solution)/shard_map/outer_sum_step_6/over_stage/ppermute | solution.py:483
  111.4 1.5 %collective-permute-start.47 = (bf16[640,512]{1,0:T(8,128)(2,1)S(1)}, bf16[640,512]{1,0:T(8,128)(2,1)S(1)}, u32[]{:S(2)}, u32[]{:S(2)}) collective-permute-start(bf16[640,512]{1,0:T(8,128)(2,1)S(1)} %pad_maximum_fusion.rest_0_), channel_id=1, source_target_pairs={{0,2},{1,5},{2,0},{3,7},{4,6},{5,1},{6,4},{7,3},{8,10},{9,13},{10,... | collective-permute-start | bytes 1966088 | tf_op jit(solution)/shard_map/inner_sum_step_7/over_stage/ppermute | solution.py:483
  114.3 1.2 collective-permute-start.52
  115.5 3.3 %collective-permute-done.46 = bf16[96,512]{1,0:T(8,128)(2,1)S(1)} collective-permute-done((bf16[96,512]{1,0:T(8,128)(2,1)S(1)}, bf16[96,512]{1,0:T(8,128)(2,1)S(1)}, u32[]{:S(2)}, u32[]{:S(2)}) %collective-permute-start.46) | collective-permute-done | bytes 98336 | tf_op jit(solution)/shard_map/attend_sum_step_5/over_stage/ppermute | solution.py:483
  118.8 3.2 %collective-permute-done.47.rest_1_ = bf16[640,512]{1,0:T(8,128)(2,1)S(1)} collective-permute-done((bf16[640,512]{1,0:T(8,128)(2,1)S(1)}, bf16[640,512]{1,0:T(8,128)(2,1)S(1)}, u32[]{:S(2)}, u32[]{:S(2)}) %collective-permute-start.47) | collective-permute-done | bytes 655392 | tf_op jit(solution)/shard_map/inner_sum_step_7/over_stage/ppermute | solution.py:483
  122.1 1.2 collective-permute-start.51
  123.3 3.9 %collective-permute-done.49.rest_1_ = bf16[384,512]{1,0:T(8,128)(2,1)S(1)} collective-permute-done((bf16[384,512]{1,0:T(8,128)(2,1)S(1)}, bf16[384,512]{1,0:T(8,128)(2,1)S(1)}, u32[]{:S(2)}, u32[]{:S(2)}) %collective-permute-start.49) | collective-permute-done | bytes 393248 | tf_op jit(solution)/shard_map/joining_sum_step_7/over_stage/ppermute | solution.py:483
  127.8 1.5 %collective-permute-done.52.rest_1_ = bf16[512,512]{1,0:T(8,128)(2,1)S(1)} collective-permute-done((bf16[512,512]{1,0:T(8,128)(2,1)S(1)}, bf16[512,512]{1,0:T(8,128)(2,1)S(1)}, u32[]{:S(2)}, u32[]{:S(2)}) %collective-permute-start.52) | collective-permute-done | bytes 524320 | tf_op jit(solution)/shard_map/outer_sum_step_7/over_stage/ppermute | solution.py:483
  130.5 2.7 %finish_inner.1 = (f32[512,2048]{1,0:T(8,128)}, f32[512,512]{1,0:T(8,128)}) custom-call(bf16[640,512]{1,0:T(8,128)(2,1)S(1)} %pad_maximum_fusion.rest_0_, bf16[640,512]{1,0:T(8,128)(2,1)S(1)} %collective-permute-done.47.rest_1_, bf16[640,512]{1,0:T(8,128)(2,1)S(1)} %collective-permute-done.48.rest_2_, bf16[640,512]{1,0:T(8,128)(2,1)S(1)} %collective-permute-done.54.rest_3_), custom_call_target="tpu_custom_call" | custom-call | flops 20000 | bytes 200 | tf_op jit(solution)/shard_map/finish_inner/pallas_call | solution.py:450
  133.1 2.3 %finish_outer.1 = f32[2048,512]{1,0:T(8,128)} custom-call(bf16[512,512]{1,0:T(8,128)(2,1)S(1)} %pad_maximum_fusion.2.rest_0_, bf16[512,512]{1,0:T(8,128)(2,1)S(1)} %collective-permute-done.52.rest_1_, bf16[512,512]{1,0:T(8,128)(2,1)S(1)} %collective-permute-done.53.rest_2_, bf16[512,512]{1,0:T(8,128)(2,1)S(1)} %collective-permute-done.55.rest_3_), custom_call_target="tpu_custom_call" | custom-call | flops 20000 | bytes 200 | tf_op jit(solution)/shard_map/finish_outer/pallas_call | solution.py:450
  135.4 1.9 %finish_joining.1 = (f32[512,512]{1,0:T(8,128)}, f32[512,512]{1,0:T(8,128)}, f32[512,512]{1,0:T(8,128)}) custom-call(bf16[384,512]{1,0:T(8,128)(2,1)S(1)} %pad_maximum_fusion.3.rest_0_, bf16[384,512]{1,0:T(8,128)(2,1)S(1)} %collective-permute-done.49.rest_1_, bf16[384,512]{1,0:T(8,128)(2,1)S(1)} %collective-permute-done.50.rest_2_, ...), custom_call_target="tpu_custom_call" | custom-call | flops 20000 | bytes 200 | tf_op jit(solution)/shard_map/finish_joining/pallas_call | solution.py:450
  137.9 1.3 finish_half.1
  139.4 2.0 %finish_attend.1 = (f32[512,512]{1,0:T(8,128)}, f32[512,512]{1,0:T(8,128)}, f32[512,512]{1,0:T(8,128)}, f32[1,512]{1,0:T(1,128)}, f32[1,512]{1,0:T(1,128)}, /*in...) custom-call(bf16[384,512]{1,0:T(8,128)(2,1)S(1)} %collective-permute, ...), custom_call_target="tpu_custom_call", output_to_operand_aliasing={{0}: (3, {}), {1}: (4, {}), {2}: (5, {})} | custom-call | flops 20000 | bytes 200 | tf_op jit(solution)/shard_map/finish_attend/pallas_call | solution.py:450
  (150 shorter events, 12.2 us)
Async XLA Ops:
  0.7 12.0 %copy-start.12 = (bf16[512,512]{1,0:T(8,128)(2,1)S(1)}, bf16[512,512]{1,0:T(8,128)(2,1)}, u32[]{:S(2)}) copy-start(bf16[512,512]{1,0:T(8,128)(2,1)} %param.26) | copy-start | bytes 1572868
  0.7 12.0 %copy-start.13 = (bf16[512,512]{1,0:T(8,128)(2,1)S(1)}, bf16[512,512]{1,0:T(8,128)(2,1)}, u32[]{:S(2)}) copy-start(bf16[512,512]{1,0:T(8,128)(2,1)} %param.27) | copy-start | bytes 1572868
  0.7 12.1 %copy-start.14 = (bf16[512,512]{1,0:T(8,128)(2,1)S(1)}, bf16[512,512]{1,0:T(8,128)(2,1)}, u32[]{:S(2)}) copy-start(bf16[512,512]{1,0:T(8,128)(2,1)} %param.35) | copy-start | bytes 1572868
  1.6 6.8 %collective-permute-start = (bf16[1,3,64,256]{3,2,1,0:T(8,128)(2,1)S(1)}, bf16[1,3,64,256]{3,2,1,0:T(8,128)(2,1)S(1)}, u32[]{:S(2)}, u32[]{:S(2)}) collective-permute-start(bf16[1,3,64,256]{3,2,1,0:T(8,128)(2,1)S(1)} %fusion.4), channel_id=1, source_target_pairs={{0,4},{1,17},{2,6},{3,19},{4,0},{5,21},{6,2},{7,23},{8,12},{9,25},... | collective-permute-start | bytes 294920 | tf_op jit(solution)/shard_map/weights_first/ppermute | solution.py:483
  4.6 8.4 %collective-permute-start.4 = (s32[2,128]{1,0:T(2,128)}, s32[2,128]{1,0:T(2,128)S(1)}, u32[]{:S(2)}, u32[]{:S(2)}) collective-permute-start(s32[2,128]{1,0:T(2,128)} %bitcast.45), channel_id=1, source_target_pairs={{0,3},{1,2},{2,1},{3,0},{4,7},{5,6},{6,5},{7,4},{8,11},{9,10},{10,... | collective-permute-start | bytes 3080 | tf_op jit(solution)/shard_map/segments/ppermute | solution.py:483
  6.3 6.7 %collective-permute-start.3 = (s32[2,128]{1,0:T(2,128)}, s32[2,128]{1,0:T(2,128)S(1)}, u32[]{:S(2)}, u32[]{:S(2)}) collective-permute-start(s32[2,128]{1,0:T(2,128)} %bitcast.46), channel_id=1, source_target_pairs={{0,2},{1,3},{2,0},{3,1},{4,6},{5,7},{6,4},{7,5},{8,10},{9,11},{10,... | collective-permute-start | bytes 3080 | tf_op jit(solution)/shard_map/segments/ppermute | solution.py:483
  6.9 8.1 %collective-permute-start.5 = (bf16[256,512]{1,0:T(8,128)(2,1)}, bf16[256,512]{1,0:T(8,128)(2,1)S(1)}, u32[]{:S(2)}, u32[]{:S(2)}) collective-permute-start(bf16[256,512]{1,0:T(8,128)(2,1)} %bitcast.50), channel_id=1, source_target_pairs={{0,2},{1,3},{2,0},{3,1},{4,6},{5,7},{6,4},{7,5},{8,10},{9,11},{10,... | collective-permute-start | bytes 786440 | tf_op jit(solution)/shard_map/row_far/ppermute | solution.py:483
  8.4 4.5 %collective-permute-start.1 = (bf16[256,512]{1,0:T(8,128)(2,1)}, bf16[256,512]{1,0:T(8,128)(2,1)S(1)}, u32[]{:S(2)}, u32[]{:S(2)}) collective-permute-start(bf16[256,512]{1,0:T(8,128)(2,1)} %bitcast.51), channel_id=1, source_target_pairs={{0,1},{1,0},{2,3},{3,2},{4,5},{5,4},{6,7},{7,6},{8,9},{9,8},{10,11... | collective-permute-start | bytes 786440 | tf_op jit(solution)/shard_map/row_near/ppermute | solution.py:483
  8.4 8.8 %collective-permute-start.6 = (bf16[2,3,64,256]{3,2,1,0:T(8,128)(2,1)S(1)}, bf16[2,3,64,256]{3,2,1,0:T(8,128)(2,1)S(1)}, u32[]{:S(2)}, u32[]{:S(2)}) collective-permute-start(bf16[2,3,64,256]{3,2,1,0:T(8,128)(2,1)S(1)} %pad_maximum_fusion.8.rest_0_), channel_id=1, source_target_pairs={{0,16},{1,9},{2,18},{3,11},{4,20},{5,13},{6,22},{7,15},{8,24},{9,1... | collective-permute-start | bytes 589832 | tf_op jit(solution)/shard_map/weights_second/ppermute | solution.py:483
  12.8 11.8 %copy-start = (bf16[512,2048]{1,0:T(8,128)(2,1)S(1)}, bf16[512,2048]{1,0:T(8,128)(2,1)}, u32[]{:S(2)}) copy-start(bf16[512,2048]{1,0:T(8,128)(2,1)} %wi.3) | copy-start | bytes 6291460
  12.9 1.2 collective-permute-start.2
  14.9 2.8 %collective-permute-start.7 = (bf16[256,512]{1,0:T(8,128)(2,1)S(1)}, bf16[256,512]{1,0:T(8,128)(2,1)S(1)}, u32[]{:S(2)}, u32[]{:S(2)}) collective-permute-start(bf16[256,512]{1,0:T(8,128)(2,1)S(1)} %collective-permute-done.5.x2), channel_id=1, source_target_pairs={{0,1},{1,0},{2,3},{3,2},{4,5},{5,4},{6,7},{7,6},{8,9},{9,8},{10,11... | collective-permute-start | bytes 786440 | tf_op jit(solution)/shard_map/row_cross/ppermute | solution.py:483
  14.9 8.6 %collective-permute-start.8 = (bf16[2,3,64,256]{3,2,1,0:T(8,128)(2,1)S(1)}, bf16[2,3,64,256]{3,2,1,0:T(8,128)(2,1)S(1)}, u32[]{:S(2)}, u32[]{:S(2)}) collective-permute-start(bf16[2,3,64,256]{3,2,1,0:T(8,128)(2,1)S(1)} %pad_maximum_fusion.8.rest_0_), channel_id=1, source_target_pairs={{0,8},{1,5},{2,10},{3,7},{4,12},{5,1},{6,14},{7,3},{8,0},{9,13},{1... | collective-permute-start | bytes 589832 | tf_op jit(solution)/shard_map/weights_third/ppermute | solution.py:483
  17.2 6.3 %collective-permute-start.9 = (bf16[2,3,64,256]{3,2,1,0:T(8,128)(2,1)S(1)}, bf16[2,3,64,256]{3,2,1,0:T(8,128)(2,1)S(1)}, u32[]{:S(2)}, u32[]{:S(2)}) collective-permute-start(bf16[2,3,64,256]{3,2,1,0:T(8,128)(2,1)S(1)} %collective-permute-done.6.rest_1_), channel_id=1, source_target_pairs={{0,8},{1,5},{2,10},{3,7},{4,12},{5,1},{6,14},{7,3},{8,0},{9,13},{1... | collective-permute-start | bytes 589832 | tf_op jit(solution)/shard_map/weights_third/ppermute | solution.py:483
  23.5 3.9 %collective-permute-start.10 = (bf16[2,3,64,256]{3,2,1,0:T(8,128)(2,1)S(1)}, bf16[2,3,64,256]{3,2,1,0:T(8,128)(2,1)S(1)}, u32[]{:S(2)}, u32[]{:S(2)}) collective-permute-start(bf16[2,3,64,256]{3,2,1,0:T(8,128)(2,1)S(1)} %pad_maximum_fusion.8.rest_0_), channel_id=1, source_target_pairs={{0,1},{1,0},{2,3},{3,2},{4,5},{5,4},{6,7},{7,6},{8,9},{9,8},{10,11... | collective-permute-start | bytes 589832 | tf_op jit(solution)/shard_map/weights_core/ppermute | solution.py:483
  23.6 3.8 %collective-permute-start.11 = (bf16[2,3,64,256]{3,2,1,0:T(8,128)(2,1)S(1)}, bf16[2,3,64,256]{3,2,1,0:T(8,128)(2,1)S(1)}, u32[]{:S(2)}, u32[]{:S(2)}) collective-permute-start(bf16[2,3,64,256]{3,2,1,0:T(8,128)(2,1)S(1)} %collective-permute-done.6.rest_1_), channel_id=1, source_target_pairs={{0,1},{1,0},{2,3},{3,2},{4,5},{5,4},{6,7},{7,6},{8,9},{9,8},{10,11... | collective-permute-start | bytes 589832 | tf_op jit(solution)/shard_map/weights_core/ppermute | solution.py:483
  24.1 3.3 %collective-permute-start.13 = (bf16[2,3,64,256]{3,2,1,0:T(8,128)(2,1)S(1)}, bf16[2,3,64,256]{3,2,1,0:T(8,128)(2,1)S(1)}, u32[]{:S(2)}, u32[]{:S(2)}) collective-permute-start(bf16[2,3,64,256]{3,2,1,0:T(8,128)(2,1)S(1)} %collective-permute-done.9.rest_3_), channel_id=1, source_target_pairs={{0,1},{1,0},{2,3},{3,2},{4,5},{5,4},{6,7},{7,6},{8,9},{9,8},{10,11... | collective-permute-start | bytes 589832 | tf_op jit(solution)/shard_map/weights_core/ppermute | solution.py:483
  24.2 3.3 %collective-permute-start.12 = (bf16[2,3,64,256]{3,2,1,0:T(8,128)(2,1)S(1)}, bf16[2,3,64,256]{3,2,1,0:T(8,128)(2,1)S(1)}, u32[]{:S(2)}, u32[]{:S(2)}) collective-permute-start(bf16[2,3,64,256]{3,2,1,0:T(8,128)(2,1)S(1)} %collective-permute-done.8.rest_2_), channel_id=1, source_target_pairs={{0,1},{1,0},{2,3},{3,2},{4,5},{5,4},{6,7},{7,6},{8,9},{9,8},{10,11... | collective-permute-start | bytes 589832 | tf_op jit(solution)/shard_map/weights_core/ppermute | solution.py:483
  32.4 4.7 %collective-permute-start.14 = (bf16[768,512]{1,0:T(8,128)(2,1)S(1)}, bf16[768,512]{1,0:T(8,128)(2,1)S(1)}, u32[]{:S(2)}, u32[]{:S(2)}) collective-permute-start(bf16[768,512]{1,0:T(8,128)(2,1)S(1)} %get-tuple-element.330), channel_id=1, source_target_pairs={{0,1},{1,0},{2,3},{3,2},{4,5},{5,4},{6,7},{7,6},{8,9},{9,8},{10,11... | collective-permute-start | bytes 2359304 | tf_op jit(solution)/shard_map/joining_sum_core/over_bit/ppermute | solution.py:483
  33.9 3.3 %collective-permute-start.15 = (bf16[1024,512]{1,0:T(8,128)(2,1)S(1)}, bf16[1024,512]{1,0:T(8,128)(2,1)S(1)}, u32[]{:S(2)}, u32[]{:S(2)}) collective-permute-start(bf16[1024,512]{1,0:T(8,128)(2,1)S(1)} %get-tuple-element.334), channel_id=1, source_target_pairs={{0,1},{1,0},{2,3},{3,2},{4,5},{5,4},{6,7},{7,6},{8,9},{9,8},{10,11... | collective-permute-start | bytes 3145736 | tf_op jit(solution)/shard_map/outer_sum_core/over_bit/ppermute | solution.py:483
  36.9 3.1 %collective-permute-start.16 = (bf16[1280,512]{1,0:T(8,128)(2,1)S(1)}, bf16[1280,512]{1,0:T(8,128)(2,1)S(1)}, u32[]{:S(2)}, u32[]{:S(2)}) collective-permute-start(bf16[1280,512]{1,0:T(8,128)(2,1)S(1)} %get-tuple-element.338), channel_id=1, source_target_pairs={{0,1},{1,0},{2,3},{3,2},{4,5},{5,4},{6,7},{7,6},{8,9},{9,8},{10,11... | collective-permute-start | bytes 3932168 | tf_op jit(solution)/shard_map/inner_sum_core/over_bit/ppermute | solution.py:483
  37.3 9.3 %collective-permute-start.17 = (bf16[384,512]{1,0:T(8,128)(2,1)S(1)}, bf16[384,512]{1,0:T(8,128)(2,1)S(1)}, u32[]{:S(2)}, u32[]{:S(2)}) collective-permute-start(bf16[384,512]{1,0:T(8,128)(2,1)S(1)} %get-tuple-element.351), channel_id=1, source_target_pairs={{0,2},{1,5},{2,0},{3,7},{4,6},{5,1},{6,4},{7,3},{8,10},{9,13},{10,... | collective-permute-start | bytes 1179656 | tf_op jit(solution)/shard_map/joining_sum_step_0/over_stage/ppermute | solution.py:483
  38.8 13.8 %collective-permute-start.18 = (bf16[512,512]{1,0:T(8,128)(2,1)S(1)}, bf16[512,512]{1,0:T(8,128)(2,1)S(1)}, u32[]{:S(2)}, u32[]{:S(2)}) collective-permute-start(bf16[512,512]{1,0:T(8,128)(2,1)S(1)} %get-tuple-element.354), channel_id=1, source_target_pairs={{0,8},{1,17},{2,10},{3,19},{4,12},{5,21},{6,14},{7,23},{8,0},{9,25... | collective-permute-start | bytes 1572872 | tf_op jit(solution)/shard_map/outer_sum_step_0/over_stage/ppermute | solution.py:483
  40.2 12.4 %collective-permute-start.19 = (bf16[640,512]{1,0:T(8,128)(2,1)S(1)}, bf16[640,512]{1,0:T(8,128)(2,1)S(1)}, u32[]{:S(2)}, u32[]{:S(2)}) collective-permute-start(bf16[640,512]{1,0:T(8,128)(2,1)S(1)} %get-tuple-element.357), channel_id=1, source_target_pairs={{0,2},{1,5},{2,0},{3,7},{4,6},{5,1},{6,4},{7,3},{8,10},{9,13},{10,... | collective-permute-start | bytes 1966088 | tf_op jit(solution)/shard_map/inner_sum_step_0/over_stage/ppermute | solution.py:483
  46.1 6.7 %collective-permute-start.20 = (bf16[784,512]{1,0:T(8,128)(2,1)S(1)}, bf16[784,512]{1,0:T(8,128)(2,1)S(1)}, u32[]{:S(2)}, u32[]{:S(2)}) collective-permute-start(bf16[784,512]{1,0:T(8,128)(2,1)S(1)} %get-tuple-element.361), channel_id=1, source_target_pairs={{0,1},{1,0},{2,3},{3,2},{4,5},{5,4},{6,7},{7,6},{8,9},{9,8},{10,11... | collective-permute-start | bytes 2408456 | tf_op jit(solution)/shard_map/attend_sum_core/over_bit/ppermute | solution.py:483
  52.8 7.6 %collective-permute-start.21 = (bf16[320,512]{1,0:T(8,128)(2,1)S(1)}, bf16[320,512]{1,0:T(8,128)(2,1)S(1)}, u32[]{:S(2)}, u32[]{:S(2)}) collective-permute-start(bf16[320,512]{1,0:T(8,128)(2,1)S(1)} %get-tuple-element.371), channel_id=1, source_target_pairs={{0,4},{1,3},{2,6},{3,1},{4,0},{5,7},{6,2},{7,5},{8,12},{9,11},{10,... | collective-permute-start | bytes 983048 | tf_op jit(solution)/shard_map/inner_sum_step_1/over_stage/ppermute | solution.py:483
  53.9 9.2 %collective-permute-start.22 = (bf16[256,512]{1,0:T(8,128)(2,1)S(1)}, bf16[256,512]{1,0:T(8,128)(2,1)S(1)}, u32[]{:S(2)}, u32[]{:S(2)}) collective-permute-start(bf16[256,512]{1,0:T(8,128)(2,1)S(1)} %get-tuple-element.375), channel_id=1, source_target_pairs={{0,16},{1,9},{2,18},{3,11},{4,20},{5,13},{6,22},{7,15},{8,24},{9,1... | collective-permute-start | bytes 786440 | tf_op jit(solution)/shard_map/outer_sum_step_1/over_stage/ppermute | solution.py:483
  58.3 12.7 %collective-permute-start.25 = (bf16[192,512]{1,0:T(8,128)(2,1)S(1)}, bf16[192,512]{1,0:T(8,128)(2,1)S(1)}, u32[]{:S(2)}, u32[]{:S(2)}) collective-permute-start(bf16[192,512]{1,0:T(8,128)(2,1)S(1)} %get-tuple-element.386), channel_id=1, source_target_pairs={{0,4},{1,3},{2,6},{3,1},{4,0},{5,7},{6,2},{7,5},{8,12},{9,11},{10,... | collective-permute-start | bytes 589832 | tf_op jit(solution)/shard_map/joining_sum_step_1/over_stage/ppermute | solution.py:483
  59.2 8.0 %collective-permute-start.23 = (bf16[400,512]{1,0:T(8,128)(2,1)S(1)}, bf16[400,512]{1,0:T(8,128)(2,1)S(1)}, u32[]{:S(2)}, u32[]{:S(2)}) collective-permute-start(bf16[400,512]{1,0:T(8,128)(2,1)S(1)} %slice_add_fusion.4), channel_id=1, source_target_pairs={{0,2},{1,5},{2,0},{3,7},{4,6},{5,1},{6,4},{7,3},{8,10},{9,13},{10,... | collective-permute-start | bytes 1228808 | tf_op jit(solution)/shard_map/attend_sum_step_0/over_stage/ppermute | solution.py:483
  63.1 8.0 %collective-permute-start.27 = (bf16[128,512]{1,0:T(8,128)(2,1)S(1)}, bf16[128,512]{1,0:T(8,128)(2,1)S(1)}, u32[]{:S(2)}, u32[]{:S(2)}) collective-permute-start(bf16[128,512]{1,0:T(8,128)(2,1)S(1)} %get-tuple-element.394), channel_id=1, source_target_pairs={{0,2},{1,5},{2,0},{3,7},{4,6},{5,1},{6,4},{7,3},{8,10},{9,13},{10,... | collective-permute-start | bytes 393224 | tf_op jit(solution)/shard_map/outer_sum_step_2/over_stage/ppermute | solution.py:483
  65.7 5.3 %collective-permute-start.24 = (bf16[160,512]{1,0:T(8,128)(2,1)S(1)}, bf16[160,512]{1,0:T(8,128)(2,1)S(1)}, u32[]{:S(2)}, u32[]{:S(2)}) collective-permute-start(bf16[160,512]{1,0:T(8,128)(2,1)S(1)} %get-tuple-element.382), channel_id=1, source_target_pairs={{0,8},{1,9},{2,10},{3,11},{4,12},{5,13},{6,14},{7,15},{8,0},{9,1},... | collective-permute-start | bytes 491528 | tf_op jit(solution)/shard_map/inner_sum_step_2/over_stage/ppermute | solution.py:483
  65.7 5.3 %collective-permute-start.26 = (bf16[512,512]{1,0:T(8,128)(2,1)S(1)}, bf16[512,512]{1,0:T(8,128)(2,1)S(1)}, u32[]{:S(2)}, u32[]{:S(2)}) collective-permute-start(bf16[512,512]{1,0:T(8,128)(2,1)S(1)} %get-tuple-element.391), channel_id=1, source_target_pairs={{0,1},{1,0},{2,3},{3,2},{4,5},{5,4},{6,7},{7,6},{8,9},{9,8},{10,11... | collective-permute-start | bytes 1572872 | tf_op jit(solution)/shard_map/over_bit/ppermute | solution.py:483
  67.2 5.9 %collective-permute-start.28 = (bf16[208,512]{1,0:T(8,128)(2,1)S(1)}, bf16[208,512]{1,0:T(8,128)(2,1)S(1)}, u32[]{:S(2)}, u32[]{:S(2)}) collective-permute-start(bf16[208,512]{1,0:T(8,128)(2,1)S(1)} %fusion), channel_id=1, source_target_pairs={{0,4},{1,3},{2,6},{3,1},{4,0},{5,7},{6,2},{7,5},{8,12},{9,11},{10,... | collective-permute-start | bytes 638984 | tf_op jit(solution)/shard_map/attend_sum_step_1/over_stage/ppermute | solution.py:483
  73.2 6.2 %collective-permute-start.29 = (bf16[80,512]{1,0:T(8,128)(2,1)S(1)}, bf16[80,512]{1,0:T(8,128)(2,1)S(1)}, u32[]{:S(2)}, u32[]{:S(2)}) collective-permute-start(bf16[80,512]{1,0:T(8,128)(2,1)S(1)} %slice_add_fusion.24), channel_id=1, source_target_pairs={{0,16},{1,17},{2,18},{3,19},{4,20},{5,21},{6,22},{7,23},{8,24},{9,... | collective-permute-start | bytes 245768 | tf_op jit(solution)/shard_map/inner_sum_step_3/over_stage/ppermute | solution.py:483
  75.3 4.3 %collective-permute-start.30 = (bf16[64,512]{1,0:T(8,128)(2,1)S(1)}, bf16[64,512]{1,0:T(8,128)(2,1)S(1)}, u32[]{:S(2)}, u32[]{:S(2)}) collective-permute-start(bf16[64,512]{1,0:T(8,128)(2,1)S(1)} %slice_add_fusion.26), channel_id=1, source_target_pairs={{0,4},{1,3},{2,6},{3,1},{4,0},{5,7},{6,2},{7,5},{8,12},{9,11},{10,... | collective-permute-start | bytes 196616 | tf_op jit(solution)/shard_map/outer_sum_step_3/over_stage/ppermute | solution.py:483
  76.3 5.8 %collective-permute-start.31 = (bf16[96,512]{1,0:T(8,128)(2,1)S(1)}, bf16[96,512]{1,0:T(8,128)(2,1)S(1)}, u32[]{:S(2)}, u32[]{:S(2)}) collective-permute-start(bf16[96,512]{1,0:T(8,128)(2,1)S(1)} %get-tuple-element.409), channel_id=1, source_target_pairs={{0,8},{1,9},{2,10},{3,11},{4,12},{5,13},{6,14},{7,15},{8,0},{9,1},... | collective-permute-start | bytes 294920 | tf_op jit(solution)/shard_map/joining_sum_step_2/over_stage/ppermute | solution.py:483
  76.6 11.0 %collective-permute-start.34 = (bf16[112,512]{1,0:T(8,128)(2,1)S(1)}, bf16[112,512]{1,0:T(8,128)(2,1)S(1)}, u32[]{:S(2)}, u32[]{:S(2)}) collective-permute-start(bf16[112,512]{1,0:T(8,128)(2,1)S(1)} %fusion.1), channel_id=1, source_target_pairs={{0,8},{1,9},{2,10},{3,11},{4,12},{5,13},{6,14},{7,15},{8,0},{9,1},... | collective-permute-start | bytes 344072 | tf_op jit(solution)/shard_map/attend_sum_step_2/over_stage/ppermute | solution.py:483
  78.4 18.3 %collective-permute-start.40 = (bf16[256,512]{1,0:T(8,128)(2,1)S(1)}, bf16[256,512]{1,0:T(8,128)(2,1)S(1)}, u32[]{:S(2)}, u32[]{:S(2)}) collective-permute-start(bf16[256,512]{1,0:T(8,128)(2,1)S(1)} %slice_add_fusion.12), channel_id=1, source_target_pairs={{0,2},{1,3},{2,0},{3,1},{4,6},{5,7},{6,4},{7,5},{8,10},{9,11},{10,... | collective-permute-start | bytes 786440 | tf_op jit(solution)/shard_map/over_bit/ppermute | solution.py:483
  79.6 6.7 %collective-permute-start.32 = (bf16[80,512]{1,0:T(8,128)(2,1)S(1)}, bf16[80,512]{1,0:T(8,128)(2,1)S(1)}, u32[]{:S(2)}, u32[]{:S(2)}) collective-permute-start(bf16[80,512]{1,0:T(8,128)(2,1)S(1)} %fusion.5), channel_id=1, source_target_pairs={{0,16},{1,17},{2,18},{3,19},{4,20},{5,21},{6,22},{7,23},{8,24},{9,... | collective-permute-start | bytes 245768 | tf_op jit(solution)/shard_map/inner_sum_step_4/over_stage/ppermute | solution.py:483
  82.1 5.6 %collective-permute-start.35 = (bf16[48,512]{1,0:T(8,128)(2,1)S(1)}, bf16[48,512]{1,0:T(8,128)(2,1)S(1)}, u32[]{:S(2)}, u32[]{:S(2)}) collective-permute-start(bf16[48,512]{1,0:T(8,128)(2,1)S(1)} %slice_add_fusion.29), channel_id=1, source_target_pairs={{0,16},{1,17},{2,18},{3,19},{4,20},{5,21},{6,22},{7,23},{8,24},{9,... | collective-permute-start | bytes 147464 | tf_op jit(solution)/shard_map/joining_sum_step_3/over_stage/ppermute | solution.py:483
  83.2 4.3 %collective-permute-start.33 = (bf16[64,512]{1,0:T(8,128)(2,1)S(1)}, bf16[64,512]{1,0:T(8,128)(2,1)S(1)}, u32[]{:S(2)}, u32[]{:S(2)}) collective-permute-start(bf16[64,512]{1,0:T(8,128)(2,1)S(1)} %fusion.7), channel_id=1, source_target_pairs={{0,4},{1,3},{2,6},{3,1},{4,0},{5,7},{6,2},{7,5},{8,12},{9,11},{10,... | collective-permute-start | bytes 196616 | tf_op jit(solution)/shard_map/outer_sum_step_4/over_stage/ppermute | solution.py:483
  86.4 8.6 %collective-permute-start.37 = (bf16[160,512]{1,0:T(8,128)(2,1)S(1)}, bf16[160,512]{1,0:T(8,128)(2,1)S(1)}, u32[]{:S(2)}, u32[]{:S(2)}) collective-permute-start(bf16[160,512]{1,0:T(8,128)(2,1)S(1)} %pad_maximum_fusion.11), channel_id=1, source_target_pairs={{0,8},{1,9},{2,10},{3,11},{4,12},{5,13},{6,14},{7,15},{8,0},{9,1},... | collective-permute-start | bytes 491528 | tf_op jit(solution)/shard_map/inner_sum_step_5/over_stage/ppermute | solution.py:483
  87.8 5.2 %collective-permute-start.36 = (bf16[48,512]{1,0:T(8,128)(2,1)S(1)}, bf16[48,512]{1,0:T(8,128)(2,1)S(1)}, u32[]{:S(2)}, u32[]{:S(2)}) collective-permute-start(bf16[48,512]{1,0:T(8,128)(2,1)S(1)} %fusion.8), channel_id=1, source_target_pairs={{0,16},{1,17},{2,18},{3,19},{4,20},{5,21},{6,22},{7,23},{8,24},{9,... | collective-permute-start | bytes 147464 | tf_op jit(solution)/shard_map/joining_sum_step_4/over_stage/ppermute | solution.py:483
  89.6 7.0 %collective-permute-start.39 = (bf16[64,512]{1,0:T(8,128)(2,1)S(1)}, bf16[64,512]{1,0:T(8,128)(2,1)S(1)}, u32[]{:S(2)}, u32[]{:S(2)}) collective-permute-start(bf16[64,512]{1,0:T(8,128)(2,1)S(1)} %fusion.6), channel_id=1, source_target_pairs={{0,16},{1,17},{2,18},{3,19},{4,20},{5,21},{6,22},{7,23},{8,24},{9,... | collective-permute-start | bytes 196616 | tf_op jit(solution)/shard_map/attend_sum_step_3/over_stage/ppermute | solution.py:483
  90.8 5.8 %collective-permute-start.38 = (bf16[128,512]{1,0:T(8,128)(2,1)S(1)}, bf16[128,512]{1,0:T(8,128)(2,1)S(1)}, u32[]{:S(2)}, u32[]{:S(2)}) collective-permute-start(bf16[128,512]{1,0:T(8,128)(2,1)S(1)} %pad_maximum_fusion.12), channel_id=1, source_target_pairs={{0,2},{1,5},{2,0},{3,7},{4,6},{5,1},{6,4},{7,3},{8,10},{9,13},{10,... | collective-permute-start | bytes 393224 | tf_op jit(solution)/shard_map/outer_sum_step_5/over_stage/ppermute | solution.py:483
  92.9 8.6 %collective-permute-start.41 = (bf16[96,512]{1,0:T(8,128)(2,1)S(1)}, bf16[96,512]{1,0:T(8,128)(2,1)S(1)}, u32[]{:S(2)}, u32[]{:S(2)}) collective-permute-start(bf16[96,512]{1,0:T(8,128)(2,1)S(1)} %pad_maximum_fusion.14), channel_id=1, source_target_pairs={{0,8},{1,9},{2,10},{3,11},{4,12},{5,13},{6,14},{7,15},{8,0},{9,1},... | collective-permute-start | bytes 294920 | tf_op jit(solution)/shard_map/joining_sum_step_5/over_stage/ppermute | solution.py:483
  97.5 7.3 %collective-permute-start.43 = (bf16[320,512]{1,0:T(8,128)(2,1)S(1)}, bf16[320,512]{1,0:T(8,128)(2,1)S(1)}, u32[]{:S(2)}, u32[]{:S(2)}) collective-permute-start(bf16[320,512]{1,0:T(8,128)(2,1)S(1)} %pad_maximum_fusion.5), channel_id=1, source_target_pairs={{0,4},{1,3},{2,6},{3,1},{4,0},{5,7},{6,2},{7,5},{8,12},{9,11},{10,... | collective-permute-start | bytes 983048 | tf_op jit(solution)/shard_map/inner_sum_step_6/over_stage/ppermute | solution.py:483
  99.1 5.5 %collective-permute-start.42 = (bf16[48,512]{1,0:T(8,128)(2,1)S(1)}, bf16[48,512]{1,0:T(8,128)(2,1)S(1)}, u32[]{:S(2)}, u32[]{:S(2)}) collective-permute-start(bf16[48,512]{1,0:T(8,128)(2,1)S(1)} %slice.313), channel_id=1, source_target_pairs={{0,16},{1,17},{2,18},{3,19},{4,20},{5,21},{6,22},{7,23},{8,24},{9,... | collective-permute-start | bytes 147464 | tf_op jit(solution)/shard_map/attend_sum_step_4/over_stage/ppermute | solution.py:483
  101.6 7.8 %collective-permute-start.44 = (bf16[192,512]{1,0:T(8,128)(2,1)S(1)}, bf16[192,512]{1,0:T(8,128)(2,1)S(1)}, u32[]{:S(2)}, u32[]{:S(2)}) collective-permute-start(bf16[192,512]{1,0:T(8,128)(2,1)S(1)} %pad_maximum_fusion.9), channel_id=1, source_target_pairs={{0,4},{1,3},{2,6},{3,1},{4,0},{5,7},{6,2},{7,5},{8,12},{9,11},{10,... | collective-permute-start | bytes 589832 | tf_op jit(solution)/shard_map/joining_sum_step_6/over_stage/ppermute | solution.py:483
  101.6 9.7 %collective-permute-start.45 = (bf16[256,512]{1,0:T(8,128)(2,1)S(1)}, bf16[256,512]{1,0:T(8,128)(2,1)S(1)}, u32[]{:S(2)}, u32[]{:S(2)}) collective-permute-start(bf16[256,512]{1,0:T(8,128)(2,1)S(1)} %pad_maximum_fusion.6), channel_id=1, source_target_pairs={{0,16},{1,9},{2,18},{3,11},{4,20},{5,13},{6,22},{7,15},{8,24},{9,1... | collective-permute-start | bytes 786440 | tf_op jit(solution)/shard_map/outer_sum_step_6/over_stage/ppermute | solution.py:483
  111.4 10.7 %collective-permute-start.47 = (bf16[640,512]{1,0:T(8,128)(2,1)S(1)}, bf16[640,512]{1,0:T(8,128)(2,1)S(1)}, u32[]{:S(2)}, u32[]{:S(2)}) collective-permute-start(bf16[640,512]{1,0:T(8,128)(2,1)S(1)} %pad_maximum_fusion.rest_0_), channel_id=1, source_target_pairs={{0,2},{1,5},{2,0},{3,7},{4,6},{5,1},{6,4},{7,3},{8,10},{9,13},{10,... | collective-permute-start | bytes 1966088 | tf_op jit(solution)/shard_map/inner_sum_step_7/over_stage/ppermute | solution.py:483
  112.9 9.1 %collective-permute-start.48 = (bf16[640,512]{1,0:T(8,128)(2,1)S(1)}, bf16[640,512]{1,0:T(8,128)(2,1)S(1)}, u32[]{:S(2)}, u32[]{:S(2)}) collective-permute-start(bf16[640,512]{1,0:T(8,128)(2,1)S(1)} %pad_maximum_fusion.rest_0_), channel_id=1, source_target_pairs={{0,1},{1,0},{2,3},{3,2},{4,5},{5,4},{6,7},{7,6},{8,9},{9,8},{10,11... | collective-permute-start | bytes 1966088 | tf_op jit(solution)/shard_map/inner_sum_sibling/over_bit/ppermute | solution.py:483
  112.9 5.9 %collective-permute-start.46 = (bf16[96,512]{1,0:T(8,128)(2,1)S(1)}, bf16[96,512]{1,0:T(8,128)(2,1)S(1)}, u32[]{:S(2)}, u32[]{:S(2)}) collective-permute-start(bf16[96,512]{1,0:T(8,128)(2,1)S(1)} %pad_maximum_fusion.15), channel_id=1, source_target_pairs={{0,8},{1,9},{2,10},{3,11},{4,12},{5,13},{6,14},{7,15},{8,0},{9,1},... | collective-permute-start | bytes 294920 | tf_op jit(solution)/shard_map/attend_sum_step_5/over_stage/ppermute | solution.py:483
  113.6 13.6 %collective-permute-start.49 = (bf16[384,512]{1,0:T(8,128)(2,1)S(1)}, bf16[384,512]{1,0:T(8,128)(2,1)S(1)}, u32[]{:S(2)}, u32[]{:S(2)}) collective-permute-start(bf16[384,512]{1,0:T(8,128)(2,1)S(1)} %pad_maximum_fusion.3.rest_0_), channel_id=1, source_target_pairs={{0,2},{1,5},{2,0},{3,7},{4,6},{5,1},{6,4},{7,3},{8,10},{9,13},{10,... | collective-permute-start | bytes 1179656 | tf_op jit(solution)/shard_map/joining_sum_step_7/over_stage/ppermute | solution.py:483
  114.3 15.1 %collective-permute-start.52 = (bf16[512,512]{1,0:T(8,128)(2,1)S(1)}, bf16[512,512]{1,0:T(8,128)(2,1)S(1)}, u32[]{:S(2)}, u32[]{:S(2)}) collective-permute-start(bf16[512,512]{1,0:T(8,128)(2,1)S(1)} %pad_maximum_fusion.2.rest_0_), channel_id=1, source_target_pairs={{0,8},{1,17},{2,10},{3,19},{4,12},{5,21},{6,14},{7,23},{8,0},{9,25... | collective-permute-start | bytes 1572872 | tf_op jit(solution)/shard_map/outer_sum_step_7/over_stage/ppermute | solution.py:483
  118.8 10.6 %collective-permute-start.53 = (bf16[512,512]{1,0:T(8,128)(2,1)S(1)}, bf16[512,512]{1,0:T(8,128)(2,1)S(1)}, u32[]{:S(2)}, u32[]{:S(2)}) collective-permute-start(bf16[512,512]{1,0:T(8,128)(2,1)S(1)} %pad_maximum_fusion.2.rest_0_), channel_id=1, source_target_pairs={{0,1},{1,0},{2,3},{3,2},{4,5},{5,4},{6,7},{7,6},{8,9},{9,8},{10,11... | collective-permute-start | bytes 1572872 | tf_op jit(solution)/shard_map/outer_sum_sibling/over_bit/ppermute | solution.py:483
  122.0 5.2 %collective-permute-start.50 = (bf16[384,512]{1,0:T(8,128)(2,1)S(1)}, bf16[384,512]{1,0:T(8,128)(2,1)S(1)}, u32[]{:S(2)}, u32[]{:S(2)}) collective-permute-start(bf16[384,512]{1,0:T(8,128)(2,1)S(1)} %pad_maximum_fusion.3.rest_0_), channel_id=1, source_target_pairs={{0,1},{1,0},{2,3},{3,2},{4,5},{5,4},{6,7},{7,6},{8,9},{9,8},{10,11... | collective-permute-start | bytes 1179656 | tf_op jit(solution)/shard_map/joining_sum_sibling/over_bit/ppermute | solution.py:483
  122.1 5.7 %collective-permute-start.51 = (bf16[192,512]{1,0:T(8,128)(2,1)S(1)}, bf16[192,512]{1,0:T(8,128)(2,1)S(1)}, u32[]{:S(2)}, u32[]{:S(2)}) collective-permute-start(bf16[192,512]{1,0:T(8,128)(2,1)S(1)} %pad_maximum_fusion.10), channel_id=1, source_target_pairs={{0,4},{1,3},{2,6},{3,1},{4,0},{5,7},{6,2},{7,5},{8,12},{9,11},{10,... | collective-permute-start | bytes 589832 | tf_op jit(solution)/shard_map/attend_sum_step_6/over_stage/ppermute | solution.py:483
  127.2 3.2 %collective-permute-start.54 = (bf16[640,512]{1,0:T(8,128)(2,1)S(1)}, bf16[640,512]{1,0:T(8,128)(2,1)S(1)}, u32[]{:S(2)}, u32[]{:S(2)}) collective-permute-start(bf16[640,512]{1,0:T(8,128)(2,1)S(1)} %collective-permute-done.47.rest_1_), channel_id=1, source_target_pairs={{0,1},{1,0},{2,3},{3,2},{4,5},{5,4},{6,7},{7,6},{8,9},{9,8},{10,11... | collective-permute-start | bytes 1966088 | tf_op jit(solution)/shard_map/inner_sum_upper/over_bit/ppermute | solution.py:483
  129.4 3.7 %collective-permute-start.55 = (bf16[512,512]{1,0:T(8,128)(2,1)S(1)}, bf16[512,512]{1,0:T(8,128)(2,1)S(1)}, u32[]{:S(2)}, u32[]{:S(2)}) collective-permute-start(bf16[512,512]{1,0:T(8,128)(2,1)S(1)} %collective-permute-done.52.rest_1_), channel_id=1, source_target_pairs={{0,1},{1,0},{2,3},{3,2},{4,5},{5,4},{6,7},{7,6},{8,9},{9,8},{10,11... | collective-permute-start | bytes 1572872 | tf_op jit(solution)/shard_map/outer_sum_upper/over_bit/ppermute | solution.py:483
  129.4 6.0 %collective-permute-start.56 = (bf16[384,512]{1,0:T(8,128)(2,1)S(1)}, bf16[384,512]{1,0:T(8,128)(2,1)S(1)}, u32[]{:S(2)}, u32[]{:S(2)}) collective-permute-start(bf16[384,512]{1,0:T(8,128)(2,1)S(1)} %collective-permute-done.49.rest_1_), channel_id=1, source_target_pairs={{0,1},{1,0},{2,3},{3,2},{4,5},{5,4},{6,7},{7,6},{8,9},{9,8},{10,11... | collective-permute-start | bytes 1179656 | tf_op jit(solution)/shard_map/joining_sum_upper/over_bit/ppermute | solution.py:483
  129.9 7.8 %collective-permute-start.57 = (bf16[384,512]{1,0:T(8,128)(2,1)S(1)}, bf16[384,512]{1,0:T(8,128)(2,1)S(1)}, u32[]{:S(2)}, u32[]{:S(2)}) collective-permute-start(bf16[384,512]{1,0:T(8,128)(2,1)S(1)} %pad_maximum_fusion.4.rest_0_), channel_id=1, source_target_pairs={{0,2},{1,5},{2,0},{3,7},{4,6},{5,1},{6,4},{7,3},{8,10},{9,13},{10,... | collective-permute-start | bytes 1179656 | tf_op jit(solution)/shard_map/attend_sum_step_7/over_stage/ppermute | solution.py:483
  130.4 7.2 %collective-permute-start.58 = (bf16[384,512]{1,0:T(8,128)(2,1)S(1)}, bf16[384,512]{1,0:T(8,128)(2,1)S(1)}, u32[]{:S(2)}, u32[]{:S(2)}) collective-permute-start(bf16[384,512]{1,0:T(8,128)(2,1)S(1)} %pad_maximum_fusion.4.rest_0_), channel_id=1, source_target_pairs={{0,1},{1,0},{2,3},{3,2},{4,5},{5,4},{6,7},{7,6},{8,9},{9,8},{10,11... | collective-permute-start | bytes 1179656 | tf_op jit(solution)/shard_map/attend_sum_sibling/over_bit/ppermute | solution.py:483
  137.7 1.7 %collective-permute-start.59 = (bf16[384,512]{1,0:T(8,128)(2,1)S(1)}, bf16[384,512]{1,0:T(8,128)(2,1)S(1)}, u32[]{:S(2)}, u32[]{:S(2)}) collective-permute-start(bf16[384,512]{1,0:T(8,128)(2,1)S(1)} %collective-permute-done.57.rest_1_), channel_id=1, source_target_pairs={{0,1},{1,0},{2,3},{3,2},{4,5},{5,4},{6,7},{7,6},{8,9},{9,8},{10,11... | collective-permute-start | bytes 1179656 | tf_op jit(solution)/shard_map/attend_sum_upper/over_bit/ppermute | solution.py:483
  (12 other events, 79.9 us)

commit v4 on v3

--- a/solution.py
+++ b/solution.py
@@ -22,10 +22,10 @@
 GROUP = 32
 THREE = ((0, 1, False), (1, 1, False), (2, 1, False))
 PLAN = (
-    ("KJ",), ("KU",), ("KI",), ("J", "U",), ("I",), ("KT",), ("J", "U", "I", "T",), ("KG", "I", "U",),
+    ("KJ",), ("KU",), ("KI",), ("J", "U",), ("I",), ("KT",), ("KG", "J", "U", "I", "T",), ("I", "U",),
     ("T",), ("I", "J", "g0", "U", "T",), ("I",), ("U", "J",), ("I",), ("U", "T", "J",), ("J",),
-    ("I", "U", "T", "g1",), ("J",), ("T",), ("I", "J", "U",), ("T", "I",), ("J", "T",), ("U",),
-    ("fI", "fU", "fJ",), ("T",), ("hT",), ("fT",),
+    ("I", "U", "T",), ("g1",), ("J",), ("T",), ("I", "J", "U",), ("I", "T",), ("J", "T",), ("U",),
+    ("fI", "fJ", "fU",), ("T",), ("hT",), ("fT",),
 )
 HALF = GROUP // 2
 

time: 142 us -> 139 us (0.979)
  waiting for transfers between devices: 46.1 us -> 44.2 us
    ppermute x60, waiting for transfers between devices: 46.1 us -> 44.2 us  [swap(): return lax.ppermute(values, AXES, [(d, partner(d)) for d in range(devices)])]
  transfers between devices with their start and end apart: 60 -> 60, of which waited for: 27 -> 26; matrix products, arithmetic and copies ran while one was open for 3% -> 3% of each run, Pallas kernels for 19% -> 19%
where the time goes in v4:
time: 139 us; the launch traced here: 138 us
  starting transfers between devices  53.8 us (39%)
  waiting for transfers between devices  44.2 us (32%)
  Pallas kernels  33.3 us (24%)
  other arithmetic  3.02 us (2%)
  local copies, waits for them, and re-layouts  2.37 us (2%)
  between operations  1.57 us (1%)
    ppermute x60, starting transfers between devices, swap(): return lax.ppermute(values, AXES, [(d, partner(d)) for d in range(devices)])  53.8 us
    ppermute x60, waiting for transfers between devices, swap(): return lax.ppermute(values, AXES, [(d, partner(d)) for d in range(devices)])  44.2 us
    pallas_call x12, Pallas kernels, call(): pl.pallas_call(kernel, out_shape=out_shapes, in_specs=in_specs, out_specs...  33.3 us
  transfers between devices with their start and end apart: 60, of which 26 were waited for; matrix products, arithmetic and copies ran while one was open for 3% of the time, Pallas kernels for 19%

profile of v4, /device:TPU:0, one launch (start us, length us, event | category | flops | bytes accessed | tf_op | source)
XLA Modules:
  0.0 138.3 jit_solution(386149101569552771)
XLA Ops:
  0.7 0.9 fusion.4
  1.6 3.0 %collective-permute-start = (bf16[1,3,64,256]{3,2,1,0:T(8,128)(2,1)S(1)}, bf16[1,3,64,256]{3,2,1,0:T(8,128)(2,1)S(1)}, u32[]{:S(2)}, u32[]{:S(2)}) collective-permute-start(bf16[1,3,64,256]{3,2,1,0:T(8,128)(2,1)S(1)} %fusion.4), channel_id=1, source_target_pairs={{0,4},{1,17},{2,6},{3,19},{4,0},{5,21},{6,2},{7,23},{8,12},{9,25},... | collective-permute-start | bytes 294920 | tf_op jit(solution)/shard_map/weights_first/ppermute | solution.py:483
  4.6 1.7 %collective-permute-start.4 = (s32[2,128]{1,0:T(2,128)}, s32[2,128]{1,0:T(2,128)S(1)}, u32[]{:S(2)}, u32[]{:S(2)}) collective-permute-start(s32[2,128]{1,0:T(2,128)} %bitcast.45), channel_id=1, source_target_pairs={{0,3},{1,2},{2,1},{3,0},{4,7},{5,6},{6,5},{7,4},{8,11},{9,10},{10,... | collective-permute-start | bytes 3080 | tf_op jit(solution)/shard_map/segments/ppermute | solution.py:483
  6.9 1.5 %collective-permute-start.5 = (bf16[256,512]{1,0:T(8,128)(2,1)}, bf16[256,512]{1,0:T(8,128)(2,1)S(1)}, u32[]{:S(2)}, u32[]{:S(2)}) collective-permute-start(bf16[256,512]{1,0:T(8,128)(2,1)} %bitcast.50), channel_id=1, source_target_pairs={{0,2},{1,3},{2,0},{3,1},{4,6},{5,7},{6,4},{7,5},{8,10},{9,11},{10,... | collective-permute-start | bytes 786440 | tf_op jit(solution)/shard_map/row_far/ppermute | solution.py:483
  8.4 2.0 %collective-permute-start.6 = (bf16[2,3,64,256]{3,2,1,0:T(8,128)(2,1)S(1)}, bf16[2,3,64,256]{3,2,1,0:T(8,128)(2,1)S(1)}, u32[]{:S(2)}, u32[]{:S(2)}) collective-permute-start(bf16[2,3,64,256]{3,2,1,0:T(8,128)(2,1)S(1)} %pad_maximum_fusion.8.rest_0_), channel_id=1, source_target_pairs={{0,16},{1,9},{2,18},{3,11},{4,20},{5,13},{6,22},{7,15},{8,24},{9,1... | collective-permute-start | bytes 589832 | tf_op jit(solution)/shard_map/weights_second/ppermute | solution.py:483
  10.4 1.1 constant_dynamic-update-slice_fusion.4
  11.5 1.1 constant_dynamic-update-slice_fusion.3
  13.0 1.1 collective-permute-done.2.seg1
  14.1 0.9 collective-permute-done.5.x2
  14.9 1.6 %collective-permute-start.8 = (bf16[2,3,64,256]{3,2,1,0:T(8,128)(2,1)S(1)}, bf16[2,3,64,256]{3,2,1,0:T(8,128)(2,1)S(1)}, u32[]{:S(2)}, u32[]{:S(2)}) collective-permute-start(bf16[2,3,64,256]{3,2,1,0:T(8,128)(2,1)S(1)} %pad_maximum_fusion.8.rest_0_), channel_id=1, source_target_pairs={{0,8},{1,5},{2,10},{3,7},{4,12},{5,1},{6,14},{7,3},{8,0},{9,13},{1... | collective-permute-start | bytes 589832 | tf_op jit(solution)/shard_map/weights_third/ppermute | solution.py:483
  16.5 0.7 collective-permute-done.6.rest_1_
  17.7 5.8 %attend.1 = (bf16[256,512]{1,0:T(8,128)(2,1)S(1)}, bf16[1024,512]{1,0:T(8,128)(2,1)S(1)}, bf16[1024,512]{1,0:T(8,128)(2,1)S(1)}, bf16[8,512,256]{2,1,0:T(8,128)(...) custom-call(bf16[512,512]{1,0:T(8,128)(2,1)S(1)} %pad_maximum_fusion.1.x01, ...), custom_call_target="tpu_custom_call" | custom-call | flops 60000 | bytes 600 | tf_op jit(solution)/shard_map/attend/pallas_call | solution.py:450
  24.7 2.7 %feed.1 = (bf16[256,2048]{1,0:T(8,128)(2,1)S(1)}, bf16[256,2048]{1,0:T(8,128)(2,1)S(1)}, f32[256,512]{1,0:T(8,128)S(1)}, f32[256,128]{1,0:T(8,128)S(1)}, bf16[25...) custom-call(f32[256,512]{1,0:T(8,128)S(1)} %get-tuple-element.297.n1_ref, f32[1,512]{1,0:T(1,128)S(1)} %bitcast.32, ...), custom_call_target="tpu_custom_call" | custom-call | flops 30000 | bytes 300 | tf_op jit(solution)/shard_map/feed/pallas_call | solution.py:450
  27.5 4.9 %joining.1 = (bf16[256,512]{1,0:T(8,128)(2,1)}, bf16[768,512]{1,0:T(8,128)(2,1)S(1)}, bf16[768,512]{1,0:T(8,128)(2,1)S(1)}, f32[256,512]{1,0:T(8,128)S(1)}, bf16...) custom-call(f32[256,512]{1,0:T(8,128)S(1)} %get-tuple-element.300.n2_ref, f32[1,512]{1,0:T(1,128)S(1)} %bitcast.38, ...), custom_call_target="tpu_custom_call" | custom-call | flops 80000 | bytes 800 | tf_op jit(solution)/shard_map/joining/pallas_call | solution.py:450
  32.5 1.5 %outer_back.1 = (f32[256,512]{1,0:T(8,128)S(1)}, f32[8,512]{1,0:T(8,128)S(1)}, bf16[1024,512]{1,0:T(8,128)(2,1)S(1)}, bf16[1024,512]{1,0:T(8,128)(2,1)S(1)}) custom-call(f32[256,512]{1,0:T(8,128)S(1)} %get-tuple-element.313.dhp_ref, bf16[256,512]{1,0:T(8,128)(2,1)S(1)} %get-tuple-element.314.dt_ref, ...), custom_call_target="tpu_custom_call" | custom-call | flops 40000 | bytes 400 | tf_op jit(solution)/shard_map/outer_back/pallas_call | solution.py:450
  34.4 2.5 %inner_back.1 = (f32[256,512]{1,0:T(8,128)S(1)}, bf16[16,512]{1,0:T(8,128)(2,1)S(1)}, bf16[1280,512]{1,0:T(8,128)(2,1)S(1)}, bf16[1280,512]{1,0:T(8,128)(2,1)S(1)}) custom-call(f32[256,512]{1,0:T(8,128)S(1)} %get-tuple-element.320.d2_ref, bf16[256,2048]{1,0:T(8,128)(2,1)S(1)} %get-tuple-element.321.sz_ref, bf16[512,2048]{1,0:T(8,128)(2,1)S(1)} %copy-done, ...), custom_call_target="tpu_custom_call" | custom-call | flops 60000 | bytes 600 | tf_op jit(solution)/shard_map/inner_back/pallas_call | solution.py:450
  37.3 1.5 %collective-permute-start.17 = (bf16[384,512]{1,0:T(8,128)(2,1)S(1)}, bf16[384,512]{1,0:T(8,128)(2,1)S(1)}, u32[]{:S(2)}, u32[]{:S(2)}) collective-permute-start(bf16[384,512]{1,0:T(8,128)(2,1)S(1)} %get-tuple-element.357), channel_id=1, source_target_pairs={{0,2},{1,5},{2,0},{3,7},{4,6},{5,1},{6,4},{7,3},{8,10},{9,13},{10,... | collective-permute-start | bytes 1179656 | tf_op jit(solution)/shard_map/joining_sum_step_0/over_stage/ppermute | solution.py:483
  38.8 0.9 collective-permute-start.18
  40.2 1.5 %collective-permute-start.19 = (bf16[640,512]{1,0:T(8,128)(2,1)S(1)}, bf16[640,512]{1,0:T(8,128)(2,1)S(1)}, u32[]{:S(2)}, u32[]{:S(2)}) collective-permute-start(bf16[640,512]{1,0:T(8,128)(2,1)S(1)} %get-tuple-element.363), channel_id=1, source_target_pairs={{0,2},{1,5},{2,0},{3,7},{4,6},{5,1},{6,4},{7,3},{8,10},{9,13},{10,... | collective-permute-start | bytes 1966088 | tf_op jit(solution)/shard_map/inner_sum_step_0/over_stage/ppermute | solution.py:483
  41.6 4.4 %attend_back.1 = (bf16[784,512]{1,0:T(8,128)(2,1)S(1)}, bf16[784,512]{1,0:T(8,128)(2,1)S(1)}, bf16[256,512]{1,0:T(8,128)(2,1)S(1)}, bf16[1024,512]{1,0:T(8,128)(2,1)S(1)}, bf16[1024,512]{1,0:T(8,128)(2,1)S(1)}) custom-call(f32[256,512]{1,0:T(8,128)S(1)} %get-tuple-element.350.d1_ref, bf16[512,2560]{1,0:T(8,128)(2,1)S(1)} %constant_dynamic-update-slice_fusion.bank, ...), custom_call_target="tpu_custom_call" | custom-call | flops 80000 | bytes 800 | tf_op jit(solution)/shard_map/attend_back/pallas_call | solution.py:450
  46.6 1.4 %input_back.1 = (f32[256,512]{1,0:T(8,128)S(1)}, bf16[256,512]{1,0:T(8,128)(2,1)S(1)}, bf16[512,512]{1,0:T(8,128)(2,1)S(1)}) custom-call(f32[256,512]{1,0:T(8,128)S(1)} %get-tuple-element.350.d1_ref, bf16[256,512]{1,0:T(8,128)(2,1)S(1)} %get-tuple-element.351.dq_ref, bf16[1024,512]{1,0:T(8,128)(2,1)S(1)} %get-tuple-element.352.dk_ref, ...), custom_call_target="tpu_custom_call" | custom-call | flops 20000 | bytes 200 | tf_op jit(solution)/shard_map/input_back/pallas_call | solution.py:450
  48.1 4.5 %collective-permute-done.18 = bf16[512,512]{1,0:T(8,128)(2,1)S(1)} collective-permute-done((bf16[512,512]{1,0:T(8,128)(2,1)S(1)}, bf16[512,512]{1,0:T(8,128)(2,1)S(1)}, u32[]{:S(2)}, u32[]{:S(2)}) %collective-permute-start.18) | collective-permute-done | bytes 524320 | tf_op jit(solution)/shard_map/outer_sum_step_0/over_stage/ppermute | solution.py:483
  52.8 1.1 collective-permute-start.21
  53.9 2.9 %collective-permute-start.22 = (bf16[256,512]{1,0:T(8,128)(2,1)S(1)}, bf16[256,512]{1,0:T(8,128)(2,1)S(1)}, u32[]{:S(2)}, u32[]{:S(2)}) collective-permute-start(bf16[256,512]{1,0:T(8,128)(2,1)S(1)} %get-tuple-element.375), channel_id=1, source_target_pairs={{0,16},{1,9},{2,18},{3,11},{4,20},{5,13},{6,22},{7,15},{8,24},{9,1... | collective-permute-start | bytes 786440 | tf_op jit(solution)/shard_map/outer_sum_step_1/over_stage/ppermute | solution.py:483
  56.9 0.9 collective-permute-start.25
  57.8 1.2 collective-permute-start.23
  59.0 2.5 %collective-permute-done.21 = bf16[320,512]{1,0:T(8,128)(2,1)S(1)} collective-permute-done((bf16[320,512]{1,0:T(8,128)(2,1)S(1)}, bf16[320,512]{1,0:T(8,128)(2,1)S(1)}, u32[]{:S(2)}, u32[]{:S(2)}) %collective-permute-start.21) | collective-permute-done | bytes 327712 | tf_op jit(solution)/shard_map/inner_sum_step_1/over_stage/ppermute | solution.py:483
  61.5 1.6 %collective-permute-done.22 = bf16[256,512]{1,0:T(8,128)(2,1)S(1)} collective-permute-done((bf16[256,512]{1,0:T(8,128)(2,1)S(1)}, bf16[256,512]{1,0:T(8,128)(2,1)S(1)}, u32[]{:S(2)}, u32[]{:S(2)}) %collective-permute-start.22) | collective-permute-done | bytes 262176 | tf_op jit(solution)/shard_map/outer_sum_step_1/over_stage/ppermute | solution.py:483
  63.1 2.5 %collective-permute-start.27 = (bf16[128,512]{1,0:T(8,128)(2,1)S(1)}, bf16[128,512]{1,0:T(8,128)(2,1)S(1)}, u32[]{:S(2)}, u32[]{:S(2)}) collective-permute-start(bf16[128,512]{1,0:T(8,128)(2,1)S(1)} %get-tuple-element.394), channel_id=1, source_target_pairs={{0,2},{1,5},{2,0},{3,7},{4,6},{5,1},{6,4},{7,3},{8,10},{9,13},{10,... | collective-permute-start | bytes 393224 | tf_op jit(solution)/shard_map/outer_sum_step_2/over_stage/ppermute | solution.py:483
  65.7 1.0 collective-permute-done.23
  67.4 3.6 %collective-permute-done.24 = bf16[160,512]{1,0:T(8,128)(2,1)S(1)} collective-permute-done((bf16[160,512]{1,0:T(8,128)(2,1)S(1)}, bf16[160,512]{1,0:T(8,128)(2,1)S(1)}, u32[]{:S(2)}, u32[]{:S(2)}) %collective-permute-start.24) | collective-permute-done | bytes 163872 | tf_op jit(solution)/shard_map/inner_sum_step_2/over_stage/ppermute | solution.py:483
  71.1 1.6 %collective-permute-done.28 = bf16[208,512]{1,0:T(8,128)(2,1)S(1)} collective-permute-done((bf16[208,512]{1,0:T(8,128)(2,1)S(1)}, bf16[208,512]{1,0:T(8,128)(2,1)S(1)}, u32[]{:S(2)}, u32[]{:S(2)}) %collective-permute-start.28) | collective-permute-done | bytes 213024 | tf_op jit(solution)/shard_map/attend_sum_step_1/over_stage/ppermute | solution.py:483
  72.8 2.5 %collective-permute-start.29 = (bf16[80,512]{1,0:T(8,128)(2,1)S(1)}, bf16[80,512]{1,0:T(8,128)(2,1)S(1)}, u32[]{:S(2)}, u32[]{:S(2)}) collective-permute-start(bf16[80,512]{1,0:T(8,128)(2,1)S(1)} %slice_add_fusion.24), channel_id=1, source_target_pairs={{0,16},{1,17},{2,18},{3,19},{4,20},{5,21},{6,22},{7,23},{8,24},{9,... | collective-permute-start | bytes 245768 | tf_op jit(solution)/shard_map/inner_sum_step_3/over_stage/ppermute | solution.py:483
  75.3 1.0 collective-permute-start.30
  76.8 1.5 %collective-permute-start.34 = (bf16[112,512]{1,0:T(8,128)(2,1)S(1)}, bf16[112,512]{1,0:T(8,128)(2,1)S(1)}, u32[]{:S(2)}, u32[]{:S(2)}) collective-permute-start(bf16[112,512]{1,0:T(8,128)(2,1)S(1)} %fusion.1), channel_id=1, source_target_pairs={{0,8},{1,9},{2,10},{3,11},{4,12},{5,13},{6,14},{7,15},{8,0},{9,1},... | collective-permute-start | bytes 344072 | tf_op jit(solution)/shard_map/attend_sum_step_2/over_stage/ppermute | solution.py:483
  78.3 1.1 collective-permute-start.40
  79.6 2.0 %collective-permute-start.32 = (bf16[80,512]{1,0:T(8,128)(2,1)S(1)}, bf16[80,512]{1,0:T(8,128)(2,1)S(1)}, u32[]{:S(2)}, u32[]{:S(2)}) collective-permute-start(bf16[80,512]{1,0:T(8,128)(2,1)S(1)} %fusion.5), channel_id=1, source_target_pairs={{0,16},{1,17},{2,18},{3,19},{4,20},{5,21},{6,22},{7,23},{8,24},{9,... | collective-permute-start | bytes 245768 | tf_op jit(solution)/shard_map/inner_sum_step_4/over_stage/ppermute | solution.py:483
  81.6 0.9 collective-permute-done.31
  82.7 1.1 collective-permute-start.33
  83.8 2.5 %collective-permute-done.32 = bf16[80,512]{1,0:T(8,128)(2,1)S(1)} collective-permute-done((bf16[80,512]{1,0:T(8,128)(2,1)S(1)}, bf16[80,512]{1,0:T(8,128)(2,1)S(1)}, u32[]{:S(2)}, u32[]{:S(2)}) %collective-permute-start.32) | collective-permute-done | bytes 81952 | tf_op jit(solution)/shard_map/inner_sum_step_4/over_stage/ppermute | solution.py:483
  87.0 0.8 collective-permute-done.35
  87.8 2.2 %collective-permute-start.36 = (bf16[48,512]{1,0:T(8,128)(2,1)S(1)}, bf16[48,512]{1,0:T(8,128)(2,1)S(1)}, u32[]{:S(2)}, u32[]{:S(2)}) collective-permute-start(bf16[48,512]{1,0:T(8,128)(2,1)S(1)} %fusion.8), channel_id=1, source_target_pairs={{0,16},{1,17},{2,18},{3,19},{4,20},{5,21},{6,22},{7,23},{8,24},{9,... | collective-permute-start | bytes 147464 | tf_op jit(solution)/shard_map/joining_sum_step_4/over_stage/ppermute | solution.py:483
  90.1 0.7 collective-permute-start.39
  90.8 1.0 collective-permute-start.38
  91.8 1.2 collective-permute-done.36
  93.0 1.0 collective-permute-start.41
  94.1 1.7 %collective-permute-done.38 = bf16[128,512]{1,0:T(8,128)(2,1)S(1)} collective-permute-done((bf16[128,512]{1,0:T(8,128)(2,1)S(1)}, bf16[128,512]{1,0:T(8,128)(2,1)S(1)}, u32[]{:S(2)}, u32[]{:S(2)}) %collective-permute-start.38) | collective-permute-done | bytes 131104 | tf_op jit(solution)/shard_map/outer_sum_step_5/over_stage/ppermute | solution.py:483
  96.3 1.8 %collective-permute-start.42 = (bf16[48,512]{1,0:T(8,128)(2,1)S(1)}, bf16[48,512]{1,0:T(8,128)(2,1)S(1)}, u32[]{:S(2)}, u32[]{:S(2)}) collective-permute-start(bf16[48,512]{1,0:T(8,128)(2,1)S(1)} %slice.313), channel_id=1, source_target_pairs={{0,16},{1,17},{2,18},{3,19},{4,20},{5,21},{6,22},{7,23},{8,24},{9,... | collective-permute-start | bytes 147464 | tf_op jit(solution)/shard_map/attend_sum_step_4/over_stage/ppermute | solution.py:483
  98.1 1.1 collective-permute-start.45
  99.3 1.6 %collective-permute-start.43 = (bf16[320,512]{1,0:T(8,128)(2,1)S(1)}, bf16[320,512]{1,0:T(8,128)(2,1)S(1)}, u32[]{:S(2)}, u32[]{:S(2)}) collective-permute-start(bf16[320,512]{1,0:T(8,128)(2,1)S(1)} %pad_maximum_fusion.5), channel_id=1, source_target_pairs={{0,4},{1,3},{2,6},{3,1},{4,0},{5,7},{6,2},{7,5},{8,12},{9,11},{10,... | collective-permute-start | bytes 983048 | tf_op jit(solution)/shard_map/inner_sum_step_6/over_stage/ppermute | solution.py:483
  100.8 0.8 add_convert_fusion
  102.2 4.1 %collective-permute-done.43 = bf16[320,512]{1,0:T(8,128)(2,1)S(1)} collective-permute-done((bf16[320,512]{1,0:T(8,128)(2,1)S(1)}, bf16[320,512]{1,0:T(8,128)(2,1)S(1)}, u32[]{:S(2)}, u32[]{:S(2)}) %collective-permute-start.43) | collective-permute-done | bytes 327712 | tf_op jit(solution)/shard_map/inner_sum_step_6/over_stage/ppermute | solution.py:483
  106.4 2.1 %collective-permute-done.44 = bf16[192,512]{1,0:T(8,128)(2,1)S(1)} collective-permute-done((bf16[192,512]{1,0:T(8,128)(2,1)S(1)}, bf16[192,512]{1,0:T(8,128)(2,1)S(1)}, u32[]{:S(2)}, u32[]{:S(2)}) %collective-permute-start.44) | collective-permute-done | bytes 196640 | tf_op jit(solution)/shard_map/joining_sum_step_6/over_stage/ppermute | solution.py:483
  109.3 1.1 collective-permute-start.48
  111.0 1.7 %collective-permute-start.52 = (bf16[512,512]{1,0:T(8,128)(2,1)S(1)}, bf16[512,512]{1,0:T(8,128)(2,1)S(1)}, u32[]{:S(2)}, u32[]{:S(2)}) collective-permute-start(bf16[512,512]{1,0:T(8,128)(2,1)S(1)} %pad_maximum_fusion.2.rest_0_), channel_id=1, source_target_pairs={{0,8},{1,17},{2,10},{3,19},{4,12},{5,21},{6,14},{7,23},{8,0},{9,25... | collective-permute-start | bytes 1572872 | tf_op jit(solution)/shard_map/outer_sum_step_7/over_stage/ppermute | solution.py:483
  112.7 6.5 %collective-permute-done.46.rest_1_ = bf16[640,512]{1,0:T(8,128)(2,1)S(1)} collective-permute-done((bf16[640,512]{1,0:T(8,128)(2,1)S(1)}, bf16[640,512]{1,0:T(8,128)(2,1)S(1)}, u32[]{:S(2)}, u32[]{:S(2)}) %collective-permute-start.46) | collective-permute-done | bytes 655392 | tf_op jit(solution)/shard_map/inner_sum_step_7/over_stage/ppermute | solution.py:483
  119.3 1.6 %collective-permute-start.51 = (bf16[192,512]{1,0:T(8,128)(2,1)S(1)}, bf16[192,512]{1,0:T(8,128)(2,1)S(1)}, u32[]{:S(2)}, u32[]{:S(2)}) collective-permute-start(bf16[192,512]{1,0:T(8,128)(2,1)S(1)} %pad_maximum_fusion.10), channel_id=1, source_target_pairs={{0,4},{1,3},{2,6},{3,1},{4,0},{5,7},{6,2},{7,5},{8,12},{9,11},{10,... | collective-permute-start | bytes 589832 | tf_op jit(solution)/shard_map/attend_sum_step_6/over_stage/ppermute | solution.py:483
  120.9 3.5 %collective-permute-done.49.rest_1_ = bf16[384,512]{1,0:T(8,128)(2,1)S(1)} collective-permute-done((bf16[384,512]{1,0:T(8,128)(2,1)S(1)}, bf16[384,512]{1,0:T(8,128)(2,1)S(1)}, u32[]{:S(2)}, u32[]{:S(2)}) %collective-permute-start.49) | collective-permute-done | bytes 393248 | tf_op jit(solution)/shard_map/joining_sum_step_7/over_stage/ppermute | solution.py:483
  125.1 1.1 collective-permute-done.52.rest_1_
  127.4 2.7 %finish_inner.1 = (f32[512,2048]{1,0:T(8,128)}, f32[512,512]{1,0:T(8,128)}) custom-call(bf16[640,512]{1,0:T(8,128)(2,1)S(1)} %pad_maximum_fusion.rest_0_, bf16[640,512]{1,0:T(8,128)(2,1)S(1)} %collective-permute-done.46.rest_1_, bf16[640,512]{1,0:T(8,128)(2,1)S(1)} %collective-permute-done.47.rest_2_, bf16[640,512]{1,0:T(8,128)(2,1)S(1)} %collective-permute-done.54.rest_3_), custom_call_target="tpu_custom_call" | custom-call | flops 20000 | bytes 200 | tf_op jit(solution)/shard_map/finish_inner/pallas_call | solution.py:450
  130.0 1.9 %finish_joining.1 = (f32[512,512]{1,0:T(8,128)}, f32[512,512]{1,0:T(8,128)}, f32[512,512]{1,0:T(8,128)}) custom-call(bf16[384,512]{1,0:T(8,128)(2,1)S(1)} %pad_maximum_fusion.3.rest_0_, bf16[384,512]{1,0:T(8,128)(2,1)S(1)} %collective-permute-done.49.rest_1_, bf16[384,512]{1,0:T(8,128)(2,1)S(1)} %collective-permute-done.50.rest_2_, ...), custom_call_target="tpu_custom_call" | custom-call | flops 20000 | bytes 200 | tf_op jit(solution)/shard_map/finish_joining/pallas_call | solution.py:450
  131.9 2.3 %finish_outer.1 = f32[2048,512]{1,0:T(8,128)} custom-call(bf16[512,512]{1,0:T(8,128)(2,1)S(1)} %pad_maximum_fusion.2.rest_0_, bf16[512,512]{1,0:T(8,128)(2,1)S(1)} %collective-permute-done.52.rest_1_, bf16[512,512]{1,0:T(8,128)(2,1)S(1)} %collective-permute-done.53.rest_2_, bf16[512,512]{1,0:T(8,128)(2,1)S(1)} %collective-permute-done.56.rest_3_), custom_call_target="tpu_custom_call" | custom-call | flops 20000 | bytes 200 | tf_op jit(solution)/shard_map/finish_outer/pallas_call | solution.py:450
  134.7 1.3 finish_half.1
  136.2 2.0 %finish_attend.1 = (f32[512,512]{1,0:T(8,128)}, f32[512,512]{1,0:T(8,128)}, f32[512,512]{1,0:T(8,128)}, f32[1,512]{1,0:T(1,128)}, f32[1,512]{1,0:T(1,128)}, /*in...) custom-call(bf16[384,512]{1,0:T(8,128)(2,1)S(1)} %collective-permute, ...), custom_call_target="tpu_custom_call", output_to_operand_aliasing={{0}: (3, {}), {1}: (4, {}), {2}: (5, {})} | custom-call | flops 20000 | bytes 200 | tf_op jit(solution)/shard_map/finish_attend/pallas_call | solution.py:450
  (150 shorter events, 12.2 us)
Async XLA Ops:
  0.7 12.0 %copy-start.12 = (bf16[512,512]{1,0:T(8,128)(2,1)S(1)}, bf16[512,512]{1,0:T(8,128)(2,1)}, u32[]{:S(2)}) copy-start(bf16[512,512]{1,0:T(8,128)(2,1)} %param.26) | copy-start | bytes 1572868
  0.7 12.0 %copy-start.13 = (bf16[512,512]{1,0:T(8,128)(2,1)S(1)}, bf16[512,512]{1,0:T(8,128)(2,1)}, u32[]{:S(2)}) copy-start(bf16[512,512]{1,0:T(8,128)(2,1)} %param.27) | copy-start | bytes 1572868
  0.7 12.1 %copy-start.14 = (bf16[512,512]{1,0:T(8,128)(2,1)S(1)}, bf16[512,512]{1,0:T(8,128)(2,1)}, u32[]{:S(2)}) copy-start(bf16[512,512]{1,0:T(8,128)(2,1)} %param.35) | copy-start | bytes 1572868
  1.6 6.8 %collective-permute-start = (bf16[1,3,64,256]{3,2,1,0:T(8,128)(2,1)S(1)}, bf16[1,3,64,256]{3,2,1,0:T(8,128)(2,1)S(1)}, u32[]{:S(2)}, u32[]{:S(2)}) collective-permute-start(bf16[1,3,64,256]{3,2,1,0:T(8,128)(2,1)S(1)} %fusion.4), channel_id=1, source_target_pairs={{0,4},{1,17},{2,6},{3,19},{4,0},{5,21},{6,2},{7,23},{8,12},{9,25},... | collective-permute-start | bytes 294920 | tf_op jit(solution)/shard_map/weights_first/ppermute | solution.py:483
  4.6 8.4 %collective-permute-start.4 = (s32[2,128]{1,0:T(2,128)}, s32[2,128]{1,0:T(2,128)S(1)}, u32[]{:S(2)}, u32[]{:S(2)}) collective-permute-start(s32[2,128]{1,0:T(2,128)} %bitcast.45), channel_id=1, source_target_pairs={{0,3},{1,2},{2,1},{3,0},{4,7},{5,6},{6,5},{7,4},{8,11},{9,10},{10,... | collective-permute-start | bytes 3080 | tf_op jit(solution)/shard_map/segments/ppermute | solution.py:483
  6.3 6.7 %collective-permute-start.3 = (s32[2,128]{1,0:T(2,128)}, s32[2,128]{1,0:T(2,128)S(1)}, u32[]{:S(2)}, u32[]{:S(2)}) collective-permute-start(s32[2,128]{1,0:T(2,128)} %bitcast.46), channel_id=1, source_target_pairs={{0,2},{1,3},{2,0},{3,1},{4,6},{5,7},{6,4},{7,5},{8,10},{9,11},{10,... | collective-permute-start | bytes 3080 | tf_op jit(solution)/shard_map/segments/ppermute | solution.py:483
  6.9 8.1 %collective-permute-start.5 = (bf16[256,512]{1,0:T(8,128)(2,1)}, bf16[256,512]{1,0:T(8,128)(2,1)S(1)}, u32[]{:S(2)}, u32[]{:S(2)}) collective-permute-start(bf16[256,512]{1,0:T(8,128)(2,1)} %bitcast.50), channel_id=1, source_target_pairs={{0,2},{1,3},{2,0},{3,1},{4,6},{5,7},{6,4},{7,5},{8,10},{9,11},{10,... | collective-permute-start | bytes 786440 | tf_op jit(solution)/shard_map/row_far/ppermute | solution.py:483
  8.4 4.5 %collective-permute-start.1 = (bf16[256,512]{1,0:T(8,128)(2,1)}, bf16[256,512]{1,0:T(8,128)(2,1)S(1)}, u32[]{:S(2)}, u32[]{:S(2)}) collective-permute-start(bf16[256,512]{1,0:T(8,128)(2,1)} %bitcast.51), channel_id=1, source_target_pairs={{0,1},{1,0},{2,3},{3,2},{4,5},{5,4},{6,7},{7,6},{8,9},{9,8},{10,11... | collective-permute-start | bytes 786440 | tf_op jit(solution)/shard_map/row_near/ppermute | solution.py:483
  8.4 8.8 %collective-permute-start.6 = (bf16[2,3,64,256]{3,2,1,0:T(8,128)(2,1)S(1)}, bf16[2,3,64,256]{3,2,1,0:T(8,128)(2,1)S(1)}, u32[]{:S(2)}, u32[]{:S(2)}) collective-permute-start(bf16[2,3,64,256]{3,2,1,0:T(8,128)(2,1)S(1)} %pad_maximum_fusion.8.rest_0_), channel_id=1, source_target_pairs={{0,16},{1,9},{2,18},{3,11},{4,20},{5,13},{6,22},{7,15},{8,24},{9,1... | collective-permute-start | bytes 589832 | tf_op jit(solution)/shard_map/weights_second/ppermute | solution.py:483
  12.8 11.8 %copy-start = (bf16[512,2048]{1,0:T(8,128)(2,1)S(1)}, bf16[512,2048]{1,0:T(8,128)(2,1)}, u32[]{:S(2)}) copy-start(bf16[512,2048]{1,0:T(8,128)(2,1)} %wi.3) | copy-start | bytes 6291460
  12.9 1.2 collective-permute-start.2
  14.9 2.8 %collective-permute-start.7 = (bf16[256,512]{1,0:T(8,128)(2,1)S(1)}, bf16[256,512]{1,0:T(8,128)(2,1)S(1)}, u32[]{:S(2)}, u32[]{:S(2)}) collective-permute-start(bf16[256,512]{1,0:T(8,128)(2,1)S(1)} %collective-permute-done.5.x2), channel_id=1, source_target_pairs={{0,1},{1,0},{2,3},{3,2},{4,5},{5,4},{6,7},{7,6},{8,9},{9,8},{10,11... | collective-permute-start | bytes 786440 | tf_op jit(solution)/shard_map/row_cross/ppermute | solution.py:483
  14.9 8.6 %collective-permute-start.8 = (bf16[2,3,64,256]{3,2,1,0:T(8,128)(2,1)S(1)}, bf16[2,3,64,256]{3,2,1,0:T(8,128)(2,1)S(1)}, u32[]{:S(2)}, u32[]{:S(2)}) collective-permute-start(bf16[2,3,64,256]{3,2,1,0:T(8,128)(2,1)S(1)} %pad_maximum_fusion.8.rest_0_), channel_id=1, source_target_pairs={{0,8},{1,5},{2,10},{3,7},{4,12},{5,1},{6,14},{7,3},{8,0},{9,13},{1... | collective-permute-start | bytes 589832 | tf_op jit(solution)/shard_map/weights_third/ppermute | solution.py:483
  17.2 6.3 %collective-permute-start.9 = (bf16[2,3,64,256]{3,2,1,0:T(8,128)(2,1)S(1)}, bf16[2,3,64,256]{3,2,1,0:T(8,128)(2,1)S(1)}, u32[]{:S(2)}, u32[]{:S(2)}) collective-permute-start(bf16[2,3,64,256]{3,2,1,0:T(8,128)(2,1)S(1)} %collective-permute-done.6.rest_1_), channel_id=1, source_target_pairs={{0,8},{1,5},{2,10},{3,7},{4,12},{5,1},{6,14},{7,3},{8,0},{9,13},{1... | collective-permute-start | bytes 589832 | tf_op jit(solution)/shard_map/weights_third/ppermute | solution.py:483
  23.5 3.9 %collective-permute-start.10 = (bf16[2,3,64,256]{3,2,1,0:T(8,128)(2,1)S(1)}, bf16[2,3,64,256]{3,2,1,0:T(8,128)(2,1)S(1)}, u32[]{:S(2)}, u32[]{:S(2)}) collective-permute-start(bf16[2,3,64,256]{3,2,1,0:T(8,128)(2,1)S(1)} %pad_maximum_fusion.8.rest_0_), channel_id=1, source_target_pairs={{0,1},{1,0},{2,3},{3,2},{4,5},{5,4},{6,7},{7,6},{8,9},{9,8},{10,11... | collective-permute-start | bytes 589832 | tf_op jit(solution)/shard_map/weights_core/ppermute | solution.py:483
  23.6 3.8 %collective-permute-start.11 = (bf16[2,3,64,256]{3,2,1,0:T(8,128)(2,1)S(1)}, bf16[2,3,64,256]{3,2,1,0:T(8,128)(2,1)S(1)}, u32[]{:S(2)}, u32[]{:S(2)}) collective-permute-start(bf16[2,3,64,256]{3,2,1,0:T(8,128)(2,1)S(1)} %collective-permute-done.6.rest_1_), channel_id=1, source_target_pairs={{0,1},{1,0},{2,3},{3,2},{4,5},{5,4},{6,7},{7,6},{8,9},{9,8},{10,11... | collective-permute-start | bytes 589832 | tf_op jit(solution)/shard_map/weights_core/ppermute | solution.py:483
  24.1 3.3 %collective-permute-start.13 = (bf16[2,3,64,256]{3,2,1,0:T(8,128)(2,1)S(1)}, bf16[2,3,64,256]{3,2,1,0:T(8,128)(2,1)S(1)}, u32[]{:S(2)}, u32[]{:S(2)}) collective-permute-start(bf16[2,3,64,256]{3,2,1,0:T(8,128)(2,1)S(1)} %collective-permute-done.9.rest_3_), channel_id=1, source_target_pairs={{0,1},{1,0},{2,3},{3,2},{4,5},{5,4},{6,7},{7,6},{8,9},{9,8},{10,11... | collective-permute-start | bytes 589832 | tf_op jit(solution)/shard_map/weights_core/ppermute | solution.py:483
  24.2 3.3 %collective-permute-start.12 = (bf16[2,3,64,256]{3,2,1,0:T(8,128)(2,1)S(1)}, bf16[2,3,64,256]{3,2,1,0:T(8,128)(2,1)S(1)}, u32[]{:S(2)}, u32[]{:S(2)}) collective-permute-start(bf16[2,3,64,256]{3,2,1,0:T(8,128)(2,1)S(1)} %collective-permute-done.8.rest_2_), channel_id=1, source_target_pairs={{0,1},{1,0},{2,3},{3,2},{4,5},{5,4},{6,7},{7,6},{8,9},{9,8},{10,11... | collective-permute-start | bytes 589832 | tf_op jit(solution)/shard_map/weights_core/ppermute | solution.py:483
  32.4 4.7 %collective-permute-start.14 = (bf16[768,512]{1,0:T(8,128)(2,1)S(1)}, bf16[768,512]{1,0:T(8,128)(2,1)S(1)}, u32[]{:S(2)}, u32[]{:S(2)}) collective-permute-start(bf16[768,512]{1,0:T(8,128)(2,1)S(1)} %get-tuple-element.330), channel_id=1, source_target_pairs={{0,1},{1,0},{2,3},{3,2},{4,5},{5,4},{6,7},{7,6},{8,9},{9,8},{10,11... | collective-permute-start | bytes 2359304 | tf_op jit(solution)/shard_map/joining_sum_core/over_bit/ppermute | solution.py:483
  33.9 3.3 %collective-permute-start.15 = (bf16[1024,512]{1,0:T(8,128)(2,1)S(1)}, bf16[1024,512]{1,0:T(8,128)(2,1)S(1)}, u32[]{:S(2)}, u32[]{:S(2)}) collective-permute-start(bf16[1024,512]{1,0:T(8,128)(2,1)S(1)} %get-tuple-element.334), channel_id=1, source_target_pairs={{0,1},{1,0},{2,3},{3,2},{4,5},{5,4},{6,7},{7,6},{8,9},{9,8},{10,11... | collective-permute-start | bytes 3145736 | tf_op jit(solution)/shard_map/outer_sum_core/over_bit/ppermute | solution.py:483
  36.9 3.1 %collective-permute-start.16 = (bf16[1280,512]{1,0:T(8,128)(2,1)S(1)}, bf16[1280,512]{1,0:T(8,128)(2,1)S(1)}, u32[]{:S(2)}, u32[]{:S(2)}) collective-permute-start(bf16[1280,512]{1,0:T(8,128)(2,1)S(1)} %get-tuple-element.338), channel_id=1, source_target_pairs={{0,1},{1,0},{2,3},{3,2},{4,5},{5,4},{6,7},{7,6},{8,9},{9,8},{10,11... | collective-permute-start | bytes 3932168 | tf_op jit(solution)/shard_map/inner_sum_core/over_bit/ppermute | solution.py:483
  37.3 10.7 %collective-permute-start.17 = (bf16[384,512]{1,0:T(8,128)(2,1)S(1)}, bf16[384,512]{1,0:T(8,128)(2,1)S(1)}, u32[]{:S(2)}, u32[]{:S(2)}) collective-permute-start(bf16[384,512]{1,0:T(8,128)(2,1)S(1)} %get-tuple-element.357), channel_id=1, source_target_pairs={{0,2},{1,5},{2,0},{3,7},{4,6},{5,1},{6,4},{7,3},{8,10},{9,13},{10,... | collective-permute-start | bytes 1179656 | tf_op jit(solution)/shard_map/joining_sum_step_0/over_stage/ppermute | solution.py:483
  38.8 13.8 %collective-permute-start.18 = (bf16[512,512]{1,0:T(8,128)(2,1)S(1)}, bf16[512,512]{1,0:T(8,128)(2,1)S(1)}, u32[]{:S(2)}, u32[]{:S(2)}) collective-permute-start(bf16[512,512]{1,0:T(8,128)(2,1)S(1)} %get-tuple-element.360), channel_id=1, source_target_pairs={{0,8},{1,17},{2,10},{3,19},{4,12},{5,21},{6,14},{7,23},{8,0},{9,25... | collective-permute-start | bytes 1572872 | tf_op jit(solution)/shard_map/outer_sum_step_0/over_stage/ppermute | solution.py:483
  40.2 12.4 %collective-permute-start.19 = (bf16[640,512]{1,0:T(8,128)(2,1)S(1)}, bf16[640,512]{1,0:T(8,128)(2,1)S(1)}, u32[]{:S(2)}, u32[]{:S(2)}) collective-permute-start(bf16[640,512]{1,0:T(8,128)(2,1)S(1)} %get-tuple-element.363), channel_id=1, source_target_pairs={{0,2},{1,5},{2,0},{3,7},{4,6},{5,1},{6,4},{7,3},{8,10},{9,13},{10,... | collective-permute-start | bytes 1966088 | tf_op jit(solution)/shard_map/inner_sum_step_0/over_stage/ppermute | solution.py:483
  46.1 6.7 %collective-permute-start.20 = (bf16[784,512]{1,0:T(8,128)(2,1)S(1)}, bf16[784,512]{1,0:T(8,128)(2,1)S(1)}, u32[]{:S(2)}, u32[]{:S(2)}) collective-permute-start(bf16[784,512]{1,0:T(8,128)(2,1)S(1)} %get-tuple-element.367), channel_id=1, source_target_pairs={{0,1},{1,0},{2,3},{3,2},{4,5},{5,4},{6,7},{7,6},{8,9},{9,8},{10,11... | collective-permute-start | bytes 2408456 | tf_op jit(solution)/shard_map/attend_sum_core/over_bit/ppermute | solution.py:483
  52.8 8.7 %collective-permute-start.21 = (bf16[320,512]{1,0:T(8,128)(2,1)S(1)}, bf16[320,512]{1,0:T(8,128)(2,1)S(1)}, u32[]{:S(2)}, u32[]{:S(2)}) collective-permute-start(bf16[320,512]{1,0:T(8,128)(2,1)S(1)} %get-tuple-element.371), channel_id=1, source_target_pairs={{0,4},{1,3},{2,6},{3,1},{4,0},{5,7},{6,2},{7,5},{8,12},{9,11},{10,... | collective-permute-start | bytes 983048 | tf_op jit(solution)/shard_map/inner_sum_step_1/over_stage/ppermute | solution.py:483
  53.9 9.2 %collective-permute-start.22 = (bf16[256,512]{1,0:T(8,128)(2,1)S(1)}, bf16[256,512]{1,0:T(8,128)(2,1)S(1)}, u32[]{:S(2)}, u32[]{:S(2)}) collective-permute-start(bf16[256,512]{1,0:T(8,128)(2,1)S(1)} %get-tuple-element.375), channel_id=1, source_target_pairs={{0,16},{1,9},{2,18},{3,11},{4,20},{5,13},{6,22},{7,15},{8,24},{9,1... | collective-permute-start | bytes 786440 | tf_op jit(solution)/shard_map/outer_sum_step_1/over_stage/ppermute | solution.py:483
  56.9 14.1 %collective-permute-start.25 = (bf16[192,512]{1,0:T(8,128)(2,1)S(1)}, bf16[192,512]{1,0:T(8,128)(2,1)S(1)}, u32[]{:S(2)}, u32[]{:S(2)}) collective-permute-start(bf16[192,512]{1,0:T(8,128)(2,1)S(1)} %get-tuple-element.386), channel_id=1, source_target_pairs={{0,4},{1,3},{2,6},{3,1},{4,0},{5,7},{6,2},{7,5},{8,12},{9,11},{10,... | collective-permute-start | bytes 589832 | tf_op jit(solution)/shard_map/joining_sum_step_1/over_stage/ppermute | solution.py:483
  57.8 9.0 %collective-permute-start.23 = (bf16[400,512]{1,0:T(8,128)(2,1)S(1)}, bf16[400,512]{1,0:T(8,128)(2,1)S(1)}, u32[]{:S(2)}, u32[]{:S(2)}) collective-permute-start(bf16[400,512]{1,0:T(8,128)(2,1)S(1)} %slice_add_fusion.4), channel_id=1, source_target_pairs={{0,2},{1,5},{2,0},{3,7},{4,6},{5,1},{6,4},{7,3},{8,10},{9,13},{10,... | collective-permute-start | bytes 1228808 | tf_op jit(solution)/shard_map/attend_sum_step_0/over_stage/ppermute | solution.py:483
  59.0 12.1 %collective-permute-start.26 = (bf16[512,512]{1,0:T(8,128)(2,1)S(1)}, bf16[512,512]{1,0:T(8,128)(2,1)S(1)}, u32[]{:S(2)}, u32[]{:S(2)}) collective-permute-start(bf16[512,512]{1,0:T(8,128)(2,1)S(1)} %get-tuple-element.391), channel_id=1, source_target_pairs={{0,1},{1,0},{2,3},{3,2},{4,5},{5,4},{6,7},{7,6},{8,9},{9,8},{10,11... | collective-permute-start | bytes 1572872 | tf_op jit(solution)/shard_map/over_bit/ppermute | solution.py:483
  63.1 8.0 %collective-permute-start.27 = (bf16[128,512]{1,0:T(8,128)(2,1)S(1)}, bf16[128,512]{1,0:T(8,128)(2,1)S(1)}, u32[]{:S(2)}, u32[]{:S(2)}) collective-permute-start(bf16[128,512]{1,0:T(8,128)(2,1)S(1)} %get-tuple-element.394), channel_id=1, source_target_pairs={{0,2},{1,5},{2,0},{3,7},{4,6},{5,1},{6,4},{7,3},{8,10},{9,13},{10,... | collective-permute-start | bytes 393224 | tf_op jit(solution)/shard_map/outer_sum_step_2/over_stage/ppermute | solution.py:483
  65.7 5.3 %collective-permute-start.24 = (bf16[160,512]{1,0:T(8,128)(2,1)S(1)}, bf16[160,512]{1,0:T(8,128)(2,1)S(1)}, u32[]{:S(2)}, u32[]{:S(2)}) collective-permute-start(bf16[160,512]{1,0:T(8,128)(2,1)S(1)} %get-tuple-element.382), channel_id=1, source_target_pairs={{0,8},{1,9},{2,10},{3,11},{4,12},{5,13},{6,14},{7,15},{8,0},{9,1},... | collective-permute-start | bytes 491528 | tf_op jit(solution)/shard_map/inner_sum_step_2/over_stage/ppermute | solution.py:483
  66.8 5.9 %collective-permute-start.28 = (bf16[208,512]{1,0:T(8,128)(2,1)S(1)}, bf16[208,512]{1,0:T(8,128)(2,1)S(1)}, u32[]{:S(2)}, u32[]{:S(2)}) collective-permute-start(bf16[208,512]{1,0:T(8,128)(2,1)S(1)} %fusion), channel_id=1, source_target_pairs={{0,4},{1,3},{2,6},{3,1},{4,0},{5,7},{6,2},{7,5},{8,12},{9,11},{10,... | collective-permute-start | bytes 638984 | tf_op jit(solution)/shard_map/attend_sum_step_1/over_stage/ppermute | solution.py:483
  72.8 6.7 %collective-permute-start.29 = (bf16[80,512]{1,0:T(8,128)(2,1)S(1)}, bf16[80,512]{1,0:T(8,128)(2,1)S(1)}, u32[]{:S(2)}, u32[]{:S(2)}) collective-permute-start(bf16[80,512]{1,0:T(8,128)(2,1)S(1)} %slice_add_fusion.24), channel_id=1, source_target_pairs={{0,16},{1,17},{2,18},{3,19},{4,20},{5,21},{6,22},{7,23},{8,24},{9,... | collective-permute-start | bytes 245768 | tf_op jit(solution)/shard_map/inner_sum_step_3/over_stage/ppermute | solution.py:483
  75.3 4.3 %collective-permute-start.30 = (bf16[64,512]{1,0:T(8,128)(2,1)S(1)}, bf16[64,512]{1,0:T(8,128)(2,1)S(1)}, u32[]{:S(2)}, u32[]{:S(2)}) collective-permute-start(bf16[64,512]{1,0:T(8,128)(2,1)S(1)} %slice_add_fusion.26), channel_id=1, source_target_pairs={{0,4},{1,3},{2,6},{3,1},{4,0},{5,7},{6,2},{7,5},{8,12},{9,11},{10,... | collective-permute-start | bytes 196616 | tf_op jit(solution)/shard_map/outer_sum_step_3/over_stage/ppermute | solution.py:483
  76.3 6.2 %collective-permute-start.31 = (bf16[96,512]{1,0:T(8,128)(2,1)S(1)}, bf16[96,512]{1,0:T(8,128)(2,1)S(1)}, u32[]{:S(2)}, u32[]{:S(2)}) collective-permute-start(bf16[96,512]{1,0:T(8,128)(2,1)S(1)} %get-tuple-element.409), channel_id=1, source_target_pairs={{0,8},{1,9},{2,10},{3,11},{4,12},{5,13},{6,14},{7,15},{8,0},{9,1},... | collective-permute-start | bytes 294920 | tf_op jit(solution)/shard_map/joining_sum_step_2/over_stage/ppermute | solution.py:483
  76.8 10.2 %collective-permute-start.34 = (bf16[112,512]{1,0:T(8,128)(2,1)S(1)}, bf16[112,512]{1,0:T(8,128)(2,1)S(1)}, u32[]{:S(2)}, u32[]{:S(2)}) collective-permute-start(bf16[112,512]{1,0:T(8,128)(2,1)S(1)} %fusion.1), channel_id=1, source_target_pairs={{0,8},{1,9},{2,10},{3,11},{4,12},{5,13},{6,14},{7,15},{8,0},{9,1},... | collective-permute-start | bytes 344072 | tf_op jit(solution)/shard_map/attend_sum_step_2/over_stage/ppermute | solution.py:483
  78.3 21.0 %collective-permute-start.40 = (bf16[256,512]{1,0:T(8,128)(2,1)S(1)}, bf16[256,512]{1,0:T(8,128)(2,1)S(1)}, u32[]{:S(2)}, u32[]{:S(2)}) collective-permute-start(bf16[256,512]{1,0:T(8,128)(2,1)S(1)} %slice_add_fusion.12), channel_id=1, source_target_pairs={{0,2},{1,3},{2,0},{3,1},{4,6},{5,7},{6,4},{7,5},{8,10},{9,11},{10,... | collective-permute-start | bytes 786440 | tf_op jit(solution)/shard_map/over_bit/ppermute | solution.py:483
  79.6 6.7 %collective-permute-start.32 = (bf16[80,512]{1,0:T(8,128)(2,1)S(1)}, bf16[80,512]{1,0:T(8,128)(2,1)S(1)}, u32[]{:S(2)}, u32[]{:S(2)}) collective-permute-start(bf16[80,512]{1,0:T(8,128)(2,1)S(1)} %fusion.5), channel_id=1, source_target_pairs={{0,16},{1,17},{2,18},{3,19},{4,20},{5,21},{6,22},{7,23},{8,24},{9,... | collective-permute-start | bytes 245768 | tf_op jit(solution)/shard_map/inner_sum_step_4/over_stage/ppermute | solution.py:483
  82.5 5.3 %collective-permute-start.35 = (bf16[48,512]{1,0:T(8,128)(2,1)S(1)}, bf16[48,512]{1,0:T(8,128)(2,1)S(1)}, u32[]{:S(2)}, u32[]{:S(2)}) collective-permute-start(bf16[48,512]{1,0:T(8,128)(2,1)S(1)} %slice_add_fusion.29), channel_id=1, source_target_pairs={{0,16},{1,17},{2,18},{3,19},{4,20},{5,21},{6,22},{7,23},{8,24},{9,... | collective-permute-start | bytes 147464 | tf_op jit(solution)/shard_map/joining_sum_step_3/over_stage/ppermute | solution.py:483
  82.7 4.3 %collective-permute-start.33 = (bf16[64,512]{1,0:T(8,128)(2,1)S(1)}, bf16[64,512]{1,0:T(8,128)(2,1)S(1)}, u32[]{:S(2)}, u32[]{:S(2)}) collective-permute-start(bf16[64,512]{1,0:T(8,128)(2,1)S(1)} %fusion.7), channel_id=1, source_target_pairs={{0,4},{1,3},{2,6},{3,1},{4,0},{5,7},{6,2},{7,5},{8,12},{9,11},{10,... | collective-permute-start | bytes 196616 | tf_op jit(solution)/shard_map/outer_sum_step_4/over_stage/ppermute | solution.py:483
  86.3 7.7 %collective-permute-start.37 = (bf16[160,512]{1,0:T(8,128)(2,1)S(1)}, bf16[160,512]{1,0:T(8,128)(2,1)S(1)}, u32[]{:S(2)}, u32[]{:S(2)}) collective-permute-start(bf16[160,512]{1,0:T(8,128)(2,1)S(1)} %pad_maximum_fusion.11), channel_id=1, source_target_pairs={{0,8},{1,9},{2,10},{3,11},{4,12},{5,13},{6,14},{7,15},{8,0},{9,1},... | collective-permute-start | bytes 491528 | tf_op jit(solution)/shard_map/inner_sum_step_5/over_stage/ppermute | solution.py:483
  87.8 5.2 %collective-permute-start.36 = (bf16[48,512]{1,0:T(8,128)(2,1)S(1)}, bf16[48,512]{1,0:T(8,128)(2,1)S(1)}, u32[]{:S(2)}, u32[]{:S(2)}) collective-permute-start(bf16[48,512]{1,0:T(8,128)(2,1)S(1)} %fusion.8), channel_id=1, source_target_pairs={{0,16},{1,17},{2,18},{3,19},{4,20},{5,21},{6,22},{7,23},{8,24},{9,... | collective-permute-start | bytes 147464 | tf_op jit(solution)/shard_map/joining_sum_step_4/over_stage/ppermute | solution.py:483
  90.1 6.1 %collective-permute-start.39 = (bf16[64,512]{1,0:T(8,128)(2,1)S(1)}, bf16[64,512]{1,0:T(8,128)(2,1)S(1)}, u32[]{:S(2)}, u32[]{:S(2)}) collective-permute-start(bf16[64,512]{1,0:T(8,128)(2,1)S(1)} %fusion.6), channel_id=1, source_target_pairs={{0,16},{1,17},{2,18},{3,19},{4,20},{5,21},{6,22},{7,23},{8,24},{9,... | collective-permute-start | bytes 196616 | tf_op jit(solution)/shard_map/attend_sum_step_3/over_stage/ppermute | solution.py:483
  90.8 5.0 %collective-permute-start.38 = (bf16[128,512]{1,0:T(8,128)(2,1)S(1)}, bf16[128,512]{1,0:T(8,128)(2,1)S(1)}, u32[]{:S(2)}, u32[]{:S(2)}) collective-permute-start(bf16[128,512]{1,0:T(8,128)(2,1)S(1)} %pad_maximum_fusion.12), channel_id=1, source_target_pairs={{0,2},{1,5},{2,0},{3,7},{4,6},{5,1},{6,4},{7,3},{8,10},{9,13},{10,... | collective-permute-start | bytes 393224 | tf_op jit(solution)/shard_map/outer_sum_step_5/over_stage/ppermute | solution.py:483
  93.0 8.7 %collective-permute-start.41 = (bf16[96,512]{1,0:T(8,128)(2,1)S(1)}, bf16[96,512]{1,0:T(8,128)(2,1)S(1)}, u32[]{:S(2)}, u32[]{:S(2)}) collective-permute-start(bf16[96,512]{1,0:T(8,128)(2,1)S(1)} %pad_maximum_fusion.14), channel_id=1, source_target_pairs={{0,8},{1,9},{2,10},{3,11},{4,12},{5,13},{6,14},{7,15},{8,0},{9,1},... | collective-permute-start | bytes 294920 | tf_op jit(solution)/shard_map/joining_sum_step_5/over_stage/ppermute | solution.py:483
  96.3 5.9 %collective-permute-start.42 = (bf16[48,512]{1,0:T(8,128)(2,1)S(1)}, bf16[48,512]{1,0:T(8,128)(2,1)S(1)}, u32[]{:S(2)}, u32[]{:S(2)}) collective-permute-start(bf16[48,512]{1,0:T(8,128)(2,1)S(1)} %slice.313), channel_id=1, source_target_pairs={{0,16},{1,17},{2,18},{3,19},{4,20},{5,21},{6,22},{7,23},{8,24},{9,... | collective-permute-start | bytes 147464 | tf_op jit(solution)/shard_map/attend_sum_step_4/over_stage/ppermute | solution.py:483
  98.1 10.4 %collective-permute-start.45 = (bf16[256,512]{1,0:T(8,128)(2,1)S(1)}, bf16[256,512]{1,0:T(8,128)(2,1)S(1)}, u32[]{:S(2)}, u32[]{:S(2)}) collective-permute-start(bf16[256,512]{1,0:T(8,128)(2,1)S(1)} %pad_maximum_fusion.6), channel_id=1, source_target_pairs={{0,16},{1,9},{2,18},{3,11},{4,20},{5,13},{6,22},{7,15},{8,24},{9,1... | collective-permute-start | bytes 786440 | tf_op jit(solution)/shard_map/outer_sum_step_6/over_stage/ppermute | solution.py:483
  99.3 7.1 %collective-permute-start.43 = (bf16[320,512]{1,0:T(8,128)(2,1)S(1)}, bf16[320,512]{1,0:T(8,128)(2,1)S(1)}, u32[]{:S(2)}, u32[]{:S(2)}) collective-permute-start(bf16[320,512]{1,0:T(8,128)(2,1)S(1)} %pad_maximum_fusion.5), channel_id=1, source_target_pairs={{0,4},{1,3},{2,6},{3,1},{4,0},{5,7},{6,2},{7,5},{8,12},{9,11},{10,... | collective-permute-start | bytes 983048 | tf_op jit(solution)/shard_map/inner_sum_step_6/over_stage/ppermute | solution.py:483
  101.7 6.8 %collective-permute-start.44 = (bf16[192,512]{1,0:T(8,128)(2,1)S(1)}, bf16[192,512]{1,0:T(8,128)(2,1)S(1)}, u32[]{:S(2)}, u32[]{:S(2)}) collective-permute-start(bf16[192,512]{1,0:T(8,128)(2,1)S(1)} %pad_maximum_fusion.9), channel_id=1, source_target_pairs={{0,4},{1,3},{2,6},{3,1},{4,0},{5,7},{6,2},{7,5},{8,12},{9,11},{10,... | collective-permute-start | bytes 589832 | tf_op jit(solution)/shard_map/joining_sum_step_6/over_stage/ppermute | solution.py:483
  108.5 4.2 %collective-permute-start.47 = (bf16[640,512]{1,0:T(8,128)(2,1)S(1)}, bf16[640,512]{1,0:T(8,128)(2,1)S(1)}, u32[]{:S(2)}, u32[]{:S(2)}) collective-permute-start(bf16[640,512]{1,0:T(8,128)(2,1)S(1)} %pad_maximum_fusion.rest_0_), channel_id=1, source_target_pairs={{0,1},{1,0},{2,3},{3,2},{4,5},{5,4},{6,7},{7,6},{8,9},{9,8},{10,11... | collective-permute-start | bytes 1966088 | tf_op jit(solution)/shard_map/inner_sum_sibling/over_bit/ppermute | solution.py:483
  108.6 10.7 %collective-permute-start.46 = (bf16[640,512]{1,0:T(8,128)(2,1)S(1)}, bf16[640,512]{1,0:T(8,128)(2,1)S(1)}, u32[]{:S(2)}, u32[]{:S(2)}) collective-permute-start(bf16[640,512]{1,0:T(8,128)(2,1)S(1)} %pad_maximum_fusion.rest_0_), channel_id=1, source_target_pairs={{0,2},{1,5},{2,0},{3,7},{4,6},{5,1},{6,4},{7,3},{8,10},{9,13},{10,... | collective-permute-start | bytes 1966088 | tf_op jit(solution)/shard_map/inner_sum_step_7/over_stage/ppermute | solution.py:483
  109.3 10.0 %collective-permute-start.48 = (bf16[96,512]{1,0:T(8,128)(2,1)S(1)}, bf16[96,512]{1,0:T(8,128)(2,1)S(1)}, u32[]{:S(2)}, u32[]{:S(2)}) collective-permute-start(bf16[96,512]{1,0:T(8,128)(2,1)S(1)} %pad_maximum_fusion.15), channel_id=1, source_target_pairs={{0,8},{1,9},{2,10},{3,11},{4,12},{5,13},{6,14},{7,15},{8,0},{9,1},... | collective-permute-start | bytes 294920 | tf_op jit(solution)/shard_map/attend_sum_step_5/over_stage/ppermute | solution.py:483
  110.3 14.1 %collective-permute-start.49 = (bf16[384,512]{1,0:T(8,128)(2,1)S(1)}, bf16[384,512]{1,0:T(8,128)(2,1)S(1)}, u32[]{:S(2)}, u32[]{:S(2)}) collective-permute-start(bf16[384,512]{1,0:T(8,128)(2,1)S(1)} %pad_maximum_fusion.3.rest_0_), channel_id=1, source_target_pairs={{0,2},{1,5},{2,0},{3,7},{4,6},{5,1},{6,4},{7,3},{8,10},{9,13},{10,... | collective-permute-start | bytes 1179656 | tf_op jit(solution)/shard_map/joining_sum_step_7/over_stage/ppermute | solution.py:483
  111.0 15.2 %collective-permute-start.52 = (bf16[512,512]{1,0:T(8,128)(2,1)S(1)}, bf16[512,512]{1,0:T(8,128)(2,1)S(1)}, u32[]{:S(2)}, u32[]{:S(2)}) collective-permute-start(bf16[512,512]{1,0:T(8,128)(2,1)S(1)} %pad_maximum_fusion.2.rest_0_), channel_id=1, source_target_pairs={{0,8},{1,17},{2,10},{3,19},{4,12},{5,21},{6,14},{7,23},{8,0},{9,25... | collective-permute-start | bytes 1572872 | tf_op jit(solution)/shard_map/outer_sum_step_7/over_stage/ppermute | solution.py:483
  112.7 13.4 %collective-permute-start.53 = (bf16[512,512]{1,0:T(8,128)(2,1)S(1)}, bf16[512,512]{1,0:T(8,128)(2,1)S(1)}, u32[]{:S(2)}, u32[]{:S(2)}) collective-permute-start(bf16[512,512]{1,0:T(8,128)(2,1)S(1)} %pad_maximum_fusion.2.rest_0_), channel_id=1, source_target_pairs={{0,1},{1,0},{2,3},{3,2},{4,5},{5,4},{6,7},{7,6},{8,9},{9,8},{10,11... | collective-permute-start | bytes 1572872 | tf_op jit(solution)/shard_map/outer_sum_sibling/over_bit/ppermute | solution.py:483
  119.3 5.2 %collective-permute-start.50 = (bf16[384,512]{1,0:T(8,128)(2,1)S(1)}, bf16[384,512]{1,0:T(8,128)(2,1)S(1)}, u32[]{:S(2)}, u32[]{:S(2)}) collective-permute-start(bf16[384,512]{1,0:T(8,128)(2,1)S(1)} %pad_maximum_fusion.3.rest_0_), channel_id=1, source_target_pairs={{0,1},{1,0},{2,3},{3,2},{4,5},{5,4},{6,7},{7,6},{8,9},{9,8},{10,11... | collective-permute-start | bytes 1179656 | tf_op jit(solution)/shard_map/joining_sum_sibling/over_bit/ppermute | solution.py:483
  119.3 5.8 %collective-permute-start.51 = (bf16[192,512]{1,0:T(8,128)(2,1)S(1)}, bf16[192,512]{1,0:T(8,128)(2,1)S(1)}, u32[]{:S(2)}, u32[]{:S(2)}) collective-permute-start(bf16[192,512]{1,0:T(8,128)(2,1)S(1)} %pad_maximum_fusion.10), channel_id=1, source_target_pairs={{0,4},{1,3},{2,6},{3,1},{4,0},{5,7},{6,2},{7,5},{8,12},{9,11},{10,... | collective-permute-start | bytes 589832 | tf_op jit(solution)/shard_map/attend_sum_step_6/over_stage/ppermute | solution.py:483
  124.4 2.9 %collective-permute-start.54 = (bf16[640,512]{1,0:T(8,128)(2,1)S(1)}, bf16[640,512]{1,0:T(8,128)(2,1)S(1)}, u32[]{:S(2)}, u32[]{:S(2)}) collective-permute-start(bf16[640,512]{1,0:T(8,128)(2,1)S(1)} %collective-permute-done.46.rest_1_), channel_id=1, source_target_pairs={{0,1},{1,0},{2,3},{3,2},{4,5},{5,4},{6,7},{7,6},{8,9},{9,8},{10,11... | collective-permute-start | bytes 1966088 | tf_op jit(solution)/shard_map/inner_sum_upper/over_bit/ppermute | solution.py:483
  126.2 5.8 %collective-permute-start.56 = (bf16[512,512]{1,0:T(8,128)(2,1)S(1)}, bf16[512,512]{1,0:T(8,128)(2,1)S(1)}, u32[]{:S(2)}, u32[]{:S(2)}) collective-permute-start(bf16[512,512]{1,0:T(8,128)(2,1)S(1)} %collective-permute-done.52.rest_1_), channel_id=1, source_target_pairs={{0,1},{1,0},{2,3},{3,2},{4,5},{5,4},{6,7},{7,6},{8,9},{9,8},{10,11... | collective-permute-start | bytes 1572872 | tf_op jit(solution)/shard_map/outer_sum_upper/over_bit/ppermute | solution.py:483
  126.2 3.8 %collective-permute-start.55 = (bf16[384,512]{1,0:T(8,128)(2,1)S(1)}, bf16[384,512]{1,0:T(8,128)(2,1)S(1)}, u32[]{:S(2)}, u32[]{:S(2)}) collective-permute-start(bf16[384,512]{1,0:T(8,128)(2,1)S(1)} %collective-permute-done.49.rest_1_), channel_id=1, source_target_pairs={{0,1},{1,0},{2,3},{3,2},{4,5},{5,4},{6,7},{7,6},{8,9},{9,8},{10,11... | collective-permute-start | bytes 1179656 | tf_op jit(solution)/shard_map/joining_sum_upper/over_bit/ppermute | solution.py:483
  126.7 7.8 %collective-permute-start.57 = (bf16[384,512]{1,0:T(8,128)(2,1)S(1)}, bf16[384,512]{1,0:T(8,128)(2,1)S(1)}, u32[]{:S(2)}, u32[]{:S(2)}) collective-permute-start(bf16[384,512]{1,0:T(8,128)(2,1)S(1)} %pad_maximum_fusion.4.rest_0_), channel_id=1, source_target_pairs={{0,2},{1,5},{2,0},{3,7},{4,6},{5,1},{6,4},{7,3},{8,10},{9,13},{10,... | collective-permute-start | bytes 1179656 | tf_op jit(solution)/shard_map/attend_sum_step_7/over_stage/ppermute | solution.py:483
  127.2 7.3 %collective-permute-start.58 = (bf16[384,512]{1,0:T(8,128)(2,1)S(1)}, bf16[384,512]{1,0:T(8,128)(2,1)S(1)}, u32[]{:S(2)}, u32[]{:S(2)}) collective-permute-start(bf16[384,512]{1,0:T(8,128)(2,1)S(1)} %pad_maximum_fusion.4.rest_0_), channel_id=1, source_target_pairs={{0,1},{1,0},{2,3},{3,2},{4,5},{5,4},{6,7},{7,6},{8,9},{9,8},{10,11... | collective-permute-start | bytes 1179656 | tf_op jit(solution)/shard_map/attend_sum_sibling/over_bit/ppermute | solution.py:483
  134.5 1.7 %collective-permute-start.59 = (bf16[384,512]{1,0:T(8,128)(2,1)S(1)}, bf16[384,512]{1,0:T(8,128)(2,1)S(1)}, u32[]{:S(2)}, u32[]{:S(2)}) collective-permute-start(bf16[384,512]{1,0:T(8,128)(2,1)S(1)} %collective-permute-done.57.rest_1_), channel_id=1, source_target_pairs={{0,1},{1,0},{2,3},{3,2},{4,5},{5,4},{6,7},{7,6},{8,9},{9,8},{10,11... | collective-permute-start | bytes 1179656 | tf_op jit(solution)/shard_map/attend_sum_upper/over_bit/ppermute | solution.py:483
  (12 other events, 79.9 us)

commit v5 on v4

--- a/solution.py
+++ b/solution.py
@@ -23,9 +23,9 @@
 THREE = ((0, 1, False), (1, 1, False), (2, 1, False))
 PLAN = (
     ("KJ",), ("KU",), ("KI",), ("J", "U",), ("I",), ("KT",), ("KG", "J", "U", "I", "T",), ("I", "U",),
-    ("T",), ("I", "J", "g0", "U", "T",), ("I",), ("U", "J",), ("I",), ("U", "T", "J",), ("J",),
+    ("T",), ("I", "J", "g0", "U", "T",), ("I",), ("J", "U",), ("I",), ("U", "T", "J",), ("J",),
     ("I", "U", "T",), ("g1",), ("J",), ("T",), ("I", "J", "U",), ("I", "T",), ("J", "T",), ("U",),
-    ("fI", "fJ", "fU",), ("T",), ("hT",), ("fT",),
+    ("fI", "fU",), ("fJ", "T",), ("hT",), ("fT",),
 )
 HALF = GROUP // 2
 

time: 139 us -> 139 us (level)
  transfers between devices with their start and end apart: 60 -> 60, of which waited for: 26 -> 25; matrix products, arithmetic and copies ran while one was open for 3% -> 3% of each run, Pallas kernels for 19% -> 19%
where the time goes in v5:
time: 139 us; the launch traced here: 138 us
  starting transfers between devices  53.5 us (38%)
  waiting for transfers between devices  44.5 us (32%)
  Pallas kernels  33.3 us (24%)
  other arithmetic  3.02 us (2%)
  local copies, waits for them, and re-layouts  2.37 us (2%)
  between operations  1.59 us (1%)
    ppermute x60, starting transfers between devices, swap(): return lax.ppermute(values, AXES, [(d, partner(d)) for d in range(devices)])  53.5 us
    ppermute x60, waiting for transfers between devices, swap(): return lax.ppermute(values, AXES, [(d, partner(d)) for d in range(devices)])  44.5 us
    pallas_call x12, Pallas kernels, call(): pl.pallas_call(kernel, out_shape=out_shapes, in_specs=in_specs, out_specs...  33.3 us
  transfers between devices with their start and end apart: 60, of which 25 were waited for; matrix products, arithmetic and copies ran while one was open for 3% of the time, Pallas kernels for 19%

profile of v5, /device:TPU:0, one launch (start us, length us, event | category | flops | bytes accessed | tf_op | source)
XLA Modules:
  0.0 138.3 jit_solution(1234572901000416413)
XLA Ops:
  0.7 0.9 fusion.4
  1.6 3.0 %collective-permute-start = (bf16[1,3,64,256]{3,2,1,0:T(8,128)(2,1)S(1)}, bf16[1,3,64,256]{3,2,1,0:T(8,128)(2,1)S(1)}, u32[]{:S(2)}, u32[]{:S(2)}) collective-permute-start(bf16[1,3,64,256]{3,2,1,0:T(8,128)(2,1)S(1)} %fusion.4), channel_id=1, source_target_pairs={{0,4},{1,17},{2,6},{3,19},{4,0},{5,21},{6,2},{7,23},{8,12},{9,25},... | collective-permute-start | bytes 294920 | tf_op jit(solution)/shard_map/weights_first/ppermute | solution.py:483
  4.6 1.7 %collective-permute-start.4 = (s32[2,128]{1,0:T(2,128)}, s32[2,128]{1,0:T(2,128)S(1)}, u32[]{:S(2)}, u32[]{:S(2)}) collective-permute-start(s32[2,128]{1,0:T(2,128)} %bitcast.45), channel_id=1, source_target_pairs={{0,3},{1,2},{2,1},{3,0},{4,7},{5,6},{6,5},{7,4},{8,11},{9,10},{10,... | collective-permute-start | bytes 3080 | tf_op jit(solution)/shard_map/segments/ppermute | solution.py:483
  6.9 1.5 %collective-permute-start.5 = (bf16[256,512]{1,0:T(8,128)(2,1)}, bf16[256,512]{1,0:T(8,128)(2,1)S(1)}, u32[]{:S(2)}, u32[]{:S(2)}) collective-permute-start(bf16[256,512]{1,0:T(8,128)(2,1)} %bitcast.50), channel_id=1, source_target_pairs={{0,2},{1,3},{2,0},{3,1},{4,6},{5,7},{6,4},{7,5},{8,10},{9,11},{10,... | collective-permute-start | bytes 786440 | tf_op jit(solution)/shard_map/row_far/ppermute | solution.py:483
  8.4 2.0 %collective-permute-start.6 = (bf16[2,3,64,256]{3,2,1,0:T(8,128)(2,1)S(1)}, bf16[2,3,64,256]{3,2,1,0:T(8,128)(2,1)S(1)}, u32[]{:S(2)}, u32[]{:S(2)}) collective-permute-start(bf16[2,3,64,256]{3,2,1,0:T(8,128)(2,1)S(1)} %pad_maximum_fusion.8.rest_0_), channel_id=1, source_target_pairs={{0,16},{1,9},{2,18},{3,11},{4,20},{5,13},{6,22},{7,15},{8,24},{9,1... | collective-permute-start | bytes 589832 | tf_op jit(solution)/shard_map/weights_second/ppermute | solution.py:483
  10.4 1.1 constant_dynamic-update-slice_fusion.4
  11.5 1.1 constant_dynamic-update-slice_fusion.3
  13.0 1.1 collective-permute-done.2.seg1
  14.1 0.9 collective-permute-done.5.x2
  14.9 1.6 %collective-permute-start.8 = (bf16[2,3,64,256]{3,2,1,0:T(8,128)(2,1)S(1)}, bf16[2,3,64,256]{3,2,1,0:T(8,128)(2,1)S(1)}, u32[]{:S(2)}, u32[]{:S(2)}) collective-permute-start(bf16[2,3,64,256]{3,2,1,0:T(8,128)(2,1)S(1)} %pad_maximum_fusion.8.rest_0_), channel_id=1, source_target_pairs={{0,8},{1,5},{2,10},{3,7},{4,12},{5,1},{6,14},{7,3},{8,0},{9,13},{1... | collective-permute-start | bytes 589832 | tf_op jit(solution)/shard_map/weights_third/ppermute | solution.py:483
  17.7 5.8 %attend.1 = (bf16[256,512]{1,0:T(8,128)(2,1)S(1)}, bf16[1024,512]{1,0:T(8,128)(2,1)S(1)}, bf16[1024,512]{1,0:T(8,128)(2,1)S(1)}, bf16[8,512,256]{2,1,0:T(8,128)(...) custom-call(bf16[512,512]{1,0:T(8,128)(2,1)S(1)} %pad_maximum_fusion.1.x01, ...), custom_call_target="tpu_custom_call" | custom-call | flops 60000 | bytes 600 | tf_op jit(solution)/shard_map/attend/pallas_call | solution.py:450
  24.7 2.7 %feed.1 = (bf16[256,2048]{1,0:T(8,128)(2,1)S(1)}, bf16[256,2048]{1,0:T(8,128)(2,1)S(1)}, f32[256,512]{1,0:T(8,128)S(1)}, f32[256,128]{1,0:T(8,128)S(1)}, bf16[25...) custom-call(f32[256,512]{1,0:T(8,128)S(1)} %get-tuple-element.297.n1_ref, f32[1,512]{1,0:T(1,128)S(1)} %bitcast.32, ...), custom_call_target="tpu_custom_call" | custom-call | flops 30000 | bytes 300 | tf_op jit(solution)/shard_map/feed/pallas_call | solution.py:450
  27.5 4.9 %joining.1 = (bf16[256,512]{1,0:T(8,128)(2,1)}, bf16[768,512]{1,0:T(8,128)(2,1)S(1)}, bf16[768,512]{1,0:T(8,128)(2,1)S(1)}, f32[256,512]{1,0:T(8,128)S(1)}, bf16...) custom-call(f32[256,512]{1,0:T(8,128)S(1)} %get-tuple-element.300.n2_ref, f32[1,512]{1,0:T(1,128)S(1)} %bitcast.38, ...), custom_call_target="tpu_custom_call" | custom-call | flops 80000 | bytes 800 | tf_op jit(solution)/shard_map/joining/pallas_call | solution.py:450
  32.5 1.5 %outer_back.1 = (f32[256,512]{1,0:T(8,128)S(1)}, f32[8,512]{1,0:T(8,128)S(1)}, bf16[1024,512]{1,0:T(8,128)(2,1)S(1)}, bf16[1024,512]{1,0:T(8,128)(2,1)S(1)}) custom-call(f32[256,512]{1,0:T(8,128)S(1)} %get-tuple-element.313.dhp_ref, bf16[256,512]{1,0:T(8,128)(2,1)S(1)} %get-tuple-element.314.dt_ref, ...), custom_call_target="tpu_custom_call" | custom-call | flops 40000 | bytes 400 | tf_op jit(solution)/shard_map/outer_back/pallas_call | solution.py:450
  34.4 2.5 %inner_back.1 = (f32[256,512]{1,0:T(8,128)S(1)}, bf16[16,512]{1,0:T(8,128)(2,1)S(1)}, bf16[1280,512]{1,0:T(8,128)(2,1)S(1)}, bf16[1280,512]{1,0:T(8,128)(2,1)S(1)}) custom-call(f32[256,512]{1,0:T(8,128)S(1)} %get-tuple-element.320.d2_ref, bf16[256,2048]{1,0:T(8,128)(2,1)S(1)} %get-tuple-element.321.sz_ref, bf16[512,2048]{1,0:T(8,128)(2,1)S(1)} %copy-done, ...), custom_call_target="tpu_custom_call" | custom-call | flops 60000 | bytes 600 | tf_op jit(solution)/shard_map/inner_back/pallas_call | solution.py:450
  37.3 1.5 %collective-permute-start.17 = (bf16[384,512]{1,0:T(8,128)(2,1)S(1)}, bf16[384,512]{1,0:T(8,128)(2,1)S(1)}, u32[]{:S(2)}, u32[]{:S(2)}) collective-permute-start(bf16[384,512]{1,0:T(8,128)(2,1)S(1)} %get-tuple-element.357), channel_id=1, source_target_pairs={{0,2},{1,5},{2,0},{3,7},{4,6},{5,1},{6,4},{7,3},{8,10},{9,13},{10,... | collective-permute-start | bytes 1179656 | tf_op jit(solution)/shard_map/joining_sum_step_0/over_stage/ppermute | solution.py:483
  38.8 0.9 collective-permute-start.18
  40.2 1.5 %collective-permute-start.19 = (bf16[640,512]{1,0:T(8,128)(2,1)S(1)}, bf16[640,512]{1,0:T(8,128)(2,1)S(1)}, u32[]{:S(2)}, u32[]{:S(2)}) collective-permute-start(bf16[640,512]{1,0:T(8,128)(2,1)S(1)} %get-tuple-element.363), channel_id=1, source_target_pairs={{0,2},{1,5},{2,0},{3,7},{4,6},{5,1},{6,4},{7,3},{8,10},{9,13},{10,... | collective-permute-start | bytes 1966088 | tf_op jit(solution)/shard_map/inner_sum_step_0/over_stage/ppermute | solution.py:483
  41.6 4.4 %attend_back.1 = (bf16[784,512]{1,0:T(8,128)(2,1)S(1)}, bf16[784,512]{1,0:T(8,128)(2,1)S(1)}, bf16[256,512]{1,0:T(8,128)(2,1)S(1)}, bf16[1024,512]{1,0:T(8,128)(2,1)S(1)}, bf16[1024,512]{1,0:T(8,128)(2,1)S(1)}) custom-call(f32[256,512]{1,0:T(8,128)S(1)} %get-tuple-element.350.d1_ref, bf16[512,2560]{1,0:T(8,128)(2,1)S(1)} %constant_dynamic-update-slice_fusion.bank, ...), custom_call_target="tpu_custom_call" | custom-call | flops 80000 | bytes 800 | tf_op jit(solution)/shard_map/attend_back/pallas_call | solution.py:450
  46.6 1.4 %input_back.1 = (f32[256,512]{1,0:T(8,128)S(1)}, bf16[256,512]{1,0:T(8,128)(2,1)S(1)}, bf16[512,512]{1,0:T(8,128)(2,1)S(1)}) custom-call(f32[256,512]{1,0:T(8,128)S(1)} %get-tuple-element.350.d1_ref, bf16[256,512]{1,0:T(8,128)(2,1)S(1)} %get-tuple-element.351.dq_ref, bf16[1024,512]{1,0:T(8,128)(2,1)S(1)} %get-tuple-element.352.dk_ref, ...), custom_call_target="tpu_custom_call" | custom-call | flops 20000 | bytes 200 | tf_op jit(solution)/shard_map/input_back/pallas_call | solution.py:450
  48.1 4.5 %collective-permute-done.18 = bf16[512,512]{1,0:T(8,128)(2,1)S(1)} collective-permute-done((bf16[512,512]{1,0:T(8,128)(2,1)S(1)}, bf16[512,512]{1,0:T(8,128)(2,1)S(1)}, u32[]{:S(2)}, u32[]{:S(2)}) %collective-permute-start.18) | collective-permute-done | bytes 524320 | tf_op jit(solution)/shard_map/outer_sum_step_0/over_stage/ppermute | solution.py:483
  52.8 1.1 collective-permute-start.21
  53.9 2.9 %collective-permute-start.22 = (bf16[256,512]{1,0:T(8,128)(2,1)S(1)}, bf16[256,512]{1,0:T(8,128)(2,1)S(1)}, u32[]{:S(2)}, u32[]{:S(2)}) collective-permute-start(bf16[256,512]{1,0:T(8,128)(2,1)S(1)} %get-tuple-element.375), channel_id=1, source_target_pairs={{0,16},{1,9},{2,18},{3,11},{4,20},{5,13},{6,22},{7,15},{8,24},{9,1... | collective-permute-start | bytes 786440 | tf_op jit(solution)/shard_map/outer_sum_step_1/over_stage/ppermute | solution.py:483
  56.9 0.9 collective-permute-start.25
  57.8 1.2 collective-permute-start.23
  59.0 2.5 %collective-permute-done.21 = bf16[320,512]{1,0:T(8,128)(2,1)S(1)} collective-permute-done((bf16[320,512]{1,0:T(8,128)(2,1)S(1)}, bf16[320,512]{1,0:T(8,128)(2,1)S(1)}, u32[]{:S(2)}, u32[]{:S(2)}) %collective-permute-start.21) | collective-permute-done | bytes 327712 | tf_op jit(solution)/shard_map/inner_sum_step_1/over_stage/ppermute | solution.py:483
  61.5 1.6 %collective-permute-done.22 = bf16[256,512]{1,0:T(8,128)(2,1)S(1)} collective-permute-done((bf16[256,512]{1,0:T(8,128)(2,1)S(1)}, bf16[256,512]{1,0:T(8,128)(2,1)S(1)}, u32[]{:S(2)}, u32[]{:S(2)}) %collective-permute-start.22) | collective-permute-done | bytes 262176 | tf_op jit(solution)/shard_map/outer_sum_step_1/over_stage/ppermute | solution.py:483
  63.1 2.5 %collective-permute-start.27 = (bf16[128,512]{1,0:T(8,128)(2,1)S(1)}, bf16[128,512]{1,0:T(8,128)(2,1)S(1)}, u32[]{:S(2)}, u32[]{:S(2)}) collective-permute-start(bf16[128,512]{1,0:T(8,128)(2,1)S(1)} %get-tuple-element.394), channel_id=1, source_target_pairs={{0,2},{1,5},{2,0},{3,7},{4,6},{5,1},{6,4},{7,3},{8,10},{9,13},{10,... | collective-permute-start | bytes 393224 | tf_op jit(solution)/shard_map/outer_sum_step_2/over_stage/ppermute | solution.py:483
  65.7 1.0 collective-permute-done.23
  67.4 3.6 %collective-permute-done.24 = bf16[160,512]{1,0:T(8,128)(2,1)S(1)} collective-permute-done((bf16[160,512]{1,0:T(8,128)(2,1)S(1)}, bf16[160,512]{1,0:T(8,128)(2,1)S(1)}, u32[]{:S(2)}, u32[]{:S(2)}) %collective-permute-start.24) | collective-permute-done | bytes 163872 | tf_op jit(solution)/shard_map/inner_sum_step_2/over_stage/ppermute | solution.py:483
  71.1 1.6 %collective-permute-done.28 = bf16[208,512]{1,0:T(8,128)(2,1)S(1)} collective-permute-done((bf16[208,512]{1,0:T(8,128)(2,1)S(1)}, bf16[208,512]{1,0:T(8,128)(2,1)S(1)}, u32[]{:S(2)}, u32[]{:S(2)}) %collective-permute-start.28) | collective-permute-done | bytes 213024 | tf_op jit(solution)/shard_map/attend_sum_step_1/over_stage/ppermute | solution.py:483
  72.8 2.5 %collective-permute-start.29 = (bf16[80,512]{1,0:T(8,128)(2,1)S(1)}, bf16[80,512]{1,0:T(8,128)(2,1)S(1)}, u32[]{:S(2)}, u32[]{:S(2)}) collective-permute-start(bf16[80,512]{1,0:T(8,128)(2,1)S(1)} %slice_add_fusion.24), channel_id=1, source_target_pairs={{0,16},{1,17},{2,18},{3,19},{4,20},{5,21},{6,22},{7,23},{8,24},{9,... | collective-permute-start | bytes 245768 | tf_op jit(solution)/shard_map/inner_sum_step_3/over_stage/ppermute | solution.py:483
  75.3 1.0 collective-permute-start.31
  76.8 1.5 %collective-permute-start.34 = (bf16[112,512]{1,0:T(8,128)(2,1)S(1)}, bf16[112,512]{1,0:T(8,128)(2,1)S(1)}, u32[]{:S(2)}, u32[]{:S(2)}) collective-permute-start(bf16[112,512]{1,0:T(8,128)(2,1)S(1)} %fusion.1), channel_id=1, source_target_pairs={{0,8},{1,9},{2,10},{3,11},{4,12},{5,13},{6,14},{7,15},{8,0},{9,1},... | collective-permute-start | bytes 344072 | tf_op jit(solution)/shard_map/attend_sum_step_2/over_stage/ppermute | solution.py:483
  78.3 1.1 collective-permute-start.40
  79.4 2.1 %collective-permute-start.32 = (bf16[80,512]{1,0:T(8,128)(2,1)S(1)}, bf16[80,512]{1,0:T(8,128)(2,1)S(1)}, u32[]{:S(2)}, u32[]{:S(2)}) collective-permute-start(bf16[80,512]{1,0:T(8,128)(2,1)S(1)} %fusion.5), channel_id=1, source_target_pairs={{0,16},{1,17},{2,18},{3,19},{4,20},{5,21},{6,22},{7,23},{8,24},{9,... | collective-permute-start | bytes 245768 | tf_op jit(solution)/shard_map/inner_sum_step_4/over_stage/ppermute | solution.py:483
  81.6 0.9 collective-permute-done.30
  82.6 1.2 collective-permute-start.33
  83.8 2.6 %collective-permute-done.32 = bf16[80,512]{1,0:T(8,128)(2,1)S(1)} collective-permute-done((bf16[80,512]{1,0:T(8,128)(2,1)S(1)}, bf16[80,512]{1,0:T(8,128)(2,1)S(1)}, u32[]{:S(2)}, u32[]{:S(2)}) %collective-permute-start.32) | collective-permute-done | bytes 81952 | tf_op jit(solution)/shard_map/inner_sum_step_4/over_stage/ppermute | solution.py:483
  87.0 0.9 collective-permute-done.35
  87.9 2.2 %collective-permute-start.36 = (bf16[48,512]{1,0:T(8,128)(2,1)S(1)}, bf16[48,512]{1,0:T(8,128)(2,1)S(1)}, u32[]{:S(2)}, u32[]{:S(2)}) collective-permute-start(bf16[48,512]{1,0:T(8,128)(2,1)S(1)} %fusion.8), channel_id=1, source_target_pairs={{0,16},{1,17},{2,18},{3,19},{4,20},{5,21},{6,22},{7,23},{8,24},{9,... | collective-permute-start | bytes 147464 | tf_op jit(solution)/shard_map/joining_sum_step_4/over_stage/ppermute | solution.py:483
  90.1 0.8 collective-permute-start.39
  90.9 1.0 collective-permute-start.38
  91.8 1.6 %collective-permute-done.36 = bf16[48,512]{1,0:T(8,128)(2,1)S(1)} collective-permute-done((bf16[48,512]{1,0:T(8,128)(2,1)S(1)}, bf16[48,512]{1,0:T(8,128)(2,1)S(1)}, u32[]{:S(2)}, u32[]{:S(2)}) %collective-permute-start.36) | collective-permute-done | bytes 49184 | tf_op jit(solution)/shard_map/joining_sum_step_4/over_stage/ppermute | solution.py:483
  94.1 1.7 %collective-permute-done.38 = bf16[128,512]{1,0:T(8,128)(2,1)S(1)} collective-permute-done((bf16[128,512]{1,0:T(8,128)(2,1)S(1)}, bf16[128,512]{1,0:T(8,128)(2,1)S(1)}, u32[]{:S(2)}, u32[]{:S(2)}) %collective-permute-start.38) | collective-permute-done | bytes 131104 | tf_op jit(solution)/shard_map/outer_sum_step_5/over_stage/ppermute | solution.py:483
  96.2 1.9 %collective-permute-start.42 = (bf16[48,512]{1,0:T(8,128)(2,1)S(1)}, bf16[48,512]{1,0:T(8,128)(2,1)S(1)}, u32[]{:S(2)}, u32[]{:S(2)}) collective-permute-start(bf16[48,512]{1,0:T(8,128)(2,1)S(1)} %slice.313), channel_id=1, source_target_pairs={{0,16},{1,17},{2,18},{3,19},{4,20},{5,21},{6,22},{7,23},{8,24},{9,... | collective-permute-start | bytes 147464 | tf_op jit(solution)/shard_map/attend_sum_step_4/over_stage/ppermute | solution.py:483
  98.1 1.1 collective-permute-start.45
  99.2 1.6 %collective-permute-start.43 = (bf16[320,512]{1,0:T(8,128)(2,1)S(1)}, bf16[320,512]{1,0:T(8,128)(2,1)S(1)}, u32[]{:S(2)}, u32[]{:S(2)}) collective-permute-start(bf16[320,512]{1,0:T(8,128)(2,1)S(1)} %pad_maximum_fusion.5), channel_id=1, source_target_pairs={{0,4},{1,3},{2,6},{3,1},{4,0},{5,7},{6,2},{7,5},{8,12},{9,11},{10,... | collective-permute-start | bytes 983048 | tf_op jit(solution)/shard_map/inner_sum_step_6/over_stage/ppermute | solution.py:483
  100.8 0.8 add_convert_fusion
  102.1 4.1 %collective-permute-done.43 = bf16[320,512]{1,0:T(8,128)(2,1)S(1)} collective-permute-done((bf16[320,512]{1,0:T(8,128)(2,1)S(1)}, bf16[320,512]{1,0:T(8,128)(2,1)S(1)}, u32[]{:S(2)}, u32[]{:S(2)}) %collective-permute-start.43) | collective-permute-done | bytes 327712 | tf_op jit(solution)/shard_map/inner_sum_step_6/over_stage/ppermute | solution.py:483
  106.3 2.1 %collective-permute-done.44 = bf16[192,512]{1,0:T(8,128)(2,1)S(1)} collective-permute-done((bf16[192,512]{1,0:T(8,128)(2,1)S(1)}, bf16[192,512]{1,0:T(8,128)(2,1)S(1)}, u32[]{:S(2)}, u32[]{:S(2)}) %collective-permute-start.44) | collective-permute-done | bytes 196640 | tf_op jit(solution)/shard_map/joining_sum_step_6/over_stage/ppermute | solution.py:483
  108.5 0.7 collective-permute-start.46
  109.3 0.8 collective-permute-start.48
  110.1 0.9 collective-permute-start.49
  111.0 1.6 %collective-permute-start.52 = (bf16[512,512]{1,0:T(8,128)(2,1)S(1)}, bf16[512,512]{1,0:T(8,128)(2,1)S(1)}, u32[]{:S(2)}, u32[]{:S(2)}) collective-permute-start(bf16[512,512]{1,0:T(8,128)(2,1)S(1)} %pad_maximum_fusion.2.rest_0_), channel_id=1, source_target_pairs={{0,8},{1,17},{2,10},{3,19},{4,12},{5,21},{6,14},{7,23},{8,0},{9,25... | collective-permute-start | bytes 1572872 | tf_op jit(solution)/shard_map/outer_sum_step_7/over_stage/ppermute | solution.py:483
  112.7 6.5 %collective-permute-done.46.rest_1_ = bf16[640,512]{1,0:T(8,128)(2,1)S(1)} collective-permute-done((bf16[640,512]{1,0:T(8,128)(2,1)S(1)}, bf16[640,512]{1,0:T(8,128)(2,1)S(1)}, u32[]{:S(2)}, u32[]{:S(2)}) %collective-permute-start.46) | collective-permute-done | bytes 655392 | tf_op jit(solution)/shard_map/inner_sum_step_7/over_stage/ppermute | solution.py:483
  119.2 1.7 %collective-permute-start.51 = (bf16[192,512]{1,0:T(8,128)(2,1)S(1)}, bf16[192,512]{1,0:T(8,128)(2,1)S(1)}, u32[]{:S(2)}, u32[]{:S(2)}) collective-permute-start(bf16[192,512]{1,0:T(8,128)(2,1)S(1)} %pad_maximum_fusion.10), channel_id=1, source_target_pairs={{0,4},{1,3},{2,6},{3,1},{4,0},{5,7},{6,2},{7,5},{8,12},{9,11},{10,... | collective-permute-start | bytes 589832 | tf_op jit(solution)/shard_map/attend_sum_step_6/over_stage/ppermute | solution.py:483
  120.9 3.5 %collective-permute-done.49.rest_1_ = bf16[384,512]{1,0:T(8,128)(2,1)S(1)} collective-permute-done((bf16[384,512]{1,0:T(8,128)(2,1)S(1)}, bf16[384,512]{1,0:T(8,128)(2,1)S(1)}, u32[]{:S(2)}, u32[]{:S(2)}) %collective-permute-start.49) | collective-permute-done | bytes 393248 | tf_op jit(solution)/shard_map/joining_sum_step_7/over_stage/ppermute | solution.py:483
  125.0 1.2 collective-permute-done.52.rest_1_
  127.3 2.7 %finish_inner.1 = (f32[512,2048]{1,0:T(8,128)}, f32[512,512]{1,0:T(8,128)}) custom-call(bf16[640,512]{1,0:T(8,128)(2,1)S(1)} %pad_maximum_fusion.rest_0_, bf16[640,512]{1,0:T(8,128)(2,1)S(1)} %collective-permute-done.46.rest_1_, bf16[640,512]{1,0:T(8,128)(2,1)S(1)} %collective-permute-done.47.rest_2_, bf16[640,512]{1,0:T(8,128)(2,1)S(1)} %collective-permute-done.54.rest_3_), custom_call_target="tpu_custom_call" | custom-call | flops 20000 | bytes 200 | tf_op jit(solution)/shard_map/finish_inner/pallas_call | solution.py:450
  130.0 2.3 %finish_outer.1 = f32[2048,512]{1,0:T(8,128)} custom-call(bf16[512,512]{1,0:T(8,128)(2,1)S(1)} %pad_maximum_fusion.2.rest_0_, bf16[512,512]{1,0:T(8,128)(2,1)S(1)} %collective-permute-done.52.rest_1_, bf16[512,512]{1,0:T(8,128)(2,1)S(1)} %collective-permute-done.53.rest_2_, bf16[512,512]{1,0:T(8,128)(2,1)S(1)} %collective-permute-done.55.rest_3_), custom_call_target="tpu_custom_call" | custom-call | flops 20000 | bytes 200 | tf_op jit(solution)/shard_map/finish_outer/pallas_call | solution.py:450
  132.3 1.9 %finish_joining.1 = (f32[512,512]{1,0:T(8,128)}, f32[512,512]{1,0:T(8,128)}, f32[512,512]{1,0:T(8,128)}) custom-call(bf16[384,512]{1,0:T(8,128)(2,1)S(1)} %pad_maximum_fusion.3.rest_0_, bf16[384,512]{1,0:T(8,128)(2,1)S(1)} %collective-permute-done.49.rest_1_, bf16[384,512]{1,0:T(8,128)(2,1)S(1)} %collective-permute-done.50.rest_2_, ...), custom_call_target="tpu_custom_call" | custom-call | flops 20000 | bytes 200 | tf_op jit(solution)/shard_map/finish_joining/pallas_call | solution.py:450
  134.7 1.3 finish_half.1
  136.2 2.0 %finish_attend.1 = (f32[512,512]{1,0:T(8,128)}, f32[512,512]{1,0:T(8,128)}, f32[512,512]{1,0:T(8,128)}, f32[1,512]{1,0:T(1,128)}, f32[1,512]{1,0:T(1,128)}, /*in...) custom-call(bf16[384,512]{1,0:T(8,128)(2,1)S(1)} %collective-permute, ...), custom_call_target="tpu_custom_call", output_to_operand_aliasing={{0}: (3, {}), {1}: (4, {}), {2}: (5, {})} | custom-call | flops 20000 | bytes 200 | tf_op jit(solution)/shard_map/finish_attend/pallas_call | solution.py:450
  (150 shorter events, 11.6 us)
Async XLA Ops:
  0.7 12.0 %copy-start.12 = (bf16[512,512]{1,0:T(8,128)(2,1)S(1)}, bf16[512,512]{1,0:T(8,128)(2,1)}, u32[]{:S(2)}) copy-start(bf16[512,512]{1,0:T(8,128)(2,1)} %param.26) | copy-start | bytes 1572868
  0.7 12.0 %copy-start.13 = (bf16[512,512]{1,0:T(8,128)(2,1)S(1)}, bf16[512,512]{1,0:T(8,128)(2,1)}, u32[]{:S(2)}) copy-start(bf16[512,512]{1,0:T(8,128)(2,1)} %param.27) | copy-start | bytes 1572868
  0.7 12.1 %copy-start.14 = (bf16[512,512]{1,0:T(8,128)(2,1)S(1)}, bf16[512,512]{1,0:T(8,128)(2,1)}, u32[]{:S(2)}) copy-start(bf16[512,512]{1,0:T(8,128)(2,1)} %param.35) | copy-start | bytes 1572868
  1.6 6.8 %collective-permute-start = (bf16[1,3,64,256]{3,2,1,0:T(8,128)(2,1)S(1)}, bf16[1,3,64,256]{3,2,1,0:T(8,128)(2,1)S(1)}, u32[]{:S(2)}, u32[]{:S(2)}) collective-permute-start(bf16[1,3,64,256]{3,2,1,0:T(8,128)(2,1)S(1)} %fusion.4), channel_id=1, source_target_pairs={{0,4},{1,17},{2,6},{3,19},{4,0},{5,21},{6,2},{7,23},{8,12},{9,25},... | collective-permute-start | bytes 294920 | tf_op jit(solution)/shard_map/weights_first/ppermute | solution.py:483
  4.6 8.4 %collective-permute-start.4 = (s32[2,128]{1,0:T(2,128)}, s32[2,128]{1,0:T(2,128)S(1)}, u32[]{:S(2)}, u32[]{:S(2)}) collective-permute-start(s32[2,128]{1,0:T(2,128)} %bitcast.45), channel_id=1, source_target_pairs={{0,3},{1,2},{2,1},{3,0},{4,7},{5,6},{6,5},{7,4},{8,11},{9,10},{10,... | collective-permute-start | bytes 3080 | tf_op jit(solution)/shard_map/segments/ppermute | solution.py:483
  6.3 6.7 %collective-permute-start.3 = (s32[2,128]{1,0:T(2,128)}, s32[2,128]{1,0:T(2,128)S(1)}, u32[]{:S(2)}, u32[]{:S(2)}) collective-permute-start(s32[2,128]{1,0:T(2,128)} %bitcast.46), channel_id=1, source_target_pairs={{0,2},{1,3},{2,0},{3,1},{4,6},{5,7},{6,4},{7,5},{8,10},{9,11},{10,... | collective-permute-start | bytes 3080 | tf_op jit(solution)/shard_map/segments/ppermute | solution.py:483
  6.9 8.1 %collective-permute-start.5 = (bf16[256,512]{1,0:T(8,128)(2,1)}, bf16[256,512]{1,0:T(8,128)(2,1)S(1)}, u32[]{:S(2)}, u32[]{:S(2)}) collective-permute-start(bf16[256,512]{1,0:T(8,128)(2,1)} %bitcast.50), channel_id=1, source_target_pairs={{0,2},{1,3},{2,0},{3,1},{4,6},{5,7},{6,4},{7,5},{8,10},{9,11},{10,... | collective-permute-start | bytes 786440 | tf_op jit(solution)/shard_map/row_far/ppermute | solution.py:483
  8.4 4.5 %collective-permute-start.1 = (bf16[256,512]{1,0:T(8,128)(2,1)}, bf16[256,512]{1,0:T(8,128)(2,1)S(1)}, u32[]{:S(2)}, u32[]{:S(2)}) collective-permute-start(bf16[256,512]{1,0:T(8,128)(2,1)} %bitcast.51), channel_id=1, source_target_pairs={{0,1},{1,0},{2,3},{3,2},{4,5},{5,4},{6,7},{7,6},{8,9},{9,8},{10,11... | collective-permute-start | bytes 786440 | tf_op jit(solution)/shard_map/row_near/ppermute | solution.py:483
  8.4 8.8 %collective-permute-start.6 = (bf16[2,3,64,256]{3,2,1,0:T(8,128)(2,1)S(1)}, bf16[2,3,64,256]{3,2,1,0:T(8,128)(2,1)S(1)}, u32[]{:S(2)}, u32[]{:S(2)}) collective-permute-start(bf16[2,3,64,256]{3,2,1,0:T(8,128)(2,1)S(1)} %pad_maximum_fusion.8.rest_0_), channel_id=1, source_target_pairs={{0,16},{1,9},{2,18},{3,11},{4,20},{5,13},{6,22},{7,15},{8,24},{9,1... | collective-permute-start | bytes 589832 | tf_op jit(solution)/shard_map/weights_second/ppermute | solution.py:483
  12.8 11.8 %copy-start = (bf16[512,2048]{1,0:T(8,128)(2,1)S(1)}, bf16[512,2048]{1,0:T(8,128)(2,1)}, u32[]{:S(2)}) copy-start(bf16[512,2048]{1,0:T(8,128)(2,1)} %wi.3) | copy-start | bytes 6291460
  12.9 1.2 collective-permute-start.2
  14.9 2.8 %collective-permute-start.7 = (bf16[256,512]{1,0:T(8,128)(2,1)S(1)}, bf16[256,512]{1,0:T(8,128)(2,1)S(1)}, u32[]{:S(2)}, u32[]{:S(2)}) collective-permute-start(bf16[256,512]{1,0:T(8,128)(2,1)S(1)} %collective-permute-done.5.x2), channel_id=1, source_target_pairs={{0,1},{1,0},{2,3},{3,2},{4,5},{5,4},{6,7},{7,6},{8,9},{9,8},{10,11... | collective-permute-start | bytes 786440 | tf_op jit(solution)/shard_map/row_cross/ppermute | solution.py:483
  14.9 8.6 %collective-permute-start.8 = (bf16[2,3,64,256]{3,2,1,0:T(8,128)(2,1)S(1)}, bf16[2,3,64,256]{3,2,1,0:T(8,128)(2,1)S(1)}, u32[]{:S(2)}, u32[]{:S(2)}) collective-permute-start(bf16[2,3,64,256]{3,2,1,0:T(8,128)(2,1)S(1)} %pad_maximum_fusion.8.rest_0_), channel_id=1, source_target_pairs={{0,8},{1,5},{2,10},{3,7},{4,12},{5,1},{6,14},{7,3},{8,0},{9,13},{1... | collective-permute-start | bytes 589832 | tf_op jit(solution)/shard_map/weights_third/ppermute | solution.py:483
  17.2 6.3 %collective-permute-start.9 = (bf16[2,3,64,256]{3,2,1,0:T(8,128)(2,1)S(1)}, bf16[2,3,64,256]{3,2,1,0:T(8,128)(2,1)S(1)}, u32[]{:S(2)}, u32[]{:S(2)}) collective-permute-start(bf16[2,3,64,256]{3,2,1,0:T(8,128)(2,1)S(1)} %collective-permute-done.6.rest_1_), channel_id=1, source_target_pairs={{0,8},{1,5},{2,10},{3,7},{4,12},{5,1},{6,14},{7,3},{8,0},{9,13},{1... | collective-permute-start | bytes 589832 | tf_op jit(solution)/shard_map/weights_third/ppermute | solution.py:483
  23.5 3.9 %collective-permute-start.10 = (bf16[2,3,64,256]{3,2,1,0:T(8,128)(2,1)S(1)}, bf16[2,3,64,256]{3,2,1,0:T(8,128)(2,1)S(1)}, u32[]{:S(2)}, u32[]{:S(2)}) collective-permute-start(bf16[2,3,64,256]{3,2,1,0:T(8,128)(2,1)S(1)} %pad_maximum_fusion.8.rest_0_), channel_id=1, source_target_pairs={{0,1},{1,0},{2,3},{3,2},{4,5},{5,4},{6,7},{7,6},{8,9},{9,8},{10,11... | collective-permute-start | bytes 589832 | tf_op jit(solution)/shard_map/weights_core/ppermute | solution.py:483
  23.6 3.8 %collective-permute-start.11 = (bf16[2,3,64,256]{3,2,1,0:T(8,128)(2,1)S(1)}, bf16[2,3,64,256]{3,2,1,0:T(8,128)(2,1)S(1)}, u32[]{:S(2)}, u32[]{:S(2)}) collective-permute-start(bf16[2,3,64,256]{3,2,1,0:T(8,128)(2,1)S(1)} %collective-permute-done.6.rest_1_), channel_id=1, source_target_pairs={{0,1},{1,0},{2,3},{3,2},{4,5},{5,4},{6,7},{7,6},{8,9},{9,8},{10,11... | collective-permute-start | bytes 589832 | tf_op jit(solution)/shard_map/weights_core/ppermute | solution.py:483
  24.1 3.3 %collective-permute-start.13 = (bf16[2,3,64,256]{3,2,1,0:T(8,128)(2,1)S(1)}, bf16[2,3,64,256]{3,2,1,0:T(8,128)(2,1)S(1)}, u32[]{:S(2)}, u32[]{:S(2)}) collective-permute-start(bf16[2,3,64,256]{3,2,1,0:T(8,128)(2,1)S(1)} %collective-permute-done.9.rest_3_), channel_id=1, source_target_pairs={{0,1},{1,0},{2,3},{3,2},{4,5},{5,4},{6,7},{7,6},{8,9},{9,8},{10,11... | collective-permute-start | bytes 589832 | tf_op jit(solution)/shard_map/weights_core/ppermute | solution.py:483
  24.2 3.3 %collective-permute-start.12 = (bf16[2,3,64,256]{3,2,1,0:T(8,128)(2,1)S(1)}, bf16[2,3,64,256]{3,2,1,0:T(8,128)(2,1)S(1)}, u32[]{:S(2)}, u32[]{:S(2)}) collective-permute-start(bf16[2,3,64,256]{3,2,1,0:T(8,128)(2,1)S(1)} %collective-permute-done.8.rest_2_), channel_id=1, source_target_pairs={{0,1},{1,0},{2,3},{3,2},{4,5},{5,4},{6,7},{7,6},{8,9},{9,8},{10,11... | collective-permute-start | bytes 589832 | tf_op jit(solution)/shard_map/weights_core/ppermute | solution.py:483
  32.4 4.7 %collective-permute-start.14 = (bf16[768,512]{1,0:T(8,128)(2,1)S(1)}, bf16[768,512]{1,0:T(8,128)(2,1)S(1)}, u32[]{:S(2)}, u32[]{:S(2)}) collective-permute-start(bf16[768,512]{1,0:T(8,128)(2,1)S(1)} %get-tuple-element.330), channel_id=1, source_target_pairs={{0,1},{1,0},{2,3},{3,2},{4,5},{5,4},{6,7},{7,6},{8,9},{9,8},{10,11... | collective-permute-start | bytes 2359304 | tf_op jit(solution)/shard_map/joining_sum_core/over_bit/ppermute | solution.py:483
  33.9 3.3 %collective-permute-start.15 = (bf16[1024,512]{1,0:T(8,128)(2,1)S(1)}, bf16[1024,512]{1,0:T(8,128)(2,1)S(1)}, u32[]{:S(2)}, u32[]{:S(2)}) collective-permute-start(bf16[1024,512]{1,0:T(8,128)(2,1)S(1)} %get-tuple-element.334), channel_id=1, source_target_pairs={{0,1},{1,0},{2,3},{3,2},{4,5},{5,4},{6,7},{7,6},{8,9},{9,8},{10,11... | collective-permute-start | bytes 3145736 | tf_op jit(solution)/shard_map/outer_sum_core/over_bit/ppermute | solution.py:483
  36.9 3.1 %collective-permute-start.16 = (bf16[1280,512]{1,0:T(8,128)(2,1)S(1)}, bf16[1280,512]{1,0:T(8,128)(2,1)S(1)}, u32[]{:S(2)}, u32[]{:S(2)}) collective-permute-start(bf16[1280,512]{1,0:T(8,128)(2,1)S(1)} %get-tuple-element.338), channel_id=1, source_target_pairs={{0,1},{1,0},{2,3},{3,2},{4,5},{5,4},{6,7},{7,6},{8,9},{9,8},{10,11... | collective-permute-start | bytes 3932168 | tf_op jit(solution)/shard_map/inner_sum_core/over_bit/ppermute | solution.py:483
  37.3 10.7 %collective-permute-start.17 = (bf16[384,512]{1,0:T(8,128)(2,1)S(1)}, bf16[384,512]{1,0:T(8,128)(2,1)S(1)}, u32[]{:S(2)}, u32[]{:S(2)}) collective-permute-start(bf16[384,512]{1,0:T(8,128)(2,1)S(1)} %get-tuple-element.357), channel_id=1, source_target_pairs={{0,2},{1,5},{2,0},{3,7},{4,6},{5,1},{6,4},{7,3},{8,10},{9,13},{10,... | collective-permute-start | bytes 1179656 | tf_op jit(solution)/shard_map/joining_sum_step_0/over_stage/ppermute | solution.py:483
  38.8 13.8 %collective-permute-start.18 = (bf16[512,512]{1,0:T(8,128)(2,1)S(1)}, bf16[512,512]{1,0:T(8,128)(2,1)S(1)}, u32[]{:S(2)}, u32[]{:S(2)}) collective-permute-start(bf16[512,512]{1,0:T(8,128)(2,1)S(1)} %get-tuple-element.360), channel_id=1, source_target_pairs={{0,8},{1,17},{2,10},{3,19},{4,12},{5,21},{6,14},{7,23},{8,0},{9,25... | collective-permute-start | bytes 1572872 | tf_op jit(solution)/shard_map/outer_sum_step_0/over_stage/ppermute | solution.py:483
  40.2 12.4 %collective-permute-start.19 = (bf16[640,512]{1,0:T(8,128)(2,1)S(1)}, bf16[640,512]{1,0:T(8,128)(2,1)S(1)}, u32[]{:S(2)}, u32[]{:S(2)}) collective-permute-start(bf16[640,512]{1,0:T(8,128)(2,1)S(1)} %get-tuple-element.363), channel_id=1, source_target_pairs={{0,2},{1,5},{2,0},{3,7},{4,6},{5,1},{6,4},{7,3},{8,10},{9,13},{10,... | collective-permute-start | bytes 1966088 | tf_op jit(solution)/shard_map/inner_sum_step_0/over_stage/ppermute | solution.py:483
  46.1 6.7 %collective-permute-start.20 = (bf16[784,512]{1,0:T(8,128)(2,1)S(1)}, bf16[784,512]{1,0:T(8,128)(2,1)S(1)}, u32[]{:S(2)}, u32[]{:S(2)}) collective-permute-start(bf16[784,512]{1,0:T(8,128)(2,1)S(1)} %get-tuple-element.367), channel_id=1, source_target_pairs={{0,1},{1,0},{2,3},{3,2},{4,5},{5,4},{6,7},{7,6},{8,9},{9,8},{10,11... | collective-permute-start | bytes 2408456 | tf_op jit(solution)/shard_map/attend_sum_core/over_bit/ppermute | solution.py:483
  52.8 8.7 %collective-permute-start.21 = (bf16[320,512]{1,0:T(8,128)(2,1)S(1)}, bf16[320,512]{1,0:T(8,128)(2,1)S(1)}, u32[]{:S(2)}, u32[]{:S(2)}) collective-permute-start(bf16[320,512]{1,0:T(8,128)(2,1)S(1)} %get-tuple-element.371), channel_id=1, source_target_pairs={{0,4},{1,3},{2,6},{3,1},{4,0},{5,7},{6,2},{7,5},{8,12},{9,11},{10,... | collective-permute-start | bytes 983048 | tf_op jit(solution)/shard_map/inner_sum_step_1/over_stage/ppermute | solution.py:483
  53.9 9.2 %collective-permute-start.22 = (bf16[256,512]{1,0:T(8,128)(2,1)S(1)}, bf16[256,512]{1,0:T(8,128)(2,1)S(1)}, u32[]{:S(2)}, u32[]{:S(2)}) collective-permute-start(bf16[256,512]{1,0:T(8,128)(2,1)S(1)} %get-tuple-element.375), channel_id=1, source_target_pairs={{0,16},{1,9},{2,18},{3,11},{4,20},{5,13},{6,22},{7,15},{8,24},{9,1... | collective-permute-start | bytes 786440 | tf_op jit(solution)/shard_map/outer_sum_step_1/over_stage/ppermute | solution.py:483
  56.9 14.1 %collective-permute-start.25 = (bf16[192,512]{1,0:T(8,128)(2,1)S(1)}, bf16[192,512]{1,0:T(8,128)(2,1)S(1)}, u32[]{:S(2)}, u32[]{:S(2)}) collective-permute-start(bf16[192,512]{1,0:T(8,128)(2,1)S(1)} %get-tuple-element.386), channel_id=1, source_target_pairs={{0,4},{1,3},{2,6},{3,1},{4,0},{5,7},{6,2},{7,5},{8,12},{9,11},{10,... | collective-permute-start | bytes 589832 | tf_op jit(solution)/shard_map/joining_sum_step_1/over_stage/ppermute | solution.py:483
  57.8 9.0 %collective-permute-start.23 = (bf16[400,512]{1,0:T(8,128)(2,1)S(1)}, bf16[400,512]{1,0:T(8,128)(2,1)S(1)}, u32[]{:S(2)}, u32[]{:S(2)}) collective-permute-start(bf16[400,512]{1,0:T(8,128)(2,1)S(1)} %slice_add_fusion.4), channel_id=1, source_target_pairs={{0,2},{1,5},{2,0},{3,7},{4,6},{5,1},{6,4},{7,3},{8,10},{9,13},{10,... | collective-permute-start | bytes 1228808 | tf_op jit(solution)/shard_map/attend_sum_step_0/over_stage/ppermute | solution.py:483
  59.0 12.1 %collective-permute-start.26 = (bf16[512,512]{1,0:T(8,128)(2,1)S(1)}, bf16[512,512]{1,0:T(8,128)(2,1)S(1)}, u32[]{:S(2)}, u32[]{:S(2)}) collective-permute-start(bf16[512,512]{1,0:T(8,128)(2,1)S(1)} %get-tuple-element.391), channel_id=1, source_target_pairs={{0,1},{1,0},{2,3},{3,2},{4,5},{5,4},{6,7},{7,6},{8,9},{9,8},{10,11... | collective-permute-start | bytes 1572872 | tf_op jit(solution)/shard_map/over_bit/ppermute | solution.py:483
  63.1 8.0 %collective-permute-start.27 = (bf16[128,512]{1,0:T(8,128)(2,1)S(1)}, bf16[128,512]{1,0:T(8,128)(2,1)S(1)}, u32[]{:S(2)}, u32[]{:S(2)}) collective-permute-start(bf16[128,512]{1,0:T(8,128)(2,1)S(1)} %get-tuple-element.394), channel_id=1, source_target_pairs={{0,2},{1,5},{2,0},{3,7},{4,6},{5,1},{6,4},{7,3},{8,10},{9,13},{10,... | collective-permute-start | bytes 393224 | tf_op jit(solution)/shard_map/outer_sum_step_2/over_stage/ppermute | solution.py:483
  65.7 5.3 %collective-permute-start.24 = (bf16[160,512]{1,0:T(8,128)(2,1)S(1)}, bf16[160,512]{1,0:T(8,128)(2,1)S(1)}, u32[]{:S(2)}, u32[]{:S(2)}) collective-permute-start(bf16[160,512]{1,0:T(8,128)(2,1)S(1)} %get-tuple-element.382), channel_id=1, source_target_pairs={{0,8},{1,9},{2,10},{3,11},{4,12},{5,13},{6,14},{7,15},{8,0},{9,1},... | collective-permute-start | bytes 491528 | tf_op jit(solution)/shard_map/inner_sum_step_2/over_stage/ppermute | solution.py:483
  66.8 5.9 %collective-permute-start.28 = (bf16[208,512]{1,0:T(8,128)(2,1)S(1)}, bf16[208,512]{1,0:T(8,128)(2,1)S(1)}, u32[]{:S(2)}, u32[]{:S(2)}) collective-permute-start(bf16[208,512]{1,0:T(8,128)(2,1)S(1)} %fusion), channel_id=1, source_target_pairs={{0,4},{1,3},{2,6},{3,1},{4,0},{5,7},{6,2},{7,5},{8,12},{9,11},{10,... | collective-permute-start | bytes 638984 | tf_op jit(solution)/shard_map/attend_sum_step_1/over_stage/ppermute | solution.py:483
  72.8 6.7 %collective-permute-start.29 = (bf16[80,512]{1,0:T(8,128)(2,1)S(1)}, bf16[80,512]{1,0:T(8,128)(2,1)S(1)}, u32[]{:S(2)}, u32[]{:S(2)}) collective-permute-start(bf16[80,512]{1,0:T(8,128)(2,1)S(1)} %slice_add_fusion.24), channel_id=1, source_target_pairs={{0,16},{1,17},{2,18},{3,19},{4,20},{5,21},{6,22},{7,23},{8,24},{9,... | collective-permute-start | bytes 245768 | tf_op jit(solution)/shard_map/inner_sum_step_3/over_stage/ppermute | solution.py:483
  75.3 7.2 %collective-permute-start.31 = (bf16[64,512]{1,0:T(8,128)(2,1)S(1)}, bf16[64,512]{1,0:T(8,128)(2,1)S(1)}, u32[]{:S(2)}, u32[]{:S(2)}) collective-permute-start(bf16[64,512]{1,0:T(8,128)(2,1)S(1)} %slice_add_fusion.26), channel_id=1, source_target_pairs={{0,4},{1,3},{2,6},{3,1},{4,0},{5,7},{6,2},{7,5},{8,12},{9,11},{10,... | collective-permute-start | bytes 196616 | tf_op jit(solution)/shard_map/outer_sum_step_3/over_stage/ppermute | solution.py:483
  76.3 6.2 %collective-permute-start.30 = (bf16[96,512]{1,0:T(8,128)(2,1)S(1)}, bf16[96,512]{1,0:T(8,128)(2,1)S(1)}, u32[]{:S(2)}, u32[]{:S(2)}) collective-permute-start(bf16[96,512]{1,0:T(8,128)(2,1)S(1)} %get-tuple-element.405), channel_id=1, source_target_pairs={{0,8},{1,9},{2,10},{3,11},{4,12},{5,13},{6,14},{7,15},{8,0},{9,1},... | collective-permute-start | bytes 294920 | tf_op jit(solution)/shard_map/joining_sum_step_2/over_stage/ppermute | solution.py:483
  76.8 10.2 %collective-permute-start.34 = (bf16[112,512]{1,0:T(8,128)(2,1)S(1)}, bf16[112,512]{1,0:T(8,128)(2,1)S(1)}, u32[]{:S(2)}, u32[]{:S(2)}) collective-permute-start(bf16[112,512]{1,0:T(8,128)(2,1)S(1)} %fusion.1), channel_id=1, source_target_pairs={{0,8},{1,9},{2,10},{3,11},{4,12},{5,13},{6,14},{7,15},{8,0},{9,1},... | collective-permute-start | bytes 344072 | tf_op jit(solution)/shard_map/attend_sum_step_2/over_stage/ppermute | solution.py:483
  78.3 20.9 %collective-permute-start.40 = (bf16[256,512]{1,0:T(8,128)(2,1)S(1)}, bf16[256,512]{1,0:T(8,128)(2,1)S(1)}, u32[]{:S(2)}, u32[]{:S(2)}) collective-permute-start(bf16[256,512]{1,0:T(8,128)(2,1)S(1)} %slice_add_fusion.12), channel_id=1, source_target_pairs={{0,2},{1,3},{2,0},{3,1},{4,6},{5,7},{6,4},{7,5},{8,10},{9,11},{10,... | collective-permute-start | bytes 786440 | tf_op jit(solution)/shard_map/over_bit/ppermute | solution.py:483
  79.4 6.9 %collective-permute-start.32 = (bf16[80,512]{1,0:T(8,128)(2,1)S(1)}, bf16[80,512]{1,0:T(8,128)(2,1)S(1)}, u32[]{:S(2)}, u32[]{:S(2)}) collective-permute-start(bf16[80,512]{1,0:T(8,128)(2,1)S(1)} %fusion.5), channel_id=1, source_target_pairs={{0,16},{1,17},{2,18},{3,19},{4,20},{5,21},{6,22},{7,23},{8,24},{9,... | collective-permute-start | bytes 245768 | tf_op jit(solution)/shard_map/inner_sum_step_4/over_stage/ppermute | solution.py:483
  82.5 5.3 %collective-permute-start.35 = (bf16[48,512]{1,0:T(8,128)(2,1)S(1)}, bf16[48,512]{1,0:T(8,128)(2,1)S(1)}, u32[]{:S(2)}, u32[]{:S(2)}) collective-permute-start(bf16[48,512]{1,0:T(8,128)(2,1)S(1)} %slice_add_fusion.29), channel_id=1, source_target_pairs={{0,16},{1,17},{2,18},{3,19},{4,20},{5,21},{6,22},{7,23},{8,24},{9,... | collective-permute-start | bytes 147464 | tf_op jit(solution)/shard_map/joining_sum_step_3/over_stage/ppermute | solution.py:483
  82.6 4.3 %collective-permute-start.33 = (bf16[64,512]{1,0:T(8,128)(2,1)S(1)}, bf16[64,512]{1,0:T(8,128)(2,1)S(1)}, u32[]{:S(2)}, u32[]{:S(2)}) collective-permute-start(bf16[64,512]{1,0:T(8,128)(2,1)S(1)} %fusion.7), channel_id=1, source_target_pairs={{0,4},{1,3},{2,6},{3,1},{4,0},{5,7},{6,2},{7,5},{8,12},{9,11},{10,... | collective-permute-start | bytes 196616 | tf_op jit(solution)/shard_map/outer_sum_step_4/over_stage/ppermute | solution.py:483
  86.4 7.7 %collective-permute-start.37 = (bf16[160,512]{1,0:T(8,128)(2,1)S(1)}, bf16[160,512]{1,0:T(8,128)(2,1)S(1)}, u32[]{:S(2)}, u32[]{:S(2)}) collective-permute-start(bf16[160,512]{1,0:T(8,128)(2,1)S(1)} %pad_maximum_fusion.11), channel_id=1, source_target_pairs={{0,8},{1,9},{2,10},{3,11},{4,12},{5,13},{6,14},{7,15},{8,0},{9,1},... | collective-permute-start | bytes 491528 | tf_op jit(solution)/shard_map/inner_sum_step_5/over_stage/ppermute | solution.py:483
  87.9 5.6 %collective-permute-start.36 = (bf16[48,512]{1,0:T(8,128)(2,1)S(1)}, bf16[48,512]{1,0:T(8,128)(2,1)S(1)}, u32[]{:S(2)}, u32[]{:S(2)}) collective-permute-start(bf16[48,512]{1,0:T(8,128)(2,1)S(1)} %fusion.8), channel_id=1, source_target_pairs={{0,16},{1,17},{2,18},{3,19},{4,20},{5,21},{6,22},{7,23},{8,24},{9,... | collective-permute-start | bytes 147464 | tf_op jit(solution)/shard_map/joining_sum_step_4/over_stage/ppermute | solution.py:483
  90.1 6.1 %collective-permute-start.39 = (bf16[64,512]{1,0:T(8,128)(2,1)S(1)}, bf16[64,512]{1,0:T(8,128)(2,1)S(1)}, u32[]{:S(2)}, u32[]{:S(2)}) collective-permute-start(bf16[64,512]{1,0:T(8,128)(2,1)S(1)} %fusion.6), channel_id=1, source_target_pairs={{0,16},{1,17},{2,18},{3,19},{4,20},{5,21},{6,22},{7,23},{8,24},{9,... | collective-permute-start | bytes 196616 | tf_op jit(solution)/shard_map/attend_sum_step_3/over_stage/ppermute | solution.py:483
  90.9 5.0 %collective-permute-start.38 = (bf16[128,512]{1,0:T(8,128)(2,1)S(1)}, bf16[128,512]{1,0:T(8,128)(2,1)S(1)}, u32[]{:S(2)}, u32[]{:S(2)}) collective-permute-start(bf16[128,512]{1,0:T(8,128)(2,1)S(1)} %pad_maximum_fusion.12), channel_id=1, source_target_pairs={{0,2},{1,5},{2,0},{3,7},{4,6},{5,1},{6,4},{7,3},{8,10},{9,13},{10,... | collective-permute-start | bytes 393224 | tf_op jit(solution)/shard_map/outer_sum_step_5/over_stage/ppermute | solution.py:483
  93.5 8.2 %collective-permute-start.41 = (bf16[96,512]{1,0:T(8,128)(2,1)S(1)}, bf16[96,512]{1,0:T(8,128)(2,1)S(1)}, u32[]{:S(2)}, u32[]{:S(2)}) collective-permute-start(bf16[96,512]{1,0:T(8,128)(2,1)S(1)} %pad_maximum_fusion.14), channel_id=1, source_target_pairs={{0,8},{1,9},{2,10},{3,11},{4,12},{5,13},{6,14},{7,15},{8,0},{9,1},... | collective-permute-start | bytes 294920 | tf_op jit(solution)/shard_map/joining_sum_step_5/over_stage/ppermute | solution.py:483
  96.2 5.9 %collective-permute-start.42 = (bf16[48,512]{1,0:T(8,128)(2,1)S(1)}, bf16[48,512]{1,0:T(8,128)(2,1)S(1)}, u32[]{:S(2)}, u32[]{:S(2)}) collective-permute-start(bf16[48,512]{1,0:T(8,128)(2,1)S(1)} %slice.313), channel_id=1, source_target_pairs={{0,16},{1,17},{2,18},{3,19},{4,20},{5,21},{6,22},{7,23},{8,24},{9,... | collective-permute-start | bytes 147464 | tf_op jit(solution)/shard_map/attend_sum_step_4/over_stage/ppermute | solution.py:483
  98.1 10.3 %collective-permute-start.45 = (bf16[256,512]{1,0:T(8,128)(2,1)S(1)}, bf16[256,512]{1,0:T(8,128)(2,1)S(1)}, u32[]{:S(2)}, u32[]{:S(2)}) collective-permute-start(bf16[256,512]{1,0:T(8,128)(2,1)S(1)} %pad_maximum_fusion.6), channel_id=1, source_target_pairs={{0,16},{1,9},{2,18},{3,11},{4,20},{5,13},{6,22},{7,15},{8,24},{9,1... | collective-permute-start | bytes 786440 | tf_op jit(solution)/shard_map/outer_sum_step_6/over_stage/ppermute | solution.py:483
  99.2 7.1 %collective-permute-start.43 = (bf16[320,512]{1,0:T(8,128)(2,1)S(1)}, bf16[320,512]{1,0:T(8,128)(2,1)S(1)}, u32[]{:S(2)}, u32[]{:S(2)}) collective-permute-start(bf16[320,512]{1,0:T(8,128)(2,1)S(1)} %pad_maximum_fusion.5), channel_id=1, source_target_pairs={{0,4},{1,3},{2,6},{3,1},{4,0},{5,7},{6,2},{7,5},{8,12},{9,11},{10,... | collective-permute-start | bytes 983048 | tf_op jit(solution)/shard_map/inner_sum_step_6/over_stage/ppermute | solution.py:483
  101.7 6.7 %collective-permute-start.44 = (bf16[192,512]{1,0:T(8,128)(2,1)S(1)}, bf16[192,512]{1,0:T(8,128)(2,1)S(1)}, u32[]{:S(2)}, u32[]{:S(2)}) collective-permute-start(bf16[192,512]{1,0:T(8,128)(2,1)S(1)} %pad_maximum_fusion.9), channel_id=1, source_target_pairs={{0,4},{1,3},{2,6},{3,1},{4,0},{5,7},{6,2},{7,5},{8,12},{9,11},{10,... | collective-permute-start | bytes 589832 | tf_op jit(solution)/shard_map/joining_sum_step_6/over_stage/ppermute | solution.py:483
  108.5 4.2 %collective-permute-start.47 = (bf16[640,512]{1,0:T(8,128)(2,1)S(1)}, bf16[640,512]{1,0:T(8,128)(2,1)S(1)}, u32[]{:S(2)}, u32[]{:S(2)}) collective-permute-start(bf16[640,512]{1,0:T(8,128)(2,1)S(1)} %pad_maximum_fusion.rest_0_), channel_id=1, source_target_pairs={{0,1},{1,0},{2,3},{3,2},{4,5},{5,4},{6,7},{7,6},{8,9},{9,8},{10,11... | collective-permute-start | bytes 1966088 | tf_op jit(solution)/shard_map/inner_sum_sibling/over_bit/ppermute | solution.py:483
  108.5 10.7 %collective-permute-start.46 = (bf16[640,512]{1,0:T(8,128)(2,1)S(1)}, bf16[640,512]{1,0:T(8,128)(2,1)S(1)}, u32[]{:S(2)}, u32[]{:S(2)}) collective-permute-start(bf16[640,512]{1,0:T(8,128)(2,1)S(1)} %pad_maximum_fusion.rest_0_), channel_id=1, source_target_pairs={{0,2},{1,5},{2,0},{3,7},{4,6},{5,1},{6,4},{7,3},{8,10},{9,13},{10,... | collective-permute-start | bytes 1966088 | tf_op jit(solution)/shard_map/inner_sum_step_7/over_stage/ppermute | solution.py:483
  109.3 9.9 %collective-permute-start.48 = (bf16[96,512]{1,0:T(8,128)(2,1)S(1)}, bf16[96,512]{1,0:T(8,128)(2,1)S(1)}, u32[]{:S(2)}, u32[]{:S(2)}) collective-permute-start(bf16[96,512]{1,0:T(8,128)(2,1)S(1)} %pad_maximum_fusion.15), channel_id=1, source_target_pairs={{0,8},{1,9},{2,10},{3,11},{4,12},{5,13},{6,14},{7,15},{8,0},{9,1},... | collective-permute-start | bytes 294920 | tf_op jit(solution)/shard_map/attend_sum_step_5/over_stage/ppermute | solution.py:483
  110.1 14.3 %collective-permute-start.49 = (bf16[384,512]{1,0:T(8,128)(2,1)S(1)}, bf16[384,512]{1,0:T(8,128)(2,1)S(1)}, u32[]{:S(2)}, u32[]{:S(2)}) collective-permute-start(bf16[384,512]{1,0:T(8,128)(2,1)S(1)} %pad_maximum_fusion.3.rest_0_), channel_id=1, source_target_pairs={{0,2},{1,5},{2,0},{3,7},{4,6},{5,1},{6,4},{7,3},{8,10},{9,13},{10,... | collective-permute-start | bytes 1179656 | tf_op jit(solution)/shard_map/joining_sum_step_7/over_stage/ppermute | solution.py:483
  111.0 15.1 %collective-permute-start.52 = (bf16[512,512]{1,0:T(8,128)(2,1)S(1)}, bf16[512,512]{1,0:T(8,128)(2,1)S(1)}, u32[]{:S(2)}, u32[]{:S(2)}) collective-permute-start(bf16[512,512]{1,0:T(8,128)(2,1)S(1)} %pad_maximum_fusion.2.rest_0_), channel_id=1, source_target_pairs={{0,8},{1,17},{2,10},{3,19},{4,12},{5,21},{6,14},{7,23},{8,0},{9,25... | collective-permute-start | bytes 1572872 | tf_op jit(solution)/shard_map/outer_sum_step_7/over_stage/ppermute | solution.py:483
  112.7 13.5 %collective-permute-start.53 = (bf16[512,512]{1,0:T(8,128)(2,1)S(1)}, bf16[512,512]{1,0:T(8,128)(2,1)S(1)}, u32[]{:S(2)}, u32[]{:S(2)}) collective-permute-start(bf16[512,512]{1,0:T(8,128)(2,1)S(1)} %pad_maximum_fusion.2.rest_0_), channel_id=1, source_target_pairs={{0,1},{1,0},{2,3},{3,2},{4,5},{5,4},{6,7},{7,6},{8,9},{9,8},{10,11... | collective-permute-start | bytes 1572872 | tf_op jit(solution)/shard_map/outer_sum_sibling/over_bit/ppermute | solution.py:483
  119.2 5.2 %collective-permute-start.50 = (bf16[384,512]{1,0:T(8,128)(2,1)S(1)}, bf16[384,512]{1,0:T(8,128)(2,1)S(1)}, u32[]{:S(2)}, u32[]{:S(2)}) collective-permute-start(bf16[384,512]{1,0:T(8,128)(2,1)S(1)} %pad_maximum_fusion.3.rest_0_), channel_id=1, source_target_pairs={{0,1},{1,0},{2,3},{3,2},{4,5},{5,4},{6,7},{7,6},{8,9},{9,8},{10,11... | collective-permute-start | bytes 1179656 | tf_op jit(solution)/shard_map/joining_sum_sibling/over_bit/ppermute | solution.py:483
  119.2 5.8 %collective-permute-start.51 = (bf16[192,512]{1,0:T(8,128)(2,1)S(1)}, bf16[192,512]{1,0:T(8,128)(2,1)S(1)}, u32[]{:S(2)}, u32[]{:S(2)}) collective-permute-start(bf16[192,512]{1,0:T(8,128)(2,1)S(1)} %pad_maximum_fusion.10), channel_id=1, source_target_pairs={{0,4},{1,3},{2,6},{3,1},{4,0},{5,7},{6,2},{7,5},{8,12},{9,11},{10,... | collective-permute-start | bytes 589832 | tf_op jit(solution)/shard_map/attend_sum_step_6/over_stage/ppermute | solution.py:483
  124.4 3.0 %collective-permute-start.54 = (bf16[640,512]{1,0:T(8,128)(2,1)S(1)}, bf16[640,512]{1,0:T(8,128)(2,1)S(1)}, u32[]{:S(2)}, u32[]{:S(2)}) collective-permute-start(bf16[640,512]{1,0:T(8,128)(2,1)S(1)} %collective-permute-done.46.rest_1_), channel_id=1, source_target_pairs={{0,1},{1,0},{2,3},{3,2},{4,5},{5,4},{6,7},{7,6},{8,9},{9,8},{10,11... | collective-permute-start | bytes 1966088 | tf_op jit(solution)/shard_map/inner_sum_upper/over_bit/ppermute | solution.py:483
  126.2 3.8 %collective-permute-start.55 = (bf16[512,512]{1,0:T(8,128)(2,1)S(1)}, bf16[512,512]{1,0:T(8,128)(2,1)S(1)}, u32[]{:S(2)}, u32[]{:S(2)}) collective-permute-start(bf16[512,512]{1,0:T(8,128)(2,1)S(1)} %collective-permute-done.52.rest_1_), channel_id=1, source_target_pairs={{0,1},{1,0},{2,3},{3,2},{4,5},{5,4},{6,7},{7,6},{8,9},{9,8},{10,11... | collective-permute-start | bytes 1572872 | tf_op jit(solution)/shard_map/outer_sum_upper/over_bit/ppermute | solution.py:483
  126.2 6.1 %collective-permute-start.56 = (bf16[384,512]{1,0:T(8,128)(2,1)S(1)}, bf16[384,512]{1,0:T(8,128)(2,1)S(1)}, u32[]{:S(2)}, u32[]{:S(2)}) collective-permute-start(bf16[384,512]{1,0:T(8,128)(2,1)S(1)} %collective-permute-done.49.rest_1_), channel_id=1, source_target_pairs={{0,1},{1,0},{2,3},{3,2},{4,5},{5,4},{6,7},{7,6},{8,9},{9,8},{10,11... | collective-permute-start | bytes 1179656 | tf_op jit(solution)/shard_map/joining_sum_upper/over_bit/ppermute | solution.py:483
  126.7 7.8 %collective-permute-start.57 = (bf16[384,512]{1,0:T(8,128)(2,1)S(1)}, bf16[384,512]{1,0:T(8,128)(2,1)S(1)}, u32[]{:S(2)}, u32[]{:S(2)}) collective-permute-start(bf16[384,512]{1,0:T(8,128)(2,1)S(1)} %pad_maximum_fusion.4.rest_0_), channel_id=1, source_target_pairs={{0,2},{1,5},{2,0},{3,7},{4,6},{5,1},{6,4},{7,3},{8,10},{9,13},{10,... | collective-permute-start | bytes 1179656 | tf_op jit(solution)/shard_map/attend_sum_step_7/over_stage/ppermute | solution.py:483
  127.2 7.2 %collective-permute-start.58 = (bf16[384,512]{1,0:T(8,128)(2,1)S(1)}, bf16[384,512]{1,0:T(8,128)(2,1)S(1)}, u32[]{:S(2)}, u32[]{:S(2)}) collective-permute-start(bf16[384,512]{1,0:T(8,128)(2,1)S(1)} %pad_maximum_fusion.4.rest_0_), channel_id=1, source_target_pairs={{0,1},{1,0},{2,3},{3,2},{4,5},{5,4},{6,7},{7,6},{8,9},{9,8},{10,11... | collective-permute-start | bytes 1179656 | tf_op jit(solution)/shard_map/attend_sum_sibling/over_bit/ppermute | solution.py:483
  134.5 1.7 %collective-permute-start.59 = (bf16[384,512]{1,0:T(8,128)(2,1)S(1)}, bf16[384,512]{1,0:T(8,128)(2,1)S(1)}, u32[]{:S(2)}, u32[]{:S(2)}) collective-permute-start(bf16[384,512]{1,0:T(8,128)(2,1)S(1)} %collective-permute-done.57.rest_1_), channel_id=1, source_target_pairs={{0,1},{1,0},{2,3},{3,2},{4,5},{5,4},{6,7},{7,6},{8,9},{9,8},{10,11... | collective-permute-start | bytes 1179656 | tf_op jit(solution)/shard_map/attend_sum_upper/over_bit/ppermute | solution.py:483
  (12 other events, 79.9 us)
